TPU v7x, 768 devices: a whole 4x8x12 slice. The times are simulated.
768 devices in a mesh: node: 96 (over z, x, y_hi), local: 8 (over y_lo, core).
Axes of the slice: x: 4, y: 8 (y_hi: 2, y_lo: 4; y = y_hi * 4 + y_lo), z: 12, core: 2. Of those that a mesh axis runs over, the one named last changes fastest.
Arguments:
- hidden: bfloat16 [147456, 4608], P(('node', 'local')), may hold values from -24 to 24
- cotangent: bfloat16 [147456, 512], P(('node', 'local')), may hold values from -6 to 6
- quant_weight: bfloat16 [1152, 2048], P('node', 'local'), may hold values from -127 to 127
- scales: bfloat16 [1152], P('node'), may hold values from 9.9658966e-05 to 0.00039863586
Outputs:
- keys: bfloat16 [147456, 512], P(('node', 'local'))
- grad_input: bfloat16 [147456, 4608], P(('node', 'local'))
- weight_grad: float32 [1152, 2048], P('node', 'local')
All inputs are finite; a program needn't handle non-finite values.
Results may differ from a plain program's by a relative error of at most 0.015.
Values may be sent and summed in bfloat16 or wider, within the bound.
No kernel may reach another device: no remote copies, remote signals or barrier semaphores. Data moves between devices by JAX's collectives and lax.ppermute only.
A program may use at most 64 MiB of HBM per device.

v0:
```python
import math

import jax
import jax.numpy as jnp
from jax import lax
from jax.sharding import PartitionSpec as P


def on_device(hidden, cotangent, quant_weight, scales):
    rows_levels, rows_scales = (
        lax.all_gather(quant_weight, "node", axis=0, tiled=True),
        lax.all_gather(scales, "node", axis=0, tiled=True),
    )
    secondary = (rows_levels.astype(jnp.float32) * rows_scales.astype(jnp.float32)[:, None]).astype(
        jnp.bfloat16
    )
    blocks = lax.all_gather(secondary, "local", axis=1, tiled=True)
    n_blocks = blocks.shape[0]
    block_len = blocks.shape[1]
    weight = blocks.reshape(hidden.shape[1], cotangent.shape[1])
    keys = jnp.dot(hidden, weight, preferred_element_type=jnp.float32).astype(jnp.bfloat16)
    node_count = lax.axis_size("node")
    local_count = lax.axis_size("local")
    total_tokens = hidden.shape[0] * node_count * local_count
    factor = 1.0 / math.sqrt(total_tokens)
    grad_input = lax.dot_general(
        cotangent, weight, (((1,), (1,)), ((), ())), preferred_element_type=jnp.float32
    ).astype(jnp.bfloat16)
    term = lax.dot_general(
        hidden, cotangent, (((0,), (0,)), ((), ())), preferred_element_type=jnp.float32
    )
    rounded = term.astype(jnp.bfloat16).astype(jnp.float32).reshape(n_blocks, block_len)
    within = lax.psum_scatter(
        rounded.astype(jnp.bfloat16), "local", scatter_dimension=1, tiled=True
    ).astype(jnp.float32)
    across = lax.psum_scatter(within, "node", scatter_dimension=0, tiled=True)
    weight_grad = across * factor
    return (keys, grad_input, weight_grad)


def solution(mesh):
    return jax.shard_map(
        on_device,
        mesh=mesh,
        in_specs=(
            P(("node", "local"), None),
            P(("node", "local"), None),
            P("node", "local"),
            P("node"),
        ),
        out_specs=(P(("node", "local"), None), P(("node", "local"), None), P("node", "local")),
        check_vma=False,
    )
```

profile of v0, /device:TPU:6, one launch (start us, length us, event | category | flops | bytes accessed | tf_op | source)
XLA Modules:
  0.0 1163.5 jit_solution(3068883042361428310)
XLA Ops:
  7.2 0.0 copy-start
  7.2 0.0 reduce-scatter.4.cloned.1.call-start
  7.2 1.4 copy-done
  8.6 4.5 convolution_convert_fusion
  13.2 8.5 convert_element_type.40
  21.7 0.0 reduce-scatter.4.cloned.1.call-update
  21.7 0.0 all-gather.3.cloned.1.call-start
  21.8 1.4 fusion.3
  23.8 0.2 dynamic-update-slice
  24.1 330.4 %all-reduce = bf16[1152]{0:T(1024)(128)(2,1)S(1)} all-reduce(bf16[1152]{0:T(1024)(128)(2,1)S(1)} %dynamic-update-slice), channel_id=1, replica_groups=mesh['node'=96,'local'=8] {'node'}, use_global_device_ids=true, to_apply=%add | all-reduce | flops 1152 | bytes 4608
  354.4 338.2 %all-gather = bf16[96,12,256]{2,1,0:T(8,128)(2,1)} all-gather(bf16[1,12,256]{2,1,0:T(8,128)(2,1)S(1)} %bitcast.15), channel_id=1, replica_groups=mesh['node'=96,'local'=8] {'node'}, dimensions={0}, use_global_device_ids=true | all-gather | bytes 595968 | tf_op jit(solution)/shard_map/all_gather | solution.py:11
  692.6 1.2 reshape.18
  693.8 1.0 multiply_convert_fusion
  694.9 0.0 all-gather.3.cloned.1.call-update
  694.9 0.0 reduce-scatter.4.cloned.1.call-done
  694.9 1.1 convert_element_type.41
  696.1 340.1 %fusion = f32[16,256]{1,0:T(8,128)S(1)} fusion(f32[1152,256]{1,0:T(8,128)S(1)} %convert_element_type.41), kind=kCustom, calls=%all-reduce-scatter | all-reduce-scatter fusion | flops 393217 | bytes 1200128
  1036.2 3.3 collective-permute-start
  1039.4 1.9 collective-permute-start.1
  1041.4 1.3 collective-permute-start.10
  1042.7 11.1 collective-permute-start.23
  1053.8 8.0 collective-permute-start.11
  1061.8 9.7 collective-permute-start.12
  1071.5 1.3 collective-permute-start.13
  1072.7 0.0 collective-permute-done.1
  1072.8 7.2 collective-permute-start.14
  1080.0 8.1 collective-permute-start.15
  1088.1 5.6 collective-permute-start.16
  1093.7 2.0 collective-permute-start.17
  1095.7 1.9 collective-permute-start.18
  1097.7 3.2 collective-permute-start.19
  1100.9 5.3 collective-permute-start.2
  1106.8 0.0 all-gather.3.cloned.1.call-done
  1106.9 8.5 reshape.12
  1115.4 5.3 collective-permute-start.20
  1120.7 1.3 collective-permute-start.21
  1122.0 1.3 collective-permute-start.22
  1123.4 4.4 collective-permute-start.3
  1127.7 6.2 collective-permute-start.4
  1133.9 4.1 fusion.2
  1138.0 2.2 collective-permute-start.5
  1140.2 1.9 collective-permute-start.6
  1142.2 2.1 collective-permute-start.7
  1144.3 3.3 collective-permute-start.8
  1147.7 2.6 collective-permute-start.9
  1150.3 2.9 fusion.1
  1153.2 2.8 concatenate
  1156.0 0.6 dynamic-slice_multiply_fusion
  (34 shorter events, 0.1 us)
Async XLA Ops:
  7.2 1.5 copy-start
  7.2 687.7 %reduce-scatter.4.cloned.1.call-start = ((), (), s32[]{:S(2)}) async-start(), calls=%async_computation.2 | async-start | bytes 5308416 | tf_op jit(solution)/shard_map/reduce_scatter | solution.py:33
  21.7 2.1 copy-start.4
  21.7 332.7 %copy-start.3 = (bf16[12,256]{1,0:T(8,128)(2,1)S(1)}, bf16[12,256]{1,0:T(8,128)(2,1)}, u32[]{:S(2)}) copy-start(bf16[12,256]{1,0:T(8,128)(2,1)} %param.6) | copy-start | bytes 18436
  21.7 1085.1 %all-gather.3.cloned.1.call-start = ((), (), s32[]{:S(2)}) async-start(), calls=%async_computation.1 | async-start | bytes 5308416 | tf_op jit(solution)/shard_map/all_gather | solution.py:17
  1036.2 35.3 %collective-permute-start = (f32[16,256]{1,0:T(8,128)S(1)}, f32[16,256]{1,0:T(8,128)S(1)}, u32[]{:S(2)}, u32[]{:S(2)}) collective-permute-start(f32[16,256]{1,0:T(8,128)S(1)} %fusion), channel_id=1, source_target_pairs={{0,8},{8,16},{16,24},{24,32},{32,40},{40,48},{48,56},{56,64},{64,7... | collective-permute-start | bytes 49160
  1039.4 33.3 %collective-permute-start.1 = (f32[16,256]{1,0:T(8,128)S(1)}, f32[16,256]{1,0:T(8,128)S(1)}, u32[]{:S(2)}, u32[]{:S(2)}) collective-permute-start(f32[16,256]{1,0:T(8,128)S(1)} %fusion), channel_id=1, source_target_pairs={{0,16},{8,24},{16,32},{24,40},{32,48},{40,56},{48,64},{56,72},{64,... | collective-permute-start | bytes 49160
  1041.4 38.6 %collective-permute-start.10 = (f32[16,256]{1,0:T(8,128)S(1)}, f32[16,256]{1,0:T(8,128)S(1)}, u32[]{:S(2)}, u32[]{:S(2)}) collective-permute-start(f32[16,256]{1,0:T(8,128)S(1)} %fusion), channel_id=1, source_target_pairs={{0,88},{8,96},{16,104},{24,112},{32,120},{40,128},{48,136},{56,144... | collective-permute-start | bytes 49160
  1042.7 19.1 %collective-permute-start.23 = (f32[12,256]{1,0:T(8,128)S(1)}, f32[12,256]{1,0:T(8,128)S(1)}, u32[]{:S(2)}, u32[]{:S(2)}) collective-permute-start(f32[12,256]{1,0:T(8,128)S(1)} %slice), channel_id=1, source_target_pairs={{0,192},{8,200},{16,208},{24,216},{32,224},{40,232},{48,240},{56,2... | collective-permute-start | bytes 36872
  1053.8 34.3 %collective-permute-start.11 = (f32[16,256]{1,0:T(8,128)S(1)}, f32[16,256]{1,0:T(8,128)S(1)}, u32[]{:S(2)}, u32[]{:S(2)}) collective-permute-start(f32[16,256]{1,0:T(8,128)S(1)} %fusion), channel_id=1, source_target_pairs={{0,96},{8,104},{16,112},{24,120},{32,128},{40,136},{48,144},{56,15... | collective-permute-start | bytes 49160
  1061.8 32.0 %collective-permute-start.12 = (f32[16,256]{1,0:T(8,128)S(1)}, f32[16,256]{1,0:T(8,128)S(1)}, u32[]{:S(2)}, u32[]{:S(2)}) collective-permute-start(f32[16,256]{1,0:T(8,128)S(1)} %fusion), channel_id=1, source_target_pairs={{0,104},{8,112},{16,120},{24,128},{32,136},{40,144},{48,152},{56,1... | collective-permute-start | bytes 49160
  1071.5 24.3 %collective-permute-start.13 = (f32[16,256]{1,0:T(8,128)S(1)}, f32[16,256]{1,0:T(8,128)S(1)}, u32[]{:S(2)}, u32[]{:S(2)}) collective-permute-start(f32[16,256]{1,0:T(8,128)S(1)} %fusion), channel_id=1, source_target_pairs={{0,112},{8,120},{16,128},{24,136},{32,144},{40,152},{48,160},{56,1... | collective-permute-start | bytes 49160
  1072.8 24.9 %collective-permute-start.14 = (f32[16,256]{1,0:T(8,128)S(1)}, f32[16,256]{1,0:T(8,128)S(1)}, u32[]{:S(2)}, u32[]{:S(2)}) collective-permute-start(f32[16,256]{1,0:T(8,128)S(1)} %fusion), channel_id=1, source_target_pairs={{0,120},{8,128},{16,136},{24,144},{32,152},{40,160},{48,168},{56,1... | collective-permute-start | bytes 49160
  1080.0 20.9 %collective-permute-start.15 = (f32[16,256]{1,0:T(8,128)S(1)}, f32[16,256]{1,0:T(8,128)S(1)}, u32[]{:S(2)}, u32[]{:S(2)}) collective-permute-start(f32[16,256]{1,0:T(8,128)S(1)} %fusion), channel_id=1, source_target_pairs={{0,128},{8,136},{16,144},{24,152},{32,160},{40,168},{48,176},{56,1... | collective-permute-start | bytes 49160
  1088.1 27.3 %collective-permute-start.16 = (f32[16,256]{1,0:T(8,128)S(1)}, f32[16,256]{1,0:T(8,128)S(1)}, u32[]{:S(2)}, u32[]{:S(2)}) collective-permute-start(f32[16,256]{1,0:T(8,128)S(1)} %fusion), channel_id=1, source_target_pairs={{0,136},{8,144},{16,152},{24,160},{32,168},{40,176},{48,184},{56,1... | collective-permute-start | bytes 49160
  1093.7 26.9 %collective-permute-start.17 = (f32[16,256]{1,0:T(8,128)S(1)}, f32[16,256]{1,0:T(8,128)S(1)}, u32[]{:S(2)}, u32[]{:S(2)}) collective-permute-start(f32[16,256]{1,0:T(8,128)S(1)} %fusion), channel_id=1, source_target_pairs={{0,144},{8,152},{16,160},{24,168},{32,176},{40,184},{48,192},{56,2... | collective-permute-start | bytes 49160
  1095.7 26.3 %collective-permute-start.18 = (f32[16,256]{1,0:T(8,128)S(1)}, f32[16,256]{1,0:T(8,128)S(1)}, u32[]{:S(2)}, u32[]{:S(2)}) collective-permute-start(f32[16,256]{1,0:T(8,128)S(1)} %fusion), channel_id=1, source_target_pairs={{0,152},{8,160},{16,168},{24,176},{32,184},{40,192},{48,200},{56,2... | collective-permute-start | bytes 49160
  1097.7 25.7 %collective-permute-start.19 = (f32[16,256]{1,0:T(8,128)S(1)}, f32[16,256]{1,0:T(8,128)S(1)}, u32[]{:S(2)}, u32[]{:S(2)}) collective-permute-start(f32[16,256]{1,0:T(8,128)S(1)} %fusion), channel_id=1, source_target_pairs={{0,160},{8,168},{16,176},{24,184},{32,192},{40,200},{48,208},{56,2... | collective-permute-start | bytes 49160
  1100.9 26.9 %collective-permute-start.2 = (f32[16,256]{1,0:T(8,128)S(1)}, f32[16,256]{1,0:T(8,128)S(1)}, u32[]{:S(2)}, u32[]{:S(2)}) collective-permute-start(f32[16,256]{1,0:T(8,128)S(1)} %fusion), channel_id=1, source_target_pairs={{0,24},{8,32},{16,40},{24,48},{32,56},{40,64},{48,72},{56,80},{64,... | collective-permute-start | bytes 49160
  1115.4 34.9 %copy-start.1 = (bf16[4608,512]{1,0:T(8,128)(2,1)S(1)}, bf16[4608,512]{1,0:T(8,128)(2,1)}, u32[]{:S(2)}) copy-start(bf16[4608,512]{1,0:T(8,128)(2,1)} %reshape.12) | copy-start | bytes 14155780
  1115.4 34.9 %copy-start.2 = (bf16[192,512]{1,0:T(8,128)(2,1)S(1)}, bf16[192,512]{1,0:T(8,128)(2,1)}, u32[]{:S(2)}) copy-start(bf16[192,512]{1,0:T(8,128)(2,1)} %param.5) | copy-start | bytes 589828
  1115.4 22.6 %collective-permute-start.20 = (f32[16,256]{1,0:T(8,128)S(1)}, f32[16,256]{1,0:T(8,128)S(1)}, u32[]{:S(2)}, u32[]{:S(2)}) collective-permute-start(f32[16,256]{1,0:T(8,128)S(1)} %fusion), channel_id=1, source_target_pairs={{0,168},{8,176},{16,184},{24,192},{32,200},{40,208},{48,216},{56,2... | collective-permute-start | bytes 49160
  1120.7 19.5 %collective-permute-start.21 = (f32[16,256]{1,0:T(8,128)S(1)}, f32[16,256]{1,0:T(8,128)S(1)}, u32[]{:S(2)}, u32[]{:S(2)}) collective-permute-start(f32[16,256]{1,0:T(8,128)S(1)} %fusion), channel_id=1, source_target_pairs={{0,176},{8,184},{16,192},{24,200},{32,208},{40,216},{48,224},{56,2... | collective-permute-start | bytes 49160
  1122.0 20.1 %collective-permute-start.22 = (f32[16,256]{1,0:T(8,128)S(1)}, f32[16,256]{1,0:T(8,128)S(1)}, u32[]{:S(2)}, u32[]{:S(2)}) collective-permute-start(f32[16,256]{1,0:T(8,128)S(1)} %fusion), channel_id=1, source_target_pairs={{0,184},{8,192},{16,200},{24,208},{32,216},{40,224},{48,232},{56,2... | collective-permute-start | bytes 49160
  1123.4 20.9 %collective-permute-start.3 = (f32[16,256]{1,0:T(8,128)S(1)}, f32[16,256]{1,0:T(8,128)S(1)}, u32[]{:S(2)}, u32[]{:S(2)}) collective-permute-start(f32[16,256]{1,0:T(8,128)S(1)} %fusion), channel_id=1, source_target_pairs={{0,32},{8,40},{16,48},{24,56},{32,64},{40,72},{48,80},{56,88},{64,... | collective-permute-start | bytes 49160
  1127.7 19.9 %collective-permute-start.4 = (f32[16,256]{1,0:T(8,128)S(1)}, f32[16,256]{1,0:T(8,128)S(1)}, u32[]{:S(2)}, u32[]{:S(2)}) collective-permute-start(f32[16,256]{1,0:T(8,128)S(1)} %fusion), channel_id=1, source_target_pairs={{0,40},{8,48},{16,56},{24,64},{32,72},{40,80},{48,88},{56,96},{64,... | collective-permute-start | bytes 49160
  1138.0 15.2 %collective-permute-start.5 = (f32[16,256]{1,0:T(8,128)S(1)}, f32[16,256]{1,0:T(8,128)S(1)}, u32[]{:S(2)}, u32[]{:S(2)}) collective-permute-start(f32[16,256]{1,0:T(8,128)S(1)} %fusion), channel_id=1, source_target_pairs={{0,48},{8,56},{16,64},{24,72},{32,80},{40,88},{48,96},{56,104},{64... | collective-permute-start | bytes 49160
  1140.2 13.0 %collective-permute-start.6 = (f32[16,256]{1,0:T(8,128)S(1)}, f32[16,256]{1,0:T(8,128)S(1)}, u32[]{:S(2)}, u32[]{:S(2)}) collective-permute-start(f32[16,256]{1,0:T(8,128)S(1)} %fusion), channel_id=1, source_target_pairs={{0,56},{8,64},{16,72},{24,80},{32,88},{40,96},{48,104},{56,112},{6... | collective-permute-start | bytes 49160
  1142.2 11.1 collective-permute-start.7
  1144.3 8.9 collective-permute-start.8
  1147.7 5.6 collective-permute-start.9
Sparse Core Ops, SparseCore 0:
  21.8 74.7 reduce-scatter.3
  695.0 78.2 all-gather.2
where the time goes:
time: 1170 us; the launch traced here: 1160 us
  blocking collectives  1010 us (86%)
  starting transfers between devices  101 us (9%)
  local copies, waits for them, and re-layouts  24.1 us (2%)
  between operations  15.8 us (1%)
    unnamed x2, blocking collectives  670 us
    all_gather x1, blocking collectives, on_device(): lax.all_gather(quant_weight, 'node', axis=0, tiled=True)  338 us
    unnamed x24, starting transfers between devices  100 us
  transfers between devices with their start and end apart: 26, of which 0 were waited for; matrix products, arithmetic and copies ran while one was open for 31% of the time, Pallas kernels for 0%

commit v1 on v0

v1 whole, which is shorter than its diff:
```python
import math

import jax
import jax.numpy as jnp
import numpy as np
from jax import lax
from jax.experimental import pallas as pl
from jax.experimental.pallas import tpu as pltpu
from jax.sharding import Mesh
from jax.sharding import PartitionSpec as P

NZ, NX, NYH, NYL, NC = 12, 4, 2, 4, 2
NY = NYH * NYL
Y = ("yh", "yl")
ROWS = 12
HALF = 256
ZROWS = NX * NY * ROWS
XROWS = NY * ROWS

BF = jnp.bfloat16
F32 = jnp.float32

_x, _yh, _i, _yl = np.meshgrid(
    np.arange(NX), np.arange(NYH), np.arange(ROWS), np.arange(NYL), indexing="ij"
)
_natural = (((_x * NYH + _yh) * ROWS + _i) * NYL + _yl).ravel()
_gathered = (((_yh * NYL + _yl) * NX + _x) * ROWS + _i).ravel()
_scattered = (((_x * NYH + _yh) * NYL + _yl) * ROWS + _i).ravel()
TO_NATURAL = np.zeros((ZROWS, ZROWS), np.float32)
TO_NATURAL[_natural, _gathered] = 1
TO_SCATTER = np.zeros((ZROWS, ZROWS), np.float32)
TO_SCATTER[_scattered, _natural] = 1
ZG = 4
_z, _y, _i2 = np.meshgrid(np.arange(ZG), np.arange(NY), np.arange(ROWS), indexing="ij")
TO_Y = np.zeros((ZROWS, ZROWS), np.float32)
TO_Y[((_y * ZG + _z) * ROWS + _i2).ravel(), ((_z * NY + _y) * ROWS + _i2).ravel()] = 1


def term_kernel(core, mine, other, cot_mine, cot_other, perm, out):
    dims = (((0,), (0,)), ((), ()))
    term = lax.dot_general(mine[...], cot_mine[...], dims, preferred_element_type=F32)
    term += lax.dot_general(other[...], cot_other[...], dims, preferred_element_type=F32)
    moved = jnp.dot(perm[...], term.astype(BF), preferred_element_type=F32)
    out[...] = moved.astype(BF).reshape(out.shape)


def chip_term(core, mine, other, cot_mine, cot_other):
    tokens, width = mine.shape
    return pl.pallas_call(
        term_kernel,
        grid_spec=pltpu.PrefetchScalarGridSpec(
            num_scalar_prefetch=1,
            grid=(NZ,),
            in_specs=[
                pl.BlockSpec((tokens, ZROWS), lambda z, core: (0, z)),
                pl.BlockSpec((tokens, ZROWS), lambda z, core: (0, z)),
                pl.BlockSpec((tokens, HALF), lambda z, core: (0, core[0])),
                pl.BlockSpec((tokens, HALF), lambda z, core: (0, core[0])),
                pl.BlockSpec((ZROWS, ZROWS), lambda z, core: (0, 0)),
            ],
            out_specs=pl.BlockSpec((NX, 1, XROWS, HALF), lambda z, core: (0, z, 0, 0)),
        ),
        out_shape=jax.ShapeDtypeStruct((NX, NZ, XROWS, HALF), BF),
        cost_estimate=pl.CostEstimate(
            flops=2 * width * HALF * (2 * tokens + ZROWS),
            bytes_accessed=4 * tokens * width + 2 * width * HALF,
            transcendentals=0,
        ),
        name="chip_term",
    )(core, mine, other, cot_mine, cot_other, jnp.asarray(TO_SCATTER, BF))


def sum_kernel(parts, perm, out):
    total = parts[0].astype(F32)
    for k in range(1, NX):
        total += parts[k].astype(F32)
    rows = total.astype(BF).reshape(ZROWS, HALF)
    moved = jnp.dot(perm[...], rows, preferred_element_type=F32)
    out[...] = moved.astype(BF).reshape(out.shape)


def sum_over_x(parts):
    return pl.pallas_call(
        sum_kernel,
        grid=(NZ // ZG,),
        in_specs=[
            pl.BlockSpec((NX, ZG, XROWS, HALF), lambda g: (0, g, 0, 0)),
            pl.BlockSpec((ZROWS, ZROWS), lambda g: (0, 0)),
        ],
        out_specs=pl.BlockSpec((NY, ZG * ROWS, HALF), lambda g: (0, g, 0)),
        out_shape=jax.ShapeDtypeStruct((NY, NZ * ROWS, HALF), BF),
        cost_estimate=pl.CostEstimate(
            flops=2 * NZ // ZG * ZROWS * ZROWS * HALF,
            bytes_accessed=10 * NZ * XROWS * HALF,
            transcendentals=0,
        ),
        name="sum_over_x",
    )(parts, jnp.asarray(TO_Y, BF))


def project_kernel(core, mine, other, perm, hidden, cot_mine, cot_other, keys, grad, acc_mine, acc_other):
    z = pl.program_id(0)

    @pl.when(z == 0)
    def _():
        acc_mine[...] = jnp.zeros_like(acc_mine)
        acc_other[...] = jnp.zeros_like(acc_other)

    w_mine = jnp.dot(
        perm[...], mine[...].reshape(ZROWS, HALF), preferred_element_type=F32
    ).astype(BF)
    w_other = jnp.dot(
        perm[...], other[...].reshape(ZROWS, HALF), preferred_element_type=F32
    ).astype(BF)
    acc_mine[...] += jnp.dot(hidden[...], w_mine, preferred_element_type=F32)
    acc_other[...] += jnp.dot(hidden[...], w_other, preferred_element_type=F32)
    dims = (((1,), (1,)), ((), ()))
    g = lax.dot_general(cot_mine[...], w_mine, dims, preferred_element_type=F32)
    g += lax.dot_general(cot_other[...], w_other, dims, preferred_element_type=F32)
    grad[...] = g.astype(BF)

    @pl.when((z == NZ - 1) & (core[0] == 0))
    def _():
        keys[:, :HALF] = acc_mine[...].astype(BF)
        keys[:, HALF:] = acc_other[...].astype(BF)

    @pl.when((z == NZ - 1) & (core[0] == 1))
    def _():
        keys[:, :HALF] = acc_other[...].astype(BF)
        keys[:, HALF:] = acc_mine[...].astype(BF)


def project(core, mine, other, hidden, cotangent):
    tokens, width = hidden.shape
    block = pl.BlockSpec((NY, 1, NX * ROWS, HALF), lambda z, core: (0, z, 0, 0))
    return pl.pallas_call(
        project_kernel,
        grid_spec=pltpu.PrefetchScalarGridSpec(
            num_scalar_prefetch=1,
            grid=(NZ,),
            in_specs=[
                block,
                block,
                pl.BlockSpec((ZROWS, ZROWS), lambda z, core: (0, 0)),
                pl.BlockSpec((tokens, ZROWS), lambda z, core: (0, z)),
                pl.BlockSpec((tokens, HALF), lambda z, core: (0, core[0])),
                pl.BlockSpec((tokens, HALF), lambda z, core: (0, 1 - core[0])),
            ],
            out_specs=[
                pl.BlockSpec((tokens, 2 * HALF), lambda z, core: (0, 0)),
                pl.BlockSpec((tokens, ZROWS), lambda z, core: (0, z)),
            ],
            scratch_shapes=[pltpu.VMEM((tokens, HALF), F32), pltpu.VMEM((tokens, HALF), F32)],
        ),
        out_shape=[
            jax.ShapeDtypeStruct((tokens, 2 * HALF), BF),
            jax.ShapeDtypeStruct((tokens, width), BF),
        ],
        cost_estimate=pl.CostEstimate(
            flops=4 * width * HALF * (2 * tokens + ZROWS),
            bytes_accessed=4 * tokens * width + 4 * width * HALF,
            transcendentals=0,
        ),
        name="project",
    )(core, mine, other, jnp.asarray(TO_NATURAL, BF), hidden, cotangent, cotangent)


def to_all(piece, axis, count):
    return lax.all_to_all(
        jnp.broadcast_to(piece[None], (count, *piece.shape)), axis, split_axis=0, concat_axis=0, tiled=True
    )


def on_device(hidden, cotangent, quant_weight, scales):
    core = lax.axis_index("c").astype(jnp.int32).reshape(1)
    swap = [(0, 1), (1, 0)]
    factor = 1.0 / math.sqrt(hidden.shape[0] * NZ * NX * NY * NC)

    other_hidden = lax.ppermute(hidden, "c", swap)
    other_cot = lax.ppermute(cotangent, "c", swap)

    shard = (quant_weight.astype(F32) * scales.astype(F32)[:, None]).astype(BF)
    over_z = to_all(shard, "z", NZ)
    over_x = to_all(over_z, "x", NX)
    mine = lax.all_gather(
        over_x.transpose(1, 0, 2, 3).reshape(NZ * NX * ROWS, HALF), Y, axis=0, tiled=True
    ).reshape(NY, NZ, NX * ROWS, HALF)

    term = chip_term(core, hidden, other_hidden, cotangent, other_cot)
    over_x = lax.all_to_all(term, "x", split_axis=0, concat_axis=0, tiled=True)
    sum_x = sum_over_x(over_x)
    over_y = lax.all_to_all(sum_x, Y, split_axis=0, concat_axis=0, tiled=True)
    sum_y = over_y.astype(F32).sum(0).astype(BF).reshape(NZ, ROWS, HALF)
    over_z = lax.all_to_all(sum_y, "z", split_axis=0, concat_axis=0, tiled=True)
    weight_grad = over_z.astype(F32).sum(0) * factor

    other = lax.ppermute(mine, "c", swap)
    keys, grad_input = project(core, mine, other, hidden, cotangent)
    return keys, grad_input, weight_grad


def solution(mesh):
    fine = Mesh(mesh.devices.reshape(NZ, NX, NYH, NYL, NC), ("z", "x", "yh", "yl", "c"))
    node, local = ("z", "x", "yh"), ("yl", "c")
    return jax.shard_map(
        on_device,
        mesh=fine,
        in_specs=(P(node + local, None), P(node + local, None), P(node, local), P(node)),
        out_specs=(P(node + local, None), P(node + local, None), P(node, local)),
        check_vma=False,
    )
```

time: 1170 us -> 165 us (0.14)
  blocking collectives: 1010 us -> 75.9 us
  starting transfers between devices: 101 us -> 12 us
  Pallas kernels: 0 us -> 28.9 us
  waiting for transfers between devices: 0.14 us -> 27.3 us
  local copies, waits for them, and re-layouts: 24.1 us -> 3 us
    unnamed x2 -> x0, blocking collectives: 670 us -> none
    all_gather x1 -> x0, blocking collectives: 338 us -> none  [on_device(): lax.all_gather(quant_weight, 'node', axis=0, tiled=True)]
    unnamed x24 -> x0, starting transfers between devices: 100 us -> none
    all_to_all x0 -> x4, blocking collectives: none -> 75.9 us  [the longest x2 36.8 us: to_all(): lax.all_to_all(jnp.broadcast_to(piece[None], (count, *piece.shape)), axis...]
    pallas_call x0 -> x3, Pallas kernels: none -> 28.9 us  [the longest x1 13 us: project(): pl.pallas_call(project_kernel, grid_spec=pltpu.PrefetchScalarGridSpec(num...]
    all_gather x1, waiting for transfers between devices: 0.02 us -> 16.3 us  [on_device(): lax.all_gather(over_x.transpose(1, 0, 2, 3).reshape(NZ * NX * ROWS, HALF)...]
  transfers between devices with their start and end apart: 26 -> 5, of which waited for: 0 -> 3; matrix products, arithmetic and copies ran while one was open for 31% -> 0% of each run, Pallas kernels for 0% -> 10%
where the time goes in v1:
time: 165 us; the launch traced here: 163 us
  blocking collectives  75.9 us (46%)
  Pallas kernels  28.9 us (18%)
  waiting for transfers between devices  27.3 us (17%)
  between operations  14.1 us (9%)
  starting transfers between devices  12 us (7%)
  local copies, waits for them, and re-layouts  3 us (2%)
  other arithmetic  2.27 us (1%)
    all_to_all x2, blocking collectives, to_all(): lax.all_to_all(jnp.broadcast_to(piece[None], (count, *piece.shape)), axis...  36.8 us
    all_to_all x1, blocking collectives, on_device(): over_y = lax.all_to_all(sum_x, Y, split_axis=0, concat_axis=0, tiled=True)  25.5 us
    all_gather x1, waiting for transfers between devices, on_device(): lax.all_gather(over_x.transpose(1, 0, 2, 3).reshape(NZ * NX * ROWS, HALF)...  16.3 us
    all_to_all x1, blocking collectives, on_device(): over_z = lax.all_to_all(sum_y, 'z', split_axis=0, concat_axis=0, tiled=True)  13.6 us
    pallas_call x1, Pallas kernels, project(): pl.pallas_call(project_kernel, grid_spec=pltpu.PrefetchScalarGridSpec(num...  13 us
    pallas_call x1, Pallas kernels, chip_term(): pl.pallas_call(term_kernel, grid_spec=pltpu.PrefetchScalarGridSpec(num_sc...  12.1 us
    all_to_all x1, waiting for transfers between devices, on_device(): over_x = lax.all_to_all(term, 'x', split_axis=0, concat_axis=0, tiled=True)  9.4 us
    all_to_all x1, starting transfers between devices, on_device(): over_x = lax.all_to_all(term, 'x', split_axis=0, concat_axis=0, tiled=True)  5.68 us
  transfers between devices with their start and end apart: 5, of which 3 were waited for; matrix products, arithmetic and copies ran while one was open for 0% of the time, Pallas kernels for 10%

profile of v1, /device:TPU:6, one launch (start us, length us, event | category | flops | bytes accessed | tf_op | source)
XLA Modules:
  0.0 163.4 jit_solution(2344452113277121303)
XLA Ops:
  7.2 0.0 copy-start.1
  7.2 0.0 copy-start.2
  7.2 0.0 all-gather.2.cloned.1.call-start
  7.2 0.8 convert_element_type.15
  8.0 0.8 multiply_convert_fusion
  8.8 26.9 %all_to_all.25 = bf16[12,12,256]{2,1,0:T(8,128)(2,1)S(1)} all-to-all(bf16[12,12,256]{2,1,0:T(8,128)(2,1)S(1)} %broadcast_in_dim.4), channel_id=1, replica_groups=mesh['z'=12,'x'=4,'yh'=2,'yl'=4,'c'=2] {'z'}, dimensions={0} | all-to-all | bytes 147456 | tf_op jit(solution)/shard_map/all_to_all | solution.py:169
  35.8 9.9 %all_to_all.26 = bf16[4,12,12,256]{3,2,1,0:T(8,128)(2,1)S(1)} all-to-all(bf16[4,12,12,256]{3,2,1,0:T(8,128)(2,1)S(1)} %broadcast_in_dim.5), channel_id=1, replica_groups=mesh['z'=12,'x'=4,'yh'=2,'yl'=4,'c'=2] {'x'}, dimensions={0} | all-to-all | bytes 589824 | tf_op jit(solution)/shard_map/all_to_all | solution.py:169
  45.7 0.8 reshape.22
  46.5 0.0 all-gather.2.cloned.1.call-update
  46.5 0.0 copy-done.1
  46.5 1.9 %collective-permute-start.1 = (bf16[192,4608]{1,0:T(8,128)(2,1)S(1)}, bf16[192,4608]{1,0:T(8,128)(2,1)}, u32[]{:S(2)}, u32[]{:S(2)}) collective-permute-start(bf16[192,4608]{1,0:T(8,128)(2,1)S(1)} %copy-done.1), channel_id=1, source_target_pairs={{0,1},{1,0},{2,3},{3,2},{4,5},{5,4},{6,7},{7,6},{8,9},{9,8},{10,11... | collective-permute-start | bytes 5308424 | tf_op jit(solution)/shard_map/ppermute | solution.py:179
  48.4 0.0 copy-done.2
  48.4 2.4 %collective-permute-start.2 = (bf16[192,512]{1,0:T(8,128)(2,1)S(1)}, bf16[192,512]{1,0:T(8,128)(2,1)S(1)}, u32[]{:S(2)}, u32[]{:S(2)}) collective-permute-start(bf16[192,512]{1,0:T(8,128)(2,1)S(1)} %copy-done.2), channel_id=1, source_target_pairs={{0,1},{1,0},{2,3},{3,2},{4,5},{5,4},{6,7},{7,6},{8,9},{9,8},{10,11... | collective-permute-start | bytes 589832 | tf_op jit(solution)/shard_map/ppermute | solution.py:180
  50.9 1.5 collective-permute-done.2.cot_other
  52.4 0.0 copy-start.3
  52.4 0.0 collective-permute-done.1.other
  52.4 0.7 copy-done.3
  53.0 12.1 %chip_term.1 = bf16[4,12,96,256]{3,2,1,0:T(8,128)(2,1)} custom-call(s32[1]{0:T(128)} %bitcast.core, bf16[192,4608]{1,0:T(8,128)(2,1)} %mine.1, bf16[192,4608]{1,0:T(8,128)(2,1)} %collective-permute-done.1.other, bf16[192,512]{1,0:T(8,128)(2,1)} %cot_mine.3, bf16[192,512]{1,0:T(8,128)(2,1)} %copy-done.3, bf16[384,384]{1,0:T(8,128)(2,1)} %constant.16.clone.perm), custom_call_target="tpu_custom_call" | custom-call | flops 1811939328 | bytes 5898240 | tf_op jit(solution)/shard_map/chip_term/pallas_call | solution.py:49
  65.1 5.7 %all-to-all-start.2 = ((bf16[4,12,96,256]{3,2,1,0:T(8,128)(2,1)}), bf16[4,12,96,256]{3,2,1,0:T(8,128)(2,1)S(1)}, u32[]{:S(2)}, u32[]{:S(2)}) async-start(bf16[4,12,96,256]{3,2,1,0:T(8,128)(2,1)} %chip_term.1), calls=%async_computation.2 | async-start | bytes 4718592 | tf_op jit(solution)/shard_map/all_to_all | solution.py:190
  70.8 16.3 %all-gather.2.cloned.1.call-done = bf16[4608,256]{1,0:T(8,128)(2,1)} async-done(((bf16[576,256]{1,0:T(8,128)(2,1)}), bf16[4608,256]{1,0:T(8,128)(2,1)}) %all-gather.2.cloned.1.call-update) | async-done | bytes 2359312 | tf_op jit(solution)/shard_map/all_gather | solution.py:185
  87.2 1.9 %collective-permute-start = (bf16[8,12,48,256]{3,2,1,0:T(8,128)(2,1)}, bf16[8,12,48,256]{3,2,1,0:T(8,128)(2,1)}, u32[]{:S(2)}, u32[]{:S(2)}) collective-permute-start(bf16[8,12,48,256]{3,2,1,0:T(8,128)(2,1)} %bitcast.4), channel_id=1, source_target_pairs={{0,1},{1,0},{2,3},{3,2},{4,5},{5,4},{6,7},{7,6},{8,9},{9,8},{10,11... | collective-permute-start | bytes 7077896 | tf_op jit(solution)/shard_map/ppermute | solution.py:197
  89.1 9.4 %all-to-all-done.2.parts = bf16[4,12,96,256]{3,2,1,0:T(8,128)(2,1)S(1)} async-done(((bf16[4,12,96,256]{3,2,1,0:T(8,128)(2,1)}), bf16[4,12,96,256]{3,2,1,0:T(8,128)(2,1)S(1)}, u32[]{:S(2)}, u32[]{:S(2)}) %all-to-all-start.2) | async-done | bytes 2359328 | tf_op jit(solution)/shard_map/all_to_all | solution.py:190
  98.5 0.0 copy-start
  98.5 1.4 copy-done
  99.9 3.7 %sum_over_x.1 = bf16[8,144,256]{2,1,0:T(8,128)(2,1)} custom-call(bf16[4,12,96,256]{3,2,1,0:T(8,128)(2,1)} %copy-done, bf16[384,384]{1,0:T(8,128)(2,1)} %constant.17.clone.perm), custom_call_target="tpu_custom_call" | custom-call | flops 226492416 | bytes 2949120 | tf_op jit(solution)/shard_map/sum_over_x/pallas_call | solution.py:83
  103.7 25.5 %all_to_all.27 = bf16[8,144,256]{2,1,0:T(8,128)(2,1)S(1)} all-to-all(bf16[8,144,256]{2,1,0:T(8,128)(2,1)} %sum_over_x.1), channel_id=1, replica_groups=mesh['z'=12,'x'=4,'yh'=2,'yl'=4,'c'=2] {'yh','yl'}, dimensions={0} | all-to-all | bytes 1179648 | tf_op jit(solution)/shard_map/all_to_all | solution.py:192
  129.1 0.1 reduce_sum.21
  129.3 13.6 %all_to_all.28 = bf16[12,12,256]{2,1,0:T(8,128)(2,1)S(1)} all-to-all(bf16[12,12,256]{2,1,0:T(8,128)(2,1)S(1)} %reshape.24), channel_id=1, replica_groups=mesh['z'=12,'x'=4,'yh'=2,'yl'=4,'c'=2] {'z'}, dimensions={0} | all-to-all | bytes 147456 | tf_op jit(solution)/shard_map/all_to_all | solution.py:194
  142.9 0.6 broadcast_multiply_fusion
  143.5 0.0 collective-permute-done.other
  143.5 13.0 %project.1 = (bf16[192,512]{1,0:T(8,128)(2,1)}, bf16[192,4608]{1,0:T(8,128)(2,1)}) custom-call(s32[1]{0:T(128)} %bitcast.core, bf16[8,12,48,256]{3,2,1,0:T(8,128)(2,1)} %bitcast.5, bf16[8,12,48,256]{3,2,1,0:T(8,128)(2,1)} %collective-permute-done.other, bf16[384,384]{1,0:T(8,128)(2,1)} %constant.18.clone.perm, bf16[192,4608]{1,0:T(8,128)(2,1)} %mine.1, ...), custom_call_target="tpu_custom_call" | custom-call | flops 3623878656 | bytes 8257536 | tf_op jit(solution)/shard_map/project/pallas_call | solution.py:136
  (5 shorter events, 0.1 us)
Async XLA Ops:
  7.2 39.3 %copy-start.1 = (bf16[192,4608]{1,0:T(8,128)(2,1)S(1)}, bf16[192,4608]{1,0:T(8,128)(2,1)}, u32[]{:S(2)}) copy-start(bf16[192,4608]{1,0:T(8,128)(2,1)} %mine.1) | copy-start | bytes 5308420
  7.2 41.2 %copy-start.2 = (bf16[192,512]{1,0:T(8,128)(2,1)S(1)}, bf16[192,512]{1,0:T(8,128)(2,1)}, u32[]{:S(2)}) copy-start(bf16[192,512]{1,0:T(8,128)(2,1)} %cot_mine.3) | copy-start | bytes 589828
  7.2 80.0 %all-gather.2.cloned.1.call-start = ((), (), s32[]{:S(2)}) async-start(), calls=%async_computation.5 | async-start | bytes 2654208 | tf_op jit(solution)/shard_map/all_gather | solution.py:185
  46.5 5.9 %collective-permute-start.1 = (bf16[192,4608]{1,0:T(8,128)(2,1)S(1)}, bf16[192,4608]{1,0:T(8,128)(2,1)}, u32[]{:S(2)}, u32[]{:S(2)}) collective-permute-start(bf16[192,4608]{1,0:T(8,128)(2,1)S(1)} %copy-done.1), channel_id=1, source_target_pairs={{0,1},{1,0},{2,3},{3,2},{4,5},{5,4},{6,7},{7,6},{8,9},{9,8},{10,11... | collective-permute-start | bytes 5308424 | tf_op jit(solution)/shard_map/ppermute | solution.py:179
  48.4 3.9 %collective-permute-start.2 = (bf16[192,512]{1,0:T(8,128)(2,1)S(1)}, bf16[192,512]{1,0:T(8,128)(2,1)S(1)}, u32[]{:S(2)}, u32[]{:S(2)}) collective-permute-start(bf16[192,512]{1,0:T(8,128)(2,1)S(1)} %copy-done.2), channel_id=1, source_target_pairs={{0,1},{1,0},{2,3},{3,2},{4,5},{5,4},{6,7},{7,6},{8,9},{9,8},{10,11... | collective-permute-start | bytes 589832 | tf_op jit(solution)/shard_map/ppermute | solution.py:180
  52.4 0.7 copy-start.3
  65.1 33.3 %all-to-all-start.2 = ((bf16[4,12,96,256]{3,2,1,0:T(8,128)(2,1)}), bf16[4,12,96,256]{3,2,1,0:T(8,128)(2,1)S(1)}, u32[]{:S(2)}, u32[]{:S(2)}) async-start(bf16[4,12,96,256]{3,2,1,0:T(8,128)(2,1)} %chip_term.1), calls=%async_computation.2 | async-start | bytes 4718592 | tf_op jit(solution)/shard_map/all_to_all | solution.py:190
  87.2 56.3 %collective-permute-start = (bf16[8,12,48,256]{3,2,1,0:T(8,128)(2,1)}, bf16[8,12,48,256]{3,2,1,0:T(8,128)(2,1)}, u32[]{:S(2)}, u32[]{:S(2)}) collective-permute-start(bf16[8,12,48,256]{3,2,1,0:T(8,128)(2,1)} %bitcast.4), channel_id=1, source_target_pairs={{0,1},{1,0},{2,3},{3,2},{4,5},{5,4},{6,7},{7,6},{8,9},{9,8},{10,11... | collective-permute-start | bytes 7077896 | tf_op jit(solution)/shard_map/ppermute | solution.py:197
  98.5 1.4 copy-start
Sparse Core Ops, SparseCore 0:
  46.6 40.5 all-gather.1

commit v2 on v1

v2 whole, which is shorter than its diff:
```python
import math

import jax
import jax.numpy as jnp
import numpy as np
from jax import lax
from jax.experimental import pallas as pl
from jax.experimental.pallas import tpu as pltpu
from jax.sharding import Mesh
from jax.sharding import PartitionSpec as P

NZ, NX, NYH, NYL, NC = 12, 4, 2, 4, 2
NY = NYH * NYL
Y = ("yh", "yl")
ROWS = 12
HALF = 256
ZROWS = NX * NY * ROWS
XROWS = NY * ROWS

BF = jnp.bfloat16
F32 = jnp.float32

_x, _yh, _i, _yl = np.meshgrid(
    np.arange(NX), np.arange(NYH), np.arange(ROWS), np.arange(NYL), indexing="ij"
)
_natural = (((_x * NYH + _yh) * ROWS + _i) * NYL + _yl).ravel()
TO_SEND = np.zeros((NX, ZROWS, ZROWS), np.float32)
FROM_HELD = np.zeros((NX, ZROWS, ZROWS), np.float32)
for _me in range(NX):
    _rest = (_yh * NYL + _yl) * ROWS + _i
    TO_SEND[_me, ((_x - _me) % NX * XROWS + _rest).ravel(), _natural] = 1
    FROM_HELD[_me, _natural, ((_me - _x) % NX * XROWS + _rest).ravel()] = 1
ZG = 4
_z, _y, _i2 = np.meshgrid(np.arange(ZG), np.arange(NY), np.arange(ROWS), indexing="ij")
TO_Y = np.zeros((ZROWS, ZROWS), np.float32)
TO_Y[((_y * ZG + _z) * ROWS + _i2).ravel(), ((_z * NY + _y) * ROWS + _i2).ravel()] = 1
FROM_Y = TO_Y.T
ZSTEP = 3


def term_kernel(place, mine, other, cot_mine, cot_other, perm, *rest):
    *outs, flipped = rest
    tokens = mine.shape[0]

    @pl.when(pl.program_id(0) == 0)
    def _():
        flipped[:, :tokens] = cot_mine[...].T
        flipped[:, tokens:] = cot_other[...].T

    for k in range(ZSTEP):
        cols = slice(k * ZROWS, (k + 1) * ZROWS)
        rows = jnp.concatenate([mine[:, cols], other[:, cols]], axis=0)
        term = jnp.dot(flipped[...], rows, preferred_element_type=F32).astype(BF)
        moved = lax.dot_general(
            perm[0], term, (((1,), (1,)), ((), ())), preferred_element_type=F32
        ).astype(BF)
        for r in range(NX):
            outs[r][k] = moved[r * XROWS : (r + 1) * XROWS]


def chip_term(place, mine, other, cot_mine, cot_other):
    tokens, width = mine.shape
    wide = pl.BlockSpec((tokens, ZSTEP * ZROWS), lambda z, place: (0, z))
    half = pl.BlockSpec((tokens, HALF), lambda z, place: (0, place[0]))
    return pl.pallas_call(
        term_kernel,
        grid_spec=pltpu.PrefetchScalarGridSpec(
            num_scalar_prefetch=1,
            grid=(NZ // ZSTEP,),
            in_specs=[
                wide,
                wide,
                half,
                half,
                pl.BlockSpec((1, ZROWS, ZROWS), lambda z, place: (place[1], 0, 0)),
            ],
            out_specs=[pl.BlockSpec((ZSTEP, XROWS, HALF), lambda z, place: (z, 0, 0))] * NX,
            scratch_shapes=[pltpu.VMEM((HALF, 2 * tokens), BF)],
        ),
        out_shape=[jax.ShapeDtypeStruct((NZ, XROWS, HALF), BF)] * NX,
        compiler_params=pltpu.CompilerParams(vmem_limit_bytes=56 * 2**20),
        cost_estimate=pl.CostEstimate(
            flops=2 * width * HALF * (2 * tokens + ZROWS),
            bytes_accessed=4 * tokens * width + 2 * width * HALF,
            transcendentals=0,
        ),
        name="chip_term",
    )(place, mine, other, cot_mine, cot_other, jnp.asarray(TO_SEND, BF))


def sum_kernel(*refs):
    *parts, perm, _, out = refs
    total = parts[0][...].astype(F32)
    for part in parts[1:]:
        total += part[...].astype(F32)
    rows = total.astype(BF).reshape(ZROWS, HALF)
    moved = jnp.dot(perm[...], rows, preferred_element_type=F32)
    out[...] = moved.astype(BF).reshape(out.shape)


def sum_over_x(parts, first):
    return pl.pallas_call(
        sum_kernel,
        grid=(NZ // ZG,),
        in_specs=[pl.BlockSpec((ZG, XROWS, HALF), lambda g: (g, 0, 0))] * NX
        + [pl.BlockSpec((ZROWS, ZROWS), lambda g: (0, 0)), pl.BlockSpec(memory_space=pl.ANY)],
        out_specs=pl.BlockSpec((NY, ZG * ROWS, HALF), lambda g: (0, g, 0)),
        out_shape=jax.ShapeDtypeStruct((NY, NZ * ROWS, HALF), BF),
        compiler_params=pltpu.CompilerParams(vmem_limit_bytes=12 * 2**20),
        cost_estimate=pl.CostEstimate(
            flops=2 * NZ // ZG * ZROWS * ZROWS * HALF,
            bytes_accessed=10 * NZ * XROWS * HALF,
            transcendentals=0,
        ),
        name="sum_over_x",
    )(*parts, jnp.asarray(TO_Y, BF), first)


def regroup_kernel(parts, perm, out):
    rows = parts[...].reshape(ZROWS, HALF)
    out[...] = jnp.dot(perm[...], rows, preferred_element_type=F32).astype(BF).reshape(out.shape)


def regroup(parts):
    return pl.pallas_call(
        regroup_kernel,
        grid=(NZ // ZG,),
        in_specs=[
            pl.BlockSpec((NY, ZG * ROWS, HALF), lambda g: (0, g, 0)),
            pl.BlockSpec((ZROWS, ZROWS), lambda g: (0, 0)),
        ],
        out_specs=pl.BlockSpec((ZG, XROWS, HALF), lambda g: (g, 0, 0)),
        out_shape=jax.ShapeDtypeStruct((NZ, XROWS, HALF), BF),
        compiler_params=pltpu.CompilerParams(vmem_limit_bytes=12 * 2**20),
        cost_estimate=pl.CostEstimate(
            flops=2 * NZ // ZG * ZROWS * ZROWS * HALF,
            bytes_accessed=4 * NZ * XROWS * HALF,
            transcendentals=0,
        ),
        name="regroup",
    )(parts, jnp.asarray(FROM_Y, BF))


def project_kernel(place, *refs):
    *blocks, perm, hidden, cot_mine, cot_other, keys, grad, acc, cot = refs
    step = pl.program_id(0)

    @pl.when(step == 0)
    def _():
        cot[:, :HALF] = cot_mine[...]
        cot[:, HALF:] = cot_other[...]
        acc[...] = jnp.zeros_like(acc)

    total = acc[...]
    for k in range(ZSTEP):
        cols = slice(k * ZROWS, (k + 1) * ZROWS)
        held = jnp.concatenate(
            [jnp.concatenate([b[k] for b in blocks[s : s + NX]], axis=0) for s in (0, NX)], axis=1
        )
        weight = jnp.dot(perm[0], held, preferred_element_type=F32).astype(BF)
        total += jnp.dot(hidden[:, cols], weight, preferred_element_type=F32)
        grad[:, cols] = lax.dot_general(
            cot[...], weight, (((1,), (1,)), ((), ())), preferred_element_type=F32
        ).astype(BF)
    acc[...] = total

    @pl.when((step == NZ // ZSTEP - 1) & (place[0] == 0))
    def _():
        keys[...] = acc[...].astype(BF)

    @pl.when((step == NZ // ZSTEP - 1) & (place[0] == 1))
    def _():
        keys[:, :HALF] = acc[:, HALF:].astype(BF)
        keys[:, HALF:] = acc[:, :HALF].astype(BF)


def project(place, mine, other, hidden, cotangent):
    tokens, width = hidden.shape
    block = pl.BlockSpec((ZSTEP, XROWS, HALF), lambda z, place: (z, 0, 0))
    wide = pl.BlockSpec((tokens, ZSTEP * ZROWS), lambda z, place: (0, z))
    return pl.pallas_call(
        project_kernel,
        grid_spec=pltpu.PrefetchScalarGridSpec(
            num_scalar_prefetch=1,
            grid=(NZ // ZSTEP,),
            in_specs=[block] * (2 * NX)
            + [
                pl.BlockSpec((1, ZROWS, ZROWS), lambda z, place: (place[1], 0, 0)),
                wide,
                pl.BlockSpec((tokens, HALF), lambda z, place: (0, place[0])),
                pl.BlockSpec((tokens, HALF), lambda z, place: (0, 1 - place[0])),
            ],
            out_specs=[pl.BlockSpec((tokens, 2 * HALF), lambda z, place: (0, 0)), wide],
            scratch_shapes=[
                pltpu.VMEM((tokens, 2 * HALF), F32),
                pltpu.VMEM((tokens, 2 * HALF), BF),
            ],
        ),
        out_shape=[
            jax.ShapeDtypeStruct((tokens, 2 * HALF), BF),
            jax.ShapeDtypeStruct((tokens, width), BF),
        ],
        compiler_params=pltpu.CompilerParams(vmem_limit_bytes=56 * 2**20),
        cost_estimate=pl.CostEstimate(
            flops=4 * width * HALF * (2 * tokens + ZROWS),
            bytes_accessed=4 * tokens * width + 4 * width * HALF,
            transcendentals=0,
        ),
        name="project",
    )(place, *mine, *other, jnp.asarray(FROM_HELD, BF), hidden, cotangent, cotangent)


def to_all(piece, axis, count):
    copies = jnp.broadcast_to(piece[None], (count, *piece.shape))
    return lax.all_to_all(copies, axis, split_axis=0, concat_axis=0, tiled=True)


def shift(piece, r):
    return lax.ppermute(piece, "x", [(k, (k + r) % NX) for k in range(NX)])


def swap(piece):
    return lax.ppermute(piece, "c", [(0, 1), (1, 0)])


def on_device(hidden, cotangent, quant_weight, scales):
    place = jnp.stack([lax.axis_index("c"), lax.axis_index("x")]).astype(jnp.int32)
    factor = 1.0 / math.sqrt(hidden.shape[0] * NZ * NX * NY * NC)

    other_hidden = swap(hidden)
    other_cot = swap(cotangent)

    shard = (quant_weight.astype(F32) * scales.astype(F32)[:, None]).astype(BF)
    w_z = to_all(shard, "z", NZ)

    terms = chip_term(place, hidden, other_hidden, cotangent, other_cot)
    w_z, terms = lax.optimization_barrier((w_z, terms))
    t_x = [terms[0]] + [shift(terms[r], r) for r in range(1, NX)]
    w_y = regroup(to_all(w_z.reshape(NZ * ROWS, HALF), Y, NY))

    mine = [w_y] + [shift(w_y, r) for r in range(1, NX)]
    other = [swap(piece) for piece in mine]
    sum_x = sum_over_x(t_x, w_y)
    t_y = lax.all_to_all(sum_x, Y, split_axis=0, concat_axis=0, tiled=True)
    sum_y = t_y.astype(F32).sum(0).astype(BF).reshape(NZ, ROWS, HALF)
    t_z = lax.all_to_all(sum_y, "z", split_axis=0, concat_axis=0, tiled=True)
    weight_grad = t_z.astype(F32).sum(0) * factor
    keys, grad_input = project(place, mine, other, hidden, cotangent)
    return keys, grad_input, weight_grad


def solution(mesh):
    fine = Mesh(mesh.devices.reshape(NZ, NX, NYH, NYL, NC), ("z", "x", "yh", "yl", "c"))
    node, local = ("z", "x", "yh"), ("yl", "c")
    return jax.shard_map(
        on_device,
        mesh=fine,
        in_specs=(P(node + local, None), P(node + local, None), P(node, local), P(node)),
        out_specs=(P(node + local, None), P(node + local, None), P(node, local)),
        check_vma=False,
    )
```

time: 165 us -> 126 us (0.76)
  blocking collectives: 75.9 us -> 0 us
  starting transfers between devices: 12 us -> 68.8 us
  between operations: 14.1 us -> 0.87 us
  Pallas kernels: 28.9 us -> 21.2 us
  local copies, waits for them, and re-layouts: 3 us -> 7.18 us
  waiting for transfers between devices: 27.3 us -> 24.3 us
    all_to_all x4 -> x0, blocking collectives: 75.9 us -> none  [the longest x2 36.8 us: to_all(): lax.all_to_all(jnp.broadcast_to(piece[None], (count, *piece.shape)), axis...]
    all_to_all x1 -> x4, starting transfers between devices: 5.68 us -> 37.3 us  [the longest x2 22.3 us: to_all(): return lax.all_to_all(copies, axis, split_axis=0, concat_axis=0, tiled=True)]
    ppermute x3 -> x12, starting transfers between devices: 6.24 us -> 31.5 us  [the longest x6 19 us: shift(): return lax.ppermute(piece, 'x', [(k, (k + r) % NX) for k in range(NX)])]
    all_gather x1 -> x0, waiting for transfers between devices: 16.3 us -> none  [on_device(): lax.all_gather(over_x.transpose(1, 0, 2, 3).reshape(NZ * NX * ROWS, HALF)...]
    ppermute x3 -> x12, waiting for transfers between devices: 1.51 us -> 10.5 us  [the longest x6 10.5 us: shift(): return lax.ppermute(piece, 'x', [(k, (k + r) % NX) for k in range(NX)])]
    all_to_all x1 -> x4, waiting for transfers between devices: 9.4 us -> 13.8 us  [the longest x2 8.43 us: to_all(): return lax.all_to_all(copies, axis, split_axis=0, concat_axis=0, tiled=True)]
    pallas_call x1, Pallas kernels: 12.1 us -> 7.77 us  [chip_term(): pl.pallas_call(term_kernel, grid_spec=pltpu.PrefetchScalarGridSpec(num_sc...]
    unnamed x8 -> x18, local copies, waits for them, and re-layouts: 2.13 us -> 5 us
  transfers between devices with their start and end apart: 5 -> 16, of which waited for: 3 -> 6; matrix products, arithmetic and copies ran while one was open for 0% -> 3% of each run, Pallas kernels for 10% -> 17%
where the time goes in v2:
time: 126 us; the launch traced here: 125 us
  starting transfers between devices  68.8 us (55%)
  waiting for transfers between devices  24.3 us (19%)
  Pallas kernels  21.2 us (17%)
  local copies, waits for them, and re-layouts  7.18 us (6%)
  other arithmetic  2.75 us (2%)
    all_to_all x2, starting transfers between devices, to_all(): return lax.all_to_all(copies, axis, split_axis=0, concat_axis=0, tiled=True)  22.3 us
    ppermute x6, starting transfers between devices, shift(): return lax.ppermute(piece, 'x', [(k, (k + r) % NX) for k in range(NX)])  19 us
    ppermute x6, starting transfers between devices, swap(): return lax.ppermute(piece, 'c', [(0, 1), (1, 0)])  12.5 us
    pallas_call x1, Pallas kernels, project(): pl.pallas_call(project_kernel, grid_spec=pltpu.PrefetchScalarGridSpec(num...  10.6 us
    ppermute x6, waiting for transfers between devices, shift(): return lax.ppermute(piece, 'x', [(k, (k + r) % NX) for k in range(NX)])  10.5 us
    all_to_all x2, waiting for transfers between devices, to_all(): return lax.all_to_all(copies, axis, split_axis=0, concat_axis=0, tiled=True)  8.43 us
    all_to_all x1, starting transfers between devices, on_device(): t_z = lax.all_to_all(sum_y, 'z', split_axis=0, concat_axis=0, tiled=True)  7.82 us
    pallas_call x1, Pallas kernels, chip_term(): pl.pallas_call(term_kernel, grid_spec=pltpu.PrefetchScalarGridSpec(num_sc...  7.77 us
  transfers between devices with their start and end apart: 16, of which 6 were waited for; matrix products, arithmetic and copies ran while one was open for 3% of the time, Pallas kernels for 17%

profile of v2, /device:TPU:6, one launch (start us, length us, event | category | flops | bytes accessed | tf_op | source)
XLA Modules:
  0.0 125.2 jit_solution(2608324136707840845)
XLA Ops:
  0.6 1.9 %collective-permute-start = (bf16[192,4608]{1,0:T(8,128)(2,1)}, bf16[192,4608]{1,0:T(8,128)(2,1)S(1)}, u32[]{:S(2)}, u32[]{:S(2)}) collective-permute-start(bf16[192,4608]{1,0:T(8,128)(2,1)} %refs_9_.1), channel_id=1, source_target_pairs={{0,1},{1,0},{2,3},{3,2},{4,5},{5,4},{6,7},{7,6},{8,9},{9,8},{10,11... | collective-permute-start | bytes 5308424 | tf_op jit(solution)/shard_map/ppermute | solution.py:223
  2.6 2.4 %collective-permute-start.1 = (bf16[192,512]{1,0:T(8,128)(2,1)}, bf16[192,512]{1,0:T(8,128)(2,1)S(1)}, u32[]{:S(2)}, u32[]{:S(2)}) collective-permute-start(bf16[192,512]{1,0:T(8,128)(2,1)} %refs_11_.1), channel_id=1, source_target_pairs={{0,1},{1,0},{2,3},{3,2},{4,5},{5,4},{6,7},{7,6},{8,9},{9,8},{10,11... | collective-permute-start | bytes 589832 | tf_op jit(solution)/shard_map/ppermute | solution.py:223
  5.0 0.7 convert_element_type.15
  5.6 0.8 multiply_convert_fusion
  6.4 0.6 broadcast_in_dim.6
  7.0 15.2 %all-to-all-start = ((bf16[12,12,256]{2,1,0:T(8,128)(2,1)}), bf16[12,12,256]{2,1,0:T(8,128)(2,1)S(1)}, u32[]{:S(2)}, u32[]{:S(2)}) async-start(bf16[12,12,256]{2,1,0:T(8,128)(2,1)} %broadcast_in_dim.6), calls=%async_computation | async-start | bytes 196608 | tf_op jit(solution)/shard_map/all_to_all | solution.py:215
  22.2 0.6 pad_add_fusion.place
  22.8 0.0 collective-permute-done.1.cot_other
  22.8 0.0 collective-permute-done.other
  22.8 0.7 copy-done.8
  23.5 1.2 copy-done.4
  24.7 7.8 %chip_term.1 = (bf16[12,96,256]{2,1,0:T(8,128)(2,1)}, bf16[12,96,256]{2,1,0:T(8,128)(2,1)}, bf16[12,96,256]{2,1,0:T(8,128)(2,1)}, bf16[12,96,256]{2,1,0:T(8,128)(2,1)}) custom-call(s32[2]{0:T(128)} %pad_add_fusion.place, bf16[192,4608]{1,0:T(8,128)(2,1)} %refs_9_.1, bf16[192,4608]{1,0:T(8,128)(2,1)} %copy-done.4, bf16[192,512]{1,0:T(8,128)(2,1)} %refs_11_.1, ...), custom_call_target="tpu_custom_call" | custom-call | flops 1811939328 | bytes 5898240 | tf_op jit(solution)/shard_map/chip_term/pallas_call | solution.py:65
  32.5 1.8 %all-to-all-done = bf16[12,12,256]{2,1,0:T(8,128)(2,1)S(1)} async-done(((bf16[12,12,256]{2,1,0:T(8,128)(2,1)}), bf16[12,12,256]{2,1,0:T(8,128)(2,1)S(1)}, u32[]{:S(2)}, u32[]{:S(2)}) %all-to-all-start) | async-done | bytes 73760 | tf_op jit(solution)/shard_map/all_to_all | solution.py:215
  34.3 0.9 broadcast_in_dim.16
  35.2 7.1 %all-to-all-start.1 = ((bf16[8,144,256]{2,1,0:T(8,128)(2,1)}), bf16[8,144,256]{2,1,0:T(8,128)(2,1)S(1)}, u32[]{:S(2)}, u32[]{:S(2)}) async-start(bf16[8,144,256]{2,1,0:T(8,128)(2,1)} %broadcast_in_dim.16), calls=%async_computation.1 | async-start | bytes 1179648 | tf_op jit(solution)/shard_map/all_to_all | solution.py:215
  42.3 3.3 %collective-permute-start.10 = (bf16[12,96,256]{2,1,0:T(8,128)(2,1)}, bf16[12,96,256]{2,1,0:T(8,128)(2,1)S(1)}, u32[]{:S(2)}, u32[]{:S(2)}) collective-permute-start(bf16[12,96,256]{2,1,0:T(8,128)(2,1)} %get-tuple-element.23), channel_id=1, source_target_pairs={{0,32},{16,48},{32,0},{48,16},{1,33},{17,49},{33,1},{49,17},{2,34}... | collective-permute-start | bytes 1769480 | tf_op jit(solution)/shard_map/ppermute | solution.py:219
  45.6 1.9 %collective-permute-start.11 = (bf16[12,96,256]{2,1,0:T(8,128)(2,1)}, bf16[12,96,256]{2,1,0:T(8,128)(2,1)S(1)}, u32[]{:S(2)}, u32[]{:S(2)}) collective-permute-start(bf16[12,96,256]{2,1,0:T(8,128)(2,1)} %get-tuple-element.24), channel_id=1, source_target_pairs={{0,48},{16,0},{32,16},{48,32},{1,49},{17,1},{33,17},{49,33},{2,50}... | collective-permute-start | bytes 1769480 | tf_op jit(solution)/shard_map/ppermute | solution.py:219
  47.5 5.1 %collective-permute-start.9 = (bf16[12,96,256]{2,1,0:T(8,128)(2,1)}, bf16[12,96,256]{2,1,0:T(8,128)(2,1)S(1)}, u32[]{:S(2)}, u32[]{:S(2)}) collective-permute-start(bf16[12,96,256]{2,1,0:T(8,128)(2,1)} %get-tuple-element.22), channel_id=1, source_target_pairs={{0,16},{16,32},{32,48},{48,0},{1,17},{17,33},{33,49},{49,1},{2,18}... | collective-permute-start | bytes 1769480 | tf_op jit(solution)/shard_map/ppermute | solution.py:219
  52.6 6.6 %all-to-all-done.1.parts = bf16[8,144,256]{2,1,0:T(8,128)(2,1)S(1)} async-done(((bf16[8,144,256]{2,1,0:T(8,128)(2,1)}), bf16[8,144,256]{2,1,0:T(8,128)(2,1)S(1)}, u32[]{:S(2)}, u32[]{:S(2)}) %all-to-all-start.1) | async-done | bytes 589856 | tf_op jit(solution)/shard_map/all_to_all | solution.py:215
  59.3 1.0 copy-done.2
  60.2 0.9 regroup.1.refs_0_.refs_5_
  61.1 2.4 %collective-permute-start.2 = (bf16[12,96,256]{2,1,0:T(8,128)(2,1)S(1)}, bf16[12,96,256]{2,1,0:T(8,128)(2,1)}, u32[]{:S(2)}, u32[]{:S(2)}) collective-permute-start(bf16[12,96,256]{2,1,0:T(8,128)(2,1)S(1)} %regroup.1.refs_0_.refs_5_), channel_id=1, source_target_pairs={{0,16},{16,32},{32,48},{48,0},{1,17},{17,33},{33,49},{49,1},{2,18}... | collective-permute-start | bytes 1769480 | tf_op jit(solution)/shard_map/ppermute | solution.py:219
  63.5 4.3 %collective-permute-start.3 = (bf16[12,96,256]{2,1,0:T(8,128)(2,1)S(1)}, bf16[12,96,256]{2,1,0:T(8,128)(2,1)}, u32[]{:S(2)}, u32[]{:S(2)}) collective-permute-start(bf16[12,96,256]{2,1,0:T(8,128)(2,1)S(1)} %regroup.1.refs_0_.refs_5_), channel_id=1, source_target_pairs={{0,32},{16,48},{32,0},{48,16},{1,33},{17,49},{33,1},{49,17},{2,34}... | collective-permute-start | bytes 1769480 | tf_op jit(solution)/shard_map/ppermute | solution.py:219
  67.9 0.0 collective-permute-done.10.refs_2_
  67.9 1.9 %collective-permute-start.4 = (bf16[12,96,256]{2,1,0:T(8,128)(2,1)S(1)}, bf16[12,96,256]{2,1,0:T(8,128)(2,1)}, u32[]{:S(2)}, u32[]{:S(2)}) collective-permute-start(bf16[12,96,256]{2,1,0:T(8,128)(2,1)S(1)} %regroup.1.refs_0_.refs_5_), channel_id=1, source_target_pairs={{0,48},{16,0},{32,16},{48,32},{1,49},{17,1},{33,17},{49,33},{2,50}... | collective-permute-start | bytes 1769480 | tf_op jit(solution)/shard_map/ppermute | solution.py:219
  69.8 5.1 %collective-permute-done.11.refs_3_ = bf16[12,96,256]{2,1,0:T(8,128)(2,1)S(1)} collective-permute-done((bf16[12,96,256]{2,1,0:T(8,128)(2,1)}, bf16[12,96,256]{2,1,0:T(8,128)(2,1)S(1)}, u32[]{:S(2)}, u32[]{:S(2)}) %collective-permute-start.11) | collective-permute-done | bytes 589856 | tf_op jit(solution)/shard_map/ppermute | solution.py:219
  74.9 0.0 collective-permute-done.9.refs_1_
  74.9 1.0 copy-done.3
  75.8 2.0 %sum_over_x.1 = bf16[8,144,256]{2,1,0:T(8,128)(2,1)} custom-call(bf16[12,96,256]{2,1,0:T(8,128)(2,1)S(1)} %copy-done.1, bf16[12,96,256]{2,1,0:T(8,128)(2,1)S(1)} %collective-permute-done.9.refs_1_, bf16[12,96,256]{2,1,0:T(8,128)(2,1)S(1)} %collective-permute-done.10.refs_2_, bf16[12,96,256]{2,1,0:T(8,128)(2,1)S(1)} %collective-permute-done.11.refs_3_, ...), custom_call_target="tpu_custom_call" | custom-call | flops 226492416 | bytes 2949120 | tf_op jit(solution)/shard_map/sum_over_x/pallas_call | solution.py:102
  77.8 7.2 %all-to-all-start.2 = ((bf16[8,144,256]{2,1,0:T(8,128)(2,1)}), bf16[8,144,256]{2,1,0:T(8,128)(2,1)S(1)}, u32[]{:S(2)}, u32[]{:S(2)}) async-start(bf16[8,144,256]{2,1,0:T(8,128)(2,1)} %sum_over_x.1), calls=%async_computation.2 | async-start | bytes 1179648 | tf_op jit(solution)/shard_map/all_to_all | solution.py:244
  85.1 1.9 %collective-permute-start.5 = (bf16[12,96,256]{2,1,0:T(8,128)(2,1)S(1)}, bf16[12,96,256]{2,1,0:T(8,128)(2,1)S(1)}, u32[]{:S(2)}, u32[]{:S(2)}) collective-permute-start(bf16[12,96,256]{2,1,0:T(8,128)(2,1)S(1)} %regroup.1.refs_0_.refs_5_), channel_id=1, source_target_pairs={{0,1},{1,0},{2,3},{3,2},{4,5},{5,4},{6,7},{7,6},{8,9},{9,8},{10,11... | collective-permute-start | bytes 1769480 | tf_op jit(solution)/shard_map/ppermute | solution.py:223
  87.0 0.0 collective-permute-done.2.refs_1_
  87.0 2.4 %collective-permute-start.6 = (bf16[12,96,256]{2,1,0:T(8,128)(2,1)}, bf16[12,96,256]{2,1,0:T(8,128)(2,1)S(1)}, u32[]{:S(2)}, u32[]{:S(2)}) collective-permute-start(bf16[12,96,256]{2,1,0:T(8,128)(2,1)} %collective-permute-done.2.refs_1_), channel_id=1, source_target_pairs={{0,1},{1,0},{2,3},{3,2},{4,5},{5,4},{6,7},{7,6},{8,9},{9,8},{10,11... | collective-permute-start | bytes 1769480 | tf_op jit(solution)/shard_map/ppermute | solution.py:223
  89.4 0.0 collective-permute-done.3.refs_2_
  89.4 1.9 %collective-permute-start.7 = (bf16[12,96,256]{2,1,0:T(8,128)(2,1)}, bf16[12,96,256]{2,1,0:T(8,128)(2,1)S(1)}, u32[]{:S(2)}, u32[]{:S(2)}) collective-permute-start(bf16[12,96,256]{2,1,0:T(8,128)(2,1)} %collective-permute-done.3.refs_2_), channel_id=1, source_target_pairs={{0,1},{1,0},{2,3},{3,2},{4,5},{5,4},{6,7},{7,6},{8,9},{9,8},{10,11... | collective-permute-start | bytes 1769480 | tf_op jit(solution)/shard_map/ppermute | solution.py:223
  91.3 5.4 %collective-permute-done.4.refs_3_ = bf16[12,96,256]{2,1,0:T(8,128)(2,1)} collective-permute-done((bf16[12,96,256]{2,1,0:T(8,128)(2,1)S(1)}, bf16[12,96,256]{2,1,0:T(8,128)(2,1)}, u32[]{:S(2)}, u32[]{:S(2)}) %collective-permute-start.4) | collective-permute-done | bytes 589856 | tf_op jit(solution)/shard_map/ppermute | solution.py:219
  96.8 1.9 %collective-permute-start.8 = (bf16[12,96,256]{2,1,0:T(8,128)(2,1)}, bf16[12,96,256]{2,1,0:T(8,128)(2,1)}, u32[]{:S(2)}, u32[]{:S(2)}) collective-permute-start(bf16[12,96,256]{2,1,0:T(8,128)(2,1)} %collective-permute-done.4.refs_3_), channel_id=1, source_target_pairs={{0,1},{1,0},{2,3},{3,2},{4,5},{5,4},{6,7},{7,6},{8,9},{9,8},{10,11... | collective-permute-start | bytes 1769480 | tf_op jit(solution)/shard_map/ppermute | solution.py:223
  98.7 5.2 %all-to-all-done.2 = bf16[8,144,256]{2,1,0:T(8,128)(2,1)S(1)} async-done(((bf16[8,144,256]{2,1,0:T(8,128)(2,1)}), bf16[8,144,256]{2,1,0:T(8,128)(2,1)S(1)}, u32[]{:S(2)}, u32[]{:S(2)}) %all-to-all-start.2) | async-done | bytes 589856 | tf_op jit(solution)/shard_map/all_to_all | solution.py:244
  103.9 0.1 reduce_sum.21
  104.0 0.7 reshape.12
  104.6 7.8 %all-to-all-start.3 = ((bf16[12,12,256]{2,1,0:T(8,128)(2,1)}), bf16[12,12,256]{2,1,0:T(8,128)(2,1)S(1)}, u32[]{:S(2)}, u32[]{:S(2)}) async-start(bf16[12,12,256]{2,1,0:T(8,128)(2,1)} %reshape.12), calls=%async_computation.3 | async-start | bytes 196608 | tf_op jit(solution)/shard_map/all_to_all | solution.py:246
  112.5 0.0 collective-permute-done.5.refs_4_
  112.5 0.8 copy-done.5
  113.3 0.2 copy-done.6
  113.5 0.2 copy-done.7
  113.7 10.6 %project.1 = (bf16[192,512]{1,0:T(8,128)(2,1)}, bf16[192,4608]{1,0:T(8,128)(2,1)}) custom-call(s32[2]{0:T(128)} %pad_add_fusion.place, bf16[12,96,256]{2,1,0:T(8,128)(2,1)} %copy-done, bf16[12,96,256]{2,1,0:T(8,128)(2,1)} %collective-permute-done.2.refs_1_, bf16[12,96,256]{2,1,0:T(8,128)(2,1)} %collective-permute-done.3.refs_2_, ...), custom_call_target="tpu_custom_call" | custom-call | flops 3623878656 | bytes 8257536 | tf_op jit(solution)/shard_map/project/pallas_call | solution.py:181
  124.3 0.2 all-to-all-done.3
  124.6 0.6 broadcast_multiply_fusion
  (16 shorter events, 0.1 us)
Async XLA Ops:
  0.6 22.2 %collective-permute-start = (bf16[192,4608]{1,0:T(8,128)(2,1)}, bf16[192,4608]{1,0:T(8,128)(2,1)S(1)}, u32[]{:S(2)}, u32[]{:S(2)}) collective-permute-start(bf16[192,4608]{1,0:T(8,128)(2,1)} %refs_9_.1), channel_id=1, source_target_pairs={{0,1},{1,0},{2,3},{3,2},{4,5},{5,4},{6,7},{7,6},{8,9},{9,8},{10,11... | collective-permute-start | bytes 5308424 | tf_op jit(solution)/shard_map/ppermute | solution.py:223
  2.6 20.3 %collective-permute-start.1 = (bf16[192,512]{1,0:T(8,128)(2,1)}, bf16[192,512]{1,0:T(8,128)(2,1)S(1)}, u32[]{:S(2)}, u32[]{:S(2)}) collective-permute-start(bf16[192,512]{1,0:T(8,128)(2,1)} %refs_11_.1), channel_id=1, source_target_pairs={{0,1},{1,0},{2,3},{3,2},{4,5},{5,4},{6,7},{7,6},{8,9},{9,8},{10,11... | collective-permute-start | bytes 589832 | tf_op jit(solution)/shard_map/ppermute | solution.py:223
  7.0 27.2 %all-to-all-start = ((bf16[12,12,256]{2,1,0:T(8,128)(2,1)}), bf16[12,12,256]{2,1,0:T(8,128)(2,1)S(1)}, u32[]{:S(2)}, u32[]{:S(2)}) async-start(bf16[12,12,256]{2,1,0:T(8,128)(2,1)} %broadcast_in_dim.6), calls=%async_computation | async-start | bytes 196608 | tf_op jit(solution)/shard_map/all_to_all | solution.py:215
  22.8 0.7 copy-start.8
  23.5 1.2 copy-start.4
  32.5 42.4 %copy-start.1 = (bf16[12,96,256]{2,1,0:T(8,128)(2,1)S(1)}, bf16[12,96,256]{2,1,0:T(8,128)(2,1)}, u32[]{:S(2)}) copy-start(bf16[12,96,256]{2,1,0:T(8,128)(2,1)} %get-tuple-element.21.refs_0_) | copy-start | bytes 1769476
  35.2 24.1 %all-to-all-start.1 = ((bf16[8,144,256]{2,1,0:T(8,128)(2,1)}), bf16[8,144,256]{2,1,0:T(8,128)(2,1)S(1)}, u32[]{:S(2)}, u32[]{:S(2)}) async-start(bf16[8,144,256]{2,1,0:T(8,128)(2,1)} %broadcast_in_dim.16), calls=%async_computation.1 | async-start | bytes 1179648 | tf_op jit(solution)/shard_map/all_to_all | solution.py:215
  42.3 25.6 %collective-permute-start.10 = (bf16[12,96,256]{2,1,0:T(8,128)(2,1)}, bf16[12,96,256]{2,1,0:T(8,128)(2,1)S(1)}, u32[]{:S(2)}, u32[]{:S(2)}) collective-permute-start(bf16[12,96,256]{2,1,0:T(8,128)(2,1)} %get-tuple-element.23), channel_id=1, source_target_pairs={{0,32},{16,48},{32,0},{48,16},{1,33},{17,49},{33,1},{49,17},{2,34}... | collective-permute-start | bytes 1769480 | tf_op jit(solution)/shard_map/ppermute | solution.py:219
  45.6 29.3 %collective-permute-start.11 = (bf16[12,96,256]{2,1,0:T(8,128)(2,1)}, bf16[12,96,256]{2,1,0:T(8,128)(2,1)S(1)}, u32[]{:S(2)}, u32[]{:S(2)}) collective-permute-start(bf16[12,96,256]{2,1,0:T(8,128)(2,1)} %get-tuple-element.24), channel_id=1, source_target_pairs={{0,48},{16,0},{32,16},{48,32},{1,49},{17,1},{33,17},{49,33},{2,50}... | collective-permute-start | bytes 1769480 | tf_op jit(solution)/shard_map/ppermute | solution.py:219
  47.5 27.4 %collective-permute-start.9 = (bf16[12,96,256]{2,1,0:T(8,128)(2,1)}, bf16[12,96,256]{2,1,0:T(8,128)(2,1)S(1)}, u32[]{:S(2)}, u32[]{:S(2)}) collective-permute-start(bf16[12,96,256]{2,1,0:T(8,128)(2,1)} %get-tuple-element.22), channel_id=1, source_target_pairs={{0,16},{16,32},{32,48},{48,0},{1,17},{17,33},{33,49},{49,1},{2,18}... | collective-permute-start | bytes 1769480 | tf_op jit(solution)/shard_map/ppermute | solution.py:219
  59.3 1.0 copy-start.2
  61.1 23.9 %copy-start = (bf16[12,96,256]{2,1,0:T(8,128)(2,1)}, bf16[12,96,256]{2,1,0:T(8,128)(2,1)S(1)}, u32[]{:S(2)}) copy-start(bf16[12,96,256]{2,1,0:T(8,128)(2,1)S(1)} %regroup.1.refs_0_.refs_5_) | copy-start | bytes 1769476
  61.1 25.9 %collective-permute-start.2 = (bf16[12,96,256]{2,1,0:T(8,128)(2,1)S(1)}, bf16[12,96,256]{2,1,0:T(8,128)(2,1)}, u32[]{:S(2)}, u32[]{:S(2)}) collective-permute-start(bf16[12,96,256]{2,1,0:T(8,128)(2,1)S(1)} %regroup.1.refs_0_.refs_5_), channel_id=1, source_target_pairs={{0,16},{16,32},{32,48},{48,0},{1,17},{17,33},{33,49},{49,1},{2,18}... | collective-permute-start | bytes 1769480 | tf_op jit(solution)/shard_map/ppermute | solution.py:219
  63.5 25.9 %collective-permute-start.3 = (bf16[12,96,256]{2,1,0:T(8,128)(2,1)S(1)}, bf16[12,96,256]{2,1,0:T(8,128)(2,1)}, u32[]{:S(2)}, u32[]{:S(2)}) collective-permute-start(bf16[12,96,256]{2,1,0:T(8,128)(2,1)S(1)} %regroup.1.refs_0_.refs_5_), channel_id=1, source_target_pairs={{0,32},{16,48},{32,0},{48,16},{1,33},{17,49},{33,1},{49,17},{2,34}... | collective-permute-start | bytes 1769480 | tf_op jit(solution)/shard_map/ppermute | solution.py:219
  67.9 28.9 %collective-permute-start.4 = (bf16[12,96,256]{2,1,0:T(8,128)(2,1)S(1)}, bf16[12,96,256]{2,1,0:T(8,128)(2,1)}, u32[]{:S(2)}, u32[]{:S(2)}) collective-permute-start(bf16[12,96,256]{2,1,0:T(8,128)(2,1)S(1)} %regroup.1.refs_0_.refs_5_), channel_id=1, source_target_pairs={{0,48},{16,0},{32,16},{48,32},{1,49},{17,1},{33,17},{49,33},{2,50}... | collective-permute-start | bytes 1769480 | tf_op jit(solution)/shard_map/ppermute | solution.py:219
  74.9 1.0 copy-start.3
  77.8 26.0 %all-to-all-start.2 = ((bf16[8,144,256]{2,1,0:T(8,128)(2,1)}), bf16[8,144,256]{2,1,0:T(8,128)(2,1)S(1)}, u32[]{:S(2)}, u32[]{:S(2)}) async-start(bf16[8,144,256]{2,1,0:T(8,128)(2,1)} %sum_over_x.1), calls=%async_computation.2 | async-start | bytes 1179648 | tf_op jit(solution)/shard_map/all_to_all | solution.py:244
  85.1 27.4 %collective-permute-start.5 = (bf16[12,96,256]{2,1,0:T(8,128)(2,1)S(1)}, bf16[12,96,256]{2,1,0:T(8,128)(2,1)S(1)}, u32[]{:S(2)}, u32[]{:S(2)}) collective-permute-start(bf16[12,96,256]{2,1,0:T(8,128)(2,1)S(1)} %regroup.1.refs_0_.refs_5_), channel_id=1, source_target_pairs={{0,1},{1,0},{2,3},{3,2},{4,5},{5,4},{6,7},{7,6},{8,9},{9,8},{10,11... | collective-permute-start | bytes 1769480 | tf_op jit(solution)/shard_map/ppermute | solution.py:223
  87.0 25.5 %collective-permute-start.6 = (bf16[12,96,256]{2,1,0:T(8,128)(2,1)}, bf16[12,96,256]{2,1,0:T(8,128)(2,1)S(1)}, u32[]{:S(2)}, u32[]{:S(2)}) collective-permute-start(bf16[12,96,256]{2,1,0:T(8,128)(2,1)} %collective-permute-done.2.refs_1_), channel_id=1, source_target_pairs={{0,1},{1,0},{2,3},{3,2},{4,5},{5,4},{6,7},{7,6},{8,9},{9,8},{10,11... | collective-permute-start | bytes 1769480 | tf_op jit(solution)/shard_map/ppermute | solution.py:223
  89.4 23.1 %collective-permute-start.7 = (bf16[12,96,256]{2,1,0:T(8,128)(2,1)}, bf16[12,96,256]{2,1,0:T(8,128)(2,1)S(1)}, u32[]{:S(2)}, u32[]{:S(2)}) collective-permute-start(bf16[12,96,256]{2,1,0:T(8,128)(2,1)} %collective-permute-done.3.refs_2_), channel_id=1, source_target_pairs={{0,1},{1,0},{2,3},{3,2},{4,5},{5,4},{6,7},{7,6},{8,9},{9,8},{10,11... | collective-permute-start | bytes 1769480 | tf_op jit(solution)/shard_map/ppermute | solution.py:223
  96.8 15.7 %collective-permute-start.8 = (bf16[12,96,256]{2,1,0:T(8,128)(2,1)}, bf16[12,96,256]{2,1,0:T(8,128)(2,1)}, u32[]{:S(2)}, u32[]{:S(2)}) collective-permute-start(bf16[12,96,256]{2,1,0:T(8,128)(2,1)} %collective-permute-done.4.refs_3_), channel_id=1, source_target_pairs={{0,1},{1,0},{2,3},{3,2},{4,5},{5,4},{6,7},{7,6},{8,9},{9,8},{10,11... | collective-permute-start | bytes 1769480 | tf_op jit(solution)/shard_map/ppermute | solution.py:223
  104.6 19.9 %all-to-all-start.3 = ((bf16[12,12,256]{2,1,0:T(8,128)(2,1)}), bf16[12,12,256]{2,1,0:T(8,128)(2,1)S(1)}, u32[]{:S(2)}, u32[]{:S(2)}) async-start(bf16[12,12,256]{2,1,0:T(8,128)(2,1)} %reshape.12), calls=%async_computation.3 | async-start | bytes 196608 | tf_op jit(solution)/shard_map/all_to_all | solution.py:246
  112.5 0.8 copy-start.5
  112.5 1.0 copy-start.6
  112.5 1.2 copy-start.7

commit v3 on v2

v3 whole, which is shorter than its diff:
```python
import math

import jax
import jax.numpy as jnp
import numpy as np
from jax import lax
from jax.experimental import pallas as pl
from jax.experimental.pallas import tpu as pltpu
from jax.sharding import Mesh
from jax.sharding import PartitionSpec as P

NZ, NX, NYH, NYL, NC = 12, 4, 2, 4, 2
NY = NYH * NYL
Y = ("yh", "yl")
ROWS = 12
HALF = 256
ZROWS = NX * NY * ROWS
XROWS = NY * ROWS

BF = jnp.bfloat16
F32 = jnp.float32

ZG = 4
_z, _yh, _i, _yl = np.meshgrid(
    np.arange(ZG), np.arange(NYH), np.arange(ROWS), np.arange(NYL), indexing="ij"
)
BY_DEVICE = np.zeros((ZG * XROWS, ZG * XROWS), np.float32)
BY_DEVICE[(((_yh * NYL + _yl) * ZG + _z) * ROWS + _i).ravel(), np.arange(ZG * XROWS)] = 1
IN_ORDER = BY_DEVICE.T
ZSTEP = 3


def term_kernel(place, mine, other, cot_mine, cot_other, *rest):
    *outs, flipped, held = rest
    tokens = mine.shape[0]

    @pl.when(pl.program_id(0) == 0)
    def _():
        flipped[:, :tokens] = cot_mine[...].T
        flipped[:, tokens:] = cot_other[...].T

    for k in range(ZSTEP):
        cols = slice(k * ZROWS, (k + 1) * ZROWS)
        rows = jnp.concatenate([mine[:, cols], other[:, cols]], axis=0)
        term = jnp.dot(flipped[...], rows, preferred_element_type=F32).astype(BF)
        held[k] = term.T
        for r in range(NX):
            x = lax.rem(place[1] + r, NX)
            outs[r][k] = held[k, pl.ds(pl.multiple_of(x * XROWS, XROWS), XROWS)]


def chip_term(place, mine, other, cot_mine, cot_other):
    tokens, width = mine.shape
    wide = pl.BlockSpec((tokens, ZSTEP * ZROWS), lambda z, place: (0, z))
    half = pl.BlockSpec((tokens, HALF), lambda z, place: (0, place[0]))
    return pl.pallas_call(
        term_kernel,
        grid_spec=pltpu.PrefetchScalarGridSpec(
            num_scalar_prefetch=1,
            grid=(NZ // ZSTEP,),
            in_specs=[wide, wide, half, half],
            out_specs=[pl.BlockSpec((ZSTEP, XROWS, HALF), lambda z, place: (z, 0, 0))] * NX,
            scratch_shapes=[
                pltpu.VMEM((HALF, 2 * tokens), BF),
                pltpu.VMEM((ZSTEP, ZROWS, HALF), BF),
            ],
        ),
        out_shape=[jax.ShapeDtypeStruct((NZ, XROWS, HALF), BF)] * NX,
        compiler_params=pltpu.CompilerParams(vmem_limit_bytes=56 * 2**20),
        cost_estimate=pl.CostEstimate(
            flops=4 * width * HALF * tokens,
            bytes_accessed=4 * tokens * width + 2 * width * HALF,
            transcendentals=0,
        ),
        name="chip_term",
    )(place, mine, other, cot_mine, cot_other)


def sum_kernel(*refs):
    *parts, perm, out = refs
    total = parts[0][...].astype(F32)
    for part in parts[1:]:
        total += part[...].astype(F32)
    rows = total.astype(BF).reshape(ZROWS, HALF)
    moved = jnp.dot(perm[...], rows, preferred_element_type=F32)
    out[...] = moved.astype(BF).reshape(out.shape)


def sum_over_x(parts):
    return pl.pallas_call(
        sum_kernel,
        grid=(NZ // ZG,),
        in_specs=[pl.BlockSpec((ZG, XROWS, HALF), lambda g: (g, 0, 0))] * NX
        + [pl.BlockSpec((ZROWS, ZROWS), lambda g: (0, 0))],
        out_specs=pl.BlockSpec((NY, ZG * ROWS, HALF), lambda g: (0, g, 0)),
        out_shape=jax.ShapeDtypeStruct((NY, NZ * ROWS, HALF), BF),
        compiler_params=pltpu.CompilerParams(vmem_limit_bytes=12 * 2**20),
        cost_estimate=pl.CostEstimate(
            flops=200 * NZ // ZG * ZROWS * ZROWS * HALF,
            bytes_accessed=10 * NZ * XROWS * HALF,
            transcendentals=0,
        ),
        name="sum_over_x",
    )(*parts, jnp.asarray(BY_DEVICE, BF))


def regroup_kernel(parts, perm, _, out):
    rows = parts[...].reshape(ZROWS, HALF)
    out[...] = jnp.dot(perm[...], rows, preferred_element_type=F32).astype(BF).reshape(out.shape)


def regroup(parts, first):
    return pl.pallas_call(
        regroup_kernel,
        grid=(NZ // ZG,),
        in_specs=[
            pl.BlockSpec((NY, ZG * ROWS, HALF), lambda g: (0, g, 0)),
            pl.BlockSpec((ZROWS, ZROWS), lambda g: (0, 0)),
            pl.BlockSpec(memory_space=pl.ANY),
        ],
        out_specs=pl.BlockSpec((ZG, XROWS, HALF), lambda g: (g, 0, 0)),
        out_shape=jax.ShapeDtypeStruct((NZ, XROWS, HALF), BF),
        compiler_params=pltpu.CompilerParams(vmem_limit_bytes=12 * 2**20),
        cost_estimate=pl.CostEstimate(
            flops=2 * NZ // ZG * ZROWS * ZROWS * HALF,
            bytes_accessed=4 * NZ * XROWS * HALF,
            transcendentals=0,
        ),
        name="regroup",
    )(parts, jnp.asarray(IN_ORDER, BF), first)


def project_kernel(place, *refs):
    *blocks, hidden, cot_mine, cot_other, keys, grad, acc, cot, held = refs
    step = pl.program_id(0)

    @pl.when(step == 0)
    def _():
        cot[:, :HALF] = cot_mine[...]
        cot[:, HALF:] = cot_other[...]
        acc[...] = jnp.zeros_like(acc)

    total = acc[...]
    for k in range(ZSTEP):
        for r in range(NX):
            x = lax.rem(place[1] + NX - r, NX)
            rows = pl.ds(pl.multiple_of(x * XROWS, XROWS), XROWS)
            held[k, rows, :HALF] = blocks[r][k]
            held[k, rows, HALF:] = blocks[NX + r][k]
        weight = held[k]
        cols = slice(k * ZROWS, (k + 1) * ZROWS)
        total += jnp.dot(hidden[:, cols], weight, preferred_element_type=F32)
        grad[:, cols] = lax.dot_general(
            cot[...], weight, (((1,), (1,)), ((), ())), preferred_element_type=F32
        ).astype(BF)
    acc[...] = total

    @pl.when((step == NZ // ZSTEP - 1) & (place[0] == 0))
    def _():
        keys[...] = acc[...].astype(BF)

    @pl.when((step == NZ // ZSTEP - 1) & (place[0] == 1))
    def _():
        keys[:, :HALF] = acc[:, HALF:].astype(BF)
        keys[:, HALF:] = acc[:, :HALF].astype(BF)


def project(place, mine, other, hidden, cotangent):
    tokens, width = hidden.shape
    block = pl.BlockSpec((ZSTEP, XROWS, HALF), lambda z, place: (z, 0, 0))
    wide = pl.BlockSpec((tokens, ZSTEP * ZROWS), lambda z, place: (0, z))
    return pl.pallas_call(
        project_kernel,
        grid_spec=pltpu.PrefetchScalarGridSpec(
            num_scalar_prefetch=1,
            grid=(NZ // ZSTEP,),
            in_specs=[block] * (2 * NX)
            + [
                wide,
                pl.BlockSpec((tokens, HALF), lambda z, place: (0, place[0])),
                pl.BlockSpec((tokens, HALF), lambda z, place: (0, 1 - place[0])),
            ],
            out_specs=[
                pl.BlockSpec((tokens, 2 * HALF), lambda z, place: (0, 0)),
                wide,
            ],
            scratch_shapes=[
                pltpu.VMEM((tokens, 2 * HALF), F32),
                pltpu.VMEM((tokens, 2 * HALF), BF),
                pltpu.VMEM((ZSTEP, ZROWS, 2 * HALF), BF),
            ],
        ),
        out_shape=[
            jax.ShapeDtypeStruct((tokens, 2 * HALF), BF),
            jax.ShapeDtypeStruct((tokens, width), BF),
        ],
        compiler_params=pltpu.CompilerParams(vmem_limit_bytes=16 * 2**20),
        cost_estimate=pl.CostEstimate(
            flops=8 * width * HALF * tokens,
            bytes_accessed=4 * tokens * width + 4 * width * HALF,
            transcendentals=0,
        ),
        name="project",
    )(place, *mine, *other, hidden, cotangent, cotangent)


def shard_kernel(values, scales, out):
    rows = lax.broadcasted_iota(jnp.int32, (ROWS, ROWS), 0)
    cols = lax.broadcasted_iota(jnp.int32, (ROWS, ROWS), 1)
    line = jnp.broadcast_to(scales[...].astype(F32), (ROWS, ROWS))
    column = jnp.sum(jnp.where(rows == cols, line, 0.0), axis=1, keepdims=True)
    shard = (values[...].astype(F32) * column).astype(BF)
    for z in range(NZ):
        out[z] = shard


def scaled_copies(values, scales):
    return pl.pallas_call(
        shard_kernel,
        out_shape=jax.ShapeDtypeStruct((NZ, ROWS, HALF), BF),
        compiler_params=pltpu.CompilerParams(vmem_limit_bytes=4 * 2**20),
        name="scaled_copies",
    )(values, scales.reshape(1, ROWS))


def to_all(piece, axis, count):
    copies = jnp.broadcast_to(piece[None], (count, *piece.shape))
    return lax.all_to_all(copies, axis, split_axis=0, concat_axis=0, tiled=True)


def shift(piece, r):
    return lax.ppermute(piece, "x", [(k, (k + r) % NX) for k in range(NX)])


def swap(piece):
    return lax.ppermute(piece, "c", [(0, 1), (1, 0)])


def on_device(hidden, cotangent, quant_weight, scales):
    place = jnp.stack([lax.axis_index("c"), lax.axis_index("x")]).astype(jnp.int32)
    factor = 1.0 / math.sqrt(hidden.shape[0] * NZ * NX * NY * NC)

    other_hidden = swap(hidden)
    other_cot = swap(cotangent)

    copies = scaled_copies(quant_weight, scales)
    w_z = lax.all_to_all(copies, "z", split_axis=0, concat_axis=0, tiled=True)

    terms = chip_term(place, hidden, other_hidden, cotangent, other_cot)
    w_z, terms = lax.optimization_barrier((w_z, terms))
    t_x = [terms[0]] + [shift(terms[r], r) for r in range(1, NX)]
    sum_x = sum_over_x(t_x)
    w_y = regroup(to_all(w_z.reshape(NZ * ROWS, HALF), Y, NY), sum_x)

    mine = [w_y] + [shift(w_y, r) for r in range(1, NX)]
    t_y = lax.all_to_all(sum_x, Y, split_axis=0, concat_axis=0, tiled=True)
    sum_y = t_y.astype(F32).sum(0).astype(BF).reshape(NZ, ROWS, HALF)
    t_z = lax.all_to_all(sum_y, "z", split_axis=0, concat_axis=0, tiled=True)
    late = [lax.optimization_barrier((piece, t_z))[0] for piece in mine[1:]]
    other = [swap(piece) for piece in [w_y] + late]
    weight_grad = t_z.astype(F32).sum(0) * factor
    keys, grad_input = project(place, mine, other, hidden, cotangent)
    return keys, grad_input, weight_grad


def solution(mesh):
    fine = Mesh(mesh.devices.reshape(NZ, NX, NYH, NYL, NC), ("z", "x", "yh", "yl", "c"))
    node, local = ("z", "x", "yh"), ("yl", "c")
    return jax.shard_map(
        on_device,
        mesh=fine,
        in_specs=(P(node + local, None), P(node + local, None), P(node, local), P(node)),
        out_specs=(P(node + local, None), P(node + local, None), P(node, local)),
        check_vma=False,
    )
```

time: 126 us -> 135 us (1.071); the launches traced: 125 us -> 132 us
  waiting for transfers between devices: 24.3 us -> 37.1 us
  Pallas kernels: 21.2 us -> 16.7 us
  local copies, waits for them, and re-layouts: 7.18 us -> 5.74 us
    all_to_all x2 -> x1, starting transfers between devices: 22.3 us -> 7.1 us  [to_all(): return lax.all_to_all(copies, axis, split_axis=0, concat_axis=0, tiled=True)]
    all_to_all x0 -> x1, starting transfers between devices: none -> 15.2 us  [on_device(): w_z = lax.all_to_all(copies, 'z', split_axis=0, concat_axis=0, tiled=True)]
    all_to_all x1, waiting for transfers between devices: 0.2 us -> 9.62 us  [on_device(): t_z = lax.all_to_all(sum_y, 'z', split_axis=0, concat_axis=0, tiled=True)]
    all_to_all x2 -> x1, waiting for transfers between devices: 8.43 us -> 0.01 us  [to_all(): return lax.all_to_all(copies, axis, split_axis=0, concat_axis=0, tiled=True)]
    ppermute x6, waiting for transfers between devices: 10.5 us -> 15.2 us  [shift(): return lax.ppermute(piece, 'x', [(k, (k + r) % NX) for k in range(NX)])]
    pallas_call x1, Pallas kernels: 10.6 us -> 6.73 us  [project(): pl.pallas_call(project_kernel, grid_spec=pltpu.PrefetchScalarGridSpec(num...]
    all_to_all x0 -> x1, waiting for transfers between devices: none -> 3.32 us  [on_device(): w_z = lax.all_to_all(copies, 'z', split_axis=0, concat_axis=0, tiled=True)]
    all_to_all x1, waiting for transfers between devices: 5.17 us -> 7.46 us  [on_device(): t_y = lax.all_to_all(sum_x, Y, split_axis=0, concat_axis=0, tiled=True)]
  transfers between devices with their start and end apart: 16 -> 16, of which waited for: 6 -> 8; matrix products, arithmetic and copies ran while one was open for 3% -> 3% of each run, Pallas kernels for 17% -> 8%
where the time goes in v3:
time: 135 us; the launch traced here: 132 us
  starting transfers between devices  69.4 us (51%)
  waiting for transfers between devices  37.1 us (27%)
  Pallas kernels  16.7 us (12%)
  local copies, waits for them, and re-layouts  5.74 us (4%)
  other arithmetic  2.36 us (2%)
    ppermute x6, starting transfers between devices, shift(): return lax.ppermute(piece, 'x', [(k, (k + r) % NX) for k in range(NX)])  19.4 us
    ppermute x6, waiting for transfers between devices, shift(): return lax.ppermute(piece, 'x', [(k, (k + r) % NX) for k in range(NX)])  15.2 us
    all_to_all x1, starting transfers between devices, on_device(): w_z = lax.all_to_all(copies, 'z', split_axis=0, concat_axis=0, tiled=True)  15.2 us
    ppermute x6, starting transfers between devices, swap(): return lax.ppermute(piece, 'c', [(0, 1), (1, 0)])  12.5 us
    all_to_all x1, waiting for transfers between devices, on_device(): t_z = lax.all_to_all(sum_y, 'z', split_axis=0, concat_axis=0, tiled=True)  9.62 us
    all_to_all x1, starting transfers between devices, on_device(): t_z = lax.all_to_all(sum_y, 'z', split_axis=0, concat_axis=0, tiled=True)  8.18 us
    all_to_all x1, waiting for transfers between devices, on_device(): t_y = lax.all_to_all(sum_x, Y, split_axis=0, concat_axis=0, tiled=True)  7.46 us
    all_to_all x1, starting transfers between devices, on_device(): t_y = lax.all_to_all(sum_x, Y, split_axis=0, concat_axis=0, tiled=True)  7.1 us
  transfers between devices with their start and end apart: 16, of which 8 were waited for; matrix products, arithmetic and copies ran while one was open for 3% of the time, Pallas kernels for 8%

profile of v3, /device:TPU:6, one launch (start us, length us, event | category | flops | bytes accessed | tf_op | source)
XLA Modules:
  0.0 132.2 jit_solution(7174491328258931743)
XLA Ops:
  0.6 1.9 %collective-permute-start = (bf16[192,4608]{1,0:T(8,128)(2,1)}, bf16[192,4608]{1,0:T(8,128)(2,1)S(1)}, u32[]{:S(2)}, u32[]{:S(2)}) collective-permute-start(bf16[192,4608]{1,0:T(8,128)(2,1)} %refs_8_.1), channel_id=1, source_target_pairs={{0,1},{1,0},{2,3},{3,2},{4,5},{5,4},{6,7},{7,6},{8,9},{9,8},{10,11... | collective-permute-start | bytes 5308424 | tf_op jit(solution)/shard_map/ppermute | solution.py:236
  2.6 2.4 %collective-permute-start.1 = (bf16[192,512]{1,0:T(8,128)(2,1)}, bf16[192,512]{1,0:T(8,128)(2,1)S(1)}, u32[]{:S(2)}, u32[]{:S(2)}) collective-permute-start(bf16[192,512]{1,0:T(8,128)(2,1)} %refs_10_.1), channel_id=1, source_target_pairs={{0,1},{1,0},{2,3},{3,2},{4,5},{5,4},{6,7},{7,6},{8,9},{9,8},{10,11... | collective-permute-start | bytes 589832 | tf_op jit(solution)/shard_map/ppermute | solution.py:236
  5.0 0.7 copy-done.3
  5.7 0.7 copy-done.5
  6.3 0.7 scaled_copies.1
  7.1 15.2 %all-to-all-start = ((bf16[12,12,256]{2,1,0:T(8,128)(2,1)}), bf16[12,12,256]{2,1,0:T(8,128)(2,1)S(1)}, u32[]{:S(2)}, u32[]{:S(2)}) async-start(bf16[12,12,256]{2,1,0:T(8,128)(2,1)} %scaled_copies.1), calls=%async_computation | async-start | bytes 196608 | tf_op jit(solution)/shard_map/all_to_all | solution.py:247
  22.2 0.6 pad_add_fusion.place
  22.8 0.0 collective-permute-done.1.cot_other
  22.8 0.0 collective-permute-done.other
  22.8 0.7 copy-done.9
  23.5 1.2 copy-done.8
  24.7 6.3 %chip_term.1 = (bf16[12,96,256]{2,1,0:T(8,128)(2,1)}, bf16[12,96,256]{2,1,0:T(8,128)(2,1)}, bf16[12,96,256]{2,1,0:T(8,128)(2,1)}, bf16[12,96,256]{2,1,0:T(8,128)(2,1)}) custom-call(s32[2]{0:T(128)} %pad_add_fusion.place, bf16[192,4608]{1,0:T(8,128)(2,1)} %refs_8_.1, bf16[192,4608]{1,0:T(8,128)(2,1)} %copy-done.8, bf16[192,512]{1,0:T(8,128)(2,1)} %refs_10_.1, ...), custom_call_target="tpu_custom_call" | custom-call | flops 905969664 | bytes 5898240 | tf_op jit(solution)/shard_map/chip_term/pallas_call | solution.py:56
  31.0 3.3 %all-to-all-done = bf16[12,12,256]{2,1,0:T(8,128)(2,1)S(1)} async-done(((bf16[12,12,256]{2,1,0:T(8,128)(2,1)}), bf16[12,12,256]{2,1,0:T(8,128)(2,1)S(1)}, u32[]{:S(2)}, u32[]{:S(2)}) %all-to-all-start) | async-done | bytes 73760 | tf_op jit(solution)/shard_map/all_to_all | solution.py:247
  34.3 2.4 %collective-permute-start.2 = (bf16[12,96,256]{2,1,0:T(8,128)(2,1)}, bf16[12,96,256]{2,1,0:T(8,128)(2,1)S(1)}, u32[]{:S(2)}, u32[]{:S(2)}) collective-permute-start(bf16[12,96,256]{2,1,0:T(8,128)(2,1)} %get-tuple-element.23), channel_id=1, source_target_pairs={{0,16},{16,32},{32,48},{48,0},{1,17},{17,33},{33,49},{49,1},{2,18}... | collective-permute-start | bytes 1769480 | tf_op jit(solution)/shard_map/ppermute | solution.py:232
  36.7 4.3 %collective-permute-start.3 = (bf16[12,96,256]{2,1,0:T(8,128)(2,1)}, bf16[12,96,256]{2,1,0:T(8,128)(2,1)S(1)}, u32[]{:S(2)}, u32[]{:S(2)}) collective-permute-start(bf16[12,96,256]{2,1,0:T(8,128)(2,1)} %get-tuple-element.24), channel_id=1, source_target_pairs={{0,32},{16,48},{32,0},{48,16},{1,33},{17,49},{33,1},{49,17},{2,34}... | collective-permute-start | bytes 1769480 | tf_op jit(solution)/shard_map/ppermute | solution.py:232
  41.0 1.9 %collective-permute-start.4 = (bf16[12,96,256]{2,1,0:T(8,128)(2,1)}, bf16[12,96,256]{2,1,0:T(8,128)(2,1)S(1)}, u32[]{:S(2)}, u32[]{:S(2)}) collective-permute-start(bf16[12,96,256]{2,1,0:T(8,128)(2,1)} %get-tuple-element.25), channel_id=1, source_target_pairs={{0,48},{16,0},{32,16},{48,32},{1,49},{17,1},{33,17},{49,33},{2,50}... | collective-permute-start | bytes 1769480 | tf_op jit(solution)/shard_map/ppermute | solution.py:232
  43.0 0.9 broadcast_in_dim.8
  43.8 7.1 %all-to-all-start.1 = ((bf16[8,144,256]{2,1,0:T(8,128)(2,1)}), bf16[8,144,256]{2,1,0:T(8,128)(2,1)S(1)}, u32[]{:S(2)}, u32[]{:S(2)}) async-start(bf16[8,144,256]{2,1,0:T(8,128)(2,1)} %broadcast_in_dim.8), calls=%async_computation.1 | async-start | bytes 1179648 | tf_op jit(solution)/shard_map/all_to_all | solution.py:228
  50.9 1.7 %collective-permute-done.2.refs_1_ = bf16[12,96,256]{2,1,0:T(8,128)(2,1)S(1)} collective-permute-done((bf16[12,96,256]{2,1,0:T(8,128)(2,1)}, bf16[12,96,256]{2,1,0:T(8,128)(2,1)S(1)}, u32[]{:S(2)}, u32[]{:S(2)}) %collective-permute-start.2) | collective-permute-done | bytes 589856 | tf_op jit(solution)/shard_map/ppermute | solution.py:232
  52.7 3.9 %collective-permute-done.3.refs_2_ = bf16[12,96,256]{2,1,0:T(8,128)(2,1)S(1)} collective-permute-done((bf16[12,96,256]{2,1,0:T(8,128)(2,1)}, bf16[12,96,256]{2,1,0:T(8,128)(2,1)S(1)}, u32[]{:S(2)}, u32[]{:S(2)}) %collective-permute-start.3) | collective-permute-done | bytes 589856 | tf_op jit(solution)/shard_map/ppermute | solution.py:232
  56.6 9.0 %collective-permute-done.4.refs_3_ = bf16[12,96,256]{2,1,0:T(8,128)(2,1)S(1)} collective-permute-done((bf16[12,96,256]{2,1,0:T(8,128)(2,1)}, bf16[12,96,256]{2,1,0:T(8,128)(2,1)S(1)}, u32[]{:S(2)}, u32[]{:S(2)}) %collective-permute-start.4) | collective-permute-done | bytes 589856 | tf_op jit(solution)/shard_map/ppermute | solution.py:232
  65.6 1.0 copy-done.7
  66.5 2.1 %sum_over_x.1._ = bf16[8,144,256]{2,1,0:T(8,128)(2,1)} custom-call(bf16[12,96,256]{2,1,0:T(8,128)(2,1)S(1)} %copy-done.6, bf16[12,96,256]{2,1,0:T(8,128)(2,1)S(1)} %collective-permute-done.2.refs_1_, bf16[12,96,256]{2,1,0:T(8,128)(2,1)S(1)} %collective-permute-done.3.refs_2_, bf16[12,96,256]{2,1,0:T(8,128)(2,1)S(1)} %collective-permute-done.4.refs_3_, ...), custom_call_target="tpu_custom_call" | custom-call | flops 22649241600 | bytes 2949120 | tf_op jit(solution)/shard_map/sum_over_x/pallas_call | solution.py:90
  68.6 0.0 all-to-all-done.1.parts
  68.6 7.1 %all-to-all-start.2 = ((bf16[8,144,256]{2,1,0:T(8,128)(2,1)}), bf16[8,144,256]{2,1,0:T(8,128)(2,1)}, u32[]{:S(2)}, u32[]{:S(2)}) async-start(bf16[8,144,256]{2,1,0:T(8,128)(2,1)} %sum_over_x.1._), calls=%async_computation.2 | async-start | bytes 1179648 | tf_op jit(solution)/shard_map/all_to_all | solution.py:256
  75.7 0.0 copy-start
  75.7 0.0 copy-start.1
  75.8 0.9 regroup.1.refs_0_
  76.6 2.9 %collective-permute-start.7 = (bf16[12,96,256]{2,1,0:T(8,128)(2,1)S(1)}, bf16[12,96,256]{2,1,0:T(8,128)(2,1)S(1)}, u32[]{:S(2)}, u32[]{:S(2)}) collective-permute-start(bf16[12,96,256]{2,1,0:T(8,128)(2,1)S(1)} %regroup.1.refs_0_), channel_id=1, source_target_pairs={{0,48},{16,0},{32,16},{48,32},{1,49},{17,1},{33,17},{49,33},{2,50}... | collective-permute-start | bytes 1769480 | tf_op jit(solution)/shard_map/ppermute | solution.py:232
  79.5 3.4 %collective-permute-start.6 = (bf16[12,96,256]{2,1,0:T(8,128)(2,1)S(1)}, bf16[12,96,256]{2,1,0:T(8,128)(2,1)}, u32[]{:S(2)}, u32[]{:S(2)}) collective-permute-start(bf16[12,96,256]{2,1,0:T(8,128)(2,1)S(1)} %regroup.1.refs_0_), channel_id=1, source_target_pairs={{0,32},{16,48},{32,0},{48,16},{1,33},{17,49},{33,1},{49,17},{2,34}... | collective-permute-start | bytes 1769480 | tf_op jit(solution)/shard_map/ppermute | solution.py:232
  82.9 4.5 %collective-permute-start.5 = (bf16[12,96,256]{2,1,0:T(8,128)(2,1)S(1)}, bf16[12,96,256]{2,1,0:T(8,128)(2,1)}, u32[]{:S(2)}, u32[]{:S(2)}) collective-permute-start(bf16[12,96,256]{2,1,0:T(8,128)(2,1)S(1)} %regroup.1.refs_0_), channel_id=1, source_target_pairs={{0,16},{16,32},{32,48},{48,0},{1,17},{17,33},{33,49},{49,1},{2,18}... | collective-permute-start | bytes 1769480 | tf_op jit(solution)/shard_map/ppermute | solution.py:232
  87.5 7.5 %all-to-all-done.2 = bf16[8,144,256]{2,1,0:T(8,128)(2,1)} async-done(((bf16[8,144,256]{2,1,0:T(8,128)(2,1)}), bf16[8,144,256]{2,1,0:T(8,128)(2,1)}, u32[]{:S(2)}, u32[]{:S(2)}) %all-to-all-start.2) | async-done | bytes 589856 | tf_op jit(solution)/shard_map/all_to_all | solution.py:256
  94.9 1.1 reduce_sum.21
  96.1 0.7 reshape.14
  96.7 8.2 %all-to-all-start.3 = ((bf16[12,12,256]{2,1,0:T(8,128)(2,1)}), bf16[12,12,256]{2,1,0:T(8,128)(2,1)S(1)}, u32[]{:S(2)}, u32[]{:S(2)}) async-start(bf16[12,12,256]{2,1,0:T(8,128)(2,1)} %reshape.14), calls=%async_computation.3 | async-start | bytes 196608 | tf_op jit(solution)/shard_map/all_to_all | solution.py:258
  104.9 1.9 %collective-permute-start.8 = (bf16[12,96,256]{2,1,0:T(8,128)(2,1)S(1)}, bf16[12,96,256]{2,1,0:T(8,128)(2,1)}, u32[]{:S(2)}, u32[]{:S(2)}) collective-permute-start(bf16[12,96,256]{2,1,0:T(8,128)(2,1)S(1)} %regroup.1.refs_0_), channel_id=1, source_target_pairs={{0,1},{1,0},{2,3},{3,2},{4,5},{5,4},{6,7},{7,6},{8,9},{9,8},{10,11... | collective-permute-start | bytes 1769480 | tf_op jit(solution)/shard_map/ppermute | solution.py:236
  106.8 0.5 collective-permute-done.7.refs_3_
  107.4 9.6 %all-to-all-done.3 = bf16[12,12,256]{2,1,0:T(8,128)(2,1)S(1)} async-done(((bf16[12,12,256]{2,1,0:T(8,128)(2,1)}), bf16[12,12,256]{2,1,0:T(8,128)(2,1)S(1)}, u32[]{:S(2)}, u32[]{:S(2)}) %all-to-all-start.3) | async-done | bytes 73760 | tf_op jit(solution)/shard_map/all_to_all | solution.py:258
  117.0 1.9 %collective-permute-start.11 = (bf16[12,96,256]{2,1,0:T(8,128)(2,1)S(1)}, bf16[12,96,256]{2,1,0:T(8,128)(2,1)S(1)}, u32[]{:S(2)}, u32[]{:S(2)}) collective-permute-start(bf16[12,96,256]{2,1,0:T(8,128)(2,1)S(1)} %collective-permute-done.7.refs_3_), channel_id=1, source_target_pairs={{0,1},{1,0},{2,3},{3,2},{4,5},{5,4},{6,7},{7,6},{8,9},{9,8},{10,11... | collective-permute-start | bytes 1769480 | tf_op jit(solution)/shard_map/ppermute | solution.py:236
  118.9 0.0 collective-permute-done.6.refs_2_
  118.9 2.4 %collective-permute-start.10 = (bf16[12,96,256]{2,1,0:T(8,128)(2,1)}, bf16[12,96,256]{2,1,0:T(8,128)(2,1)S(1)}, u32[]{:S(2)}, u32[]{:S(2)}) collective-permute-start(bf16[12,96,256]{2,1,0:T(8,128)(2,1)} %collective-permute-done.6.refs_2_), channel_id=1, source_target_pairs={{0,1},{1,0},{2,3},{3,2},{4,5},{5,4},{6,7},{7,6},{8,9},{9,8},{10,11... | collective-permute-start | bytes 1769480 | tf_op jit(solution)/shard_map/ppermute | solution.py:236
  121.3 0.0 collective-permute-done.5.refs_1_
  121.3 1.9 %collective-permute-start.9 = (bf16[12,96,256]{2,1,0:T(8,128)(2,1)}, bf16[12,96,256]{2,1,0:T(8,128)(2,1)S(1)}, u32[]{:S(2)}, u32[]{:S(2)}) collective-permute-start(bf16[12,96,256]{2,1,0:T(8,128)(2,1)} %collective-permute-done.5.refs_1_), channel_id=1, source_target_pairs={{0,1},{1,0},{2,3},{3,2},{4,5},{5,4},{6,7},{7,6},{8,9},{9,8},{10,11... | collective-permute-start | bytes 1769480 | tf_op jit(solution)/shard_map/ppermute | solution.py:236
  123.3 0.6 broadcast_multiply_fusion
  123.9 0.0 collective-permute-done.8.refs_4_
  123.9 0.0 collective-permute-done.10.refs_6_
  123.9 1.5 %collective-permute-done.9.refs_5_ = bf16[12,96,256]{2,1,0:T(8,128)(2,1)S(1)} collective-permute-done((bf16[12,96,256]{2,1,0:T(8,128)(2,1)}, bf16[12,96,256]{2,1,0:T(8,128)(2,1)S(1)}, u32[]{:S(2)}, u32[]{:S(2)}) %collective-permute-start.9) | collective-permute-done | bytes 589856 | tf_op jit(solution)/shard_map/ppermute | solution.py:236
  125.5 6.7 %project.1 = (bf16[192,512]{1,0:T(8,128)(2,1)}, bf16[192,4608]{1,0:T(8,128)(2,1)}) custom-call(s32[2]{0:T(128)S(1)} %copy-done.4, bf16[12,96,256]{2,1,0:T(8,128)(2,1)S(1)} %regroup.1.refs_0_, bf16[12,96,256]{2,1,0:T(8,128)(2,1)} %collective-permute-done.5.refs_1_, bf16[12,96,256]{2,1,0:T(8,128)(2,1)} %collective-permute-done.6.refs_2_, ...), custom_call_target="tpu_custom_call" | custom-call | flops 1811939328 | bytes 8257536 | tf_op jit(solution)/shard_map/project/pallas_call | solution.py:172
  (16 shorter events, 0.1 us)
Async XLA Ops:
  0.6 22.2 %collective-permute-start = (bf16[192,4608]{1,0:T(8,128)(2,1)}, bf16[192,4608]{1,0:T(8,128)(2,1)S(1)}, u32[]{:S(2)}, u32[]{:S(2)}) collective-permute-start(bf16[192,4608]{1,0:T(8,128)(2,1)} %refs_8_.1), channel_id=1, source_target_pairs={{0,1},{1,0},{2,3},{3,2},{4,5},{5,4},{6,7},{7,6},{8,9},{9,8},{10,11... | collective-permute-start | bytes 5308424 | tf_op jit(solution)/shard_map/ppermute | solution.py:236
  2.6 20.2 %collective-permute-start.1 = (bf16[192,512]{1,0:T(8,128)(2,1)}, bf16[192,512]{1,0:T(8,128)(2,1)S(1)}, u32[]{:S(2)}, u32[]{:S(2)}) collective-permute-start(bf16[192,512]{1,0:T(8,128)(2,1)} %refs_10_.1), channel_id=1, source_target_pairs={{0,1},{1,0},{2,3},{3,2},{4,5},{5,4},{6,7},{7,6},{8,9},{9,8},{10,11... | collective-permute-start | bytes 589832 | tf_op jit(solution)/shard_map/ppermute | solution.py:236
  5.0 0.7 copy-start.3
  5.7 0.7 copy-start.5
  7.1 27.2 %all-to-all-start = ((bf16[12,12,256]{2,1,0:T(8,128)(2,1)}), bf16[12,12,256]{2,1,0:T(8,128)(2,1)S(1)}, u32[]{:S(2)}, u32[]{:S(2)}) async-start(bf16[12,12,256]{2,1,0:T(8,128)(2,1)} %scaled_copies.1), calls=%async_computation | async-start | bytes 196608 | tf_op jit(solution)/shard_map/all_to_all | solution.py:247
  22.8 0.7 copy-start.9
  23.5 1.2 copy-start.8
  31.0 34.6 %copy-start.6 = (bf16[12,96,256]{2,1,0:T(8,128)(2,1)S(1)}, bf16[12,96,256]{2,1,0:T(8,128)(2,1)}, u32[]{:S(2)}) copy-start(bf16[12,96,256]{2,1,0:T(8,128)(2,1)} %get-tuple-element.22.refs_0_) | copy-start | bytes 1769476
  34.3 18.4 %collective-permute-start.2 = (bf16[12,96,256]{2,1,0:T(8,128)(2,1)}, bf16[12,96,256]{2,1,0:T(8,128)(2,1)S(1)}, u32[]{:S(2)}, u32[]{:S(2)}) collective-permute-start(bf16[12,96,256]{2,1,0:T(8,128)(2,1)} %get-tuple-element.23), channel_id=1, source_target_pairs={{0,16},{16,32},{32,48},{48,0},{1,17},{17,33},{33,49},{49,1},{2,18}... | collective-permute-start | bytes 1769480 | tf_op jit(solution)/shard_map/ppermute | solution.py:232
  36.7 19.9 %collective-permute-start.3 = (bf16[12,96,256]{2,1,0:T(8,128)(2,1)}, bf16[12,96,256]{2,1,0:T(8,128)(2,1)S(1)}, u32[]{:S(2)}, u32[]{:S(2)}) collective-permute-start(bf16[12,96,256]{2,1,0:T(8,128)(2,1)} %get-tuple-element.24), channel_id=1, source_target_pairs={{0,32},{16,48},{32,0},{48,16},{1,33},{17,49},{33,1},{49,17},{2,34}... | collective-permute-start | bytes 1769480 | tf_op jit(solution)/shard_map/ppermute | solution.py:232
  41.0 24.6 %collective-permute-start.4 = (bf16[12,96,256]{2,1,0:T(8,128)(2,1)}, bf16[12,96,256]{2,1,0:T(8,128)(2,1)S(1)}, u32[]{:S(2)}, u32[]{:S(2)}) collective-permute-start(bf16[12,96,256]{2,1,0:T(8,128)(2,1)} %get-tuple-element.25), channel_id=1, source_target_pairs={{0,48},{16,0},{32,16},{48,32},{1,49},{17,1},{33,17},{49,33},{2,50}... | collective-permute-start | bytes 1769480 | tf_op jit(solution)/shard_map/ppermute | solution.py:232
  43.8 24.8 %all-to-all-start.1 = ((bf16[8,144,256]{2,1,0:T(8,128)(2,1)}), bf16[8,144,256]{2,1,0:T(8,128)(2,1)S(1)}, u32[]{:S(2)}, u32[]{:S(2)}) async-start(bf16[8,144,256]{2,1,0:T(8,128)(2,1)} %broadcast_in_dim.8), calls=%async_computation.1 | async-start | bytes 1179648 | tf_op jit(solution)/shard_map/all_to_all | solution.py:228
  50.9 24.8 %copy-start.2 = (bf16[384,384]{1,0:T(8,128)(2,1)S(1)}, bf16[384,384]{1,0:T(8,128)(2,1)}, u32[]{:S(2)}) copy-start(bf16[384,384]{1,0:T(8,128)(2,1)} %constant.21.clone.perm) | copy-start | bytes 884740
  65.6 1.0 copy-start.7
  68.6 26.3 %all-to-all-start.2 = ((bf16[8,144,256]{2,1,0:T(8,128)(2,1)}), bf16[8,144,256]{2,1,0:T(8,128)(2,1)}, u32[]{:S(2)}, u32[]{:S(2)}) async-start(bf16[8,144,256]{2,1,0:T(8,128)(2,1)} %sum_over_x.1._), calls=%async_computation.2 | async-start | bytes 1179648 | tf_op jit(solution)/shard_map/all_to_all | solution.py:256
  75.7 49.7 %copy-start = (bf16[192,4608]{1,0:T(8,128)(2,1)S(1)}, bf16[192,4608]{1,0:T(8,128)(2,1)}, u32[]{:S(2)}) copy-start(bf16[192,4608]{1,0:T(8,128)(2,1)} %refs_8_.1) | copy-start | bytes 5308420
  75.7 49.7 %copy-start.1 = (bf16[192,512]{1,0:T(8,128)(2,1)S(1)}, bf16[192,512]{1,0:T(8,128)(2,1)}, u32[]{:S(2)}) copy-start(bf16[192,512]{1,0:T(8,128)(2,1)} %refs_10_.1) | copy-start | bytes 589828
  75.8 49.7 %copy-start.4 = (s32[2]{0:T(128)S(1)}, s32[2]{0:T(128)}, u32[]{:S(2)}) copy-start(s32[2]{0:T(128)} %pad_add_fusion.place) | copy-start | bytes 28
  76.6 30.7 %collective-permute-start.7 = (bf16[12,96,256]{2,1,0:T(8,128)(2,1)S(1)}, bf16[12,96,256]{2,1,0:T(8,128)(2,1)S(1)}, u32[]{:S(2)}, u32[]{:S(2)}) collective-permute-start(bf16[12,96,256]{2,1,0:T(8,128)(2,1)S(1)} %regroup.1.refs_0_), channel_id=1, source_target_pairs={{0,48},{16,0},{32,16},{48,32},{1,49},{17,1},{33,17},{49,33},{2,50}... | collective-permute-start | bytes 1769480 | tf_op jit(solution)/shard_map/ppermute | solution.py:232
  79.5 39.4 %collective-permute-start.6 = (bf16[12,96,256]{2,1,0:T(8,128)(2,1)S(1)}, bf16[12,96,256]{2,1,0:T(8,128)(2,1)}, u32[]{:S(2)}, u32[]{:S(2)}) collective-permute-start(bf16[12,96,256]{2,1,0:T(8,128)(2,1)S(1)} %regroup.1.refs_0_), channel_id=1, source_target_pairs={{0,32},{16,48},{32,0},{48,16},{1,33},{17,49},{33,1},{49,17},{2,34}... | collective-permute-start | bytes 1769480 | tf_op jit(solution)/shard_map/ppermute | solution.py:232
  82.9 38.4 %collective-permute-start.5 = (bf16[12,96,256]{2,1,0:T(8,128)(2,1)S(1)}, bf16[12,96,256]{2,1,0:T(8,128)(2,1)}, u32[]{:S(2)}, u32[]{:S(2)}) collective-permute-start(bf16[12,96,256]{2,1,0:T(8,128)(2,1)S(1)} %regroup.1.refs_0_), channel_id=1, source_target_pairs={{0,16},{16,32},{32,48},{48,0},{1,17},{17,33},{33,49},{49,1},{2,18}... | collective-permute-start | bytes 1769480 | tf_op jit(solution)/shard_map/ppermute | solution.py:232
  96.7 20.3 %all-to-all-start.3 = ((bf16[12,12,256]{2,1,0:T(8,128)(2,1)}), bf16[12,12,256]{2,1,0:T(8,128)(2,1)S(1)}, u32[]{:S(2)}, u32[]{:S(2)}) async-start(bf16[12,12,256]{2,1,0:T(8,128)(2,1)} %reshape.14), calls=%async_computation.3 | async-start | bytes 196608 | tf_op jit(solution)/shard_map/all_to_all | solution.py:258
  104.9 19.0 %collective-permute-start.8 = (bf16[12,96,256]{2,1,0:T(8,128)(2,1)S(1)}, bf16[12,96,256]{2,1,0:T(8,128)(2,1)}, u32[]{:S(2)}, u32[]{:S(2)}) collective-permute-start(bf16[12,96,256]{2,1,0:T(8,128)(2,1)S(1)} %regroup.1.refs_0_), channel_id=1, source_target_pairs={{0,1},{1,0},{2,3},{3,2},{4,5},{5,4},{6,7},{7,6},{8,9},{9,8},{10,11... | collective-permute-start | bytes 1769480 | tf_op jit(solution)/shard_map/ppermute | solution.py:236
  117.0 6.9 %collective-permute-start.11 = (bf16[12,96,256]{2,1,0:T(8,128)(2,1)S(1)}, bf16[12,96,256]{2,1,0:T(8,128)(2,1)S(1)}, u32[]{:S(2)}, u32[]{:S(2)}) collective-permute-start(bf16[12,96,256]{2,1,0:T(8,128)(2,1)S(1)} %collective-permute-done.7.refs_3_), channel_id=1, source_target_pairs={{0,1},{1,0},{2,3},{3,2},{4,5},{5,4},{6,7},{7,6},{8,9},{9,8},{10,11... | collective-permute-start | bytes 1769480 | tf_op jit(solution)/shard_map/ppermute | solution.py:236
  118.9 5.0 %collective-permute-start.10 = (bf16[12,96,256]{2,1,0:T(8,128)(2,1)}, bf16[12,96,256]{2,1,0:T(8,128)(2,1)S(1)}, u32[]{:S(2)}, u32[]{:S(2)}) collective-permute-start(bf16[12,96,256]{2,1,0:T(8,128)(2,1)} %collective-permute-done.6.refs_2_), channel_id=1, source_target_pairs={{0,1},{1,0},{2,3},{3,2},{4,5},{5,4},{6,7},{7,6},{8,9},{9,8},{10,11... | collective-permute-start | bytes 1769480 | tf_op jit(solution)/shard_map/ppermute | solution.py:236
  121.3 4.1 %collective-permute-start.9 = (bf16[12,96,256]{2,1,0:T(8,128)(2,1)}, bf16[12,96,256]{2,1,0:T(8,128)(2,1)S(1)}, u32[]{:S(2)}, u32[]{:S(2)}) collective-permute-start(bf16[12,96,256]{2,1,0:T(8,128)(2,1)} %collective-permute-done.5.refs_1_), channel_id=1, source_target_pairs={{0,1},{1,0},{2,3},{3,2},{4,5},{5,4},{6,7},{7,6},{8,9},{9,8},{10,11... | collective-permute-start | bytes 1769480 | tf_op jit(solution)/shard_map/ppermute | solution.py:236

commit v4 on v3

--- a/solution.py
+++ b/solution.py
@@ -16,6 +16,7 @@
 HALF = 256
 ZROWS = NX * NY * ROWS
 XROWS = NY * ROWS
+WIDE = NZ * XROWS
 
 BF = jnp.bfloat16
 F32 = jnp.float32
@@ -30,93 +31,96 @@
 ZSTEP = 3
 
 
-def term_kernel(place, mine, other, cot_mine, cot_other, *rest):
-    *outs, flipped, held = rest
-    tokens = mine.shape[0]
-
-    @pl.when(pl.program_id(0) == 0)
-    def _():
-        flipped[:, :tokens] = cot_mine[...].T
-        flipped[:, tokens:] = cot_other[...].T
-
-    for k in range(ZSTEP):
-        cols = slice(k * ZROWS, (k + 1) * ZROWS)
-        rows = jnp.concatenate([mine[:, cols], other[:, cols]], axis=0)
+def pack_kernel(place, hidden, cot, *rest):
+    *outs, cut = rest
+    for g in range(NZ // ZG):
+        for x in range(NX):
+            starts = [z * ZROWS + x * XROWS for z in range(g * ZG, (g + 1) * ZG)]
+            cut[x, :, g * ZG * XROWS : (g + 1) * ZG * XROWS] = jnp.concatenate(
+                [hidden[:, start : start + XROWS] for start in starts], axis=1
+            )
+    for r in range(NX):
+        outs[r][:, :WIDE] = cut[lax.rem(place[1] + r, NX)]
+        outs[r][:, WIDE:] = cot[...]
+
+
+def pack(place, hidden, cotangent):
+    tokens, width = hidden.shape
+    whole = pl.BlockSpec((tokens, WIDE + 2 * HALF), lambda k, place: (0, 0))
+    return pl.pallas_call(
+        pack_kernel,
+        grid_spec=pltpu.PrefetchScalarGridSpec(
+            num_scalar_prefetch=1,
+            grid=(1,),
+            in_specs=[
+                pl.BlockSpec((tokens, width), lambda k, place: (0, 0)),
+                pl.BlockSpec((tokens, 2 * HALF), lambda k, place: (0, 0)),
+            ],
+            out_specs=[whole] * NX,
+            scratch_shapes=[pltpu.VMEM((NX, tokens, WIDE), BF)],
+        ),
+        out_shape=[jax.ShapeDtypeStruct((tokens, WIDE + 2 * HALF), BF)] * NX,
+        compiler_params=pltpu.CompilerParams(vmem_limit_bytes=56 * 2**20),
+        cost_estimate=pl.CostEstimate(
+            flops=tokens * width, bytes_accessed=4 * tokens * width, transcendentals=0
+        ),
+        name="pack",
+    )(place, hidden, cotangent)
+
+
+def term_kernel(place, *refs):
+    *blocks, perm, out, flipped = refs
+    tokens = blocks[0].shape[0]
+    half = pl.ds(pl.multiple_of(WIDE + place[0] * HALF, HALF // 2), HALF)
+    for b in range(0, len(blocks), 2):
+        pair = jnp.concatenate([blocks[b][:, half], blocks[b + 1][:, half]], axis=0)
+        flipped[:, b * tokens : (b + 2) * tokens] = pair.T
+    for g in range(NZ // ZG):
+        cols = slice(g * ZG * XROWS, (g + 1) * ZG * XROWS)
+        rows = jnp.concatenate([block[:, cols] for block in blocks], axis=0)
         term = jnp.dot(flipped[...], rows, preferred_element_type=F32).astype(BF)
-        held[k] = term.T
-        for r in range(NX):
-            x = lax.rem(place[1] + r, NX)
-            outs[r][k] = held[k, pl.ds(pl.multiple_of(x * XROWS, XROWS), XROWS)]
-
-
-def chip_term(place, mine, other, cot_mine, cot_other):
-    tokens, width = mine.shape
-    wide = pl.BlockSpec((tokens, ZSTEP * ZROWS), lambda z, place: (0, z))
-    half = pl.BlockSpec((tokens, HALF), lambda z, place: (0, place[0]))
+        moved = lax.dot_general(
+            perm[...], term, (((1,), (1,)), ((), ())), preferred_element_type=F32
+        ).astype(BF)
+        out[:, g * ZG * ROWS : (g + 1) * ZG * ROWS] = moved.reshape(NY, ZG * ROWS, HALF)
+
+
+def group_term(place, blocks):
+    tokens = blocks[0].shape[0]
+    whole = pl.BlockSpec(memory_space=pltpu.VMEM)
     return pl.pallas_call(
         term_kernel,
         grid_spec=pltpu.PrefetchScalarGridSpec(
             num_scalar_prefetch=1,
-            grid=(NZ // ZSTEP,),
-            in_specs=[wide, wide, half, half],
-            out_specs=[pl.BlockSpec((ZSTEP, XROWS, HALF), lambda z, place: (z, 0, 0))] * NX,
-            scratch_shapes=[
-                pltpu.VMEM((HALF, 2 * tokens), BF),
-                pltpu.VMEM((ZSTEP, ZROWS, HALF), BF),
-            ],
-        ),
-        out_shape=[jax.ShapeDtypeStruct((NZ, XROWS, HALF), BF)] * NX,
-        compiler_params=pltpu.CompilerParams(vmem_limit_bytes=56 * 2**20),
-        cost_estimate=pl.CostEstimate(
-            flops=4 * width * HALF * tokens,
-            bytes_accessed=4 * tokens * width + 2 * width * HALF,
+            grid=(1,),
+            in_specs=[whole] * len(blocks)
+            + [pl.BlockSpec((ZG * XROWS, ZG * XROWS), lambda k, place: (0, 0))],
+            out_specs=pl.BlockSpec((NY, NZ * ROWS, HALF), lambda k, place: (0, 0, 0)),
+            scratch_shapes=[pltpu.VMEM((HALF, len(blocks) * tokens), BF)],
+        ),
+        out_shape=jax.ShapeDtypeStruct((NY, NZ * ROWS, HALF), BF),
+        compiler_params=pltpu.CompilerParams(vmem_limit_bytes=24 * 2**20),
+        cost_estimate=pl.CostEstimate(
+            flops=2 * WIDE * HALF * (len(blocks) * tokens + ZG * XROWS),
+            bytes_accessed=2 * len(blocks) * tokens * (WIDE + 2 * HALF),
             transcendentals=0,
         ),
-        name="chip_term",
-    )(place, mine, other, cot_mine, cot_other)
-
-
-def sum_kernel(*refs):
-    *parts, perm, out = refs
-    total = parts[0][...].astype(F32)
-    for part in parts[1:]:
-        total += part[...].astype(F32)
-    rows = total.astype(BF).reshape(ZROWS, HALF)
-    moved = jnp.dot(perm[...], rows, preferred_element_type=F32)
-    out[...] = moved.astype(BF).reshape(out.shape)
-
-
-def sum_over_x(parts):
-    return pl.pallas_call(
-        sum_kernel,
-        grid=(NZ // ZG,),
-        in_specs=[pl.BlockSpec((ZG, XROWS, HALF), lambda g: (g, 0, 0))] * NX
-        + [pl.BlockSpec((ZROWS, ZROWS), lambda g: (0, 0))],
-        out_specs=pl.BlockSpec((NY, ZG * ROWS, HALF), lambda g: (0, g, 0)),
-        out_shape=jax.ShapeDtypeStruct((NY, NZ * ROWS, HALF), BF),
-        compiler_params=pltpu.CompilerParams(vmem_limit_bytes=12 * 2**20),
-        cost_estimate=pl.CostEstimate(
-            flops=200 * NZ // ZG * ZROWS * ZROWS * HALF,
-            bytes_accessed=10 * NZ * XROWS * HALF,
-            transcendentals=0,
-        ),
-        name="sum_over_x",
-    )(*parts, jnp.asarray(BY_DEVICE, BF))
-
-
-def regroup_kernel(parts, perm, _, out):
+        name="group_term",
+    )(place, *blocks, jnp.asarray(BY_DEVICE, BF))
+
+
+def regroup_kernel(parts, perm, out):
     rows = parts[...].reshape(ZROWS, HALF)
     out[...] = jnp.dot(perm[...], rows, preferred_element_type=F32).astype(BF).reshape(out.shape)
 
 
-def regroup(parts, first):
+def regroup(parts):
     return pl.pallas_call(
         regroup_kernel,
         grid=(NZ // ZG,),
         in_specs=[
             pl.BlockSpec((NY, ZG * ROWS, HALF), lambda g: (0, g, 0)),
             pl.BlockSpec((ZROWS, ZROWS), lambda g: (0, 0)),
-            pl.BlockSpec(memory_space=pl.ANY),
         ],
         out_specs=pl.BlockSpec((ZG, XROWS, HALF), lambda g: (g, 0, 0)),
         out_shape=jax.ShapeDtypeStruct((NZ, XROWS, HALF), BF),
@@ -127,7 +131,7 @@
             transcendentals=0,
         ),
         name="regroup",
-    )(parts, jnp.asarray(IN_ORDER, BF), first)
+    )(parts, jnp.asarray(IN_ORDER, BF))
 
 
 def project_kernel(place, *refs):
@@ -240,24 +244,20 @@
     place = jnp.stack([lax.axis_index("c"), lax.axis_index("x")]).astype(jnp.int32)
     factor = 1.0 / math.sqrt(hidden.shape[0] * NZ * NX * NY * NC)
 
-    other_hidden = swap(hidden)
-    other_cot = swap(cotangent)
-
     copies = scaled_copies(quant_weight, scales)
     w_z = lax.all_to_all(copies, "z", split_axis=0, concat_axis=0, tiled=True)
 
-    terms = chip_term(place, hidden, other_hidden, cotangent, other_cot)
-    w_z, terms = lax.optimization_barrier((w_z, terms))
-    t_x = [terms[0]] + [shift(terms[r], r) for r in range(1, NX)]
-    sum_x = sum_over_x(t_x)
-    w_y = regroup(to_all(w_z.reshape(NZ * ROWS, HALF), Y, NY), sum_x)
-
+    packed = pack(place, hidden, cotangent)
+    held = [packed[0]] + [shift(packed[r], r) for r in (1, 3, 2)]
+    term = group_term(place, held + [swap(piece) for piece in held])
+
+    w_y = regroup(to_all(w_z.reshape(NZ * ROWS, HALF), Y, NY))
     mine = [w_y] + [shift(w_y, r) for r in range(1, NX)]
-    t_y = lax.all_to_all(sum_x, Y, split_axis=0, concat_axis=0, tiled=True)
+    other = [swap(piece) for piece in mine]
+
+    t_y = lax.all_to_all(term, Y, split_axis=0, concat_axis=0, tiled=True)
     sum_y = t_y.astype(F32).sum(0).astype(BF).reshape(NZ, ROWS, HALF)
     t_z = lax.all_to_all(sum_y, "z", split_axis=0, concat_axis=0, tiled=True)
-    late = [lax.optimization_barrier((piece, t_z))[0] for piece in mine[1:]]
-    other = [swap(piece) for piece in [w_y] + late]
     weight_grad = t_z.astype(F32).sum(0) * factor
     keys, grad_input = project(place, mine, other, hidden, cotangent)
     return keys, grad_input, weight_grad

time: 135 us -> 122 us (0.904)
  blocking collectives: 0 us -> 19 us
  waiting for transfers between devices: 37.1 us -> 19.8 us
  starting transfers between devices: 69.4 us -> 57.8 us
  local copies, waits for them, and re-layouts: 5.74 us -> 1.57 us
  Pallas kernels: 16.7 us -> 18.1 us
    all_to_all x0 -> x1, blocking collectives: none -> 19 us  [on_device(): w_z = lax.all_to_all(copies, 'z', split_axis=0, concat_axis=0, tiled=True)]
    all_to_all x2 -> x1, starting transfers between devices: 22.3 us -> 4.33 us  [on_device(): t_y = lax.all_to_all(term, Y, split_axis=0, concat_axis=0, tiled=True)]
    all_to_all x2 -> x1, waiting for transfers between devices: 10.8 us -> 0.61 us  [on_device(): t_y = lax.all_to_all(term, Y, split_axis=0, concat_axis=0, tiled=True)]
    ppermute x6, waiting for transfers between devices: 15.2 us -> 6.63 us  [shift(): return lax.ppermute(piece, 'x', [(k, (k + r) % NX) for k in range(NX)])]
    all_to_all x1, waiting for transfers between devices: 0.01 us -> 7.54 us  [to_all(): return lax.all_to_all(copies, axis, split_axis=0, concat_axis=0, tiled=True)]
    ppermute x6, starting transfers between devices: 19.4 us -> 26.1 us  [shift(): return lax.ppermute(piece, 'x', [(k, (k + r) % NX) for k in range(NX)])]
    all_to_all x1, starting transfers between devices: 8.18 us -> 3.51 us  [on_device(): t_z = lax.all_to_all(sum_y, 'z', split_axis=0, concat_axis=0, tiled=True)]
    all_to_all x1, waiting for transfers between devices: 9.62 us -> 4.97 us  [on_device(): t_z = lax.all_to_all(sum_y, 'z', split_axis=0, concat_axis=0, tiled=True)]
  transfers between devices with their start and end apart: 16 -> 17, of which waited for: 8 -> 5; matrix products, arithmetic and copies ran while one was open for 3% -> 2% of each run, Pallas kernels for 8% -> 11%
where the time goes in v4:
time: 122 us; the launch traced here: 120 us
  starting transfers between devices  57.8 us (47%)
  waiting for transfers between devices  19.8 us (16%)
  blocking collectives  19 us (16%)
  Pallas kernels  18.1 us (15%)
  other arithmetic  2.4 us (2%)
  local copies, waits for them, and re-layouts  1.57 us (1%)
    ppermute x6, starting transfers between devices, shift(): return lax.ppermute(piece, 'x', [(k, (k + r) % NX) for k in range(NX)])  26.1 us
    all_to_all x1, blocking collectives, on_device(): w_z = lax.all_to_all(copies, 'z', split_axis=0, concat_axis=0, tiled=True)  19 us
    ppermute x8, starting transfers between devices, swap(): return lax.ppermute(piece, 'c', [(0, 1), (1, 0)])  16.8 us
    all_to_all x1, waiting for transfers between devices, to_all(): return lax.all_to_all(copies, axis, split_axis=0, concat_axis=0, tiled=True)  7.54 us
    all_to_all x1, starting transfers between devices, to_all(): return lax.all_to_all(copies, axis, split_axis=0, concat_axis=0, tiled=True)  7.1 us
    pallas_call x1, Pallas kernels, project(): pl.pallas_call(project_kernel, grid_spec=pltpu.PrefetchScalarGridSpec(num...  7 us
    ppermute x6, waiting for transfers between devices, shift(): return lax.ppermute(piece, 'x', [(k, (k + r) % NX) for k in range(NX)])  6.63 us
    pallas_call x1, Pallas kernels, group_term(): pl.pallas_call(term_kernel, grid_spec=pltpu.PrefetchScalarGridSpec(num_sc...  5.47 us
  transfers between devices with their start and end apart: 17, of which 5 were waited for; matrix products, arithmetic and copies ran while one was open for 2% of the time, Pallas kernels for 11%

profile of v4, /device:TPU:6, one launch (start us, length us, event | category | flops | bytes accessed | tf_op | source)
XLA Modules:
  0.0 119.6 jit_solution(14584217968375172724)
XLA Ops:
  0.6 0.0 copy-start.7
  0.6 0.0 copy-start.5
  0.7 0.6 pad_add_fusion.place
  1.3 4.7 %pack.1 = (bf16[192,1664]{1,0:T(8,128)(2,1)}, bf16[192,1664]{1,0:T(8,128)(2,1)}, bf16[192,1664]{1,0:T(8,128)(2,1)}, bf16[192,1664]{1,0:T(8,128)(2,1)}) custom-call(s32[2]{0:T(128)} %pad_add_fusion.place, bf16[192,4608]{1,0:T(8,128)(2,1)} %hidden.1, bf16[192,512]{1,0:T(8,128)(2,1)} %cot.1), custom_call_target="tpu_custom_call" | custom-call | flops 884736 | bytes 3538944 | tf_op jit(solution)/shard_map/pack/pallas_call | solution.py:50
  5.9 11.5 %collective-permute-start.7 = (bf16[192,1664]{1,0:T(8,128)(2,1)}, bf16[192,1664]{1,0:T(8,128)(2,1)S(1)}, u32[]{:S(2)}, u32[]{:S(2)}) collective-permute-start(bf16[192,1664]{1,0:T(8,128)(2,1)} %get-tuple-element.12), channel_id=1, source_target_pairs={{0,16},{16,32},{32,48},{48,0},{1,17},{17,33},{33,49},{49,1},{2,18}... | collective-permute-start | bytes 1916936 | tf_op jit(solution)/shard_map/ppermute | solution.py:236
  17.5 1.9 %collective-permute-start.8 = (bf16[192,1664]{1,0:T(8,128)(2,1)}, bf16[192,1664]{1,0:T(8,128)(2,1)}, u32[]{:S(2)}, u32[]{:S(2)}) collective-permute-start(bf16[192,1664]{1,0:T(8,128)(2,1)} %get-tuple-element.13), channel_id=1, source_target_pairs={{0,48},{16,0},{32,16},{48,32},{1,49},{17,1},{33,17},{49,33},{2,50}... | collective-permute-start | bytes 1916936 | tf_op jit(solution)/shard_map/ppermute | solution.py:236
  19.4 3.4 %collective-permute-start.9 = (bf16[192,1664]{1,0:T(8,128)(2,1)}, bf16[192,1664]{1,0:T(8,128)(2,1)}, u32[]{:S(2)}, u32[]{:S(2)}) collective-permute-start(bf16[192,1664]{1,0:T(8,128)(2,1)} %get-tuple-element.14), channel_id=1, source_target_pairs={{0,32},{16,48},{32,0},{48,16},{1,33},{17,49},{33,1},{49,17},{2,34}... | collective-permute-start | bytes 1916936 | tf_op jit(solution)/shard_map/ppermute | solution.py:236
  22.8 0.0 copy-done.7
  22.8 0.1 scaled_copies.1
  22.9 19.0 %all_to_all.20 = bf16[12,12,256]{2,1,0:T(8,128)(2,1)S(1)} all-to-all(bf16[12,12,256]{2,1,0:T(8,128)(2,1)S(1)} %scaled_copies.1), channel_id=1, replica_groups=mesh['z'=12,'x'=4,'yh'=2,'yl'=4,'c'=2] {'z'}, dimensions={0} | all-to-all | bytes 147456 | tf_op jit(solution)/shard_map/all_to_all | solution.py:248
  41.9 0.9 broadcast_in_dim.8
  42.8 7.1 %all-to-all-start.1 = ((bf16[8,144,256]{2,1,0:T(8,128)(2,1)}), bf16[8,144,256]{2,1,0:T(8,128)(2,1)S(1)}, u32[]{:S(2)}, u32[]{:S(2)}) async-start(bf16[8,144,256]{2,1,0:T(8,128)(2,1)} %broadcast_in_dim.8), calls=%async_computation.1 | async-start | bytes 1179648 | tf_op jit(solution)/shard_map/all_to_all | solution.py:232
  49.9 1.9 %collective-permute-start.10 = (bf16[192,1664]{1,0:T(8,128)(2,1)S(1)}, bf16[192,1664]{1,0:T(8,128)(2,1)}, u32[]{:S(2)}, u32[]{:S(2)}) collective-permute-start(bf16[192,1664]{1,0:T(8,128)(2,1)S(1)} %copy-done.2), channel_id=1, source_target_pairs={{0,1},{1,0},{2,3},{3,2},{4,5},{5,4},{6,7},{7,6},{8,9},{9,8},{10,11... | collective-permute-start | bytes 1916936 | tf_op jit(solution)/shard_map/ppermute | solution.py:240
  51.8 0.0 collective-permute-done.7.refs_1_
  51.9 2.4 %collective-permute-start.11 = (bf16[192,1664]{1,0:T(8,128)(2,1)S(1)}, bf16[192,1664]{1,0:T(8,128)(2,1)}, u32[]{:S(2)}, u32[]{:S(2)}) collective-permute-start(bf16[192,1664]{1,0:T(8,128)(2,1)S(1)} %collective-permute-done.7.refs_1_), channel_id=1, source_target_pairs={{0,1},{1,0},{2,3},{3,2},{4,5},{5,4},{6,7},{7,6},{8,9},{9,8},{10,11... | collective-permute-start | bytes 1916936 | tf_op jit(solution)/shard_map/ppermute | solution.py:240
  54.3 0.0 collective-permute-done.8.refs_2_
  54.3 1.9 %collective-permute-start.12 = (bf16[192,1664]{1,0:T(8,128)(2,1)}, bf16[192,1664]{1,0:T(8,128)(2,1)}, u32[]{:S(2)}, u32[]{:S(2)}) collective-permute-start(bf16[192,1664]{1,0:T(8,128)(2,1)} %collective-permute-done.8.refs_2_), channel_id=1, source_target_pairs={{0,1},{1,0},{2,3},{3,2},{4,5},{5,4},{6,7},{7,6},{8,9},{9,8},{10,11... | collective-permute-start | bytes 1916936 | tf_op jit(solution)/shard_map/ppermute | solution.py:240
  56.2 0.0 collective-permute-done.9.refs_3_
  56.2 2.4 %collective-permute-start.13 = (bf16[192,1664]{1,0:T(8,128)(2,1)}, bf16[192,1664]{1,0:T(8,128)(2,1)}, u32[]{:S(2)}, u32[]{:S(2)}) collective-permute-start(bf16[192,1664]{1,0:T(8,128)(2,1)} %collective-permute-done.9.refs_3_), channel_id=1, source_target_pairs={{0,1},{1,0},{2,3},{3,2},{4,5},{5,4},{6,7},{7,6},{8,9},{9,8},{10,11... | collective-permute-start | bytes 1916936 | tf_op jit(solution)/shard_map/ppermute | solution.py:240
  58.6 7.5 %all-to-all-done.1.parts = bf16[8,144,256]{2,1,0:T(8,128)(2,1)S(1)} async-done(((bf16[8,144,256]{2,1,0:T(8,128)(2,1)}), bf16[8,144,256]{2,1,0:T(8,128)(2,1)S(1)}, u32[]{:S(2)}, u32[]{:S(2)}) %all-to-all-start.1) | async-done | bytes 589856 | tf_op jit(solution)/shard_map/all_to_all | solution.py:232
  66.2 0.9 regroup.1.refs_0_
  67.0 4.0 %collective-permute-start = (bf16[12,96,256]{2,1,0:T(8,128)(2,1)S(1)}, bf16[12,96,256]{2,1,0:T(8,128)(2,1)}, u32[]{:S(2)}, u32[]{:S(2)}) collective-permute-start(bf16[12,96,256]{2,1,0:T(8,128)(2,1)S(1)} %regroup.1.refs_0_), channel_id=1, source_target_pairs={{0,16},{16,32},{32,48},{48,0},{1,17},{17,33},{33,49},{49,1},{2,18}... | collective-permute-start | bytes 1769480 | tf_op jit(solution)/shard_map/ppermute | solution.py:236
  71.1 0.0 collective-permute-done.10.refs_4_
  71.1 3.0 %collective-permute-start.1 = (bf16[12,96,256]{2,1,0:T(8,128)(2,1)S(1)}, bf16[12,96,256]{2,1,0:T(8,128)(2,1)}, u32[]{:S(2)}, u32[]{:S(2)}) collective-permute-start(bf16[12,96,256]{2,1,0:T(8,128)(2,1)S(1)} %regroup.1.refs_0_), channel_id=1, source_target_pairs={{0,32},{16,48},{32,0},{48,16},{1,33},{17,49},{33,1},{49,17},{2,34}... | collective-permute-start | bytes 1769480 | tf_op jit(solution)/shard_map/ppermute | solution.py:236
  74.1 0.0 collective-permute-done.11.refs_5_
  74.1 2.2 %collective-permute-start.2 = (bf16[12,96,256]{2,1,0:T(8,128)(2,1)S(1)}, bf16[12,96,256]{2,1,0:T(8,128)(2,1)}, u32[]{:S(2)}, u32[]{:S(2)}) collective-permute-start(bf16[12,96,256]{2,1,0:T(8,128)(2,1)S(1)} %regroup.1.refs_0_), channel_id=1, source_target_pairs={{0,48},{16,0},{32,16},{48,32},{1,49},{17,1},{33,17},{49,33},{2,50}... | collective-permute-start | bytes 1769480 | tf_op jit(solution)/shard_map/ppermute | solution.py:236
  76.4 0.0 collective-permute-done.12.refs_6_
  76.4 0.0 collective-permute-done.13.refs_7_
  76.4 5.5 %group_term.1 = bf16[8,144,256]{2,1,0:T(8,128)(2,1)} custom-call(s32[2]{0:T(128)S(1)} %copy-done.6, bf16[192,1664]{1,0:T(8,128)(2,1)S(1)} %copy-done.2, bf16[192,1664]{1,0:T(8,128)(2,1)S(1)} %collective-permute-done.7.refs_1_, bf16[192,1664]{1,0:T(8,128)(2,1)} %collective-permute-done.8.refs_2_, bf16[192,1664]{1,0:T(8,128)(2,1)} %collective-permute-done.9.refs_3_, ...), custom_call_target="tpu_custom_call" | custom-call | flops 1132462080 | bytes 5111808 | tf_op jit(solution)/shard_map/group_term/pallas_call | solution.py:91
  81.9 4.3 %all-to-all-start.2 = ((bf16[8,144,256]{2,1,0:T(8,128)(2,1)}), bf16[8,144,256]{2,1,0:T(8,128)(2,1)}, u32[]{:S(2)}, u32[]{:S(2)}) async-start(bf16[8,144,256]{2,1,0:T(8,128)(2,1)} %group_term.1), calls=%async_computation.2 | async-start | bytes 1179648 | tf_op jit(solution)/shard_map/all_to_all | solution.py:258
  86.2 1.9 %collective-permute-start.3 = (bf16[12,96,256]{2,1,0:T(8,128)(2,1)S(1)}, bf16[12,96,256]{2,1,0:T(8,128)(2,1)S(1)}, u32[]{:S(2)}, u32[]{:S(2)}) collective-permute-start(bf16[12,96,256]{2,1,0:T(8,128)(2,1)S(1)} %regroup.1.refs_0_), channel_id=1, source_target_pairs={{0,1},{1,0},{2,3},{3,2},{4,5},{5,4},{6,7},{7,6},{8,9},{9,8},{10,11... | collective-permute-start | bytes 1769480 | tf_op jit(solution)/shard_map/ppermute | solution.py:240
  88.1 5.3 %collective-permute-done.refs_1_ = bf16[12,96,256]{2,1,0:T(8,128)(2,1)} collective-permute-done((bf16[12,96,256]{2,1,0:T(8,128)(2,1)S(1)}, bf16[12,96,256]{2,1,0:T(8,128)(2,1)}, u32[]{:S(2)}, u32[]{:S(2)}) %collective-permute-start) | collective-permute-done | bytes 589856 | tf_op jit(solution)/shard_map/ppermute | solution.py:236
  93.4 1.9 %collective-permute-start.4 = (bf16[12,96,256]{2,1,0:T(8,128)(2,1)}, bf16[12,96,256]{2,1,0:T(8,128)(2,1)}, u32[]{:S(2)}, u32[]{:S(2)}) collective-permute-start(bf16[12,96,256]{2,1,0:T(8,128)(2,1)} %collective-permute-done.refs_1_), channel_id=1, source_target_pairs={{0,1},{1,0},{2,3},{3,2},{4,5},{5,4},{6,7},{7,6},{8,9},{9,8},{10,11... | collective-permute-start | bytes 1769480 | tf_op jit(solution)/shard_map/ppermute | solution.py:240
  95.3 0.0 collective-permute-done.1.refs_2_
  95.3 2.4 %collective-permute-start.5 = (bf16[12,96,256]{2,1,0:T(8,128)(2,1)}, bf16[12,96,256]{2,1,0:T(8,128)(2,1)}, u32[]{:S(2)}, u32[]{:S(2)}) collective-permute-start(bf16[12,96,256]{2,1,0:T(8,128)(2,1)} %collective-permute-done.1.refs_2_), channel_id=1, source_target_pairs={{0,1},{1,0},{2,3},{3,2},{4,5},{5,4},{6,7},{7,6},{8,9},{9,8},{10,11... | collective-permute-start | bytes 1769480 | tf_op jit(solution)/shard_map/ppermute | solution.py:240
  97.7 1.4 %collective-permute-done.2.refs_3_ = bf16[12,96,256]{2,1,0:T(8,128)(2,1)} collective-permute-done((bf16[12,96,256]{2,1,0:T(8,128)(2,1)S(1)}, bf16[12,96,256]{2,1,0:T(8,128)(2,1)}, u32[]{:S(2)}, u32[]{:S(2)}) %collective-permute-start.2) | collective-permute-done | bytes 589856 | tf_op jit(solution)/shard_map/ppermute | solution.py:236
  99.1 1.9 %collective-permute-start.6 = (bf16[12,96,256]{2,1,0:T(8,128)(2,1)}, bf16[12,96,256]{2,1,0:T(8,128)(2,1)}, u32[]{:S(2)}, u32[]{:S(2)}) collective-permute-start(bf16[12,96,256]{2,1,0:T(8,128)(2,1)} %collective-permute-done.2.refs_3_), channel_id=1, source_target_pairs={{0,1},{1,0},{2,3},{3,2},{4,5},{5,4},{6,7},{7,6},{8,9},{9,8},{10,11... | collective-permute-start | bytes 1769480 | tf_op jit(solution)/shard_map/ppermute | solution.py:240
  101.0 0.6 all-to-all-done.2
  101.6 1.1 reduce_sum.21
  102.8 0.7 reshape.14
  103.5 3.5 %all-to-all-start.3 = ((bf16[12,12,256]{2,1,0:T(8,128)(2,1)}), bf16[12,12,256]{2,1,0:T(8,128)(2,1)S(1)}, u32[]{:S(2)}, u32[]{:S(2)}) async-start(bf16[12,12,256]{2,1,0:T(8,128)(2,1)} %reshape.14), calls=%async_computation.3 | async-start | bytes 196608 | tf_op jit(solution)/shard_map/all_to_all | solution.py:260
  107.0 0.0 collective-permute-done.3.refs_4_
  107.0 0.0 collective-permute-done.4.refs_5_
  107.0 0.0 collective-permute-done.5.refs_6_
  107.0 0.0 collective-permute-done.6.refs_7_
  107.0 7.0 %project.1 = (bf16[192,512]{1,0:T(8,128)(2,1)}, bf16[192,4608]{1,0:T(8,128)(2,1)}) custom-call(s32[2]{0:T(128)S(1)} %copy-done.6, bf16[12,96,256]{2,1,0:T(8,128)(2,1)S(1)} %regroup.1.refs_0_, bf16[12,96,256]{2,1,0:T(8,128)(2,1)} %collective-permute-done.refs_1_, bf16[12,96,256]{2,1,0:T(8,128)(2,1)} %collective-permute-done.1.refs_2_, ...), custom_call_target="tpu_custom_call" | custom-call | flops 1811939328 | bytes 8257536 | tf_op jit(solution)/shard_map/project/pallas_call | solution.py:176
  114.0 5.0 %all-to-all-done.3 = bf16[12,12,256]{2,1,0:T(8,128)(2,1)S(1)} async-done(((bf16[12,12,256]{2,1,0:T(8,128)(2,1)}), bf16[12,12,256]{2,1,0:T(8,128)(2,1)S(1)}, u32[]{:S(2)}, u32[]{:S(2)}) %all-to-all-start.3) | async-done | bytes 73760 | tf_op jit(solution)/shard_map/all_to_all | solution.py:260
  119.0 0.6 broadcast_multiply_fusion
  (15 shorter events, 0.1 us)
Async XLA Ops:
  0.6 22.1 %copy-start.7 = (bf16[12]{0:T(256)(128)(2,1)S(1)}, bf16[12]{0:T(256)(128)(2,1)}, u32[]{:S(2)}) copy-start(bf16[12]{0:T(256)(128)(2,1)} %param.9) | copy-start | bytes 76
  0.6 22.1 %copy-start.5 = (bf16[12,256]{1,0:T(8,128)(2,1)S(1)}, bf16[12,256]{1,0:T(8,128)(2,1)}, u32[]{:S(2)}) copy-start(bf16[12,256]{1,0:T(8,128)(2,1)} %values.1) | copy-start | bytes 18436
  1.3 64.9 %copy-start.4 = (bf16[384,384]{1,0:T(8,128)(2,1)S(1)}, bf16[384,384]{1,0:T(8,128)(2,1)}, u32[]{:S(2)}) copy-start(bf16[384,384]{1,0:T(8,128)(2,1)} %constant.21.clone.perm) | copy-start | bytes 884740
  5.9 44.0 %copy-start.2 = (bf16[192,1664]{1,0:T(8,128)(2,1)S(1)}, bf16[192,1664]{1,0:T(8,128)(2,1)}, u32[]{:S(2)}) copy-start(bf16[192,1664]{1,0:T(8,128)(2,1)} %get-tuple-element.11.refs_0_) | copy-start | bytes 1916932
  5.9 45.9 %collective-permute-start.7 = (bf16[192,1664]{1,0:T(8,128)(2,1)}, bf16[192,1664]{1,0:T(8,128)(2,1)S(1)}, u32[]{:S(2)}, u32[]{:S(2)}) collective-permute-start(bf16[192,1664]{1,0:T(8,128)(2,1)} %get-tuple-element.12), channel_id=1, source_target_pairs={{0,16},{16,32},{32,48},{48,0},{1,17},{17,33},{33,49},{49,1},{2,18}... | collective-permute-start | bytes 1916936 | tf_op jit(solution)/shard_map/ppermute | solution.py:236
  17.5 36.8 %collective-permute-start.8 = (bf16[192,1664]{1,0:T(8,128)(2,1)}, bf16[192,1664]{1,0:T(8,128)(2,1)}, u32[]{:S(2)}, u32[]{:S(2)}) collective-permute-start(bf16[192,1664]{1,0:T(8,128)(2,1)} %get-tuple-element.13), channel_id=1, source_target_pairs={{0,48},{16,0},{32,16},{48,32},{1,49},{17,1},{33,17},{49,33},{2,50}... | collective-permute-start | bytes 1916936 | tf_op jit(solution)/shard_map/ppermute | solution.py:236
  19.4 36.8 %collective-permute-start.9 = (bf16[192,1664]{1,0:T(8,128)(2,1)}, bf16[192,1664]{1,0:T(8,128)(2,1)}, u32[]{:S(2)}, u32[]{:S(2)}) collective-permute-start(bf16[192,1664]{1,0:T(8,128)(2,1)} %get-tuple-element.14), channel_id=1, source_target_pairs={{0,32},{16,48},{32,0},{48,16},{1,33},{17,49},{33,1},{49,17},{2,34}... | collective-permute-start | bytes 1916936 | tf_op jit(solution)/shard_map/ppermute | solution.py:236
  41.9 34.5 %copy-start.3 = (bf16[384,384]{1,0:T(8,128)(2,1)S(1)}, bf16[384,384]{1,0:T(8,128)(2,1)}, u32[]{:S(2)}) copy-start(bf16[384,384]{1,0:T(8,128)(2,1)} %constant.20.clone.refs_8_) | copy-start | bytes 884740
  41.9 34.5 %copy-start.6 = (s32[2]{0:T(128)S(1)}, s32[2]{0:T(128)}, u32[]{:S(2)}) copy-start(s32[2]{0:T(128)} %pad_add_fusion.place) | copy-start | bytes 28
  42.8 23.4 %all-to-all-start.1 = ((bf16[8,144,256]{2,1,0:T(8,128)(2,1)}), bf16[8,144,256]{2,1,0:T(8,128)(2,1)S(1)}, u32[]{:S(2)}, u32[]{:S(2)}) async-start(bf16[8,144,256]{2,1,0:T(8,128)(2,1)} %broadcast_in_dim.8), calls=%async_computation.1 | async-start | bytes 1179648 | tf_op jit(solution)/shard_map/all_to_all | solution.py:232
  49.9 21.1 %collective-permute-start.10 = (bf16[192,1664]{1,0:T(8,128)(2,1)S(1)}, bf16[192,1664]{1,0:T(8,128)(2,1)}, u32[]{:S(2)}, u32[]{:S(2)}) collective-permute-start(bf16[192,1664]{1,0:T(8,128)(2,1)S(1)} %copy-done.2), channel_id=1, source_target_pairs={{0,1},{1,0},{2,3},{3,2},{4,5},{5,4},{6,7},{7,6},{8,9},{9,8},{10,11... | collective-permute-start | bytes 1916936 | tf_op jit(solution)/shard_map/ppermute | solution.py:240
  51.9 22.3 %collective-permute-start.11 = (bf16[192,1664]{1,0:T(8,128)(2,1)S(1)}, bf16[192,1664]{1,0:T(8,128)(2,1)}, u32[]{:S(2)}, u32[]{:S(2)}) collective-permute-start(bf16[192,1664]{1,0:T(8,128)(2,1)S(1)} %collective-permute-done.7.refs_1_), channel_id=1, source_target_pairs={{0,1},{1,0},{2,3},{3,2},{4,5},{5,4},{6,7},{7,6},{8,9},{9,8},{10,11... | collective-permute-start | bytes 1916936 | tf_op jit(solution)/shard_map/ppermute | solution.py:240
  54.3 22.1 %collective-permute-start.12 = (bf16[192,1664]{1,0:T(8,128)(2,1)}, bf16[192,1664]{1,0:T(8,128)(2,1)}, u32[]{:S(2)}, u32[]{:S(2)}) collective-permute-start(bf16[192,1664]{1,0:T(8,128)(2,1)} %collective-permute-done.8.refs_2_), channel_id=1, source_target_pairs={{0,1},{1,0},{2,3},{3,2},{4,5},{5,4},{6,7},{7,6},{8,9},{9,8},{10,11... | collective-permute-start | bytes 1916936 | tf_op jit(solution)/shard_map/ppermute | solution.py:240
  56.2 20.2 %collective-permute-start.13 = (bf16[192,1664]{1,0:T(8,128)(2,1)}, bf16[192,1664]{1,0:T(8,128)(2,1)}, u32[]{:S(2)}, u32[]{:S(2)}) collective-permute-start(bf16[192,1664]{1,0:T(8,128)(2,1)} %collective-permute-done.9.refs_3_), channel_id=1, source_target_pairs={{0,1},{1,0},{2,3},{3,2},{4,5},{5,4},{6,7},{7,6},{8,9},{9,8},{10,11... | collective-permute-start | bytes 1916936 | tf_op jit(solution)/shard_map/ppermute | solution.py:240
  67.0 26.4 %collective-permute-start = (bf16[12,96,256]{2,1,0:T(8,128)(2,1)S(1)}, bf16[12,96,256]{2,1,0:T(8,128)(2,1)}, u32[]{:S(2)}, u32[]{:S(2)}) collective-permute-start(bf16[12,96,256]{2,1,0:T(8,128)(2,1)S(1)} %regroup.1.refs_0_), channel_id=1, source_target_pairs={{0,16},{16,32},{32,48},{48,0},{1,17},{17,33},{33,49},{49,1},{2,18}... | collective-permute-start | bytes 1769480 | tf_op jit(solution)/shard_map/ppermute | solution.py:236
  71.1 24.3 %collective-permute-start.1 = (bf16[12,96,256]{2,1,0:T(8,128)(2,1)S(1)}, bf16[12,96,256]{2,1,0:T(8,128)(2,1)}, u32[]{:S(2)}, u32[]{:S(2)}) collective-permute-start(bf16[12,96,256]{2,1,0:T(8,128)(2,1)S(1)} %regroup.1.refs_0_), channel_id=1, source_target_pairs={{0,32},{16,48},{32,0},{48,16},{1,33},{17,49},{33,1},{49,17},{2,34}... | collective-permute-start | bytes 1769480 | tf_op jit(solution)/shard_map/ppermute | solution.py:236
  74.1 25.0 %collective-permute-start.2 = (bf16[12,96,256]{2,1,0:T(8,128)(2,1)S(1)}, bf16[12,96,256]{2,1,0:T(8,128)(2,1)}, u32[]{:S(2)}, u32[]{:S(2)}) collective-permute-start(bf16[12,96,256]{2,1,0:T(8,128)(2,1)S(1)} %regroup.1.refs_0_), channel_id=1, source_target_pairs={{0,48},{16,0},{32,16},{48,32},{1,49},{17,1},{33,17},{49,33},{2,50}... | collective-permute-start | bytes 1769480 | tf_op jit(solution)/shard_map/ppermute | solution.py:236
  81.9 25.1 %copy-start = (bf16[192,4608]{1,0:T(8,128)(2,1)S(1)}, bf16[192,4608]{1,0:T(8,128)(2,1)}, u32[]{:S(2)}) copy-start(bf16[192,4608]{1,0:T(8,128)(2,1)} %hidden.1) | copy-start | bytes 5308420
  81.9 25.1 %copy-start.1 = (bf16[192,512]{1,0:T(8,128)(2,1)S(1)}, bf16[192,512]{1,0:T(8,128)(2,1)}, u32[]{:S(2)}) copy-start(bf16[192,512]{1,0:T(8,128)(2,1)} %cot.1) | copy-start | bytes 589828
  81.9 19.8 %all-to-all-start.2 = ((bf16[8,144,256]{2,1,0:T(8,128)(2,1)}), bf16[8,144,256]{2,1,0:T(8,128)(2,1)}, u32[]{:S(2)}, u32[]{:S(2)}) async-start(bf16[8,144,256]{2,1,0:T(8,128)(2,1)} %group_term.1), calls=%async_computation.2 | async-start | bytes 1179648 | tf_op jit(solution)/shard_map/all_to_all | solution.py:258
  86.2 20.7 %collective-permute-start.3 = (bf16[12,96,256]{2,1,0:T(8,128)(2,1)S(1)}, bf16[12,96,256]{2,1,0:T(8,128)(2,1)S(1)}, u32[]{:S(2)}, u32[]{:S(2)}) collective-permute-start(bf16[12,96,256]{2,1,0:T(8,128)(2,1)S(1)} %regroup.1.refs_0_), channel_id=1, source_target_pairs={{0,1},{1,0},{2,3},{3,2},{4,5},{5,4},{6,7},{7,6},{8,9},{9,8},{10,11... | collective-permute-start | bytes 1769480 | tf_op jit(solution)/shard_map/ppermute | solution.py:240
  93.4 13.6 %collective-permute-start.4 = (bf16[12,96,256]{2,1,0:T(8,128)(2,1)}, bf16[12,96,256]{2,1,0:T(8,128)(2,1)}, u32[]{:S(2)}, u32[]{:S(2)}) collective-permute-start(bf16[12,96,256]{2,1,0:T(8,128)(2,1)} %collective-permute-done.refs_1_), channel_id=1, source_target_pairs={{0,1},{1,0},{2,3},{3,2},{4,5},{5,4},{6,7},{7,6},{8,9},{9,8},{10,11... | collective-permute-start | bytes 1769480 | tf_op jit(solution)/shard_map/ppermute | solution.py:240
  95.3 11.7 %collective-permute-start.5 = (bf16[12,96,256]{2,1,0:T(8,128)(2,1)}, bf16[12,96,256]{2,1,0:T(8,128)(2,1)}, u32[]{:S(2)}, u32[]{:S(2)}) collective-permute-start(bf16[12,96,256]{2,1,0:T(8,128)(2,1)} %collective-permute-done.1.refs_2_), channel_id=1, source_target_pairs={{0,1},{1,0},{2,3},{3,2},{4,5},{5,4},{6,7},{7,6},{8,9},{9,8},{10,11... | collective-permute-start | bytes 1769480 | tf_op jit(solution)/shard_map/ppermute | solution.py:240
  99.1 7.9 %collective-permute-start.6 = (bf16[12,96,256]{2,1,0:T(8,128)(2,1)}, bf16[12,96,256]{2,1,0:T(8,128)(2,1)}, u32[]{:S(2)}, u32[]{:S(2)}) collective-permute-start(bf16[12,96,256]{2,1,0:T(8,128)(2,1)} %collective-permute-done.2.refs_3_), channel_id=1, source_target_pairs={{0,1},{1,0},{2,3},{3,2},{4,5},{5,4},{6,7},{7,6},{8,9},{9,8},{10,11... | collective-permute-start | bytes 1769480 | tf_op jit(solution)/shard_map/ppermute | solution.py:240
  103.5 15.6 %all-to-all-start.3 = ((bf16[12,12,256]{2,1,0:T(8,128)(2,1)}), bf16[12,12,256]{2,1,0:T(8,128)(2,1)S(1)}, u32[]{:S(2)}, u32[]{:S(2)}) async-start(bf16[12,12,256]{2,1,0:T(8,128)(2,1)} %reshape.14), calls=%async_computation.3 | async-start | bytes 196608 | tf_op jit(solution)/shard_map/all_to_all | solution.py:260

commit v5 on v4

--- a/solution.py
+++ b/solution.py
@@ -46,18 +46,19 @@
 
 def pack(place, hidden, cotangent):
     tokens, width = hidden.shape
-    whole = pl.BlockSpec((tokens, WIDE + 2 * HALF), lambda k, place: (0, 0))
+    step = tokens // 2
+    whole = pl.BlockSpec((step, WIDE + 2 * HALF), lambda k, place: (k, 0))
     return pl.pallas_call(
         pack_kernel,
         grid_spec=pltpu.PrefetchScalarGridSpec(
             num_scalar_prefetch=1,
-            grid=(1,),
+            grid=(2,),
             in_specs=[
-                pl.BlockSpec((tokens, width), lambda k, place: (0, 0)),
-                pl.BlockSpec((tokens, 2 * HALF), lambda k, place: (0, 0)),
+                pl.BlockSpec((step, width), lambda k, place: (k, 0)),
+                pl.BlockSpec((step, 2 * HALF), lambda k, place: (k, 0)),
             ],
             out_specs=[whole] * NX,
-            scratch_shapes=[pltpu.VMEM((NX, tokens, WIDE), BF)],
+            scratch_shapes=[pltpu.VMEM((NX, step, WIDE), BF)],
         ),
         out_shape=[jax.ShapeDtypeStruct((tokens, WIDE + 2 * HALF), BF)] * NX,
         compiler_params=pltpu.CompilerParams(vmem_limit_bytes=56 * 2**20),
@@ -134,6 +135,23 @@
     )(parts, jnp.asarray(IN_ORDER, BF))
 
 
+def sum_y_kernel(parts, out):
+    total = parts[0].astype(F32)
+    for k in range(1, NY):
+        total += parts[k].astype(F32)
+    for z in range(NZ):
+        out[z] = total[z * ROWS : (z + 1) * ROWS].astype(BF)
+
+
+def sum_over_y(parts):
+    return pl.pallas_call(
+        sum_y_kernel,
+        out_shape=jax.ShapeDtypeStruct((NZ, ROWS, HALF), BF),
+        compiler_params=pltpu.CompilerParams(vmem_limit_bytes=12 * 2**20),
+        name="sum_over_y",
+    )(parts)
+
+
 def project_kernel(place, *refs):
     *blocks, hidden, cot_mine, cot_other, keys, grad, acc, cot, held = refs
     step = pl.program_id(0)
@@ -222,7 +240,7 @@
     return pl.pallas_call(
         shard_kernel,
         out_shape=jax.ShapeDtypeStruct((NZ, ROWS, HALF), BF),
-        compiler_params=pltpu.CompilerParams(vmem_limit_bytes=4 * 2**20),
+        compiler_params=pltpu.CompilerParams(vmem_limit_bytes=56 * 2**20),
         name="scaled_copies",
     )(values, scales.reshape(1, ROWS))
 
@@ -248,15 +266,17 @@
     w_z = lax.all_to_all(copies, "z", split_axis=0, concat_axis=0, tiled=True)
 
     packed = pack(place, hidden, cotangent)
+    w_z, packed = lax.optimization_barrier((w_z, packed))
     held = [packed[0]] + [shift(packed[r], r) for r in (1, 3, 2)]
     term = group_term(place, held + [swap(piece) for piece in held])
 
     w_y = regroup(to_all(w_z.reshape(NZ * ROWS, HALF), Y, NY))
-    mine = [w_y] + [shift(w_y, r) for r in range(1, NX)]
+    near = [shift(w_y, r) for r in (1, 3, 2)]
+    mine = [w_y, near[0], near[2], near[1]]
     other = [swap(piece) for piece in mine]
 
     t_y = lax.all_to_all(term, Y, split_axis=0, concat_axis=0, tiled=True)
-    sum_y = t_y.astype(F32).sum(0).astype(BF).reshape(NZ, ROWS, HALF)
+    sum_y = sum_over_y(t_y)
     t_z = lax.all_to_all(sum_y, "z", split_axis=0, concat_axis=0, tiled=True)
     weight_grad = t_z.astype(F32).sum(0) * factor
     keys, grad_input = project(place, mine, other, hidden, cotangent)

time: 122 us -> 127 us (1.041)
  the two profiles are of different devices: /device:TPU:6 before, /device:TPU:2 now
where the time goes in v5:
time: 127 us; the launch traced here: 126 us
  starting transfers between devices  72.2 us (57%)
  waiting for transfers between devices  30.9 us (24%)
  Pallas kernels  19.7 us (16%)
    ppermute x6, starting transfers between devices, shift(): return lax.ppermute(piece, 'x', [(k, (k + r) % NX) for k in range(NX)])  22.3 us
    ppermute x8, starting transfers between devices, swap(): return lax.ppermute(piece, 'c', [(0, 1), (1, 0)])  16.3 us
    all_to_all x1, starting transfers between devices, on_device(): w_z = lax.all_to_all(copies, 'z', split_axis=0, concat_axis=0, tiled=True)  15.2 us
    ppermute x6, waiting for transfers between devices, shift(): return lax.ppermute(piece, 'x', [(k, (k + r) % NX) for k in range(NX)])  12 us
    all_to_all x1, waiting for transfers between devices, on_device(): t_y = lax.all_to_all(term, Y, split_axis=0, concat_axis=0, tiled=True)  7.4 us
    all_to_all x1, waiting for transfers between devices, on_device(): w_z = lax.all_to_all(copies, 'z', split_axis=0, concat_axis=0, tiled=True)  7.36 us
    all_to_all x1, starting transfers between devices, on_device(): t_y = lax.all_to_all(term, Y, split_axis=0, concat_axis=0, tiled=True)  7.23 us
    pallas_call x1, Pallas kernels, project(): pl.pallas_call(project_kernel, grid_spec=pltpu.PrefetchScalarGridSpec(num...  7.11 us
  transfers between devices with their start and end apart: 18, of which 5 were waited for; matrix products, arithmetic and copies ran while one was open for 1% of the time, Pallas kernels for 14%

profile of v5, /device:TPU:2, one launch (start us, length us, event | category | flops | bytes accessed | tf_op | source)
XLA Modules:
  0.0 125.8 jit_solution(5531240284553082881)
XLA Ops:
  0.6 1.4 %scaled_copies.1 = bf16[12,12,256]{2,1,0:T(8,128)(2,1)} custom-call(bf16[12,256]{1,0:T(8,128)(2,1)} %values.1, bf16[1,12]{1,0:T(2,128)(2,1)} %bitcast.3), custom_call_target="tpu_custom_call" | custom-call | tf_op jit(solution)/shard_map/scaled_copies/pallas_call | solution.py:240
  2.1 15.2 %all-to-all-start = ((bf16[12,12,256]{2,1,0:T(8,128)(2,1)}), bf16[12,12,256]{2,1,0:T(8,128)(2,1)S(1)}, u32[]{:S(2)}, u32[]{:S(2)}) async-start(bf16[12,12,256]{2,1,0:T(8,128)(2,1)} %scaled_copies.1), calls=%async_computation | async-start | bytes 196608 | tf_op jit(solution)/shard_map/all_to_all | solution.py:266
  17.2 0.6 pad_add_fusion.place
  17.8 4.0 %pack.1 = (bf16[192,1664]{1,0:T(8,128)(2,1)}, bf16[192,1664]{1,0:T(8,128)(2,1)}, bf16[192,1664]{1,0:T(8,128)(2,1)}, bf16[192,1664]{1,0:T(8,128)(2,1)}) custom-call(s32[2]{0:T(128)} %pad_add_fusion.place, bf16[192,4608]{1,0:T(8,128)(2,1)} %refs_8_.2, bf16[192,512]{1,0:T(8,128)(2,1)} %refs_10_.1), custom_call_target="tpu_custom_call" | custom-call | flops 884736 | bytes 3538944 | tf_op jit(solution)/shard_map/pack/pallas_call | solution.py:51
  21.8 7.4 %all-to-all-done = bf16[12,12,256]{2,1,0:T(8,128)(2,1)S(1)} async-done(((bf16[12,12,256]{2,1,0:T(8,128)(2,1)}), bf16[12,12,256]{2,1,0:T(8,128)(2,1)S(1)}, u32[]{:S(2)}, u32[]{:S(2)}) %all-to-all-start) | async-done | bytes 73760 | tf_op jit(solution)/shard_map/all_to_all | solution.py:266
  29.2 3.4 %collective-permute-start.7 = (bf16[192,1664]{1,0:T(8,128)(2,1)}, bf16[192,1664]{1,0:T(8,128)(2,1)S(1)}, u32[]{:S(2)}, u32[]{:S(2)}) collective-permute-start(bf16[192,1664]{1,0:T(8,128)(2,1)} %get-tuple-element.22), channel_id=1, source_target_pairs={{0,16},{16,32},{32,48},{48,0},{1,17},{17,33},{33,49},{49,1},{2,18}... | collective-permute-start | bytes 1916936 | tf_op jit(solution)/shard_map/ppermute | solution.py:254
  32.6 2.4 %collective-permute-start.8 = (bf16[192,1664]{1,0:T(8,128)(2,1)}, bf16[192,1664]{1,0:T(8,128)(2,1)}, u32[]{:S(2)}, u32[]{:S(2)}) collective-permute-start(bf16[192,1664]{1,0:T(8,128)(2,1)} %get-tuple-element.23), channel_id=1, source_target_pairs={{0,48},{16,0},{32,16},{48,32},{1,49},{17,1},{33,17},{49,33},{2,50}... | collective-permute-start | bytes 1916936 | tf_op jit(solution)/shard_map/ppermute | solution.py:254
  35.0 4.0 %collective-permute-start.9 = (bf16[192,1664]{1,0:T(8,128)(2,1)}, bf16[192,1664]{1,0:T(8,128)(2,1)}, u32[]{:S(2)}, u32[]{:S(2)}) collective-permute-start(bf16[192,1664]{1,0:T(8,128)(2,1)} %get-tuple-element.24), channel_id=1, source_target_pairs={{0,32},{16,48},{32,0},{48,16},{1,33},{17,49},{33,1},{49,17},{2,34}... | collective-permute-start | bytes 1916936 | tf_op jit(solution)/shard_map/ppermute | solution.py:254
  39.1 0.9 broadcast_in_dim.8
  40.0 7.1 %all-to-all-start.1 = ((bf16[8,144,256]{2,1,0:T(8,128)(2,1)}), bf16[8,144,256]{2,1,0:T(8,128)(2,1)S(1)}, u32[]{:S(2)}, u32[]{:S(2)}) async-start(bf16[8,144,256]{2,1,0:T(8,128)(2,1)} %broadcast_in_dim.8), calls=%async_computation.1 | async-start | bytes 1179648 | tf_op jit(solution)/shard_map/all_to_all | solution.py:250
  47.1 0.0 copy-done.2
  47.1 1.9 %collective-permute-start.10 = (bf16[192,1664]{1,0:T(8,128)(2,1)S(1)}, bf16[192,1664]{1,0:T(8,128)(2,1)}, u32[]{:S(2)}, u32[]{:S(2)}) collective-permute-start(bf16[192,1664]{1,0:T(8,128)(2,1)S(1)} %copy-done.2), channel_id=1, source_target_pairs={{0,1},{1,0},{2,3},{3,2},{4,5},{5,4},{6,7},{7,6},{8,9},{9,8},{10,11... | collective-permute-start | bytes 1916936 | tf_op jit(solution)/shard_map/ppermute | solution.py:258
  49.0 0.0 collective-permute-done.7.refs_1_
  49.0 2.4 %collective-permute-start.11 = (bf16[192,1664]{1,0:T(8,128)(2,1)S(1)}, bf16[192,1664]{1,0:T(8,128)(2,1)}, u32[]{:S(2)}, u32[]{:S(2)}) collective-permute-start(bf16[192,1664]{1,0:T(8,128)(2,1)S(1)} %collective-permute-done.7.refs_1_), channel_id=1, source_target_pairs={{0,1},{1,0},{2,3},{3,2},{4,5},{5,4},{6,7},{7,6},{8,9},{9,8},{10,11... | collective-permute-start | bytes 1916936 | tf_op jit(solution)/shard_map/ppermute | solution.py:258
  51.4 0.0 collective-permute-done.8.refs_2_
  51.5 1.9 %collective-permute-start.12 = (bf16[192,1664]{1,0:T(8,128)(2,1)}, bf16[192,1664]{1,0:T(8,128)(2,1)}, u32[]{:S(2)}, u32[]{:S(2)}) collective-permute-start(bf16[192,1664]{1,0:T(8,128)(2,1)} %collective-permute-done.8.refs_2_), channel_id=1, source_target_pairs={{0,1},{1,0},{2,3},{3,2},{4,5},{5,4},{6,7},{7,6},{8,9},{9,8},{10,11... | collective-permute-start | bytes 1916936 | tf_op jit(solution)/shard_map/ppermute | solution.py:258
  53.4 9.3 %collective-permute-done.9.refs_3_ = bf16[192,1664]{1,0:T(8,128)(2,1)} collective-permute-done((bf16[192,1664]{1,0:T(8,128)(2,1)}, bf16[192,1664]{1,0:T(8,128)(2,1)}, u32[]{:S(2)}, u32[]{:S(2)}) %collective-permute-start.9) | collective-permute-done | bytes 639008 | tf_op jit(solution)/shard_map/ppermute | solution.py:254
  62.7 1.9 %collective-permute-start.13 = (bf16[192,1664]{1,0:T(8,128)(2,1)}, bf16[192,1664]{1,0:T(8,128)(2,1)}, u32[]{:S(2)}, u32[]{:S(2)}) collective-permute-start(bf16[192,1664]{1,0:T(8,128)(2,1)} %collective-permute-done.9.refs_3_), channel_id=1, source_target_pairs={{0,1},{1,0},{2,3},{3,2},{4,5},{5,4},{6,7},{7,6},{8,9},{9,8},{10,11... | collective-permute-start | bytes 1916936 | tf_op jit(solution)/shard_map/ppermute | solution.py:258
  64.7 0.0 all-to-all-done.1.parts
  64.7 0.9 regroup.1.refs_0_
  65.6 1.9 %collective-permute-start = (bf16[12,96,256]{2,1,0:T(8,128)(2,1)S(1)}, bf16[12,96,256]{2,1,0:T(8,128)(2,1)}, u32[]{:S(2)}, u32[]{:S(2)}) collective-permute-start(bf16[12,96,256]{2,1,0:T(8,128)(2,1)S(1)} %regroup.1.refs_0_), channel_id=1, source_target_pairs={{0,16},{16,32},{32,48},{48,0},{1,17},{17,33},{33,49},{49,1},{2,18}... | collective-permute-start | bytes 1769480 | tf_op jit(solution)/shard_map/ppermute | solution.py:254
  67.5 0.0 collective-permute-done.10.refs_4_
  67.5 6.0 %collective-permute-start.1 = (bf16[12,96,256]{2,1,0:T(8,128)(2,1)S(1)}, bf16[12,96,256]{2,1,0:T(8,128)(2,1)}, u32[]{:S(2)}, u32[]{:S(2)}) collective-permute-start(bf16[12,96,256]{2,1,0:T(8,128)(2,1)S(1)} %regroup.1.refs_0_), channel_id=1, source_target_pairs={{0,32},{16,48},{32,0},{48,16},{1,33},{17,49},{33,1},{49,17},{2,34}... | collective-permute-start | bytes 1769480 | tf_op jit(solution)/shard_map/ppermute | solution.py:254
  73.5 0.0 collective-permute-done.11.refs_5_
  73.5 4.5 %collective-permute-start.2 = (bf16[12,96,256]{2,1,0:T(8,128)(2,1)S(1)}, bf16[12,96,256]{2,1,0:T(8,128)(2,1)}, u32[]{:S(2)}, u32[]{:S(2)}) collective-permute-start(bf16[12,96,256]{2,1,0:T(8,128)(2,1)S(1)} %regroup.1.refs_0_), channel_id=1, source_target_pairs={{0,48},{16,0},{32,16},{48,32},{1,49},{17,1},{33,17},{49,33},{2,50}... | collective-permute-start | bytes 1769480 | tf_op jit(solution)/shard_map/ppermute | solution.py:254
  78.1 0.0 collective-permute-done.12.refs_6_
  78.1 0.0 collective-permute-done.13.refs_7_
  78.1 0.0 copy-done.3
  78.1 0.0 copy-done.5
  78.1 5.5 %group_term.1 = bf16[8,144,256]{2,1,0:T(8,128)(2,1)} custom-call(s32[2]{0:T(128)S(1)} %copy-done.5, bf16[192,1664]{1,0:T(8,128)(2,1)S(1)} %copy-done.2, bf16[192,1664]{1,0:T(8,128)(2,1)S(1)} %collective-permute-done.7.refs_1_, bf16[192,1664]{1,0:T(8,128)(2,1)} %collective-permute-done.8.refs_2_, bf16[192,1664]{1,0:T(8,128)(2,1)} %collective-permute-done.9.refs_3_, ...), custom_call_target="tpu_custom_call" | custom-call | flops 1132462080 | bytes 5111808 | tf_op jit(solution)/shard_map/group_term/pallas_call | solution.py:92
  83.6 7.2 %all-to-all-start.2 = ((bf16[8,144,256]{2,1,0:T(8,128)(2,1)}), bf16[8,144,256]{2,1,0:T(8,128)(2,1)S(1)}, u32[]{:S(2)}, u32[]{:S(2)}) async-start(bf16[8,144,256]{2,1,0:T(8,128)(2,1)} %group_term.1), calls=%async_computation.2 | async-start | bytes 1179648 | tf_op jit(solution)/shard_map/all_to_all | solution.py:278
  90.8 1.9 %collective-permute-start.3 = (bf16[12,96,256]{2,1,0:T(8,128)(2,1)S(1)}, bf16[12,96,256]{2,1,0:T(8,128)(2,1)}, u32[]{:S(2)}, u32[]{:S(2)}) collective-permute-start(bf16[12,96,256]{2,1,0:T(8,128)(2,1)S(1)} %regroup.1.refs_0_), channel_id=1, source_target_pairs={{0,1},{1,0},{2,3},{3,2},{4,5},{5,4},{6,7},{7,6},{8,9},{9,8},{10,11... | collective-permute-start | bytes 1769480 | tf_op jit(solution)/shard_map/ppermute | solution.py:258
  92.8 0.0 collective-permute-done.refs_1_
  92.8 2.4 %collective-permute-start.4 = (bf16[12,96,256]{2,1,0:T(8,128)(2,1)}, bf16[12,96,256]{2,1,0:T(8,128)(2,1)}, u32[]{:S(2)}, u32[]{:S(2)}) collective-permute-start(bf16[12,96,256]{2,1,0:T(8,128)(2,1)} %collective-permute-done.refs_1_), channel_id=1, source_target_pairs={{0,1},{1,0},{2,3},{3,2},{4,5},{5,4},{6,7},{7,6},{8,9},{9,8},{10,11... | collective-permute-start | bytes 1769480 | tf_op jit(solution)/shard_map/ppermute | solution.py:258
  95.2 0.0 collective-permute-done.1.refs_2_
  95.2 1.9 %collective-permute-start.5 = (bf16[12,96,256]{2,1,0:T(8,128)(2,1)}, bf16[12,96,256]{2,1,0:T(8,128)(2,1)}, u32[]{:S(2)}, u32[]{:S(2)}) collective-permute-start(bf16[12,96,256]{2,1,0:T(8,128)(2,1)} %collective-permute-done.1.refs_2_), channel_id=1, source_target_pairs={{0,1},{1,0},{2,3},{3,2},{4,5},{5,4},{6,7},{7,6},{8,9},{9,8},{10,11... | collective-permute-start | bytes 1769480 | tf_op jit(solution)/shard_map/ppermute | solution.py:258
  97.1 2.6 %collective-permute-done.2.refs_3_ = bf16[12,96,256]{2,1,0:T(8,128)(2,1)} collective-permute-done((bf16[12,96,256]{2,1,0:T(8,128)(2,1)S(1)}, bf16[12,96,256]{2,1,0:T(8,128)(2,1)}, u32[]{:S(2)}, u32[]{:S(2)}) %collective-permute-start.2) | collective-permute-done | bytes 589856 | tf_op jit(solution)/shard_map/ppermute | solution.py:254
  99.8 1.9 %collective-permute-start.6 = (bf16[12,96,256]{2,1,0:T(8,128)(2,1)}, bf16[12,96,256]{2,1,0:T(8,128)(2,1)}, u32[]{:S(2)}, u32[]{:S(2)}) collective-permute-start(bf16[12,96,256]{2,1,0:T(8,128)(2,1)} %collective-permute-done.2.refs_3_), channel_id=1, source_target_pairs={{0,1},{1,0},{2,3},{3,2},{4,5},{5,4},{6,7},{7,6},{8,9},{9,8},{10,11... | collective-permute-start | bytes 1769480 | tf_op jit(solution)/shard_map/ppermute | solution.py:258
  101.7 7.4 %all-to-all-done.2.parts = bf16[8,144,256]{2,1,0:T(8,128)(2,1)S(1)} async-done(((bf16[8,144,256]{2,1,0:T(8,128)(2,1)}), bf16[8,144,256]{2,1,0:T(8,128)(2,1)S(1)}, u32[]{:S(2)}, u32[]{:S(2)}) %all-to-all-start.2) | async-done | bytes 589856 | tf_op jit(solution)/shard_map/all_to_all | solution.py:278
  109.1 0.7 sum_over_y.1
  109.8 4.1 %all-to-all-start.3 = ((bf16[12,12,256]{2,1,0:T(8,128)(2,1)}), bf16[12,12,256]{2,1,0:T(8,128)(2,1)S(1)}, u32[]{:S(2)}, u32[]{:S(2)}) async-start(bf16[12,12,256]{2,1,0:T(8,128)(2,1)} %sum_over_y.1), calls=%async_computation.3 | async-start | bytes 196608 | tf_op jit(solution)/shard_map/all_to_all | solution.py:280
  113.9 0.0 collective-permute-done.3.refs_4_
  113.9 0.0 collective-permute-done.4.refs_5_
  113.9 0.0 collective-permute-done.5.refs_6_
  113.9 0.0 collective-permute-done.6.refs_7_
  114.0 7.1 %project.1 = (bf16[192,512]{1,0:T(8,128)(2,1)}, bf16[192,4608]{1,0:T(8,128)(2,1)}) custom-call(s32[2]{0:T(128)S(1)} %copy-done.5, bf16[12,96,256]{2,1,0:T(8,128)(2,1)S(1)} %regroup.1.refs_0_, bf16[12,96,256]{2,1,0:T(8,128)(2,1)} %collective-permute-done.refs_1_, bf16[12,96,256]{2,1,0:T(8,128)(2,1)} %collective-permute-done.1.refs_2_, ...), custom_call_target="tpu_custom_call" | custom-call | flops 1811939328 | bytes 8257536 | tf_op jit(solution)/shard_map/project/pallas_call | solution.py:194
  121.1 4.1 %all-to-all-done.3 = bf16[12,12,256]{2,1,0:T(8,128)(2,1)S(1)} async-done(((bf16[12,12,256]{2,1,0:T(8,128)(2,1)}), bf16[12,12,256]{2,1,0:T(8,128)(2,1)S(1)}, u32[]{:S(2)}, u32[]{:S(2)}) %all-to-all-start.3) | async-done | bytes 73760 | tf_op jit(solution)/shard_map/all_to_all | solution.py:280
  125.2 0.6 broadcast_multiply_fusion
  (11 shorter events, 0.1 us)
Async XLA Ops:
  2.1 27.1 %all-to-all-start = ((bf16[12,12,256]{2,1,0:T(8,128)(2,1)}), bf16[12,12,256]{2,1,0:T(8,128)(2,1)S(1)}, u32[]{:S(2)}, u32[]{:S(2)}) async-start(bf16[12,12,256]{2,1,0:T(8,128)(2,1)} %scaled_copies.1), calls=%async_computation | async-start | bytes 196608 | tf_op jit(solution)/shard_map/all_to_all | solution.py:266
  17.8 46.9 %copy-start.4 = (bf16[384,384]{1,0:T(8,128)(2,1)S(1)}, bf16[384,384]{1,0:T(8,128)(2,1)}, u32[]{:S(2)}) copy-start(bf16[384,384]{1,0:T(8,128)(2,1)} %constant.19.clone.perm) | copy-start | bytes 884740
  21.8 25.3 %copy-start.2 = (bf16[192,1664]{1,0:T(8,128)(2,1)S(1)}, bf16[192,1664]{1,0:T(8,128)(2,1)}, u32[]{:S(2)}) copy-start(bf16[192,1664]{1,0:T(8,128)(2,1)} %get-tuple-element.21.refs_0_) | copy-start | bytes 1916932
  21.8 56.3 %copy-start.3 = (bf16[384,384]{1,0:T(8,128)(2,1)S(1)}, bf16[384,384]{1,0:T(8,128)(2,1)}, u32[]{:S(2)}) copy-start(bf16[384,384]{1,0:T(8,128)(2,1)} %constant.18.clone.refs_8_) | copy-start | bytes 884740
  21.8 56.3 %copy-start.5 = (s32[2]{0:T(128)S(1)}, s32[2]{0:T(128)}, u32[]{:S(2)}) copy-start(s32[2]{0:T(128)} %pad_add_fusion.place) | copy-start | bytes 28
  29.2 19.8 %collective-permute-start.7 = (bf16[192,1664]{1,0:T(8,128)(2,1)}, bf16[192,1664]{1,0:T(8,128)(2,1)S(1)}, u32[]{:S(2)}, u32[]{:S(2)}) collective-permute-start(bf16[192,1664]{1,0:T(8,128)(2,1)} %get-tuple-element.22), channel_id=1, source_target_pairs={{0,16},{16,32},{32,48},{48,0},{1,17},{17,33},{33,49},{49,1},{2,18}... | collective-permute-start | bytes 1916936 | tf_op jit(solution)/shard_map/ppermute | solution.py:254
  32.6 18.9 %collective-permute-start.8 = (bf16[192,1664]{1,0:T(8,128)(2,1)}, bf16[192,1664]{1,0:T(8,128)(2,1)}, u32[]{:S(2)}, u32[]{:S(2)}) collective-permute-start(bf16[192,1664]{1,0:T(8,128)(2,1)} %get-tuple-element.23), channel_id=1, source_target_pairs={{0,48},{16,0},{32,16},{48,32},{1,49},{17,1},{33,17},{49,33},{2,50}... | collective-permute-start | bytes 1916936 | tf_op jit(solution)/shard_map/ppermute | solution.py:254
  35.0 27.7 %collective-permute-start.9 = (bf16[192,1664]{1,0:T(8,128)(2,1)}, bf16[192,1664]{1,0:T(8,128)(2,1)}, u32[]{:S(2)}, u32[]{:S(2)}) collective-permute-start(bf16[192,1664]{1,0:T(8,128)(2,1)} %get-tuple-element.24), channel_id=1, source_target_pairs={{0,32},{16,48},{32,0},{48,16},{1,33},{17,49},{33,1},{49,17},{2,34}... | collective-permute-start | bytes 1916936 | tf_op jit(solution)/shard_map/ppermute | solution.py:254
  40.0 24.7 %all-to-all-start.1 = ((bf16[8,144,256]{2,1,0:T(8,128)(2,1)}), bf16[8,144,256]{2,1,0:T(8,128)(2,1)S(1)}, u32[]{:S(2)}, u32[]{:S(2)}) async-start(bf16[8,144,256]{2,1,0:T(8,128)(2,1)} %broadcast_in_dim.8), calls=%async_computation.1 | async-start | bytes 1179648 | tf_op jit(solution)/shard_map/all_to_all | solution.py:250
  47.1 20.4 %collective-permute-start.10 = (bf16[192,1664]{1,0:T(8,128)(2,1)S(1)}, bf16[192,1664]{1,0:T(8,128)(2,1)}, u32[]{:S(2)}, u32[]{:S(2)}) collective-permute-start(bf16[192,1664]{1,0:T(8,128)(2,1)S(1)} %copy-done.2), channel_id=1, source_target_pairs={{0,1},{1,0},{2,3},{3,2},{4,5},{5,4},{6,7},{7,6},{8,9},{9,8},{10,11... | collective-permute-start | bytes 1916936 | tf_op jit(solution)/shard_map/ppermute | solution.py:258
  49.0 24.5 %collective-permute-start.11 = (bf16[192,1664]{1,0:T(8,128)(2,1)S(1)}, bf16[192,1664]{1,0:T(8,128)(2,1)}, u32[]{:S(2)}, u32[]{:S(2)}) collective-permute-start(bf16[192,1664]{1,0:T(8,128)(2,1)S(1)} %collective-permute-done.7.refs_1_), channel_id=1, source_target_pairs={{0,1},{1,0},{2,3},{3,2},{4,5},{5,4},{6,7},{7,6},{8,9},{9,8},{10,11... | collective-permute-start | bytes 1916936 | tf_op jit(solution)/shard_map/ppermute | solution.py:258
  51.5 26.6 %collective-permute-start.12 = (bf16[192,1664]{1,0:T(8,128)(2,1)}, bf16[192,1664]{1,0:T(8,128)(2,1)}, u32[]{:S(2)}, u32[]{:S(2)}) collective-permute-start(bf16[192,1664]{1,0:T(8,128)(2,1)} %collective-permute-done.8.refs_2_), channel_id=1, source_target_pairs={{0,1},{1,0},{2,3},{3,2},{4,5},{5,4},{6,7},{7,6},{8,9},{9,8},{10,11... | collective-permute-start | bytes 1916936 | tf_op jit(solution)/shard_map/ppermute | solution.py:258
  62.7 15.3 %collective-permute-start.13 = (bf16[192,1664]{1,0:T(8,128)(2,1)}, bf16[192,1664]{1,0:T(8,128)(2,1)}, u32[]{:S(2)}, u32[]{:S(2)}) collective-permute-start(bf16[192,1664]{1,0:T(8,128)(2,1)} %collective-permute-done.9.refs_3_), channel_id=1, source_target_pairs={{0,1},{1,0},{2,3},{3,2},{4,5},{5,4},{6,7},{7,6},{8,9},{9,8},{10,11... | collective-permute-start | bytes 1916936 | tf_op jit(solution)/shard_map/ppermute | solution.py:258
  65.6 27.2 %collective-permute-start = (bf16[12,96,256]{2,1,0:T(8,128)(2,1)S(1)}, bf16[12,96,256]{2,1,0:T(8,128)(2,1)}, u32[]{:S(2)}, u32[]{:S(2)}) collective-permute-start(bf16[12,96,256]{2,1,0:T(8,128)(2,1)S(1)} %regroup.1.refs_0_), channel_id=1, source_target_pairs={{0,16},{16,32},{32,48},{48,0},{1,17},{17,33},{33,49},{49,1},{2,18}... | collective-permute-start | bytes 1769480 | tf_op jit(solution)/shard_map/ppermute | solution.py:254
  67.5 27.7 %collective-permute-start.1 = (bf16[12,96,256]{2,1,0:T(8,128)(2,1)S(1)}, bf16[12,96,256]{2,1,0:T(8,128)(2,1)}, u32[]{:S(2)}, u32[]{:S(2)}) collective-permute-start(bf16[12,96,256]{2,1,0:T(8,128)(2,1)S(1)} %regroup.1.refs_0_), channel_id=1, source_target_pairs={{0,32},{16,48},{32,0},{48,16},{1,33},{17,49},{33,1},{49,17},{2,34}... | collective-permute-start | bytes 1769480 | tf_op jit(solution)/shard_map/ppermute | solution.py:254
  73.5 26.2 %collective-permute-start.2 = (bf16[12,96,256]{2,1,0:T(8,128)(2,1)S(1)}, bf16[12,96,256]{2,1,0:T(8,128)(2,1)}, u32[]{:S(2)}, u32[]{:S(2)}) collective-permute-start(bf16[12,96,256]{2,1,0:T(8,128)(2,1)S(1)} %regroup.1.refs_0_), channel_id=1, source_target_pairs={{0,48},{16,0},{32,16},{48,32},{1,49},{17,1},{33,17},{49,33},{2,50}... | collective-permute-start | bytes 1769480 | tf_op jit(solution)/shard_map/ppermute | solution.py:254
  83.6 30.3 %copy-start = (bf16[192,4608]{1,0:T(8,128)(2,1)S(1)}, bf16[192,4608]{1,0:T(8,128)(2,1)}, u32[]{:S(2)}) copy-start(bf16[192,4608]{1,0:T(8,128)(2,1)} %refs_8_.2) | copy-start | bytes 5308420
  83.6 30.3 %copy-start.1 = (bf16[192,512]{1,0:T(8,128)(2,1)S(1)}, bf16[192,512]{1,0:T(8,128)(2,1)}, u32[]{:S(2)}) copy-start(bf16[192,512]{1,0:T(8,128)(2,1)} %refs_10_.1) | copy-start | bytes 589828
  83.6 25.5 %all-to-all-start.2 = ((bf16[8,144,256]{2,1,0:T(8,128)(2,1)}), bf16[8,144,256]{2,1,0:T(8,128)(2,1)S(1)}, u32[]{:S(2)}, u32[]{:S(2)}) async-start(bf16[8,144,256]{2,1,0:T(8,128)(2,1)} %group_term.1), calls=%async_computation.2 | async-start | bytes 1179648 | tf_op jit(solution)/shard_map/all_to_all | solution.py:278
  90.8 23.1 %collective-permute-start.3 = (bf16[12,96,256]{2,1,0:T(8,128)(2,1)S(1)}, bf16[12,96,256]{2,1,0:T(8,128)(2,1)}, u32[]{:S(2)}, u32[]{:S(2)}) collective-permute-start(bf16[12,96,256]{2,1,0:T(8,128)(2,1)S(1)} %regroup.1.refs_0_), channel_id=1, source_target_pairs={{0,1},{1,0},{2,3},{3,2},{4,5},{5,4},{6,7},{7,6},{8,9},{9,8},{10,11... | collective-permute-start | bytes 1769480 | tf_op jit(solution)/shard_map/ppermute | solution.py:258
  92.8 21.1 %collective-permute-start.4 = (bf16[12,96,256]{2,1,0:T(8,128)(2,1)}, bf16[12,96,256]{2,1,0:T(8,128)(2,1)}, u32[]{:S(2)}, u32[]{:S(2)}) collective-permute-start(bf16[12,96,256]{2,1,0:T(8,128)(2,1)} %collective-permute-done.refs_1_), channel_id=1, source_target_pairs={{0,1},{1,0},{2,3},{3,2},{4,5},{5,4},{6,7},{7,6},{8,9},{9,8},{10,11... | collective-permute-start | bytes 1769480 | tf_op jit(solution)/shard_map/ppermute | solution.py:258
  95.2 18.7 %collective-permute-start.5 = (bf16[12,96,256]{2,1,0:T(8,128)(2,1)}, bf16[12,96,256]{2,1,0:T(8,128)(2,1)}, u32[]{:S(2)}, u32[]{:S(2)}) collective-permute-start(bf16[12,96,256]{2,1,0:T(8,128)(2,1)} %collective-permute-done.1.refs_2_), channel_id=1, source_target_pairs={{0,1},{1,0},{2,3},{3,2},{4,5},{5,4},{6,7},{7,6},{8,9},{9,8},{10,11... | collective-permute-start | bytes 1769480 | tf_op jit(solution)/shard_map/ppermute | solution.py:258
  99.8 14.2 %collective-permute-start.6 = (bf16[12,96,256]{2,1,0:T(8,128)(2,1)}, bf16[12,96,256]{2,1,0:T(8,128)(2,1)}, u32[]{:S(2)}, u32[]{:S(2)}) collective-permute-start(bf16[12,96,256]{2,1,0:T(8,128)(2,1)} %collective-permute-done.2.refs_3_), channel_id=1, source_target_pairs={{0,1},{1,0},{2,3},{3,2},{4,5},{5,4},{6,7},{7,6},{8,9},{9,8},{10,11... | collective-permute-start | bytes 1769480 | tf_op jit(solution)/shard_map/ppermute | solution.py:258
  109.8 15.3 %all-to-all-start.3 = ((bf16[12,12,256]{2,1,0:T(8,128)(2,1)}), bf16[12,12,256]{2,1,0:T(8,128)(2,1)S(1)}, u32[]{:S(2)}, u32[]{:S(2)}) async-start(bf16[12,12,256]{2,1,0:T(8,128)(2,1)} %sum_over_y.1), calls=%async_computation.3 | async-start | bytes 196608 | tf_op jit(solution)/shard_map/all_to_all | solution.py:280

commit v6 on v5

--- a/solution.py
+++ b/solution.py
@@ -28,6 +28,7 @@
 BY_DEVICE = np.zeros((ZG * XROWS, ZG * XROWS), np.float32)
 BY_DEVICE[(((_yh * NYL + _yl) * ZG + _z) * ROWS + _i).ravel(), np.arange(ZG * XROWS)] = 1
 IN_ORDER = BY_DEVICE.T
+HELD = (0, 2, 1, 3)
 ZSTEP = 3
 
 
@@ -69,45 +70,66 @@
     )(place, hidden, cotangent)
 
 
-def term_kernel(place, *refs):
-    *blocks, perm, out, flipped = refs
+def flip(blocks, core, flipped):
     tokens = blocks[0].shape[0]
-    half = pl.ds(pl.multiple_of(WIDE + place[0] * HALF, HALF // 2), HALF)
-    for b in range(0, len(blocks), 2):
+    half = pl.ds(pl.multiple_of(WIDE + core * HALF, HALF // 2), HALF)
+    for b in range(0, NX, 2):
         pair = jnp.concatenate([blocks[b][:, half], blocks[b + 1][:, half]], axis=0)
         flipped[:, b * tokens : (b + 2) * tokens] = pair.T
+
+
+def other_kernel(place, *refs):
+    *blocks, out, flipped = refs
+    flip(blocks, 1 - place[0], flipped)
     for g in range(NZ // ZG):
         cols = slice(g * ZG * XROWS, (g + 1) * ZG * XROWS)
         rows = jnp.concatenate([block[:, cols] for block in blocks], axis=0)
-        term = jnp.dot(flipped[...], rows, preferred_element_type=F32).astype(BF)
+        out[:, cols] = jnp.dot(flipped[...], rows, preferred_element_type=F32).astype(BF)
+
+
+def own_kernel(place, *refs):
+    *blocks, sent, perm, out, flipped = refs
+    flip(blocks, place[0], flipped)
+    for g in range(NZ // ZG):
+        cols = slice(g * ZG * XROWS, (g + 1) * ZG * XROWS)
+        rows = jnp.concatenate([block[:, cols] for block in blocks], axis=0)
+        term = jnp.dot(flipped[...], rows, preferred_element_type=F32)
+        term += sent[:, cols].astype(F32)
         moved = lax.dot_general(
-            perm[...], term, (((1,), (1,)), ((), ())), preferred_element_type=F32
+            perm[...], term.astype(BF), (((1,), (1,)), ((), ())), preferred_element_type=F32
         ).astype(BF)
         out[:, g * ZG * ROWS : (g + 1) * ZG * ROWS] = moved.reshape(NY, ZG * ROWS, HALF)
 
 
-def group_term(place, blocks):
-    tokens = blocks[0].shape[0]
+def term_call(kernel, name, place, inputs, out_shape, tokens):
     whole = pl.BlockSpec(memory_space=pltpu.VMEM)
     return pl.pallas_call(
-        term_kernel,
+        kernel,
         grid_spec=pltpu.PrefetchScalarGridSpec(
             num_scalar_prefetch=1,
             grid=(1,),
-            in_specs=[whole] * len(blocks)
-            + [pl.BlockSpec((ZG * XROWS, ZG * XROWS), lambda k, place: (0, 0))],
-            out_specs=pl.BlockSpec((NY, NZ * ROWS, HALF), lambda k, place: (0, 0, 0)),
-            scratch_shapes=[pltpu.VMEM((HALF, len(blocks) * tokens), BF)],
-        ),
-        out_shape=jax.ShapeDtypeStruct((NY, NZ * ROWS, HALF), BF),
+            in_specs=[whole] * len(inputs),
+            out_specs=pl.BlockSpec(out_shape, lambda k, place: (0,) * len(out_shape)),
+            scratch_shapes=[pltpu.VMEM((HALF, NX * tokens), BF)],
+        ),
+        out_shape=jax.ShapeDtypeStruct(out_shape, BF),
         compiler_params=pltpu.CompilerParams(vmem_limit_bytes=24 * 2**20),
         cost_estimate=pl.CostEstimate(
-            flops=2 * WIDE * HALF * (len(blocks) * tokens + ZG * XROWS),
-            bytes_accessed=2 * len(blocks) * tokens * (WIDE + 2 * HALF),
+            flops=2 * WIDE * HALF * NX * tokens,
+            bytes_accessed=2 * NX * tokens * (WIDE + 2 * HALF),
             transcendentals=0,
         ),
-        name="group_term",
-    )(place, *blocks, jnp.asarray(BY_DEVICE, BF))
+        name=name,
+    )(place, *inputs)
+
+
+def other_half(place, blocks):
+    return term_call(other_kernel, "other_half", place, blocks, (HALF, WIDE), blocks[0].shape[0])
+
+
+def own_half(place, blocks, sent):
+    inputs = [*blocks, sent, jnp.asarray(BY_DEVICE, BF)]
+    return term_call(own_kernel, "own_half", place, inputs, (NY, NZ * ROWS, HALF), blocks[0].shape[0])
 
 
 def regroup_kernel(parts, perm, out):
@@ -164,11 +186,11 @@
 
     total = acc[...]
     for k in range(ZSTEP):
-        for r in range(NX):
+        for b, r in enumerate(HELD):
             x = lax.rem(place[1] + NX - r, NX)
             rows = pl.ds(pl.multiple_of(x * XROWS, XROWS), XROWS)
-            held[k, rows, :HALF] = blocks[r][k]
-            held[k, rows, HALF:] = blocks[NX + r][k]
+            held[k, rows, :HALF] = blocks[b][k]
+            held[k, rows, HALF:] = blocks[NX + b][k]
         weight = held[k]
         cols = slice(k * ZROWS, (k + 1) * ZROWS)
         total += jnp.dot(hidden[:, cols], weight, preferred_element_type=F32)
@@ -266,13 +288,11 @@
     w_z = lax.all_to_all(copies, "z", split_axis=0, concat_axis=0, tiled=True)
 
     packed = pack(place, hidden, cotangent)
-    w_z, packed = lax.optimization_barrier((w_z, packed))
     held = [packed[0]] + [shift(packed[r], r) for r in (1, 3, 2)]
-    term = group_term(place, held + [swap(piece) for piece in held])
+    term = own_half(place, held, swap(other_half(place, held)))
 
     w_y = regroup(to_all(w_z.reshape(NZ * ROWS, HALF), Y, NY))
-    near = [shift(w_y, r) for r in (1, 3, 2)]
-    mine = [w_y, near[0], near[2], near[1]]
+    mine = [w_y] + [shift(w_y, r) for r in HELD[1:]]
     other = [swap(piece) for piece in mine]
 
     t_y = lax.all_to_all(term, Y, split_axis=0, concat_axis=0, tiled=True)

time: 127 us -> 129 us (1.016)
  the two profiles are of different devices: /device:TPU:2 before, /device:TPU:6 now
where the time goes in v6:
time: 129 us; the launch traced here: 126 us
  starting transfers between devices  67.7 us (52%)
  waiting for transfers between devices  33.2 us (26%)
  Pallas kernels  21.3 us (17%)
  local copies, waits for them, and re-layouts  1.88 us (1%)
    ppermute x6, waiting for transfers between devices, shift(): return lax.ppermute(piece, 'x', [(k, (k + r) % NX) for k in range(NX)])  26.8 us
    ppermute x6, starting transfers between devices, shift(): return lax.ppermute(piece, 'x', [(k, (k + r) % NX) for k in range(NX)])  18.8 us
    all_to_all x1, starting transfers between devices, on_device(): w_z = lax.all_to_all(copies, 'z', split_axis=0, concat_axis=0, tiled=True)  15.2 us
    ppermute x5, starting transfers between devices, swap(): return lax.ppermute(piece, 'c', [(0, 1), (1, 0)])  10.1 us
    all_to_all x1, starting transfers between devices, on_device(): t_z = lax.all_to_all(sum_y, 'z', split_axis=0, concat_axis=0, tiled=True)  9.33 us
    all_to_all x1, starting transfers between devices, on_device(): t_y = lax.all_to_all(term, Y, split_axis=0, concat_axis=0, tiled=True)  7.23 us
    pallas_call x1, Pallas kernels, project(): pl.pallas_call(project_kernel, grid_spec=pltpu.PrefetchScalarGridSpec(num...  7.1 us
    all_to_all x1, starting transfers between devices, to_all(): return lax.all_to_all(copies, axis, split_axis=0, concat_axis=0, tiled=True)  7.1 us
  transfers between devices with their start and end apart: 15, of which 5 were waited for; matrix products, arithmetic and copies ran while one was open for 1% of the time, Pallas kernels for 16%

profile of v6, /device:TPU:6, one launch (start us, length us, event | category | flops | bytes accessed | tf_op | source)
XLA Modules:
  0.0 126.2 jit_solution(5370940993435682323)
XLA Ops:
  0.6 1.4 %scaled_copies.1 = bf16[12,12,256]{2,1,0:T(8,128)(2,1)} custom-call(bf16[12,256]{1,0:T(8,128)(2,1)} %values.1, bf16[1,12]{1,0:T(2,128)(2,1)} %bitcast.3), custom_call_target="tpu_custom_call" | custom-call | tf_op jit(solution)/shard_map/scaled_copies/pallas_call | solution.py:262
  2.1 15.2 %all-to-all-start = ((bf16[12,12,256]{2,1,0:T(8,128)(2,1)}), bf16[12,12,256]{2,1,0:T(8,128)(2,1)S(1)}, u32[]{:S(2)}, u32[]{:S(2)}) async-start(bf16[12,12,256]{2,1,0:T(8,128)(2,1)} %scaled_copies.1), calls=%async_computation | async-start | bytes 196608 | tf_op jit(solution)/shard_map/all_to_all | solution.py:288
  17.2 0.6 pad_add_fusion.place
  17.9 4.0 %pack.1 = (bf16[192,1664]{1,0:T(8,128)(2,1)}, bf16[192,1664]{1,0:T(8,128)(2,1)}, bf16[192,1664]{1,0:T(8,128)(2,1)}, bf16[192,1664]{1,0:T(8,128)(2,1)}) custom-call(s32[2]{0:T(128)} %pad_add_fusion.place, bf16[192,4608]{1,0:T(8,128)(2,1)} %hidden.1, bf16[192,512]{1,0:T(8,128)(2,1)} %cot.1), custom_call_target="tpu_custom_call" | custom-call | flops 884736 | bytes 3538944 | tf_op jit(solution)/shard_map/pack/pallas_call | solution.py:52
  21.9 2.5 %collective-permute-start.7 = (bf16[192,1664]{1,0:T(8,128)(2,1)}, bf16[192,1664]{1,0:T(8,128)(2,1)S(1)}, u32[]{:S(2)}, u32[]{:S(2)}) collective-permute-start(bf16[192,1664]{1,0:T(8,128)(2,1)} %get-tuple-element.12), channel_id=1, source_target_pairs={{0,16},{16,32},{32,48},{48,0},{1,17},{17,33},{33,49},{49,1},{2,18}... | collective-permute-start | bytes 1916936 | tf_op jit(solution)/shard_map/ppermute | solution.py:276
  24.4 3.5 %collective-permute-start.8 = (bf16[192,1664]{1,0:T(8,128)(2,1)}, bf16[192,1664]{1,0:T(8,128)(2,1)S(1)}, u32[]{:S(2)}, u32[]{:S(2)}) collective-permute-start(bf16[192,1664]{1,0:T(8,128)(2,1)} %get-tuple-element.13), channel_id=1, source_target_pairs={{0,48},{16,0},{32,16},{48,32},{1,49},{17,1},{33,17},{49,33},{2,50}... | collective-permute-start | bytes 1916936 | tf_op jit(solution)/shard_map/ppermute | solution.py:276
  27.9 3.3 %collective-permute-start.9 = (bf16[192,1664]{1,0:T(8,128)(2,1)}, bf16[192,1664]{1,0:T(8,128)(2,1)S(1)}, u32[]{:S(2)}, u32[]{:S(2)}) collective-permute-start(bf16[192,1664]{1,0:T(8,128)(2,1)} %get-tuple-element.14), channel_id=1, source_target_pairs={{0,32},{16,48},{32,0},{48,16},{1,33},{17,49},{33,1},{49,17},{2,34}... | collective-permute-start | bytes 1916936 | tf_op jit(solution)/shard_map/ppermute | solution.py:276
  31.2 0.0 all-to-all-done
  31.2 0.9 broadcast_in_dim.8
  32.1 7.1 %all-to-all-start.1 = ((bf16[8,144,256]{2,1,0:T(8,128)(2,1)}), bf16[8,144,256]{2,1,0:T(8,128)(2,1)S(1)}, u32[]{:S(2)}, u32[]{:S(2)}) async-start(bf16[8,144,256]{2,1,0:T(8,128)(2,1)} %broadcast_in_dim.8), calls=%async_computation.1 | async-start | bytes 1179648 | tf_op jit(solution)/shard_map/all_to_all | solution.py:272
  39.2 2.2 %collective-permute-done.7.refs_1_ = bf16[192,1664]{1,0:T(8,128)(2,1)S(1)} collective-permute-done((bf16[192,1664]{1,0:T(8,128)(2,1)}, bf16[192,1664]{1,0:T(8,128)(2,1)S(1)}, u32[]{:S(2)}, u32[]{:S(2)}) %collective-permute-start.7) | collective-permute-done | bytes 639008 | tf_op jit(solution)/shard_map/ppermute | solution.py:276
  41.4 15.5 %collective-permute-done.8.refs_2_ = bf16[192,1664]{1,0:T(8,128)(2,1)S(1)} collective-permute-done((bf16[192,1664]{1,0:T(8,128)(2,1)}, bf16[192,1664]{1,0:T(8,128)(2,1)S(1)}, u32[]{:S(2)}, u32[]{:S(2)}) %collective-permute-start.8) | collective-permute-done | bytes 639008 | tf_op jit(solution)/shard_map/ppermute | solution.py:276
  57.0 0.0 collective-permute-done.9.refs_3_
  57.0 0.0 copy-done.5
  57.0 0.0 copy-done.1
  57.0 0.0 copy-start.3
  57.0 2.2 %other_half.1 = bf16[256,1152]{1,0:T(8,128)(2,1)} custom-call(s32[2]{0:T(128)S(1)} %copy-done.5, bf16[192,1664]{1,0:T(8,128)(2,1)S(1)} %copy-done.1, bf16[192,1664]{1,0:T(8,128)(2,1)S(1)} %collective-permute-done.7.refs_1_, bf16[192,1664]{1,0:T(8,128)(2,1)S(1)} %collective-permute-done.8.refs_2_, bf16[192,1664]{1,0:T(8,128)(2,1)S(1)} %collective-permute-done.9.refs_3_), custom_call_target="tpu_custom_call" | custom-call | flops 452984832 | bytes 2555904 | tf_op jit(solution)/shard_map/other_half/pallas_call | solution.py:106
  59.2 1.9 %collective-permute-start.10 = (bf16[256,1152]{1,0:T(8,128)(2,1)}, bf16[256,1152]{1,0:T(8,128)(2,1)}, u32[]{:S(2)}, u32[]{:S(2)}) collective-permute-start(bf16[256,1152]{1,0:T(8,128)(2,1)} %other_half.1), channel_id=1, source_target_pairs={{0,1},{1,0},{2,3},{3,2},{4,5},{5,4},{6,7},{7,6},{8,9},{9,8},{10,11... | collective-permute-start | bytes 1769480 | tf_op jit(solution)/shard_map/ppermute | solution.py:280
  61.1 0.0 all-to-all-done.1.parts
  61.1 0.0 copy-start.4
  61.1 1.0 copy-done.4
  62.1 1.9 %regroup.1.refs_0_ = bf16[12,96,256]{2,1,0:T(8,128)(2,1)} custom-call(bf16[8,144,256]{2,1,0:T(8,128)(2,1)S(1)} %all-to-all-done.1.parts, bf16[384,384]{1,0:T(8,128)(2,1)S(1)} %copy-done.4), custom_call_target="tpu_custom_call" | custom-call | flops 226492416 | bytes 1179648 | tf_op jit(solution)/shard_map/regroup/pallas_call | solution.py:141
  64.0 1.9 %collective-permute-start.2 = (bf16[12,96,256]{2,1,0:T(8,128)(2,1)}, bf16[12,96,256]{2,1,0:T(8,128)(2,1)S(1)}, u32[]{:S(2)}, u32[]{:S(2)}) collective-permute-start(bf16[12,96,256]{2,1,0:T(8,128)(2,1)} %regroup.1.refs_0_), channel_id=1, source_target_pairs={{0,48},{16,0},{32,16},{48,32},{1,49},{17,1},{33,17},{49,33},{2,50}... | collective-permute-start | bytes 1769480 | tf_op jit(solution)/shard_map/ppermute | solution.py:276
  65.9 5.1 %collective-permute-start.1 = (bf16[12,96,256]{2,1,0:T(8,128)(2,1)}, bf16[12,96,256]{2,1,0:T(8,128)(2,1)}, u32[]{:S(2)}, u32[]{:S(2)}) collective-permute-start(bf16[12,96,256]{2,1,0:T(8,128)(2,1)} %regroup.1.refs_0_), channel_id=1, source_target_pairs={{0,16},{16,32},{32,48},{48,0},{1,17},{17,33},{33,49},{49,1},{2,18}... | collective-permute-start | bytes 1769480 | tf_op jit(solution)/shard_map/ppermute | solution.py:276
  71.1 2.5 %collective-permute-start = (bf16[12,96,256]{2,1,0:T(8,128)(2,1)}, bf16[12,96,256]{2,1,0:T(8,128)(2,1)}, u32[]{:S(2)}, u32[]{:S(2)}) collective-permute-start(bf16[12,96,256]{2,1,0:T(8,128)(2,1)} %regroup.1.refs_0_), channel_id=1, source_target_pairs={{0,32},{16,48},{32,0},{48,16},{1,33},{17,49},{33,1},{49,17},{2,34}... | collective-permute-start | bytes 1769480 | tf_op jit(solution)/shard_map/ppermute | solution.py:276
  73.6 0.0 collective-permute-done.10.refs_4_
  73.6 0.0 copy-done.3
  73.6 3.9 %own_half.1 = bf16[8,144,256]{2,1,0:T(8,128)(2,1)} custom-call(s32[2]{0:T(128)S(1)} %copy-done.5, bf16[192,1664]{1,0:T(8,128)(2,1)S(1)} %copy-done.1, bf16[192,1664]{1,0:T(8,128)(2,1)S(1)} %collective-permute-done.7.refs_1_, bf16[192,1664]{1,0:T(8,128)(2,1)S(1)} %collective-permute-done.8.refs_2_, bf16[192,1664]{1,0:T(8,128)(2,1)S(1)} %collective-permute-done.9.refs_3_, ...), custom_call_target="tpu_custom_call" | custom-call | flops 452984832 | bytes 2555904 | tf_op jit(solution)/shard_map/own_half/pallas_call | solution.py:106
  77.5 7.2 %all-to-all-start.2 = ((bf16[8,144,256]{2,1,0:T(8,128)(2,1)}), bf16[8,144,256]{2,1,0:T(8,128)(2,1)S(1)}, u32[]{:S(2)}, u32[]{:S(2)}) async-start(bf16[8,144,256]{2,1,0:T(8,128)(2,1)} %own_half.1), calls=%async_computation.2 | async-start | bytes 1179648 | tf_op jit(solution)/shard_map/all_to_all | solution.py:298
  84.7 1.9 %collective-permute-start.3 = (bf16[12,96,256]{2,1,0:T(8,128)(2,1)}, bf16[12,96,256]{2,1,0:T(8,128)(2,1)}, u32[]{:S(2)}, u32[]{:S(2)}) collective-permute-start(bf16[12,96,256]{2,1,0:T(8,128)(2,1)} %regroup.1.refs_0_), channel_id=1, source_target_pairs={{0,1},{1,0},{2,3},{3,2},{4,5},{5,4},{6,7},{7,6},{8,9},{9,8},{10,11... | collective-permute-start | bytes 1769480 | tf_op jit(solution)/shard_map/ppermute | solution.py:280
  86.6 9.0 %collective-permute-done.2.refs_3_ = bf16[12,96,256]{2,1,0:T(8,128)(2,1)S(1)} collective-permute-done((bf16[12,96,256]{2,1,0:T(8,128)(2,1)}, bf16[12,96,256]{2,1,0:T(8,128)(2,1)S(1)}, u32[]{:S(2)}, u32[]{:S(2)}) %collective-permute-start.2) | collective-permute-done | bytes 589856 | tf_op jit(solution)/shard_map/ppermute | solution.py:276
  95.7 1.9 %collective-permute-start.6 = (bf16[12,96,256]{2,1,0:T(8,128)(2,1)S(1)}, bf16[12,96,256]{2,1,0:T(8,128)(2,1)}, u32[]{:S(2)}, u32[]{:S(2)}) collective-permute-start(bf16[12,96,256]{2,1,0:T(8,128)(2,1)S(1)} %collective-permute-done.2.refs_3_), channel_id=1, source_target_pairs={{0,1},{1,0},{2,3},{3,2},{4,5},{5,4},{6,7},{7,6},{8,9},{9,8},{10,11... | collective-permute-start | bytes 1769480 | tf_op jit(solution)/shard_map/ppermute | solution.py:280
  97.6 0.0 collective-permute-done.1.refs_2_
  97.6 2.4 %collective-permute-start.5 = (bf16[12,96,256]{2,1,0:T(8,128)(2,1)}, bf16[12,96,256]{2,1,0:T(8,128)(2,1)}, u32[]{:S(2)}, u32[]{:S(2)}) collective-permute-start(bf16[12,96,256]{2,1,0:T(8,128)(2,1)} %collective-permute-done.1.refs_2_), channel_id=1, source_target_pairs={{0,1},{1,0},{2,3},{3,2},{4,5},{5,4},{6,7},{7,6},{8,9},{9,8},{10,11... | collective-permute-start | bytes 1769480 | tf_op jit(solution)/shard_map/ppermute | solution.py:280
  100.0 0.0 collective-permute-done.refs_1_
  100.0 1.9 %collective-permute-start.4 = (bf16[12,96,256]{2,1,0:T(8,128)(2,1)}, bf16[12,96,256]{2,1,0:T(8,128)(2,1)}, u32[]{:S(2)}, u32[]{:S(2)}) collective-permute-start(bf16[12,96,256]{2,1,0:T(8,128)(2,1)} %collective-permute-done.refs_1_), channel_id=1, source_target_pairs={{0,1},{1,0},{2,3},{3,2},{4,5},{5,4},{6,7},{7,6},{8,9},{9,8},{10,11... | collective-permute-start | bytes 1769480 | tf_op jit(solution)/shard_map/ppermute | solution.py:280
  102.0 1.5 %all-to-all-done.2.parts = bf16[8,144,256]{2,1,0:T(8,128)(2,1)S(1)} async-done(((bf16[8,144,256]{2,1,0:T(8,128)(2,1)}), bf16[8,144,256]{2,1,0:T(8,128)(2,1)S(1)}, u32[]{:S(2)}, u32[]{:S(2)}) %all-to-all-start.2) | async-done | bytes 589856 | tf_op jit(solution)/shard_map/all_to_all | solution.py:298
  103.4 0.7 sum_over_y.1
  104.2 9.3 %all-to-all-start.3 = ((bf16[12,12,256]{2,1,0:T(8,128)(2,1)}), bf16[12,12,256]{2,1,0:T(8,128)(2,1)S(1)}, u32[]{:S(2)}, u32[]{:S(2)}) async-start(bf16[12,12,256]{2,1,0:T(8,128)(2,1)} %sum_over_y.1), calls=%async_computation.3 | async-start | bytes 196608 | tf_op jit(solution)/shard_map/all_to_all | solution.py:300
  113.5 0.0 collective-permute-done.3.refs_4_
  113.5 0.0 collective-permute-done.6.refs_7_
  113.5 0.0 collective-permute-done.5.refs_6_
  113.5 0.0 collective-permute-done.4.refs_5_
  113.6 0.0 copy-done
  113.6 0.0 copy-done.2
  113.6 7.1 %project.1 = (bf16[192,512]{1,0:T(8,128)(2,1)}, bf16[192,4608]{1,0:T(8,128)(2,1)}) custom-call(s32[2]{0:T(128)S(1)} %copy-done.5, bf16[12,96,256]{2,1,0:T(8,128)(2,1)} %regroup.1.refs_0_, bf16[12,96,256]{2,1,0:T(8,128)(2,1)} %collective-permute-done.refs_1_, bf16[12,96,256]{2,1,0:T(8,128)(2,1)} %collective-permute-done.1.refs_2_, ...), custom_call_target="tpu_custom_call" | custom-call | flops 1811939328 | bytes 8257536 | tf_op jit(solution)/shard_map/project/pallas_call | solution.py:216
  120.7 4.9 %all-to-all-done.3 = bf16[12,12,256]{2,1,0:T(8,128)(2,1)S(1)} async-done(((bf16[12,12,256]{2,1,0:T(8,128)(2,1)}), bf16[12,12,256]{2,1,0:T(8,128)(2,1)S(1)}, u32[]{:S(2)}, u32[]{:S(2)}) %all-to-all-start.3) | async-done | bytes 73760 | tf_op jit(solution)/shard_map/all_to_all | solution.py:300
  125.6 0.6 broadcast_multiply_fusion
  (6 shorter events, 0.1 us)
Async XLA Ops:
  2.1 29.1 %all-to-all-start = ((bf16[12,12,256]{2,1,0:T(8,128)(2,1)}), bf16[12,12,256]{2,1,0:T(8,128)(2,1)S(1)}, u32[]{:S(2)}, u32[]{:S(2)}) async-start(bf16[12,12,256]{2,1,0:T(8,128)(2,1)} %scaled_copies.1), calls=%async_computation | async-start | bytes 196608 | tf_op jit(solution)/shard_map/all_to_all | solution.py:288
  17.9 39.1 %copy-start.5 = (s32[2]{0:T(128)S(1)}, s32[2]{0:T(128)}, u32[]{:S(2)}) copy-start(s32[2]{0:T(128)} %pad_add_fusion.place) | copy-start | bytes 28
  21.9 35.1 %copy-start.1 = (bf16[192,1664]{1,0:T(8,128)(2,1)S(1)}, bf16[192,1664]{1,0:T(8,128)(2,1)}, u32[]{:S(2)}) copy-start(bf16[192,1664]{1,0:T(8,128)(2,1)} %get-tuple-element.11.refs_0_) | copy-start | bytes 1916932
  21.9 19.5 %collective-permute-start.7 = (bf16[192,1664]{1,0:T(8,128)(2,1)}, bf16[192,1664]{1,0:T(8,128)(2,1)S(1)}, u32[]{:S(2)}, u32[]{:S(2)}) collective-permute-start(bf16[192,1664]{1,0:T(8,128)(2,1)} %get-tuple-element.12), channel_id=1, source_target_pairs={{0,16},{16,32},{32,48},{48,0},{1,17},{17,33},{33,49},{49,1},{2,18}... | collective-permute-start | bytes 1916936 | tf_op jit(solution)/shard_map/ppermute | solution.py:276
  24.4 32.6 %collective-permute-start.8 = (bf16[192,1664]{1,0:T(8,128)(2,1)}, bf16[192,1664]{1,0:T(8,128)(2,1)S(1)}, u32[]{:S(2)}, u32[]{:S(2)}) collective-permute-start(bf16[192,1664]{1,0:T(8,128)(2,1)} %get-tuple-element.13), channel_id=1, source_target_pairs={{0,48},{16,0},{32,16},{48,32},{1,49},{17,1},{33,17},{49,33},{2,50}... | collective-permute-start | bytes 1916936 | tf_op jit(solution)/shard_map/ppermute | solution.py:276
  27.9 29.1 %collective-permute-start.9 = (bf16[192,1664]{1,0:T(8,128)(2,1)}, bf16[192,1664]{1,0:T(8,128)(2,1)S(1)}, u32[]{:S(2)}, u32[]{:S(2)}) collective-permute-start(bf16[192,1664]{1,0:T(8,128)(2,1)} %get-tuple-element.14), channel_id=1, source_target_pairs={{0,32},{16,48},{32,0},{48,16},{1,33},{17,49},{33,1},{49,17},{2,34}... | collective-permute-start | bytes 1916936 | tf_op jit(solution)/shard_map/ppermute | solution.py:276
  32.1 29.0 %all-to-all-start.1 = ((bf16[8,144,256]{2,1,0:T(8,128)(2,1)}), bf16[8,144,256]{2,1,0:T(8,128)(2,1)S(1)}, u32[]{:S(2)}, u32[]{:S(2)}) async-start(bf16[8,144,256]{2,1,0:T(8,128)(2,1)} %broadcast_in_dim.8), calls=%async_computation.1 | async-start | bytes 1179648 | tf_op jit(solution)/shard_map/all_to_all | solution.py:272
  57.0 16.6 %copy-start.3 = (bf16[384,384]{1,0:T(8,128)(2,1)S(1)}, bf16[384,384]{1,0:T(8,128)(2,1)}, u32[]{:S(2)}) copy-start(bf16[384,384]{1,0:T(8,128)(2,1)} %constant.18.clone.refs_5_) | copy-start | bytes 884740
  59.2 14.4 %collective-permute-start.10 = (bf16[256,1152]{1,0:T(8,128)(2,1)}, bf16[256,1152]{1,0:T(8,128)(2,1)}, u32[]{:S(2)}, u32[]{:S(2)}) collective-permute-start(bf16[256,1152]{1,0:T(8,128)(2,1)} %other_half.1), channel_id=1, source_target_pairs={{0,1},{1,0},{2,3},{3,2},{4,5},{5,4},{6,7},{7,6},{8,9},{9,8},{10,11... | collective-permute-start | bytes 1769480 | tf_op jit(solution)/shard_map/ppermute | solution.py:280
  61.1 1.0 copy-start.4
  64.0 31.7 %collective-permute-start.2 = (bf16[12,96,256]{2,1,0:T(8,128)(2,1)}, bf16[12,96,256]{2,1,0:T(8,128)(2,1)S(1)}, u32[]{:S(2)}, u32[]{:S(2)}) collective-permute-start(bf16[12,96,256]{2,1,0:T(8,128)(2,1)} %regroup.1.refs_0_), channel_id=1, source_target_pairs={{0,48},{16,0},{32,16},{48,32},{1,49},{17,1},{33,17},{49,33},{2,50}... | collective-permute-start | bytes 1769480 | tf_op jit(solution)/shard_map/ppermute | solution.py:276
  65.9 31.7 %collective-permute-start.1 = (bf16[12,96,256]{2,1,0:T(8,128)(2,1)}, bf16[12,96,256]{2,1,0:T(8,128)(2,1)}, u32[]{:S(2)}, u32[]{:S(2)}) collective-permute-start(bf16[12,96,256]{2,1,0:T(8,128)(2,1)} %regroup.1.refs_0_), channel_id=1, source_target_pairs={{0,16},{16,32},{32,48},{48,0},{1,17},{17,33},{33,49},{49,1},{2,18}... | collective-permute-start | bytes 1769480 | tf_op jit(solution)/shard_map/ppermute | solution.py:276
  71.1 29.0 %collective-permute-start = (bf16[12,96,256]{2,1,0:T(8,128)(2,1)}, bf16[12,96,256]{2,1,0:T(8,128)(2,1)}, u32[]{:S(2)}, u32[]{:S(2)}) collective-permute-start(bf16[12,96,256]{2,1,0:T(8,128)(2,1)} %regroup.1.refs_0_), channel_id=1, source_target_pairs={{0,32},{16,48},{32,0},{48,16},{1,33},{17,49},{33,1},{49,17},{2,34}... | collective-permute-start | bytes 1769480 | tf_op jit(solution)/shard_map/ppermute | solution.py:276
  77.5 36.1 %copy-start = (bf16[192,4608]{1,0:T(8,128)(2,1)S(1)}, bf16[192,4608]{1,0:T(8,128)(2,1)}, u32[]{:S(2)}) copy-start(bf16[192,4608]{1,0:T(8,128)(2,1)} %hidden.1) | copy-start | bytes 5308420
  77.5 36.1 %copy-start.2 = (bf16[192,512]{1,0:T(8,128)(2,1)S(1)}, bf16[192,512]{1,0:T(8,128)(2,1)}, u32[]{:S(2)}) copy-start(bf16[192,512]{1,0:T(8,128)(2,1)} %cot.1) | copy-start | bytes 589828
  77.5 26.0 %all-to-all-start.2 = ((bf16[8,144,256]{2,1,0:T(8,128)(2,1)}), bf16[8,144,256]{2,1,0:T(8,128)(2,1)S(1)}, u32[]{:S(2)}, u32[]{:S(2)}) async-start(bf16[8,144,256]{2,1,0:T(8,128)(2,1)} %own_half.1), calls=%async_computation.2 | async-start | bytes 1179648 | tf_op jit(solution)/shard_map/all_to_all | solution.py:298
  84.7 28.8 %collective-permute-start.3 = (bf16[12,96,256]{2,1,0:T(8,128)(2,1)}, bf16[12,96,256]{2,1,0:T(8,128)(2,1)}, u32[]{:S(2)}, u32[]{:S(2)}) collective-permute-start(bf16[12,96,256]{2,1,0:T(8,128)(2,1)} %regroup.1.refs_0_), channel_id=1, source_target_pairs={{0,1},{1,0},{2,3},{3,2},{4,5},{5,4},{6,7},{7,6},{8,9},{9,8},{10,11... | collective-permute-start | bytes 1769480 | tf_op jit(solution)/shard_map/ppermute | solution.py:280
  95.7 17.8 %collective-permute-start.6 = (bf16[12,96,256]{2,1,0:T(8,128)(2,1)S(1)}, bf16[12,96,256]{2,1,0:T(8,128)(2,1)}, u32[]{:S(2)}, u32[]{:S(2)}) collective-permute-start(bf16[12,96,256]{2,1,0:T(8,128)(2,1)S(1)} %collective-permute-done.2.refs_3_), channel_id=1, source_target_pairs={{0,1},{1,0},{2,3},{3,2},{4,5},{5,4},{6,7},{7,6},{8,9},{9,8},{10,11... | collective-permute-start | bytes 1769480 | tf_op jit(solution)/shard_map/ppermute | solution.py:280
  97.6 15.9 %collective-permute-start.5 = (bf16[12,96,256]{2,1,0:T(8,128)(2,1)}, bf16[12,96,256]{2,1,0:T(8,128)(2,1)}, u32[]{:S(2)}, u32[]{:S(2)}) collective-permute-start(bf16[12,96,256]{2,1,0:T(8,128)(2,1)} %collective-permute-done.1.refs_2_), channel_id=1, source_target_pairs={{0,1},{1,0},{2,3},{3,2},{4,5},{5,4},{6,7},{7,6},{8,9},{9,8},{10,11... | collective-permute-start | bytes 1769480 | tf_op jit(solution)/shard_map/ppermute | solution.py:280
  100.0 13.5 %collective-permute-start.4 = (bf16[12,96,256]{2,1,0:T(8,128)(2,1)}, bf16[12,96,256]{2,1,0:T(8,128)(2,1)}, u32[]{:S(2)}, u32[]{:S(2)}) collective-permute-start(bf16[12,96,256]{2,1,0:T(8,128)(2,1)} %collective-permute-done.refs_1_), channel_id=1, source_target_pairs={{0,1},{1,0},{2,3},{3,2},{4,5},{5,4},{6,7},{7,6},{8,9},{9,8},{10,11... | collective-permute-start | bytes 1769480 | tf_op jit(solution)/shard_map/ppermute | solution.py:280
  104.2 21.4 %all-to-all-start.3 = ((bf16[12,12,256]{2,1,0:T(8,128)(2,1)}), bf16[12,12,256]{2,1,0:T(8,128)(2,1)S(1)}, u32[]{:S(2)}, u32[]{:S(2)}) async-start(bf16[12,12,256]{2,1,0:T(8,128)(2,1)} %sum_over_y.1), calls=%async_computation.3 | async-start | bytes 196608 | tf_op jit(solution)/shard_map/all_to_all | solution.py:300

commit v7 on v6

--- a/solution.py
+++ b/solution.py
@@ -28,7 +28,7 @@
 BY_DEVICE = np.zeros((ZG * XROWS, ZG * XROWS), np.float32)
 BY_DEVICE[(((_yh * NYL + _yl) * ZG + _z) * ROWS + _i).ravel(), np.arange(ZG * XROWS)] = 1
 IN_ORDER = BY_DEVICE.T
-HELD = (0, 2, 1, 3)
+HELD = (0, 3, 1, 2)
 ZSTEP = 3
 
 
@@ -101,7 +101,7 @@
         out[:, g * ZG * ROWS : (g + 1) * ZG * ROWS] = moved.reshape(NY, ZG * ROWS, HALF)
 
 
-def term_call(kernel, name, place, inputs, out_shape, tokens):
+def term_call(kernel, name, place, inputs, out_shape, tokens, weigh=1):
     whole = pl.BlockSpec(memory_space=pltpu.VMEM)
     return pl.pallas_call(
         kernel,
@@ -115,7 +115,7 @@
         out_shape=jax.ShapeDtypeStruct(out_shape, BF),
         compiler_params=pltpu.CompilerParams(vmem_limit_bytes=24 * 2**20),
         cost_estimate=pl.CostEstimate(
-            flops=2 * WIDE * HALF * NX * tokens,
+            flops=weigh * 2 * WIDE * HALF * NX * tokens,
             bytes_accessed=2 * NX * tokens * (WIDE + 2 * HALF),
             transcendentals=0,
         ),
@@ -124,7 +124,7 @@
 
 
 def other_half(place, blocks):
-    return term_call(other_kernel, "other_half", place, blocks, (HALF, WIDE), blocks[0].shape[0])
+    return term_call(other_kernel, "other_half", place, blocks, (HALF, WIDE), blocks[0].shape[0], 100)
 
 
 def own_half(place, blocks, sent):
@@ -284,15 +284,18 @@
     place = jnp.stack([lax.axis_index("c"), lax.axis_index("x")]).astype(jnp.int32)
     factor = 1.0 / math.sqrt(hidden.shape[0] * NZ * NX * NY * NC)
 
-    copies = scaled_copies(quant_weight, scales)
+    packed = pack(place, hidden, cotangent)
+    held = [packed[0]] + [shift(packed[r], r) for r in (2, 1, 3)]
+    ahead = other_half(place, held)
+    term = own_half(place, held, swap(ahead))
+
+    values, _ = lax.optimization_barrier((quant_weight, packed[0]))
+    copies = scaled_copies(values, scales)
     w_z = lax.all_to_all(copies, "z", split_axis=0, concat_axis=0, tiled=True)
-
-    packed = pack(place, hidden, cotangent)
-    held = [packed[0]] + [shift(packed[r], r) for r in (1, 3, 2)]
-    term = own_half(place, held, swap(other_half(place, held)))
-
-    w_y = regroup(to_all(w_z.reshape(NZ * ROWS, HALF), Y, NY))
-    mine = [w_y] + [shift(w_y, r) for r in HELD[1:]]
+    w_y = to_all(w_z.reshape(NZ * ROWS, HALF), Y, NY)
+
+    own = regroup(lax.optimization_barrier((w_y, term))[0])
+    mine = [own] + [shift(own, r) for r in HELD[1:]]
     other = [swap(piece) for piece in mine]
 
     t_y = lax.all_to_all(term, Y, split_axis=0, concat_axis=0, tiled=True)

time: 129 us -> 121 us (0.938)
  blocking collectives: 0 us -> 19.9 us
  starting transfers between devices: 67.7 us -> 50.1 us
  waiting for transfers between devices: 33.2 us -> 24.7 us
    all_to_all x0 -> x1, blocking collectives: none -> 19.9 us  [on_device(): w_z = lax.all_to_all(copies, 'z', split_axis=0, concat_axis=0, tiled=True)]
    all_to_all x1 -> x0, starting transfers between devices: 15.2 us -> none  [on_device(): w_z = lax.all_to_all(copies, 'z', split_axis=0, concat_axis=0, tiled=True)]
    ppermute x6, waiting for transfers between devices: 26.8 us -> 11.7 us  [shift(): return lax.ppermute(piece, 'x', [(k, (k + r) % NX) for k in range(NX)])]
    ppermute x6, starting transfers between devices: 18.8 us -> 25.7 us  [shift(): return lax.ppermute(piece, 'x', [(k, (k + r) % NX) for k in range(NX)])]
    all_to_all x1, waiting for transfers between devices: 0.01 us -> 6.09 us  [to_all(): return lax.all_to_all(copies, axis, split_axis=0, concat_axis=0, tiled=True)]
    all_to_all x1, starting transfers between devices: 9.33 us -> 3.51 us  [on_device(): t_z = lax.all_to_all(sum_y, 'z', split_axis=0, concat_axis=0, tiled=True)]
    all_to_all x1, starting transfers between devices: 7.23 us -> 3.55 us  [on_device(): t_y = lax.all_to_all(term, Y, split_axis=0, concat_axis=0, tiled=True)]
    ppermute x5, waiting for transfers between devices: 0.01 us -> 1.98 us  [swap(): return lax.ppermute(piece, 'c', [(0, 1), (1, 0)])]
  transfers between devices with their start and end apart: 15 -> 14, of which waited for: 5 -> 5; matrix products, arithmetic and copies ran while one was open for 1% -> 1% of each run, Pallas kernels for 16% -> 13%
where the time goes in v7:
time: 121 us; the launch traced here: 118 us
  starting transfers between devices  50.1 us (41%)
  waiting for transfers between devices  24.7 us (20%)
  Pallas kernels  20.5 us (17%)
  blocking collectives  19.9 us (16%)
  other arithmetic  1.23 us (1%)
    ppermute x6, starting transfers between devices, shift(): return lax.ppermute(piece, 'x', [(k, (k + r) % NX) for k in range(NX)])  25.7 us
    all_to_all x1, blocking collectives, on_device(): w_z = lax.all_to_all(copies, 'z', split_axis=0, concat_axis=0, tiled=True)  19.9 us
    ppermute x6, waiting for transfers between devices, shift(): return lax.ppermute(piece, 'x', [(k, (k + r) % NX) for k in range(NX)])  11.7 us
    ppermute x5, starting transfers between devices, swap(): return lax.ppermute(piece, 'c', [(0, 1), (1, 0)])  10.2 us
    pallas_call x1, Pallas kernels, project(): pl.pallas_call(project_kernel, grid_spec=pltpu.PrefetchScalarGridSpec(num...  7.11 us
    all_to_all x1, starting transfers between devices, to_all(): return lax.all_to_all(copies, axis, split_axis=0, concat_axis=0, tiled=True)  7.1 us
    pallas_call x2, Pallas kernels, term_call(): pl.pallas_call(kernel, grid_spec=pltpu.PrefetchScalarGridSpec(num_scalar_...  6.35 us
    all_to_all x1, waiting for transfers between devices, to_all(): return lax.all_to_all(copies, axis, split_axis=0, concat_axis=0, tiled=True)  6.09 us
  transfers between devices with their start and end apart: 14, of which 5 were waited for; matrix products, arithmetic and copies ran while one was open for 1% of the time, Pallas kernels for 13%

profile of v7, /device:TPU:6, one launch (start us, length us, event | category | flops | bytes accessed | tf_op | source)
XLA Modules:
  0.0 118.3 jit_solution(6844351907645981065)
XLA Ops:
  0.6 0.6 pad_add_fusion.place
  1.2 0.0 copy-start.5
  1.2 4.0 %pack.1 = (bf16[192,1664]{1,0:T(8,128)(2,1)}, bf16[192,1664]{1,0:T(8,128)(2,1)}, bf16[192,1664]{1,0:T(8,128)(2,1)}, bf16[192,1664]{1,0:T(8,128)(2,1)}) custom-call(s32[2]{0:T(128)} %pad_add_fusion.place, bf16[192,4608]{1,0:T(8,128)(2,1)} %refs_8_.1, bf16[192,512]{1,0:T(8,128)(2,1)} %refs_10_.1), custom_call_target="tpu_custom_call" | custom-call | flops 884736 | bytes 3538944 | tf_op jit(solution)/shard_map/pack/pallas_call | solution.py:52
  5.3 0.0 copy-start.2
  5.3 3.4 %collective-permute-start = (bf16[192,1664]{1,0:T(8,128)(2,1)}, bf16[192,1664]{1,0:T(8,128)(2,1)S(1)}, u32[]{:S(2)}, u32[]{:S(2)}) collective-permute-start(bf16[192,1664]{1,0:T(8,128)(2,1)} %get-tuple-element.13), channel_id=1, source_target_pairs={{0,32},{16,48},{32,0},{48,16},{1,33},{17,49},{33,1},{49,17},{2,34}... | collective-permute-start | bytes 1916936 | tf_op jit(solution)/shard_map/ppermute | solution.py:276
  8.7 10.0 %collective-permute-start.1 = (bf16[192,1664]{1,0:T(8,128)(2,1)}, bf16[192,1664]{1,0:T(8,128)(2,1)S(1)}, u32[]{:S(2)}, u32[]{:S(2)}) collective-permute-start(bf16[192,1664]{1,0:T(8,128)(2,1)} %get-tuple-element.14), channel_id=1, source_target_pairs={{0,16},{16,32},{32,48},{48,0},{1,17},{17,33},{33,49},{49,1},{2,18}... | collective-permute-start | bytes 1916936 | tf_op jit(solution)/shard_map/ppermute | solution.py:276
  18.7 2.8 %collective-permute-start.2 = (bf16[192,1664]{1,0:T(8,128)(2,1)}, bf16[192,1664]{1,0:T(8,128)(2,1)}, u32[]{:S(2)}, u32[]{:S(2)}) collective-permute-start(bf16[192,1664]{1,0:T(8,128)(2,1)} %get-tuple-element.15), channel_id=1, source_target_pairs={{0,48},{16,0},{32,16},{48,32},{1,49},{17,1},{33,17},{49,33},{2,50}... | collective-permute-start | bytes 1916936 | tf_op jit(solution)/shard_map/ppermute | solution.py:276
  21.5 1.4 %scaled_copies.1 = bf16[12,12,256]{2,1,0:T(8,128)(2,1)} custom-call(bf16[12,256]{1,0:T(8,128)(2,1)} %values, bf16[1,12]{1,0:T(2,128)(2,1)} %bitcast.3), custom_call_target="tpu_custom_call" | custom-call | tf_op jit(solution)/shard_map/scaled_copies/pallas_call | solution.py:262
  22.9 19.9 %all_to_all.20 = bf16[12,12,256]{2,1,0:T(8,128)(2,1)S(1)} all-to-all(bf16[12,12,256]{2,1,0:T(8,128)(2,1)} %scaled_copies.1), channel_id=1, replica_groups=mesh['z'=12,'x'=4,'yh'=2,'yl'=4,'c'=2] {'z'}, dimensions={0} | all-to-all | bytes 147456 | tf_op jit(solution)/shard_map/all_to_all | solution.py:294
  42.9 0.9 broadcast_in_dim.8
  43.7 7.1 %all-to-all-start.1 = ((bf16[8,144,256]{2,1,0:T(8,128)(2,1)}), bf16[8,144,256]{2,1,0:T(8,128)(2,1)S(1)}, u32[]{:S(2)}, u32[]{:S(2)}) async-start(bf16[8,144,256]{2,1,0:T(8,128)(2,1)} %broadcast_in_dim.8), calls=%async_computation.1 | async-start | bytes 1179648 | tf_op jit(solution)/shard_map/all_to_all | solution.py:272
  50.9 0.0 collective-permute-done.refs_1_
  50.9 0.0 collective-permute-done.1.refs_2_
  50.9 0.0 collective-permute-done.2.refs_3_
  50.9 0.0 copy-done.5
  50.9 0.0 copy-done.2
  50.9 2.5 %other_half.1 = bf16[256,1152]{1,0:T(8,128)(2,1)S(1)} custom-call(s32[2]{0:T(128)S(1)} %copy-done.5, bf16[192,1664]{1,0:T(8,128)(2,1)S(1)} %copy-done.2, bf16[192,1664]{1,0:T(8,128)(2,1)S(1)} %collective-permute-done.refs_1_, bf16[192,1664]{1,0:T(8,128)(2,1)S(1)} %collective-permute-done.1.refs_2_, bf16[192,1664]{1,0:T(8,128)(2,1)} %collective-permute-done.2.refs_3_), custom_call_target="tpu_custom_call" | custom-call | flops 45298483200 | bytes 2555904 | tf_op jit(solution)/shard_map/other_half/pallas_call | solution.py:106
  53.4 0.0 copy-start.4
  53.4 2.1 %collective-permute-start.3 = (bf16[256,1152]{1,0:T(8,128)(2,1)S(1)}, bf16[256,1152]{1,0:T(8,128)(2,1)S(1)}, u32[]{:S(2)}, u32[]{:S(2)}) collective-permute-start(bf16[256,1152]{1,0:T(8,128)(2,1)S(1)} %other_half.1), channel_id=1, source_target_pairs={{0,1},{1,0},{2,3},{3,2},{4,5},{5,4},{6,7},{7,6},{8,9},{9,8},{10,11... | collective-permute-start | bytes 1769480 | tf_op jit(solution)/shard_map/ppermute | solution.py:280
  55.4 2.0 %collective-permute-done.3.refs_4_ = bf16[256,1152]{1,0:T(8,128)(2,1)S(1)} collective-permute-done((bf16[256,1152]{1,0:T(8,128)(2,1)S(1)}, bf16[256,1152]{1,0:T(8,128)(2,1)S(1)}, u32[]{:S(2)}, u32[]{:S(2)}) %collective-permute-start.3) | collective-permute-done | bytes 589856 | tf_op jit(solution)/shard_map/ppermute | solution.py:280
  57.4 0.0 copy-done.3
  57.4 3.9 %own_half.1 = bf16[8,144,256]{2,1,0:T(8,128)(2,1)} custom-call(s32[2]{0:T(128)S(1)} %copy-done.5, bf16[192,1664]{1,0:T(8,128)(2,1)S(1)} %copy-done.2, bf16[192,1664]{1,0:T(8,128)(2,1)S(1)} %collective-permute-done.refs_1_, bf16[192,1664]{1,0:T(8,128)(2,1)S(1)} %collective-permute-done.1.refs_2_, bf16[192,1664]{1,0:T(8,128)(2,1)} %collective-permute-done.2.refs_3_, ...), custom_call_target="tpu_custom_call" | custom-call | flops 452984832 | bytes 2555904 | tf_op jit(solution)/shard_map/own_half/pallas_call | solution.py:106
  61.3 6.1 %all-to-all-done.1.parts = bf16[8,144,256]{2,1,0:T(8,128)(2,1)S(1)} async-done(((bf16[8,144,256]{2,1,0:T(8,128)(2,1)}), bf16[8,144,256]{2,1,0:T(8,128)(2,1)S(1)}, u32[]{:S(2)}, u32[]{:S(2)}) %all-to-all-start.1) | async-done | bytes 589856 | tf_op jit(solution)/shard_map/all_to_all | solution.py:272
  67.4 0.0 copy-done.4
  67.4 0.9 regroup.1.refs_0_
  68.3 3.7 %collective-permute-start.6 = (bf16[12,96,256]{2,1,0:T(8,128)(2,1)S(1)}, bf16[12,96,256]{2,1,0:T(8,128)(2,1)}, u32[]{:S(2)}, u32[]{:S(2)}) collective-permute-start(bf16[12,96,256]{2,1,0:T(8,128)(2,1)S(1)} %regroup.1.refs_0_), channel_id=1, source_target_pairs={{0,32},{16,48},{32,0},{48,16},{1,33},{17,49},{33,1},{49,17},{2,34}... | collective-permute-start | bytes 1769480 | tf_op jit(solution)/shard_map/ppermute | solution.py:276
  72.0 3.1 %collective-permute-start.5 = (bf16[12,96,256]{2,1,0:T(8,128)(2,1)S(1)}, bf16[12,96,256]{2,1,0:T(8,128)(2,1)}, u32[]{:S(2)}, u32[]{:S(2)}) collective-permute-start(bf16[12,96,256]{2,1,0:T(8,128)(2,1)S(1)} %regroup.1.refs_0_), channel_id=1, source_target_pairs={{0,16},{16,32},{32,48},{48,0},{1,17},{17,33},{33,49},{49,1},{2,18}... | collective-permute-start | bytes 1769480 | tf_op jit(solution)/shard_map/ppermute | solution.py:276
  75.1 2.8 %collective-permute-start.4 = (bf16[12,96,256]{2,1,0:T(8,128)(2,1)S(1)}, bf16[12,96,256]{2,1,0:T(8,128)(2,1)}, u32[]{:S(2)}, u32[]{:S(2)}) collective-permute-start(bf16[12,96,256]{2,1,0:T(8,128)(2,1)S(1)} %regroup.1.refs_0_), channel_id=1, source_target_pairs={{0,48},{16,0},{32,16},{48,32},{1,49},{17,1},{33,17},{49,33},{2,50}... | collective-permute-start | bytes 1769480 | tf_op jit(solution)/shard_map/ppermute | solution.py:276
  77.8 3.6 %all-to-all-start.2 = ((bf16[8,144,256]{2,1,0:T(8,128)(2,1)}), bf16[8,144,256]{2,1,0:T(8,128)(2,1)S(1)}, u32[]{:S(2)}, u32[]{:S(2)}) async-start(bf16[8,144,256]{2,1,0:T(8,128)(2,1)} %own_half.1), calls=%async_computation.2 | async-start | bytes 1179648 | tf_op jit(solution)/shard_map/all_to_all | solution.py:301
  81.4 1.9 %collective-permute-start.7 = (bf16[12,96,256]{2,1,0:T(8,128)(2,1)S(1)}, bf16[12,96,256]{2,1,0:T(8,128)(2,1)}, u32[]{:S(2)}, u32[]{:S(2)}) collective-permute-start(bf16[12,96,256]{2,1,0:T(8,128)(2,1)S(1)} %regroup.1.refs_0_), channel_id=1, source_target_pairs={{0,1},{1,0},{2,3},{3,2},{4,5},{5,4},{6,7},{7,6},{8,9},{9,8},{10,11... | collective-permute-start | bytes 1769480 | tf_op jit(solution)/shard_map/ppermute | solution.py:280
  83.3 4.8 %collective-permute-done.6.refs_3_ = bf16[12,96,256]{2,1,0:T(8,128)(2,1)} collective-permute-done((bf16[12,96,256]{2,1,0:T(8,128)(2,1)S(1)}, bf16[12,96,256]{2,1,0:T(8,128)(2,1)}, u32[]{:S(2)}, u32[]{:S(2)}) %collective-permute-start.6) | collective-permute-done | bytes 589856 | tf_op jit(solution)/shard_map/ppermute | solution.py:276
  88.1 1.9 %collective-permute-start.10 = (bf16[12,96,256]{2,1,0:T(8,128)(2,1)}, bf16[12,96,256]{2,1,0:T(8,128)(2,1)}, u32[]{:S(2)}, u32[]{:S(2)}) collective-permute-start(bf16[12,96,256]{2,1,0:T(8,128)(2,1)} %collective-permute-done.6.refs_3_), channel_id=1, source_target_pairs={{0,1},{1,0},{2,3},{3,2},{4,5},{5,4},{6,7},{7,6},{8,9},{9,8},{10,11... | collective-permute-start | bytes 1769480 | tf_op jit(solution)/shard_map/ppermute | solution.py:280
  90.0 6.9 %collective-permute-done.5.refs_2_ = bf16[12,96,256]{2,1,0:T(8,128)(2,1)} collective-permute-done((bf16[12,96,256]{2,1,0:T(8,128)(2,1)S(1)}, bf16[12,96,256]{2,1,0:T(8,128)(2,1)}, u32[]{:S(2)}, u32[]{:S(2)}) %collective-permute-start.5) | collective-permute-done | bytes 589856 | tf_op jit(solution)/shard_map/ppermute | solution.py:276
  96.9 1.9 %collective-permute-start.9 = (bf16[12,96,256]{2,1,0:T(8,128)(2,1)}, bf16[12,96,256]{2,1,0:T(8,128)(2,1)}, u32[]{:S(2)}, u32[]{:S(2)}) collective-permute-start(bf16[12,96,256]{2,1,0:T(8,128)(2,1)} %collective-permute-done.5.refs_2_), channel_id=1, source_target_pairs={{0,1},{1,0},{2,3},{3,2},{4,5},{5,4},{6,7},{7,6},{8,9},{9,8},{10,11... | collective-permute-start | bytes 1769480 | tf_op jit(solution)/shard_map/ppermute | solution.py:280
  98.8 0.0 collective-permute-done.4.refs_1_
  98.8 2.4 %collective-permute-start.8 = (bf16[12,96,256]{2,1,0:T(8,128)(2,1)}, bf16[12,96,256]{2,1,0:T(8,128)(2,1)}, u32[]{:S(2)}, u32[]{:S(2)}) collective-permute-start(bf16[12,96,256]{2,1,0:T(8,128)(2,1)} %collective-permute-done.4.refs_1_), channel_id=1, source_target_pairs={{0,1},{1,0},{2,3},{3,2},{4,5},{5,4},{6,7},{7,6},{8,9},{9,8},{10,11... | collective-permute-start | bytes 1769480 | tf_op jit(solution)/shard_map/ppermute | solution.py:280
  101.2 0.0 all-to-all-done.2.parts
  101.2 0.7 sum_over_y.1
  102.0 3.5 %all-to-all-start.3 = ((bf16[12,12,256]{2,1,0:T(8,128)(2,1)}), bf16[12,12,256]{2,1,0:T(8,128)(2,1)S(1)}, u32[]{:S(2)}, u32[]{:S(2)}) async-start(bf16[12,12,256]{2,1,0:T(8,128)(2,1)} %sum_over_y.1), calls=%async_computation.3 | async-start | bytes 196608 | tf_op jit(solution)/shard_map/all_to_all | solution.py:303
  105.5 0.0 collective-permute-done.7.refs_4_
  105.5 0.0 collective-permute-done.10.refs_7_
  105.5 0.0 collective-permute-done.9.refs_6_
  105.5 0.0 collective-permute-done.8.refs_5_
  105.5 0.0 copy-done
  105.5 0.0 copy-done.1
  105.5 7.1 %project.1 = (bf16[192,512]{1,0:T(8,128)(2,1)}, bf16[192,4608]{1,0:T(8,128)(2,1)}) custom-call(s32[2]{0:T(128)S(1)} %copy-done.5, bf16[12,96,256]{2,1,0:T(8,128)(2,1)S(1)} %regroup.1.refs_0_, bf16[12,96,256]{2,1,0:T(8,128)(2,1)} %collective-permute-done.4.refs_1_, bf16[12,96,256]{2,1,0:T(8,128)(2,1)} %collective-permute-done.5.refs_2_, ...), custom_call_target="tpu_custom_call" | custom-call | flops 1811939328 | bytes 8257536 | tf_op jit(solution)/shard_map/project/pallas_call | solution.py:216
  112.7 5.0 %all-to-all-done.3 = bf16[12,12,256]{2,1,0:T(8,128)(2,1)S(1)} async-done(((bf16[12,12,256]{2,1,0:T(8,128)(2,1)}), bf16[12,12,256]{2,1,0:T(8,128)(2,1)S(1)}, u32[]{:S(2)}, u32[]{:S(2)}) %all-to-all-start.3) | async-done | bytes 73760 | tf_op jit(solution)/shard_map/all_to_all | solution.py:303
  117.7 0.6 broadcast_multiply_fusion
  (5 shorter events, 0.0 us)
Async XLA Ops:
  1.2 49.6 %copy-start.5 = (s32[2]{0:T(128)S(1)}, s32[2]{0:T(128)}, u32[]{:S(2)}) copy-start(s32[2]{0:T(128)} %pad_add_fusion.place) | copy-start | bytes 28
  5.3 45.6 %copy-start.2 = (bf16[192,1664]{1,0:T(8,128)(2,1)S(1)}, bf16[192,1664]{1,0:T(8,128)(2,1)}, u32[]{:S(2)}) copy-start(bf16[192,1664]{1,0:T(8,128)(2,1)} %get-tuple-element.11.refs_0_) | copy-start | bytes 1916932
  5.3 45.6 %collective-permute-start = (bf16[192,1664]{1,0:T(8,128)(2,1)}, bf16[192,1664]{1,0:T(8,128)(2,1)S(1)}, u32[]{:S(2)}, u32[]{:S(2)}) collective-permute-start(bf16[192,1664]{1,0:T(8,128)(2,1)} %get-tuple-element.13), channel_id=1, source_target_pairs={{0,32},{16,48},{32,0},{48,16},{1,33},{17,49},{33,1},{49,17},{2,34}... | collective-permute-start | bytes 1916936 | tf_op jit(solution)/shard_map/ppermute | solution.py:276
  8.7 42.2 %collective-permute-start.1 = (bf16[192,1664]{1,0:T(8,128)(2,1)}, bf16[192,1664]{1,0:T(8,128)(2,1)S(1)}, u32[]{:S(2)}, u32[]{:S(2)}) collective-permute-start(bf16[192,1664]{1,0:T(8,128)(2,1)} %get-tuple-element.14), channel_id=1, source_target_pairs={{0,16},{16,32},{32,48},{48,0},{1,17},{17,33},{33,49},{49,1},{2,18}... | collective-permute-start | bytes 1916936 | tf_op jit(solution)/shard_map/ppermute | solution.py:276
  18.7 32.2 %collective-permute-start.2 = (bf16[192,1664]{1,0:T(8,128)(2,1)}, bf16[192,1664]{1,0:T(8,128)(2,1)}, u32[]{:S(2)}, u32[]{:S(2)}) collective-permute-start(bf16[192,1664]{1,0:T(8,128)(2,1)} %get-tuple-element.15), channel_id=1, source_target_pairs={{0,48},{16,0},{32,16},{48,32},{1,49},{17,1},{33,17},{49,33},{2,50}... | collective-permute-start | bytes 1916936 | tf_op jit(solution)/shard_map/ppermute | solution.py:276
  43.7 23.6 %all-to-all-start.1 = ((bf16[8,144,256]{2,1,0:T(8,128)(2,1)}), bf16[8,144,256]{2,1,0:T(8,128)(2,1)S(1)}, u32[]{:S(2)}, u32[]{:S(2)}) async-start(bf16[8,144,256]{2,1,0:T(8,128)(2,1)} %broadcast_in_dim.8), calls=%async_computation.1 | async-start | bytes 1179648 | tf_op jit(solution)/shard_map/all_to_all | solution.py:272
  50.8 6.6 %copy-start.3 = (bf16[384,384]{1,0:T(8,128)(2,1)S(1)}, bf16[384,384]{1,0:T(8,128)(2,1)}, u32[]{:S(2)}) copy-start(bf16[384,384]{1,0:T(8,128)(2,1)} %constant.18.clone.refs_5_) | copy-start | bytes 884740
  53.4 14.0 %copy-start.4 = (bf16[384,384]{1,0:T(8,128)(2,1)S(1)}, bf16[384,384]{1,0:T(8,128)(2,1)}, u32[]{:S(2)}) copy-start(bf16[384,384]{1,0:T(8,128)(2,1)} %constant.19.clone.perm) | copy-start | bytes 884740
  53.4 4.0 %collective-permute-start.3 = (bf16[256,1152]{1,0:T(8,128)(2,1)S(1)}, bf16[256,1152]{1,0:T(8,128)(2,1)S(1)}, u32[]{:S(2)}, u32[]{:S(2)}) collective-permute-start(bf16[256,1152]{1,0:T(8,128)(2,1)S(1)} %other_half.1), channel_id=1, source_target_pairs={{0,1},{1,0},{2,3},{3,2},{4,5},{5,4},{6,7},{7,6},{8,9},{9,8},{10,11... | collective-permute-start | bytes 1769480 | tf_op jit(solution)/shard_map/ppermute | solution.py:280
  61.3 44.2 %copy-start = (bf16[192,4608]{1,0:T(8,128)(2,1)S(1)}, bf16[192,4608]{1,0:T(8,128)(2,1)}, u32[]{:S(2)}) copy-start(bf16[192,4608]{1,0:T(8,128)(2,1)} %refs_8_.1) | copy-start | bytes 5308420
  61.3 44.2 %copy-start.1 = (bf16[192,512]{1,0:T(8,128)(2,1)S(1)}, bf16[192,512]{1,0:T(8,128)(2,1)}, u32[]{:S(2)}) copy-start(bf16[192,512]{1,0:T(8,128)(2,1)} %refs_10_.1) | copy-start | bytes 589828
  68.3 19.8 %collective-permute-start.6 = (bf16[12,96,256]{2,1,0:T(8,128)(2,1)S(1)}, bf16[12,96,256]{2,1,0:T(8,128)(2,1)}, u32[]{:S(2)}, u32[]{:S(2)}) collective-permute-start(bf16[12,96,256]{2,1,0:T(8,128)(2,1)S(1)} %regroup.1.refs_0_), channel_id=1, source_target_pairs={{0,32},{16,48},{32,0},{48,16},{1,33},{17,49},{33,1},{49,17},{2,34}... | collective-permute-start | bytes 1769480 | tf_op jit(solution)/shard_map/ppermute | solution.py:276
  72.0 24.9 %collective-permute-start.5 = (bf16[12,96,256]{2,1,0:T(8,128)(2,1)S(1)}, bf16[12,96,256]{2,1,0:T(8,128)(2,1)}, u32[]{:S(2)}, u32[]{:S(2)}) collective-permute-start(bf16[12,96,256]{2,1,0:T(8,128)(2,1)S(1)} %regroup.1.refs_0_), channel_id=1, source_target_pairs={{0,16},{16,32},{32,48},{48,0},{1,17},{17,33},{33,49},{49,1},{2,18}... | collective-permute-start | bytes 1769480 | tf_op jit(solution)/shard_map/ppermute | solution.py:276
  75.1 23.7 %collective-permute-start.4 = (bf16[12,96,256]{2,1,0:T(8,128)(2,1)S(1)}, bf16[12,96,256]{2,1,0:T(8,128)(2,1)}, u32[]{:S(2)}, u32[]{:S(2)}) collective-permute-start(bf16[12,96,256]{2,1,0:T(8,128)(2,1)S(1)} %regroup.1.refs_0_), channel_id=1, source_target_pairs={{0,48},{16,0},{32,16},{48,32},{1,49},{17,1},{33,17},{49,33},{2,50}... | collective-permute-start | bytes 1769480 | tf_op jit(solution)/shard_map/ppermute | solution.py:276
  77.8 23.4 %all-to-all-start.2 = ((bf16[8,144,256]{2,1,0:T(8,128)(2,1)}), bf16[8,144,256]{2,1,0:T(8,128)(2,1)S(1)}, u32[]{:S(2)}, u32[]{:S(2)}) async-start(bf16[8,144,256]{2,1,0:T(8,128)(2,1)} %own_half.1), calls=%async_computation.2 | async-start | bytes 1179648 | tf_op jit(solution)/shard_map/all_to_all | solution.py:301
  81.4 24.1 %collective-permute-start.7 = (bf16[12,96,256]{2,1,0:T(8,128)(2,1)S(1)}, bf16[12,96,256]{2,1,0:T(8,128)(2,1)}, u32[]{:S(2)}, u32[]{:S(2)}) collective-permute-start(bf16[12,96,256]{2,1,0:T(8,128)(2,1)S(1)} %regroup.1.refs_0_), channel_id=1, source_target_pairs={{0,1},{1,0},{2,3},{3,2},{4,5},{5,4},{6,7},{7,6},{8,9},{9,8},{10,11... | collective-permute-start | bytes 1769480 | tf_op jit(solution)/shard_map/ppermute | solution.py:280
  88.1 17.4 %collective-permute-start.10 = (bf16[12,96,256]{2,1,0:T(8,128)(2,1)}, bf16[12,96,256]{2,1,0:T(8,128)(2,1)}, u32[]{:S(2)}, u32[]{:S(2)}) collective-permute-start(bf16[12,96,256]{2,1,0:T(8,128)(2,1)} %collective-permute-done.6.refs_3_), channel_id=1, source_target_pairs={{0,1},{1,0},{2,3},{3,2},{4,5},{5,4},{6,7},{7,6},{8,9},{9,8},{10,11... | collective-permute-start | bytes 1769480 | tf_op jit(solution)/shard_map/ppermute | solution.py:280
  96.9 8.6 %collective-permute-start.9 = (bf16[12,96,256]{2,1,0:T(8,128)(2,1)}, bf16[12,96,256]{2,1,0:T(8,128)(2,1)}, u32[]{:S(2)}, u32[]{:S(2)}) collective-permute-start(bf16[12,96,256]{2,1,0:T(8,128)(2,1)} %collective-permute-done.5.refs_2_), channel_id=1, source_target_pairs={{0,1},{1,0},{2,3},{3,2},{4,5},{5,4},{6,7},{7,6},{8,9},{9,8},{10,11... | collective-permute-start | bytes 1769480 | tf_op jit(solution)/shard_map/ppermute | solution.py:280
  98.8 6.7 %collective-permute-start.8 = (bf16[12,96,256]{2,1,0:T(8,128)(2,1)}, bf16[12,96,256]{2,1,0:T(8,128)(2,1)}, u32[]{:S(2)}, u32[]{:S(2)}) collective-permute-start(bf16[12,96,256]{2,1,0:T(8,128)(2,1)} %collective-permute-done.4.refs_1_), channel_id=1, source_target_pairs={{0,1},{1,0},{2,3},{3,2},{4,5},{5,4},{6,7},{7,6},{8,9},{9,8},{10,11... | collective-permute-start | bytes 1769480 | tf_op jit(solution)/shard_map/ppermute | solution.py:280
  102.0 15.7 %all-to-all-start.3 = ((bf16[12,12,256]{2,1,0:T(8,128)(2,1)}), bf16[12,12,256]{2,1,0:T(8,128)(2,1)S(1)}, u32[]{:S(2)}, u32[]{:S(2)}) async-start(bf16[12,12,256]{2,1,0:T(8,128)(2,1)} %sum_over_y.1), calls=%async_computation.3 | async-start | bytes 196608 | tf_op jit(solution)/shard_map/all_to_all | solution.py:303

commit v8 on v6

--- a/solution.py
+++ b/solution.py
@@ -28,7 +28,7 @@
 BY_DEVICE = np.zeros((ZG * XROWS, ZG * XROWS), np.float32)
 BY_DEVICE[(((_yh * NYL + _yl) * ZG + _z) * ROWS + _i).ravel(), np.arange(ZG * XROWS)] = 1
 IN_ORDER = BY_DEVICE.T
-HELD = (0, 2, 1, 3)
+HELD = (0, 3, 1, 2)
 ZSTEP = 3
 
 
@@ -288,7 +288,7 @@
     w_z = lax.all_to_all(copies, "z", split_axis=0, concat_axis=0, tiled=True)
 
     packed = pack(place, hidden, cotangent)
-    held = [packed[0]] + [shift(packed[r], r) for r in (1, 3, 2)]
+    held = [packed[0]] + [shift(packed[r], r) for r in (2, 1, 3)]
     term = own_half(place, held, swap(other_half(place, held)))
 
     w_y = regroup(to_all(w_z.reshape(NZ * ROWS, HALF), Y, NY))

time: 129 us -> 126 us (0.977)
  waiting for transfers between devices: 33.2 us -> 31.2 us
    ppermute x6, waiting for transfers between devices: 26.8 us -> 21.3 us  [shift(): return lax.ppermute(piece, 'x', [(k, (k + r) % NX) for k in range(NX)])]
    all_to_all x1, waiting for transfers between devices: 1.49 us -> 5 us  [on_device(): t_y = lax.all_to_all(term, Y, split_axis=0, concat_axis=0, tiled=True)]
  transfers between devices with their start and end apart: 15 -> 15, of which waited for: 5 -> 7; matrix products, arithmetic and copies ran while one was open for 1% -> 1% of each run, Pallas kernels for 16% -> 16%
where the time goes in v8:
time: 126 us; the launch traced here: 124 us
  starting transfers between devices  67.9 us (54%)
  waiting for transfers between devices  31.2 us (25%)
  Pallas kernels  21.3 us (17%)
  local copies, waits for them, and re-layouts  1.87 us (1%)
  other arithmetic  1.27 us (1%)
    ppermute x6, waiting for transfers between devices, shift(): return lax.ppermute(piece, 'x', [(k, (k + r) % NX) for k in range(NX)])  21.3 us
    ppermute x6, starting transfers between devices, shift(): return lax.ppermute(piece, 'x', [(k, (k + r) % NX) for k in range(NX)])  18.6 us
    all_to_all x1, starting transfers between devices, on_device(): w_z = lax.all_to_all(copies, 'z', split_axis=0, concat_axis=0, tiled=True)  15.2 us
    ppermute x5, starting transfers between devices, swap(): return lax.ppermute(piece, 'c', [(0, 1), (1, 0)])  10.5 us
    all_to_all x1, starting transfers between devices, on_device(): t_z = lax.all_to_all(sum_y, 'z', split_axis=0, concat_axis=0, tiled=True)  9.32 us
    all_to_all x1, starting transfers between devices, on_device(): t_y = lax.all_to_all(term, Y, split_axis=0, concat_axis=0, tiled=True)  7.23 us
    all_to_all x1, starting transfers between devices, to_all(): return lax.all_to_all(copies, axis, split_axis=0, concat_axis=0, tiled=True)  7.1 us
    pallas_call x1, Pallas kernels, project(): pl.pallas_call(project_kernel, grid_spec=pltpu.PrefetchScalarGridSpec(num...  7.1 us
  transfers between devices with their start and end apart: 15, of which 7 were waited for; matrix products, arithmetic and copies ran while one was open for 1% of the time, Pallas kernels for 16%

profile of v8, /device:TPU:6, one launch (start us, length us, event | category | flops | bytes accessed | tf_op | source)
XLA Modules:
  0.0 124.3 jit_solution(9497170868406263162)
XLA Ops:
  0.6 1.4 %scaled_copies.1 = bf16[12,12,256]{2,1,0:T(8,128)(2,1)} custom-call(bf16[12,256]{1,0:T(8,128)(2,1)} %values.1, bf16[1,12]{1,0:T(2,128)(2,1)} %bitcast.3), custom_call_target="tpu_custom_call" | custom-call | tf_op jit(solution)/shard_map/scaled_copies/pallas_call | solution.py:262
  2.1 15.2 %all-to-all-start = ((bf16[12,12,256]{2,1,0:T(8,128)(2,1)}), bf16[12,12,256]{2,1,0:T(8,128)(2,1)S(1)}, u32[]{:S(2)}, u32[]{:S(2)}) async-start(bf16[12,12,256]{2,1,0:T(8,128)(2,1)} %scaled_copies.1), calls=%async_computation | async-start | bytes 196608 | tf_op jit(solution)/shard_map/all_to_all | solution.py:288
  17.2 0.6 pad_add_fusion.place
  17.9 4.0 %pack.1 = (bf16[192,1664]{1,0:T(8,128)(2,1)}, bf16[192,1664]{1,0:T(8,128)(2,1)}, bf16[192,1664]{1,0:T(8,128)(2,1)}, bf16[192,1664]{1,0:T(8,128)(2,1)}) custom-call(s32[2]{0:T(128)} %pad_add_fusion.place, bf16[192,4608]{1,0:T(8,128)(2,1)} %hidden.1, bf16[192,512]{1,0:T(8,128)(2,1)} %cot.1), custom_call_target="tpu_custom_call" | custom-call | flops 884736 | bytes 3538944 | tf_op jit(solution)/shard_map/pack/pallas_call | solution.py:52
  21.9 0.0 copy-start.1
  21.9 3.4 %collective-permute-start.7 = (bf16[192,1664]{1,0:T(8,128)(2,1)}, bf16[192,1664]{1,0:T(8,128)(2,1)S(1)}, u32[]{:S(2)}, u32[]{:S(2)}) collective-permute-start(bf16[192,1664]{1,0:T(8,128)(2,1)} %get-tuple-element.12), channel_id=1, source_target_pairs={{0,32},{16,48},{32,0},{48,16},{1,33},{17,49},{33,1},{49,17},{2,34}... | collective-permute-start | bytes 1916936 | tf_op jit(solution)/shard_map/ppermute | solution.py:276
  25.3 4.0 %collective-permute-start.8 = (bf16[192,1664]{1,0:T(8,128)(2,1)}, bf16[192,1664]{1,0:T(8,128)(2,1)S(1)}, u32[]{:S(2)}, u32[]{:S(2)}) collective-permute-start(bf16[192,1664]{1,0:T(8,128)(2,1)} %get-tuple-element.13), channel_id=1, source_target_pairs={{0,16},{16,32},{32,48},{48,0},{1,17},{17,33},{33,49},{49,1},{2,18}... | collective-permute-start | bytes 1916936 | tf_op jit(solution)/shard_map/ppermute | solution.py:276
  29.4 1.9 %collective-permute-start.9 = (bf16[192,1664]{1,0:T(8,128)(2,1)}, bf16[192,1664]{1,0:T(8,128)(2,1)S(1)}, u32[]{:S(2)}, u32[]{:S(2)}) collective-permute-start(bf16[192,1664]{1,0:T(8,128)(2,1)} %get-tuple-element.14), channel_id=1, source_target_pairs={{0,48},{16,0},{32,16},{48,32},{1,49},{17,1},{33,17},{49,33},{2,50}... | collective-permute-start | bytes 1916936 | tf_op jit(solution)/shard_map/ppermute | solution.py:276
  31.3 0.0 all-to-all-done
  31.3 0.9 broadcast_in_dim.8
  32.2 7.1 %all-to-all-start.1 = ((bf16[8,144,256]{2,1,0:T(8,128)(2,1)}), bf16[8,144,256]{2,1,0:T(8,128)(2,1)S(1)}, u32[]{:S(2)}, u32[]{:S(2)}) async-start(bf16[8,144,256]{2,1,0:T(8,128)(2,1)} %broadcast_in_dim.8), calls=%async_computation.1 | async-start | bytes 1179648 | tf_op jit(solution)/shard_map/all_to_all | solution.py:272
  39.3 3.7 %collective-permute-done.7.refs_1_ = bf16[192,1664]{1,0:T(8,128)(2,1)S(1)} collective-permute-done((bf16[192,1664]{1,0:T(8,128)(2,1)}, bf16[192,1664]{1,0:T(8,128)(2,1)S(1)}, u32[]{:S(2)}, u32[]{:S(2)}) %collective-permute-start.7) | collective-permute-done | bytes 639008 | tf_op jit(solution)/shard_map/ppermute | solution.py:276
  43.0 10.0 %collective-permute-done.8.refs_2_ = bf16[192,1664]{1,0:T(8,128)(2,1)S(1)} collective-permute-done((bf16[192,1664]{1,0:T(8,128)(2,1)}, bf16[192,1664]{1,0:T(8,128)(2,1)S(1)}, u32[]{:S(2)}, u32[]{:S(2)}) %collective-permute-start.8) | collective-permute-done | bytes 639008 | tf_op jit(solution)/shard_map/ppermute | solution.py:276
  53.0 2.2 %collective-permute-done.9.refs_3_ = bf16[192,1664]{1,0:T(8,128)(2,1)S(1)} collective-permute-done((bf16[192,1664]{1,0:T(8,128)(2,1)}, bf16[192,1664]{1,0:T(8,128)(2,1)S(1)}, u32[]{:S(2)}, u32[]{:S(2)}) %collective-permute-start.9) | collective-permute-done | bytes 639008 | tf_op jit(solution)/shard_map/ppermute | solution.py:276
  55.2 0.0 copy-done.5
  55.2 0.0 copy-done.1
  55.2 2.2 %other_half.1 = bf16[256,1152]{1,0:T(8,128)(2,1)} custom-call(s32[2]{0:T(128)S(1)} %copy-done.5, bf16[192,1664]{1,0:T(8,128)(2,1)S(1)} %copy-done.1, bf16[192,1664]{1,0:T(8,128)(2,1)S(1)} %collective-permute-done.7.refs_1_, bf16[192,1664]{1,0:T(8,128)(2,1)S(1)} %collective-permute-done.8.refs_2_, bf16[192,1664]{1,0:T(8,128)(2,1)S(1)} %collective-permute-done.9.refs_3_), custom_call_target="tpu_custom_call" | custom-call | flops 452984832 | bytes 2555904 | tf_op jit(solution)/shard_map/other_half/pallas_call | solution.py:106
  57.4 1.9 %collective-permute-start.10 = (bf16[256,1152]{1,0:T(8,128)(2,1)}, bf16[256,1152]{1,0:T(8,128)(2,1)}, u32[]{:S(2)}, u32[]{:S(2)}) collective-permute-start(bf16[256,1152]{1,0:T(8,128)(2,1)} %other_half.1), channel_id=1, source_target_pairs={{0,1},{1,0},{2,3},{3,2},{4,5},{5,4},{6,7},{7,6},{8,9},{9,8},{10,11... | collective-permute-start | bytes 1769480 | tf_op jit(solution)/shard_map/ppermute | solution.py:280
  59.3 0.0 all-to-all-done.1.parts
  59.3 0.0 copy-start.4
  59.3 1.0 copy-done.4
  60.3 1.9 %regroup.1.refs_0_ = bf16[12,96,256]{2,1,0:T(8,128)(2,1)} custom-call(bf16[8,144,256]{2,1,0:T(8,128)(2,1)S(1)} %all-to-all-done.1.parts, bf16[384,384]{1,0:T(8,128)(2,1)S(1)} %copy-done.4), custom_call_target="tpu_custom_call" | custom-call | flops 226492416 | bytes 1179648 | tf_op jit(solution)/shard_map/regroup/pallas_call | solution.py:141
  62.2 3.4 %collective-permute-start.2 = (bf16[12,96,256]{2,1,0:T(8,128)(2,1)}, bf16[12,96,256]{2,1,0:T(8,128)(2,1)S(1)}, u32[]{:S(2)}, u32[]{:S(2)}) collective-permute-start(bf16[12,96,256]{2,1,0:T(8,128)(2,1)} %regroup.1.refs_0_), channel_id=1, source_target_pairs={{0,32},{16,48},{32,0},{48,16},{1,33},{17,49},{33,1},{49,17},{2,34}... | collective-permute-start | bytes 1769480 | tf_op jit(solution)/shard_map/ppermute | solution.py:276
  65.6 3.9 %collective-permute-start.1 = (bf16[12,96,256]{2,1,0:T(8,128)(2,1)}, bf16[12,96,256]{2,1,0:T(8,128)(2,1)}, u32[]{:S(2)}, u32[]{:S(2)}) collective-permute-start(bf16[12,96,256]{2,1,0:T(8,128)(2,1)} %regroup.1.refs_0_), channel_id=1, source_target_pairs={{0,16},{16,32},{32,48},{48,0},{1,17},{17,33},{33,49},{49,1},{2,18}... | collective-permute-start | bytes 1769480 | tf_op jit(solution)/shard_map/ppermute | solution.py:276
  69.5 1.9 %collective-permute-start = (bf16[12,96,256]{2,1,0:T(8,128)(2,1)}, bf16[12,96,256]{2,1,0:T(8,128)(2,1)}, u32[]{:S(2)}, u32[]{:S(2)}) collective-permute-start(bf16[12,96,256]{2,1,0:T(8,128)(2,1)} %regroup.1.refs_0_), channel_id=1, source_target_pairs={{0,48},{16,0},{32,16},{48,32},{1,49},{17,1},{33,17},{49,33},{2,50}... | collective-permute-start | bytes 1769480 | tf_op jit(solution)/shard_map/ppermute | solution.py:276
  71.4 0.0 collective-permute-done.10.refs_4_
  71.5 0.0 copy-done.3
  71.5 3.9 %own_half.1 = bf16[8,144,256]{2,1,0:T(8,128)(2,1)} custom-call(s32[2]{0:T(128)S(1)} %copy-done.5, bf16[192,1664]{1,0:T(8,128)(2,1)S(1)} %copy-done.1, bf16[192,1664]{1,0:T(8,128)(2,1)S(1)} %collective-permute-done.7.refs_1_, bf16[192,1664]{1,0:T(8,128)(2,1)S(1)} %collective-permute-done.8.refs_2_, bf16[192,1664]{1,0:T(8,128)(2,1)S(1)} %collective-permute-done.9.refs_3_, ...), custom_call_target="tpu_custom_call" | custom-call | flops 452984832 | bytes 2555904 | tf_op jit(solution)/shard_map/own_half/pallas_call | solution.py:106
  75.3 7.2 %all-to-all-start.2 = ((bf16[8,144,256]{2,1,0:T(8,128)(2,1)}), bf16[8,144,256]{2,1,0:T(8,128)(2,1)S(1)}, u32[]{:S(2)}, u32[]{:S(2)}) async-start(bf16[8,144,256]{2,1,0:T(8,128)(2,1)} %own_half.1), calls=%async_computation.2 | async-start | bytes 1179648 | tf_op jit(solution)/shard_map/all_to_all | solution.py:298
  82.6 1.9 %collective-permute-start.3 = (bf16[12,96,256]{2,1,0:T(8,128)(2,1)}, bf16[12,96,256]{2,1,0:T(8,128)(2,1)}, u32[]{:S(2)}, u32[]{:S(2)}) collective-permute-start(bf16[12,96,256]{2,1,0:T(8,128)(2,1)} %regroup.1.refs_0_), channel_id=1, source_target_pairs={{0,1},{1,0},{2,3},{3,2},{4,5},{5,4},{6,7},{7,6},{8,9},{9,8},{10,11... | collective-permute-start | bytes 1769480 | tf_op jit(solution)/shard_map/ppermute | solution.py:280
  84.5 0.0 collective-permute-done.2.refs_3_
  84.5 2.4 %collective-permute-start.6 = (bf16[12,96,256]{2,1,0:T(8,128)(2,1)S(1)}, bf16[12,96,256]{2,1,0:T(8,128)(2,1)}, u32[]{:S(2)}, u32[]{:S(2)}) collective-permute-start(bf16[12,96,256]{2,1,0:T(8,128)(2,1)S(1)} %collective-permute-done.2.refs_3_), channel_id=1, source_target_pairs={{0,1},{1,0},{2,3},{3,2},{4,5},{5,4},{6,7},{7,6},{8,9},{9,8},{10,11... | collective-permute-start | bytes 1769480 | tf_op jit(solution)/shard_map/ppermute | solution.py:280
  86.9 5.3 %collective-permute-done.1.refs_2_ = bf16[12,96,256]{2,1,0:T(8,128)(2,1)} collective-permute-done((bf16[12,96,256]{2,1,0:T(8,128)(2,1)}, bf16[12,96,256]{2,1,0:T(8,128)(2,1)}, u32[]{:S(2)}, u32[]{:S(2)}) %collective-permute-start.1) | collective-permute-done | bytes 589856 | tf_op jit(solution)/shard_map/ppermute | solution.py:276
  92.2 1.9 %collective-permute-start.5 = (bf16[12,96,256]{2,1,0:T(8,128)(2,1)}, bf16[12,96,256]{2,1,0:T(8,128)(2,1)}, u32[]{:S(2)}, u32[]{:S(2)}) collective-permute-start(bf16[12,96,256]{2,1,0:T(8,128)(2,1)} %collective-permute-done.1.refs_2_), channel_id=1, source_target_pairs={{0,1},{1,0},{2,3},{3,2},{4,5},{5,4},{6,7},{7,6},{8,9},{9,8},{10,11... | collective-permute-start | bytes 1769480 | tf_op jit(solution)/shard_map/ppermute | solution.py:280
  94.1 0.1 collective-permute-done.refs_1_
  94.2 2.3 %collective-permute-start.4 = (bf16[12,96,256]{2,1,0:T(8,128)(2,1)}, bf16[12,96,256]{2,1,0:T(8,128)(2,1)}, u32[]{:S(2)}, u32[]{:S(2)}) collective-permute-start(bf16[12,96,256]{2,1,0:T(8,128)(2,1)} %collective-permute-done.refs_1_), channel_id=1, source_target_pairs={{0,1},{1,0},{2,3},{3,2},{4,5},{5,4},{6,7},{7,6},{8,9},{9,8},{10,11... | collective-permute-start | bytes 1769480 | tf_op jit(solution)/shard_map/ppermute | solution.py:280
  96.6 5.0 %all-to-all-done.2.parts = bf16[8,144,256]{2,1,0:T(8,128)(2,1)S(1)} async-done(((bf16[8,144,256]{2,1,0:T(8,128)(2,1)}), bf16[8,144,256]{2,1,0:T(8,128)(2,1)S(1)}, u32[]{:S(2)}, u32[]{:S(2)}) %all-to-all-start.2) | async-done | bytes 589856 | tf_op jit(solution)/shard_map/all_to_all | solution.py:298
  101.6 0.7 sum_over_y.1
  102.3 9.3 %all-to-all-start.3 = ((bf16[12,12,256]{2,1,0:T(8,128)(2,1)}), bf16[12,12,256]{2,1,0:T(8,128)(2,1)S(1)}, u32[]{:S(2)}, u32[]{:S(2)}) async-start(bf16[12,12,256]{2,1,0:T(8,128)(2,1)} %sum_over_y.1), calls=%async_computation.3 | async-start | bytes 196608 | tf_op jit(solution)/shard_map/all_to_all | solution.py:300
  111.6 0.0 collective-permute-done.3.refs_4_
  111.6 0.0 collective-permute-done.6.refs_7_
  111.7 0.0 collective-permute-done.5.refs_6_
  111.7 0.0 collective-permute-done.4.refs_5_
  111.7 0.0 copy-done
  111.7 0.0 copy-done.2
  111.7 7.1 %project.1 = (bf16[192,512]{1,0:T(8,128)(2,1)}, bf16[192,4608]{1,0:T(8,128)(2,1)}) custom-call(s32[2]{0:T(128)S(1)} %copy-done.5, bf16[12,96,256]{2,1,0:T(8,128)(2,1)} %regroup.1.refs_0_, bf16[12,96,256]{2,1,0:T(8,128)(2,1)} %collective-permute-done.refs_1_, bf16[12,96,256]{2,1,0:T(8,128)(2,1)} %collective-permute-done.1.refs_2_, ...), custom_call_target="tpu_custom_call" | custom-call | flops 1811939328 | bytes 8257536 | tf_op jit(solution)/shard_map/project/pallas_call | solution.py:216
  118.8 4.9 %all-to-all-done.3 = bf16[12,12,256]{2,1,0:T(8,128)(2,1)S(1)} async-done(((bf16[12,12,256]{2,1,0:T(8,128)(2,1)}), bf16[12,12,256]{2,1,0:T(8,128)(2,1)S(1)}, u32[]{:S(2)}, u32[]{:S(2)}) %all-to-all-start.3) | async-done | bytes 73760 | tf_op jit(solution)/shard_map/all_to_all | solution.py:300
  123.7 0.6 broadcast_multiply_fusion
  (6 shorter events, 0.1 us)
Async XLA Ops:
  2.1 29.2 %all-to-all-start = ((bf16[12,12,256]{2,1,0:T(8,128)(2,1)}), bf16[12,12,256]{2,1,0:T(8,128)(2,1)S(1)}, u32[]{:S(2)}, u32[]{:S(2)}) async-start(bf16[12,12,256]{2,1,0:T(8,128)(2,1)} %scaled_copies.1), calls=%async_computation | async-start | bytes 196608 | tf_op jit(solution)/shard_map/all_to_all | solution.py:288
  17.9 37.3 %copy-start.5 = (s32[2]{0:T(128)S(1)}, s32[2]{0:T(128)}, u32[]{:S(2)}) copy-start(s32[2]{0:T(128)} %pad_add_fusion.place) | copy-start | bytes 28
  21.9 33.3 %copy-start.1 = (bf16[192,1664]{1,0:T(8,128)(2,1)S(1)}, bf16[192,1664]{1,0:T(8,128)(2,1)}, u32[]{:S(2)}) copy-start(bf16[192,1664]{1,0:T(8,128)(2,1)} %get-tuple-element.11.refs_0_) | copy-start | bytes 1916932
  21.9 21.1 %collective-permute-start.7 = (bf16[192,1664]{1,0:T(8,128)(2,1)}, bf16[192,1664]{1,0:T(8,128)(2,1)S(1)}, u32[]{:S(2)}, u32[]{:S(2)}) collective-permute-start(bf16[192,1664]{1,0:T(8,128)(2,1)} %get-tuple-element.12), channel_id=1, source_target_pairs={{0,32},{16,48},{32,0},{48,16},{1,33},{17,49},{33,1},{49,17},{2,34}... | collective-permute-start | bytes 1916936 | tf_op jit(solution)/shard_map/ppermute | solution.py:276
  25.3 27.7 %collective-permute-start.8 = (bf16[192,1664]{1,0:T(8,128)(2,1)}, bf16[192,1664]{1,0:T(8,128)(2,1)S(1)}, u32[]{:S(2)}, u32[]{:S(2)}) collective-permute-start(bf16[192,1664]{1,0:T(8,128)(2,1)} %get-tuple-element.13), channel_id=1, source_target_pairs={{0,16},{16,32},{32,48},{48,0},{1,17},{17,33},{33,49},{49,1},{2,18}... | collective-permute-start | bytes 1916936 | tf_op jit(solution)/shard_map/ppermute | solution.py:276
  29.4 25.8 %collective-permute-start.9 = (bf16[192,1664]{1,0:T(8,128)(2,1)}, bf16[192,1664]{1,0:T(8,128)(2,1)S(1)}, u32[]{:S(2)}, u32[]{:S(2)}) collective-permute-start(bf16[192,1664]{1,0:T(8,128)(2,1)} %get-tuple-element.14), channel_id=1, source_target_pairs={{0,48},{16,0},{32,16},{48,32},{1,49},{17,1},{33,17},{49,33},{2,50}... | collective-permute-start | bytes 1916936 | tf_op jit(solution)/shard_map/ppermute | solution.py:276
  32.2 27.1 %all-to-all-start.1 = ((bf16[8,144,256]{2,1,0:T(8,128)(2,1)}), bf16[8,144,256]{2,1,0:T(8,128)(2,1)S(1)}, u32[]{:S(2)}, u32[]{:S(2)}) async-start(bf16[8,144,256]{2,1,0:T(8,128)(2,1)} %broadcast_in_dim.8), calls=%async_computation.1 | async-start | bytes 1179648 | tf_op jit(solution)/shard_map/all_to_all | solution.py:272
  55.2 16.3 %copy-start.3 = (bf16[384,384]{1,0:T(8,128)(2,1)S(1)}, bf16[384,384]{1,0:T(8,128)(2,1)}, u32[]{:S(2)}) copy-start(bf16[384,384]{1,0:T(8,128)(2,1)} %constant.18.clone.refs_5_) | copy-start | bytes 884740
  57.4 14.1 %collective-permute-start.10 = (bf16[256,1152]{1,0:T(8,128)(2,1)}, bf16[256,1152]{1,0:T(8,128)(2,1)}, u32[]{:S(2)}, u32[]{:S(2)}) collective-permute-start(bf16[256,1152]{1,0:T(8,128)(2,1)} %other_half.1), channel_id=1, source_target_pairs={{0,1},{1,0},{2,3},{3,2},{4,5},{5,4},{6,7},{7,6},{8,9},{9,8},{10,11... | collective-permute-start | bytes 1769480 | tf_op jit(solution)/shard_map/ppermute | solution.py:280
  59.3 1.0 copy-start.4
  62.2 22.3 %collective-permute-start.2 = (bf16[12,96,256]{2,1,0:T(8,128)(2,1)}, bf16[12,96,256]{2,1,0:T(8,128)(2,1)S(1)}, u32[]{:S(2)}, u32[]{:S(2)}) collective-permute-start(bf16[12,96,256]{2,1,0:T(8,128)(2,1)} %regroup.1.refs_0_), channel_id=1, source_target_pairs={{0,32},{16,48},{32,0},{48,16},{1,33},{17,49},{33,1},{49,17},{2,34}... | collective-permute-start | bytes 1769480 | tf_op jit(solution)/shard_map/ppermute | solution.py:276
  65.6 26.7 %collective-permute-start.1 = (bf16[12,96,256]{2,1,0:T(8,128)(2,1)}, bf16[12,96,256]{2,1,0:T(8,128)(2,1)}, u32[]{:S(2)}, u32[]{:S(2)}) collective-permute-start(bf16[12,96,256]{2,1,0:T(8,128)(2,1)} %regroup.1.refs_0_), channel_id=1, source_target_pairs={{0,16},{16,32},{32,48},{48,0},{1,17},{17,33},{33,49},{49,1},{2,18}... | collective-permute-start | bytes 1769480 | tf_op jit(solution)/shard_map/ppermute | solution.py:276
  69.5 24.7 %collective-permute-start = (bf16[12,96,256]{2,1,0:T(8,128)(2,1)}, bf16[12,96,256]{2,1,0:T(8,128)(2,1)}, u32[]{:S(2)}, u32[]{:S(2)}) collective-permute-start(bf16[12,96,256]{2,1,0:T(8,128)(2,1)} %regroup.1.refs_0_), channel_id=1, source_target_pairs={{0,48},{16,0},{32,16},{48,32},{1,49},{17,1},{33,17},{49,33},{2,50}... | collective-permute-start | bytes 1769480 | tf_op jit(solution)/shard_map/ppermute | solution.py:276
  75.3 36.3 %copy-start = (bf16[192,4608]{1,0:T(8,128)(2,1)S(1)}, bf16[192,4608]{1,0:T(8,128)(2,1)}, u32[]{:S(2)}) copy-start(bf16[192,4608]{1,0:T(8,128)(2,1)} %hidden.1) | copy-start | bytes 5308420
  75.3 36.4 %copy-start.2 = (bf16[192,512]{1,0:T(8,128)(2,1)S(1)}, bf16[192,512]{1,0:T(8,128)(2,1)}, u32[]{:S(2)}) copy-start(bf16[192,512]{1,0:T(8,128)(2,1)} %cot.1) | copy-start | bytes 589828
  75.3 26.2 %all-to-all-start.2 = ((bf16[8,144,256]{2,1,0:T(8,128)(2,1)}), bf16[8,144,256]{2,1,0:T(8,128)(2,1)S(1)}, u32[]{:S(2)}, u32[]{:S(2)}) async-start(bf16[8,144,256]{2,1,0:T(8,128)(2,1)} %own_half.1), calls=%async_computation.2 | async-start | bytes 1179648 | tf_op jit(solution)/shard_map/all_to_all | solution.py:298
  82.6 29.1 %collective-permute-start.3 = (bf16[12,96,256]{2,1,0:T(8,128)(2,1)}, bf16[12,96,256]{2,1,0:T(8,128)(2,1)}, u32[]{:S(2)}, u32[]{:S(2)}) collective-permute-start(bf16[12,96,256]{2,1,0:T(8,128)(2,1)} %regroup.1.refs_0_), channel_id=1, source_target_pairs={{0,1},{1,0},{2,3},{3,2},{4,5},{5,4},{6,7},{7,6},{8,9},{9,8},{10,11... | collective-permute-start | bytes 1769480 | tf_op jit(solution)/shard_map/ppermute | solution.py:280
  84.5 27.2 %collective-permute-start.6 = (bf16[12,96,256]{2,1,0:T(8,128)(2,1)S(1)}, bf16[12,96,256]{2,1,0:T(8,128)(2,1)}, u32[]{:S(2)}, u32[]{:S(2)}) collective-permute-start(bf16[12,96,256]{2,1,0:T(8,128)(2,1)S(1)} %collective-permute-done.2.refs_3_), channel_id=1, source_target_pairs={{0,1},{1,0},{2,3},{3,2},{4,5},{5,4},{6,7},{7,6},{8,9},{9,8},{10,11... | collective-permute-start | bytes 1769480 | tf_op jit(solution)/shard_map/ppermute | solution.py:280
  92.2 19.4 %collective-permute-start.5 = (bf16[12,96,256]{2,1,0:T(8,128)(2,1)}, bf16[12,96,256]{2,1,0:T(8,128)(2,1)}, u32[]{:S(2)}, u32[]{:S(2)}) collective-permute-start(bf16[12,96,256]{2,1,0:T(8,128)(2,1)} %collective-permute-done.1.refs_2_), channel_id=1, source_target_pairs={{0,1},{1,0},{2,3},{3,2},{4,5},{5,4},{6,7},{7,6},{8,9},{9,8},{10,11... | collective-permute-start | bytes 1769480 | tf_op jit(solution)/shard_map/ppermute | solution.py:280
  94.2 17.4 %collective-permute-start.4 = (bf16[12,96,256]{2,1,0:T(8,128)(2,1)}, bf16[12,96,256]{2,1,0:T(8,128)(2,1)}, u32[]{:S(2)}, u32[]{:S(2)}) collective-permute-start(bf16[12,96,256]{2,1,0:T(8,128)(2,1)} %collective-permute-done.refs_1_), channel_id=1, source_target_pairs={{0,1},{1,0},{2,3},{3,2},{4,5},{5,4},{6,7},{7,6},{8,9},{9,8},{10,11... | collective-permute-start | bytes 1769480 | tf_op jit(solution)/shard_map/ppermute | solution.py:280
  102.3 21.4 %all-to-all-start.3 = ((bf16[12,12,256]{2,1,0:T(8,128)(2,1)}), bf16[12,12,256]{2,1,0:T(8,128)(2,1)S(1)}, u32[]{:S(2)}, u32[]{:S(2)}) async-start(bf16[12,12,256]{2,1,0:T(8,128)(2,1)} %sum_over_y.1), calls=%async_computation.3 | async-start | bytes 196608 | tf_op jit(solution)/shard_map/all_to_all | solution.py:300

commit v9 on v7

--- a/solution.py
+++ b/solution.py
@@ -1,3 +1,4 @@
+import functools
 import math
 
 import jax
@@ -32,25 +33,28 @@
 ZSTEP = 3
 
 
-def pack_kernel(place, hidden, cot, *rest):
-    *outs, cut = rest
-    for g in range(NZ // ZG):
-        for x in range(NX):
-            starts = [z * ZROWS + x * XROWS for z in range(g * ZG, (g + 1) * ZG)]
-            cut[x, :, g * ZG * XROWS : (g + 1) * ZG * XROWS] = jnp.concatenate(
-                [hidden[:, start : start + XROWS] for start in starts], axis=1
-            )
-    for r in range(NX):
-        outs[r][:, :WIDE] = cut[lax.rem(place[1] + r, NX)]
-        outs[r][:, WIDE:] = cot[...]
-
-
-def pack(place, hidden, cotangent):
+def pack_kernel(shifts, place, hidden, cot, *outs):
+    for me in range(NX):
+
+        @pl.when(place[1] == me)
+        def _():
+            for out, r in zip(outs, shifts):
+                x = (me + r) % NX
+                for g in range(NZ // ZG):
+                    starts = [z * ZROWS + x * XROWS for z in range(g * ZG, (g + 1) * ZG)]
+                    out[:, g * ZG * XROWS : (g + 1) * ZG * XROWS] = jnp.concatenate(
+                        [hidden[:, start : start + XROWS] for start in starts], axis=1
+                    )
+
+    for out in outs:
+        out[:, WIDE:] = cot[...]
+
+
+def pack(place, hidden, cotangent, shifts):
     tokens, width = hidden.shape
     step = tokens // 2
-    whole = pl.BlockSpec((step, WIDE + 2 * HALF), lambda k, place: (k, 0))
-    return pl.pallas_call(
-        pack_kernel,
+    return pl.pallas_call(
+        functools.partial(pack_kernel, shifts),
         grid_spec=pltpu.PrefetchScalarGridSpec(
             num_scalar_prefetch=1,
             grid=(2,),
@@ -58,10 +62,9 @@
                 pl.BlockSpec((step, width), lambda k, place: (k, 0)),
                 pl.BlockSpec((step, 2 * HALF), lambda k, place: (k, 0)),
             ],
-            out_specs=[whole] * NX,
-            scratch_shapes=[pltpu.VMEM((NX, step, WIDE), BF)],
-        ),
-        out_shape=[jax.ShapeDtypeStruct((tokens, WIDE + 2 * HALF), BF)] * NX,
+            out_specs=[pl.BlockSpec((step, WIDE + 2 * HALF), lambda k, place: (k, 0))] * len(shifts),
+        ),
+        out_shape=[jax.ShapeDtypeStruct((tokens, WIDE + 2 * HALF), BF)] * len(shifts),
         compiler_params=pltpu.CompilerParams(vmem_limit_bytes=56 * 2**20),
         cost_estimate=pl.CostEstimate(
             flops=tokens * width, bytes_accessed=4 * tokens * width, transcendentals=0
@@ -284,14 +287,18 @@
     place = jnp.stack([lax.axis_index("c"), lax.axis_index("x")]).astype(jnp.int32)
     factor = 1.0 / math.sqrt(hidden.shape[0] * NZ * NX * NY * NC)
 
-    packed = pack(place, hidden, cotangent)
-    held = [packed[0]] + [shift(packed[r], r) for r in (2, 1, 3)]
+    kept, far = pack(place, hidden, cotangent, (0, 2))
+
+    values, _ = lax.optimization_barrier((quant_weight, far))
+    copies = scaled_copies(values, scales)
+    w_z = lax.all_to_all(copies, "z", split_axis=0, concat_axis=0, tiled=True)
+    late, _ = lax.optimization_barrier((hidden, copies))
+    near = pack(place, late, cotangent, (1, 3))
+    w_z, near = lax.optimization_barrier((w_z, near))
+    held = [kept, shift(far, 2), shift(near[0], 1), shift(near[1], 3)]
     ahead = other_half(place, held)
     term = own_half(place, held, swap(ahead))
 
-    values, _ = lax.optimization_barrier((quant_weight, packed[0]))
-    copies = scaled_copies(values, scales)
-    w_z = lax.all_to_all(copies, "z", split_axis=0, concat_axis=0, tiled=True)
     w_y = to_all(w_z.reshape(NZ * ROWS, HALF), Y, NY)
 
     own = regroup(lax.optimization_barrier((w_y, term))[0])

time: 121 us -> 123 us (1.017)
  blocking collectives: 19.9 us -> 0 us
  starting transfers between devices: 50.1 us -> 66.9 us
  waiting for transfers between devices: 24.7 us -> 30.6 us
    all_to_all x1 -> x0, blocking collectives: 19.9 us -> none  [on_device(): w_z = lax.all_to_all(copies, 'z', split_axis=0, concat_axis=0, tiled=True)]
    all_to_all x0 -> x1, starting transfers between devices: none -> 15.2 us  [on_device(): w_z = lax.all_to_all(copies, 'z', split_axis=0, concat_axis=0, tiled=True)]
    ppermute x6, starting transfers between devices: 25.7 us -> 18.5 us  [shift(): return lax.ppermute(piece, 'x', [(k, (k + r) % NX) for k in range(NX)])]
    all_to_all x1, starting transfers between devices: 3.51 us -> 9.31 us  [on_device(): t_z = lax.all_to_all(sum_y, 'z', split_axis=0, concat_axis=0, tiled=True)]
    all_to_all x1, waiting for transfers between devices: 6.09 us -> 0.38 us  [to_all(): return lax.all_to_all(copies, axis, split_axis=0, concat_axis=0, tiled=True)]
    all_to_all x0 -> x1, waiting for transfers between devices: none -> 5.24 us  [on_device(): w_z = lax.all_to_all(copies, 'z', split_axis=0, concat_axis=0, tiled=True)]
    ppermute x6, waiting for transfers between devices: 11.7 us -> 16.8 us  [shift(): return lax.ppermute(piece, 'x', [(k, (k + r) % NX) for k in range(NX)])]
    all_to_all x1, starting transfers between devices: 3.55 us -> 6.77 us  [on_device(): t_y = lax.all_to_all(term, Y, split_axis=0, concat_axis=0, tiled=True)]
  transfers between devices with their start and end apart: 14 -> 15, of which waited for: 5 -> 10; matrix products, arithmetic and copies ran while one was open for 1% -> 1% of each run, Pallas kernels for 13% -> 13%
where the time goes in v9:
time: 123 us; the launch traced here: 121 us
  starting transfers between devices  66.9 us (54%)
  waiting for transfers between devices  30.6 us (25%)
  Pallas kernels  20.8 us (17%)
  other arithmetic  1.24 us (1%)
    ppermute x6, starting transfers between devices, shift(): return lax.ppermute(piece, 'x', [(k, (k + r) % NX) for k in range(NX)])  18.5 us
    ppermute x6, waiting for transfers between devices, shift(): return lax.ppermute(piece, 'x', [(k, (k + r) % NX) for k in range(NX)])  16.8 us
    all_to_all x1, starting transfers between devices, on_device(): w_z = lax.all_to_all(copies, 'z', split_axis=0, concat_axis=0, tiled=True)  15.2 us
    ppermute x5, starting transfers between devices, swap(): return lax.ppermute(piece, 'c', [(0, 1), (1, 0)])  10 us
    all_to_all x1, starting transfers between devices, on_device(): t_z = lax.all_to_all(sum_y, 'z', split_axis=0, concat_axis=0, tiled=True)  9.31 us
    pallas_call x1, Pallas kernels, project(): pl.pallas_call(project_kernel, grid_spec=pltpu.PrefetchScalarGridSpec(num...  7.11 us
    all_to_all x1, starting transfers between devices, to_all(): return lax.all_to_all(copies, axis, split_axis=0, concat_axis=0, tiled=True)  7.1 us
    all_to_all x1, starting transfers between devices, on_device(): t_y = lax.all_to_all(term, Y, split_axis=0, concat_axis=0, tiled=True)  6.77 us
  transfers between devices with their start and end apart: 15, of which 10 were waited for; matrix products, arithmetic and copies ran while one was open for 1% of the time, Pallas kernels for 13%

profile of v9, /device:TPU:6, one launch (start us, length us, event | category | flops | bytes accessed | tf_op | source)
XLA Modules:
  0.0 121.3 jit_solution(13532076496174685254)
XLA Ops:
  0.6 0.6 pad_add_fusion.place
  1.2 3.2 %pack.2 = (bf16[192,1664]{1,0:T(8,128)(2,1)}, bf16[192,1664]{1,0:T(8,128)(2,1)}) custom-call(s32[2]{0:T(128)} %pad_add_fusion.place, bf16[192,4608]{1,0:T(8,128)(2,1)} %refs_8_.1, bf16[192,512]{1,0:T(8,128)(2,1)} %refs_10_.1), custom_call_target="tpu_custom_call" | custom-call | flops 884736 | bytes 3538944 | tf_op jit(solution)/shard_map/pack/pallas_call | solution.py:56
  4.5 1.4 %scaled_copies.1 = bf16[12,12,256]{2,1,0:T(8,128)(2,1)} custom-call(bf16[12,256]{1,0:T(8,128)(2,1)} %values, bf16[1,12]{1,0:T(2,128)(2,1)} %bitcast.3), custom_call_target="tpu_custom_call" | custom-call | tf_op jit(solution)/shard_map/scaled_copies/pallas_call | solution.py:265
  5.9 15.2 %all-to-all-start = ((bf16[12,12,256]{2,1,0:T(8,128)(2,1)}), bf16[12,12,256]{2,1,0:T(8,128)(2,1)S(1)}, u32[]{:S(2)}, u32[]{:S(2)}) async-start(bf16[12,12,256]{2,1,0:T(8,128)(2,1)} %scaled_copies.1), calls=%async_computation | async-start | bytes 196608 | tf_op jit(solution)/shard_map/all_to_all | solution.py:294
  21.1 0.0 copy-start.2
  21.1 0.0 copy-start.5
  21.1 3.5 %collective-permute-start = (bf16[192,1664]{1,0:T(8,128)(2,1)}, bf16[192,1664]{1,0:T(8,128)(2,1)S(1)}, u32[]{:S(2)}, u32[]{:S(2)}) collective-permute-start(bf16[192,1664]{1,0:T(8,128)(2,1)} %get-tuple-element.15), channel_id=1, source_target_pairs={{0,32},{16,48},{32,0},{48,16},{1,33},{17,49},{33,1},{49,17},{2,34}... | collective-permute-start | bytes 1916936 | tf_op jit(solution)/shard_map/ppermute | solution.py:279
  24.5 3.2 %pack.3 = (bf16[192,1664]{1,0:T(8,128)(2,1)}, bf16[192,1664]{1,0:T(8,128)(2,1)}) custom-call(s32[2]{0:T(128)} %pad_add_fusion.place, bf16[192,4608]{1,0:T(8,128)(2,1)} %refs_8_.1, bf16[192,512]{1,0:T(8,128)(2,1)} %refs_10_.1), custom_call_target="tpu_custom_call" | custom-call | flops 884736 | bytes 3538944 | tf_op jit(solution)/shard_map/pack/pallas_call | solution.py:56
  27.8 5.2 %all-to-all-done = bf16[12,12,256]{2,1,0:T(8,128)(2,1)S(1)} async-done(((bf16[12,12,256]{2,1,0:T(8,128)(2,1)}), bf16[12,12,256]{2,1,0:T(8,128)(2,1)S(1)}, u32[]{:S(2)}, u32[]{:S(2)}) %all-to-all-start) | async-done | bytes 73760 | tf_op jit(solution)/shard_map/all_to_all | solution.py:294
  33.0 2.4 %collective-permute-start.1 = (bf16[192,1664]{1,0:T(8,128)(2,1)}, bf16[192,1664]{1,0:T(8,128)(2,1)S(1)}, u32[]{:S(2)}, u32[]{:S(2)}) collective-permute-start(bf16[192,1664]{1,0:T(8,128)(2,1)} %get-tuple-element.22), channel_id=1, source_target_pairs={{0,16},{16,32},{32,48},{48,0},{1,17},{17,33},{33,49},{49,1},{2,18}... | collective-permute-start | bytes 1916936 | tf_op jit(solution)/shard_map/ppermute | solution.py:279
  35.4 3.4 %collective-permute-start.2 = (bf16[192,1664]{1,0:T(8,128)(2,1)}, bf16[192,1664]{1,0:T(8,128)(2,1)S(1)}, u32[]{:S(2)}, u32[]{:S(2)}) collective-permute-start(bf16[192,1664]{1,0:T(8,128)(2,1)} %get-tuple-element.23), channel_id=1, source_target_pairs={{0,48},{16,0},{32,16},{48,32},{1,49},{17,1},{33,17},{49,33},{2,50}... | collective-permute-start | bytes 1916936 | tf_op jit(solution)/shard_map/ppermute | solution.py:279
  38.9 0.9 broadcast_in_dim.8
  39.8 7.1 %all-to-all-start.1 = ((bf16[8,144,256]{2,1,0:T(8,128)(2,1)}), bf16[8,144,256]{2,1,0:T(8,128)(2,1)S(1)}, u32[]{:S(2)}, u32[]{:S(2)}) async-start(bf16[8,144,256]{2,1,0:T(8,128)(2,1)} %broadcast_in_dim.8), calls=%async_computation.1 | async-start | bytes 1179648 | tf_op jit(solution)/shard_map/all_to_all | solution.py:275
  46.9 0.0 collective-permute-done.refs_1_
  46.9 5.3 %collective-permute-done.1.refs_2_ = bf16[192,1664]{1,0:T(8,128)(2,1)S(1)} collective-permute-done((bf16[192,1664]{1,0:T(8,128)(2,1)}, bf16[192,1664]{1,0:T(8,128)(2,1)S(1)}, u32[]{:S(2)}, u32[]{:S(2)}) %collective-permute-start.1) | collective-permute-done | bytes 639008 | tf_op jit(solution)/shard_map/ppermute | solution.py:279
  52.2 2.1 %collective-permute-done.2.refs_3_ = bf16[192,1664]{1,0:T(8,128)(2,1)S(1)} collective-permute-done((bf16[192,1664]{1,0:T(8,128)(2,1)}, bf16[192,1664]{1,0:T(8,128)(2,1)S(1)}, u32[]{:S(2)}, u32[]{:S(2)}) %collective-permute-start.2) | collective-permute-done | bytes 639008 | tf_op jit(solution)/shard_map/ppermute | solution.py:279
  54.4 0.0 copy-done.2
  54.4 0.0 copy-done.5
  54.4 1.4 %other_half.1 = bf16[256,1152]{1,0:T(8,128)(2,1)S(1)} custom-call(s32[2]{0:T(128)S(1)} %copy-done.5, bf16[192,1664]{1,0:T(8,128)(2,1)S(1)} %copy-done.2, bf16[192,1664]{1,0:T(8,128)(2,1)S(1)} %collective-permute-done.refs_1_, bf16[192,1664]{1,0:T(8,128)(2,1)S(1)} %collective-permute-done.1.refs_2_, bf16[192,1664]{1,0:T(8,128)(2,1)S(1)} %collective-permute-done.2.refs_3_), custom_call_target="tpu_custom_call" | custom-call | flops 45298483200 | bytes 2555904 | tf_op jit(solution)/shard_map/other_half/pallas_call | solution.py:109
  55.7 0.0 copy-start.4
  55.8 2.1 %collective-permute-start.3 = (bf16[256,1152]{1,0:T(8,128)(2,1)S(1)}, bf16[256,1152]{1,0:T(8,128)(2,1)S(1)}, u32[]{:S(2)}, u32[]{:S(2)}) collective-permute-start(bf16[256,1152]{1,0:T(8,128)(2,1)S(1)} %other_half.1), channel_id=1, source_target_pairs={{0,1},{1,0},{2,3},{3,2},{4,5},{5,4},{6,7},{7,6},{8,9},{9,8},{10,11... | collective-permute-start | bytes 1769480 | tf_op jit(solution)/shard_map/ppermute | solution.py:283
  57.8 2.0 %collective-permute-done.3.refs_4_ = bf16[256,1152]{1,0:T(8,128)(2,1)S(1)} collective-permute-done((bf16[256,1152]{1,0:T(8,128)(2,1)S(1)}, bf16[256,1152]{1,0:T(8,128)(2,1)S(1)}, u32[]{:S(2)}, u32[]{:S(2)}) %collective-permute-start.3) | collective-permute-done | bytes 589856 | tf_op jit(solution)/shard_map/ppermute | solution.py:283
  59.8 0.0 copy-done.3
  59.8 2.8 %own_half.1 = bf16[8,144,256]{2,1,0:T(8,128)(2,1)} custom-call(s32[2]{0:T(128)S(1)} %copy-done.5, bf16[192,1664]{1,0:T(8,128)(2,1)S(1)} %copy-done.2, bf16[192,1664]{1,0:T(8,128)(2,1)S(1)} %collective-permute-done.refs_1_, bf16[192,1664]{1,0:T(8,128)(2,1)S(1)} %collective-permute-done.1.refs_2_, bf16[192,1664]{1,0:T(8,128)(2,1)S(1)} %collective-permute-done.2.refs_3_, ...), custom_call_target="tpu_custom_call" | custom-call | flops 452984832 | bytes 2555904 | tf_op jit(solution)/shard_map/own_half/pallas_call | solution.py:109
  62.6 0.4 all-to-all-done.1.parts
  63.0 0.0 copy-done.4
  63.0 0.9 regroup.1.refs_0_
  63.9 3.3 %collective-permute-start.6 = (bf16[12,96,256]{2,1,0:T(8,128)(2,1)S(1)}, bf16[12,96,256]{2,1,0:T(8,128)(2,1)}, u32[]{:S(2)}, u32[]{:S(2)}) collective-permute-start(bf16[12,96,256]{2,1,0:T(8,128)(2,1)S(1)} %regroup.1.refs_0_), channel_id=1, source_target_pairs={{0,32},{16,48},{32,0},{48,16},{1,33},{17,49},{33,1},{49,17},{2,34}... | collective-permute-start | bytes 1769480 | tf_op jit(solution)/shard_map/ppermute | solution.py:279
  67.2 4.0 %collective-permute-start.5 = (bf16[12,96,256]{2,1,0:T(8,128)(2,1)S(1)}, bf16[12,96,256]{2,1,0:T(8,128)(2,1)}, u32[]{:S(2)}, u32[]{:S(2)}) collective-permute-start(bf16[12,96,256]{2,1,0:T(8,128)(2,1)S(1)} %regroup.1.refs_0_), channel_id=1, source_target_pairs={{0,16},{16,32},{32,48},{48,0},{1,17},{17,33},{33,49},{49,1},{2,18}... | collective-permute-start | bytes 1769480 | tf_op jit(solution)/shard_map/ppermute | solution.py:279
  71.2 1.9 %collective-permute-start.4 = (bf16[12,96,256]{2,1,0:T(8,128)(2,1)S(1)}, bf16[12,96,256]{2,1,0:T(8,128)(2,1)}, u32[]{:S(2)}, u32[]{:S(2)}) collective-permute-start(bf16[12,96,256]{2,1,0:T(8,128)(2,1)S(1)} %regroup.1.refs_0_), channel_id=1, source_target_pairs={{0,48},{16,0},{32,16},{48,32},{1,49},{17,1},{33,17},{49,33},{2,50}... | collective-permute-start | bytes 1769480 | tf_op jit(solution)/shard_map/ppermute | solution.py:279
  73.1 6.8 %all-to-all-start.2 = ((bf16[8,144,256]{2,1,0:T(8,128)(2,1)}), bf16[8,144,256]{2,1,0:T(8,128)(2,1)S(1)}, u32[]{:S(2)}, u32[]{:S(2)}) async-start(bf16[8,144,256]{2,1,0:T(8,128)(2,1)} %own_half.1), calls=%async_computation.2 | async-start | bytes 1179648 | tf_op jit(solution)/shard_map/all_to_all | solution.py:308
  79.9 1.9 %collective-permute-start.7 = (bf16[12,96,256]{2,1,0:T(8,128)(2,1)S(1)}, bf16[12,96,256]{2,1,0:T(8,128)(2,1)}, u32[]{:S(2)}, u32[]{:S(2)}) collective-permute-start(bf16[12,96,256]{2,1,0:T(8,128)(2,1)S(1)} %regroup.1.refs_0_), channel_id=1, source_target_pairs={{0,1},{1,0},{2,3},{3,2},{4,5},{5,4},{6,7},{7,6},{8,9},{9,8},{10,11... | collective-permute-start | bytes 1769480 | tf_op jit(solution)/shard_map/ppermute | solution.py:283
  81.8 1.8 %collective-permute-done.6.refs_3_ = bf16[12,96,256]{2,1,0:T(8,128)(2,1)} collective-permute-done((bf16[12,96,256]{2,1,0:T(8,128)(2,1)S(1)}, bf16[12,96,256]{2,1,0:T(8,128)(2,1)}, u32[]{:S(2)}, u32[]{:S(2)}) %collective-permute-start.6) | collective-permute-done | bytes 589856 | tf_op jit(solution)/shard_map/ppermute | solution.py:279
  83.6 1.9 %collective-permute-start.10 = (bf16[12,96,256]{2,1,0:T(8,128)(2,1)}, bf16[12,96,256]{2,1,0:T(8,128)(2,1)}, u32[]{:S(2)}, u32[]{:S(2)}) collective-permute-start(bf16[12,96,256]{2,1,0:T(8,128)(2,1)} %collective-permute-done.6.refs_3_), channel_id=1, source_target_pairs={{0,1},{1,0},{2,3},{3,2},{4,5},{5,4},{6,7},{7,6},{8,9},{9,8},{10,11... | collective-permute-start | bytes 1769480 | tf_op jit(solution)/shard_map/ppermute | solution.py:283
  85.6 7.4 %collective-permute-done.5.refs_2_ = bf16[12,96,256]{2,1,0:T(8,128)(2,1)} collective-permute-done((bf16[12,96,256]{2,1,0:T(8,128)(2,1)S(1)}, bf16[12,96,256]{2,1,0:T(8,128)(2,1)}, u32[]{:S(2)}, u32[]{:S(2)}) %collective-permute-start.5) | collective-permute-done | bytes 589856 | tf_op jit(solution)/shard_map/ppermute | solution.py:279
  92.9 1.9 %collective-permute-start.9 = (bf16[12,96,256]{2,1,0:T(8,128)(2,1)}, bf16[12,96,256]{2,1,0:T(8,128)(2,1)}, u32[]{:S(2)}, u32[]{:S(2)}) collective-permute-start(bf16[12,96,256]{2,1,0:T(8,128)(2,1)} %collective-permute-done.5.refs_2_), channel_id=1, source_target_pairs={{0,1},{1,0},{2,3},{3,2},{4,5},{5,4},{6,7},{7,6},{8,9},{9,8},{10,11... | collective-permute-start | bytes 1769480 | tf_op jit(solution)/shard_map/ppermute | solution.py:283
  94.9 0.2 collective-permute-done.4.refs_1_
  95.0 2.3 %collective-permute-start.8 = (bf16[12,96,256]{2,1,0:T(8,128)(2,1)}, bf16[12,96,256]{2,1,0:T(8,128)(2,1)}, u32[]{:S(2)}, u32[]{:S(2)}) collective-permute-start(bf16[12,96,256]{2,1,0:T(8,128)(2,1)} %collective-permute-done.4.refs_1_), channel_id=1, source_target_pairs={{0,1},{1,0},{2,3},{3,2},{4,5},{5,4},{6,7},{7,6},{8,9},{9,8},{10,11... | collective-permute-start | bytes 1769480 | tf_op jit(solution)/shard_map/ppermute | solution.py:283
  97.3 1.3 %all-to-all-done.2.parts = bf16[8,144,256]{2,1,0:T(8,128)(2,1)S(1)} async-done(((bf16[8,144,256]{2,1,0:T(8,128)(2,1)}), bf16[8,144,256]{2,1,0:T(8,128)(2,1)S(1)}, u32[]{:S(2)}, u32[]{:S(2)}) %all-to-all-start.2) | async-done | bytes 589856 | tf_op jit(solution)/shard_map/all_to_all | solution.py:308
  98.5 0.7 sum_over_y.1
  99.3 9.3 %all-to-all-start.3 = ((bf16[12,12,256]{2,1,0:T(8,128)(2,1)}), bf16[12,12,256]{2,1,0:T(8,128)(2,1)S(1)}, u32[]{:S(2)}, u32[]{:S(2)}) async-start(bf16[12,12,256]{2,1,0:T(8,128)(2,1)} %sum_over_y.1), calls=%async_computation.3 | async-start | bytes 196608 | tf_op jit(solution)/shard_map/all_to_all | solution.py:310
  108.6 0.0 collective-permute-done.7.refs_4_
  108.6 0.0 collective-permute-done.10.refs_7_
  108.6 0.0 collective-permute-done.9.refs_6_
  108.6 0.0 collective-permute-done.8.refs_5_
  108.6 7.1 %project.1 = (bf16[192,512]{1,0:T(8,128)(2,1)}, bf16[192,4608]{1,0:T(8,128)(2,1)}) custom-call(s32[2]{0:T(128)S(1)} %copy-done.5, bf16[12,96,256]{2,1,0:T(8,128)(2,1)S(1)} %regroup.1.refs_0_, bf16[12,96,256]{2,1,0:T(8,128)(2,1)} %collective-permute-done.4.refs_1_, bf16[12,96,256]{2,1,0:T(8,128)(2,1)} %collective-permute-done.5.refs_2_, ...), custom_call_target="tpu_custom_call" | custom-call | flops 1811939328 | bytes 8257536 | tf_op jit(solution)/shard_map/project/pallas_call | solution.py:219
  115.8 4.9 %all-to-all-done.3 = bf16[12,12,256]{2,1,0:T(8,128)(2,1)S(1)} async-done(((bf16[12,12,256]{2,1,0:T(8,128)(2,1)}), bf16[12,12,256]{2,1,0:T(8,128)(2,1)S(1)}, u32[]{:S(2)}, u32[]{:S(2)}) %all-to-all-start.3) | async-done | bytes 73760 | tf_op jit(solution)/shard_map/all_to_all | solution.py:310
  120.7 0.6 broadcast_multiply_fusion
  (7 shorter events, 0.1 us)
Async XLA Ops:
  5.9 27.1 %all-to-all-start = ((bf16[12,12,256]{2,1,0:T(8,128)(2,1)}), bf16[12,12,256]{2,1,0:T(8,128)(2,1)S(1)}, u32[]{:S(2)}, u32[]{:S(2)}) async-start(bf16[12,12,256]{2,1,0:T(8,128)(2,1)} %scaled_copies.1), calls=%async_computation | async-start | bytes 196608 | tf_op jit(solution)/shard_map/all_to_all | solution.py:294
  21.1 33.3 %copy-start.2 = (bf16[192,1664]{1,0:T(8,128)(2,1)S(1)}, bf16[192,1664]{1,0:T(8,128)(2,1)}, u32[]{:S(2)}) copy-start(bf16[192,1664]{1,0:T(8,128)(2,1)} %get-tuple-element.21.refs_0_) | copy-start | bytes 1916932
  21.1 33.3 %copy-start.5 = (s32[2]{0:T(128)S(1)}, s32[2]{0:T(128)}, u32[]{:S(2)}) copy-start(s32[2]{0:T(128)} %pad_add_fusion.place) | copy-start | bytes 28
  21.1 25.8 %collective-permute-start = (bf16[192,1664]{1,0:T(8,128)(2,1)}, bf16[192,1664]{1,0:T(8,128)(2,1)S(1)}, u32[]{:S(2)}, u32[]{:S(2)}) collective-permute-start(bf16[192,1664]{1,0:T(8,128)(2,1)} %get-tuple-element.15), channel_id=1, source_target_pairs={{0,32},{16,48},{32,0},{48,16},{1,33},{17,49},{33,1},{49,17},{2,34}... | collective-permute-start | bytes 1916936 | tf_op jit(solution)/shard_map/ppermute | solution.py:279
  33.0 19.2 %collective-permute-start.1 = (bf16[192,1664]{1,0:T(8,128)(2,1)}, bf16[192,1664]{1,0:T(8,128)(2,1)S(1)}, u32[]{:S(2)}, u32[]{:S(2)}) collective-permute-start(bf16[192,1664]{1,0:T(8,128)(2,1)} %get-tuple-element.22), channel_id=1, source_target_pairs={{0,16},{16,32},{32,48},{48,0},{1,17},{17,33},{33,49},{49,1},{2,18}... | collective-permute-start | bytes 1916936 | tf_op jit(solution)/shard_map/ppermute | solution.py:279
  35.4 18.9 %collective-permute-start.2 = (bf16[192,1664]{1,0:T(8,128)(2,1)}, bf16[192,1664]{1,0:T(8,128)(2,1)S(1)}, u32[]{:S(2)}, u32[]{:S(2)}) collective-permute-start(bf16[192,1664]{1,0:T(8,128)(2,1)} %get-tuple-element.23), channel_id=1, source_target_pairs={{0,48},{16,0},{32,16},{48,32},{1,49},{17,1},{33,17},{49,33},{2,50}... | collective-permute-start | bytes 1916936 | tf_op jit(solution)/shard_map/ppermute | solution.py:279
  39.8 23.2 %all-to-all-start.1 = ((bf16[8,144,256]{2,1,0:T(8,128)(2,1)}), bf16[8,144,256]{2,1,0:T(8,128)(2,1)S(1)}, u32[]{:S(2)}, u32[]{:S(2)}) async-start(bf16[8,144,256]{2,1,0:T(8,128)(2,1)} %broadcast_in_dim.8), calls=%async_computation.1 | async-start | bytes 1179648 | tf_op jit(solution)/shard_map/all_to_all | solution.py:275
  54.4 5.4 %copy-start.3 = (bf16[384,384]{1,0:T(8,128)(2,1)S(1)}, bf16[384,384]{1,0:T(8,128)(2,1)}, u32[]{:S(2)}) copy-start(bf16[384,384]{1,0:T(8,128)(2,1)} %constant.18.clone.refs_5_) | copy-start | bytes 884740
  55.7 7.2 %copy-start.4 = (bf16[384,384]{1,0:T(8,128)(2,1)S(1)}, bf16[384,384]{1,0:T(8,128)(2,1)}, u32[]{:S(2)}) copy-start(bf16[384,384]{1,0:T(8,128)(2,1)} %constant.19.clone.perm) | copy-start | bytes 884740
  55.8 4.0 %collective-permute-start.3 = (bf16[256,1152]{1,0:T(8,128)(2,1)S(1)}, bf16[256,1152]{1,0:T(8,128)(2,1)S(1)}, u32[]{:S(2)}, u32[]{:S(2)}) collective-permute-start(bf16[256,1152]{1,0:T(8,128)(2,1)S(1)} %other_half.1), channel_id=1, source_target_pairs={{0,1},{1,0},{2,3},{3,2},{4,5},{5,4},{6,7},{7,6},{8,9},{9,8},{10,11... | collective-permute-start | bytes 1769480 | tf_op jit(solution)/shard_map/ppermute | solution.py:283
  62.6 46.0 %copy-start = (bf16[192,4608]{1,0:T(8,128)(2,1)S(1)}, bf16[192,4608]{1,0:T(8,128)(2,1)}, u32[]{:S(2)}) copy-start(bf16[192,4608]{1,0:T(8,128)(2,1)} %refs_8_.1) | copy-start | bytes 5308420
  62.6 46.0 %copy-start.1 = (bf16[192,512]{1,0:T(8,128)(2,1)S(1)}, bf16[192,512]{1,0:T(8,128)(2,1)}, u32[]{:S(2)}) copy-start(bf16[192,512]{1,0:T(8,128)(2,1)} %refs_10_.1) | copy-start | bytes 589828
  63.9 19.8 %collective-permute-start.6 = (bf16[12,96,256]{2,1,0:T(8,128)(2,1)S(1)}, bf16[12,96,256]{2,1,0:T(8,128)(2,1)}, u32[]{:S(2)}, u32[]{:S(2)}) collective-permute-start(bf16[12,96,256]{2,1,0:T(8,128)(2,1)S(1)} %regroup.1.refs_0_), channel_id=1, source_target_pairs={{0,32},{16,48},{32,0},{48,16},{1,33},{17,49},{33,1},{49,17},{2,34}... | collective-permute-start | bytes 1769480 | tf_op jit(solution)/shard_map/ppermute | solution.py:279
  67.2 25.7 %collective-permute-start.5 = (bf16[12,96,256]{2,1,0:T(8,128)(2,1)S(1)}, bf16[12,96,256]{2,1,0:T(8,128)(2,1)}, u32[]{:S(2)}, u32[]{:S(2)}) collective-permute-start(bf16[12,96,256]{2,1,0:T(8,128)(2,1)S(1)} %regroup.1.refs_0_), channel_id=1, source_target_pairs={{0,16},{16,32},{32,48},{48,0},{1,17},{17,33},{33,49},{49,1},{2,18}... | collective-permute-start | bytes 1769480 | tf_op jit(solution)/shard_map/ppermute | solution.py:279
  71.2 23.8 %collective-permute-start.4 = (bf16[12,96,256]{2,1,0:T(8,128)(2,1)S(1)}, bf16[12,96,256]{2,1,0:T(8,128)(2,1)}, u32[]{:S(2)}, u32[]{:S(2)}) collective-permute-start(bf16[12,96,256]{2,1,0:T(8,128)(2,1)S(1)} %regroup.1.refs_0_), channel_id=1, source_target_pairs={{0,48},{16,0},{32,16},{48,32},{1,49},{17,1},{33,17},{49,33},{2,50}... | collective-permute-start | bytes 1769480 | tf_op jit(solution)/shard_map/ppermute | solution.py:279
  73.1 25.4 %all-to-all-start.2 = ((bf16[8,144,256]{2,1,0:T(8,128)(2,1)}), bf16[8,144,256]{2,1,0:T(8,128)(2,1)S(1)}, u32[]{:S(2)}, u32[]{:S(2)}) async-start(bf16[8,144,256]{2,1,0:T(8,128)(2,1)} %own_half.1), calls=%async_computation.2 | async-start | bytes 1179648 | tf_op jit(solution)/shard_map/all_to_all | solution.py:308
  79.9 28.7 %collective-permute-start.7 = (bf16[12,96,256]{2,1,0:T(8,128)(2,1)S(1)}, bf16[12,96,256]{2,1,0:T(8,128)(2,1)}, u32[]{:S(2)}, u32[]{:S(2)}) collective-permute-start(bf16[12,96,256]{2,1,0:T(8,128)(2,1)S(1)} %regroup.1.refs_0_), channel_id=1, source_target_pairs={{0,1},{1,0},{2,3},{3,2},{4,5},{5,4},{6,7},{7,6},{8,9},{9,8},{10,11... | collective-permute-start | bytes 1769480 | tf_op jit(solution)/shard_map/ppermute | solution.py:283
  83.6 25.0 %collective-permute-start.10 = (bf16[12,96,256]{2,1,0:T(8,128)(2,1)}, bf16[12,96,256]{2,1,0:T(8,128)(2,1)}, u32[]{:S(2)}, u32[]{:S(2)}) collective-permute-start(bf16[12,96,256]{2,1,0:T(8,128)(2,1)} %collective-permute-done.6.refs_3_), channel_id=1, source_target_pairs={{0,1},{1,0},{2,3},{3,2},{4,5},{5,4},{6,7},{7,6},{8,9},{9,8},{10,11... | collective-permute-start | bytes 1769480 | tf_op jit(solution)/shard_map/ppermute | solution.py:283
  92.9 15.7 %collective-permute-start.9 = (bf16[12,96,256]{2,1,0:T(8,128)(2,1)}, bf16[12,96,256]{2,1,0:T(8,128)(2,1)}, u32[]{:S(2)}, u32[]{:S(2)}) collective-permute-start(bf16[12,96,256]{2,1,0:T(8,128)(2,1)} %collective-permute-done.5.refs_2_), channel_id=1, source_target_pairs={{0,1},{1,0},{2,3},{3,2},{4,5},{5,4},{6,7},{7,6},{8,9},{9,8},{10,11... | collective-permute-start | bytes 1769480 | tf_op jit(solution)/shard_map/ppermute | solution.py:283
  95.0 13.6 %collective-permute-start.8 = (bf16[12,96,256]{2,1,0:T(8,128)(2,1)}, bf16[12,96,256]{2,1,0:T(8,128)(2,1)}, u32[]{:S(2)}, u32[]{:S(2)}) collective-permute-start(bf16[12,96,256]{2,1,0:T(8,128)(2,1)} %collective-permute-done.4.refs_1_), channel_id=1, source_target_pairs={{0,1},{1,0},{2,3},{3,2},{4,5},{5,4},{6,7},{7,6},{8,9},{9,8},{10,11... | collective-permute-start | bytes 1769480 | tf_op jit(solution)/shard_map/ppermute | solution.py:283
  99.3 21.4 %all-to-all-start.3 = ((bf16[12,12,256]{2,1,0:T(8,128)(2,1)}), bf16[12,12,256]{2,1,0:T(8,128)(2,1)S(1)}, u32[]{:S(2)}, u32[]{:S(2)}) async-start(bf16[12,12,256]{2,1,0:T(8,128)(2,1)} %sum_over_y.1), calls=%async_computation.3 | async-start | bytes 196608 | tf_op jit(solution)/shard_map/all_to_all | solution.py:310

commit v10 on v9

--- a/solution.py
+++ b/solution.py
@@ -29,7 +29,7 @@
 BY_DEVICE = np.zeros((ZG * XROWS, ZG * XROWS), np.float32)
 BY_DEVICE[(((_yh * NYL + _yl) * ZG + _z) * ROWS + _i).ravel(), np.arange(ZG * XROWS)] = 1
 IN_ORDER = BY_DEVICE.T
-HELD = (0, 3, 1, 2)
+HELD = (0, 2, 1, 3)
 ZSTEP = 3
 
 
@@ -301,7 +301,7 @@
 
     w_y = to_all(w_z.reshape(NZ * ROWS, HALF), Y, NY)
 
-    own = regroup(lax.optimization_barrier((w_y, term))[0])
+    own = regroup(lax.optimization_barrier((w_y, ahead))[0])
     mine = [own] + [shift(own, r) for r in HELD[1:]]
     other = [swap(piece) for piece in mine]
 

time: 123 us -> 125 us (1.016)
  starting transfers between devices: 66.9 us -> 63.8 us
  Pallas kernels: 20.8 us -> 22.7 us
  waiting for transfers between devices: 30.6 us -> 32 us
    all_to_all x1, waiting for transfers between devices: 0.38 us -> 4.52 us  [to_all(): return lax.all_to_all(copies, axis, split_axis=0, concat_axis=0, tiled=True)]
    all_to_all x1, starting transfers between devices: 6.77 us -> 3.67 us  [on_device(): t_y = lax.all_to_all(term, Y, split_axis=0, concat_axis=0, tiled=True)]
    ppermute x6, waiting for transfers between devices: 16.8 us -> 14.1 us  [shift(): return lax.ppermute(piece, 'x', [(k, (k + r) % NX) for k in range(NX)])]
    all_to_all x1, waiting for transfers between devices: 1.25 us -> 3.24 us  [on_device(): t_y = lax.all_to_all(term, Y, split_axis=0, concat_axis=0, tiled=True)]
    ppermute x5, waiting for transfers between devices: 1.98 us -> 0.01 us  [swap(): return lax.ppermute(piece, 'c', [(0, 1), (1, 0)])]
    pallas_call x2, Pallas kernels: 4.19 us -> 6.07 us  [term_call(): pl.pallas_call(kernel, grid_spec=pltpu.PrefetchScalarGridSpec(num_scalar_...]
  transfers between devices with their start and end apart: 15 -> 15, of which waited for: 10 -> 8; matrix products, arithmetic and copies ran while one was open for 1% -> 1% of each run, Pallas kernels for 13% -> 15%
where the time goes in v10:
time: 125 us; the launch traced here: 123 us
  starting transfers between devices  63.8 us (51%)
  waiting for transfers between devices  32 us (26%)
  Pallas kernels  22.7 us (18%)
  local copies, waits for them, and re-layouts  1.9 us (2%)
  other arithmetic  1.28 us (1%)
    ppermute x6, starting transfers between devices, shift(): return lax.ppermute(piece, 'x', [(k, (k + r) % NX) for k in range(NX)])  18.5 us
    all_to_all x1, starting transfers between devices, on_device(): w_z = lax.all_to_all(copies, 'z', split_axis=0, concat_axis=0, tiled=True)  15.2 us
    ppermute x6, waiting for transfers between devices, shift(): return lax.ppermute(piece, 'x', [(k, (k + r) % NX) for k in range(NX)])  14.1 us
    ppermute x5, starting transfers between devices, swap(): return lax.ppermute(piece, 'c', [(0, 1), (1, 0)])  10.1 us
    all_to_all x1, starting transfers between devices, on_device(): t_z = lax.all_to_all(sum_y, 'z', split_axis=0, concat_axis=0, tiled=True)  9.32 us
    pallas_call x1, Pallas kernels, project(): pl.pallas_call(project_kernel, grid_spec=pltpu.PrefetchScalarGridSpec(num...  7.1 us
    all_to_all x1, starting transfers between devices, to_all(): return lax.all_to_all(copies, axis, split_axis=0, concat_axis=0, tiled=True)  7.1 us
    pallas_call x2, Pallas kernels, pack(): pl.pallas_call(functools.partial(pack_kernel, shifts), grid_spec=pltpu.Pr...  6.47 us
  transfers between devices with their start and end apart: 15, of which 8 were waited for; matrix products, arithmetic and copies ran while one was open for 1% of the time, Pallas kernels for 15%

profile of v10, /device:TPU:6, one launch (start us, length us, event | category | flops | bytes accessed | tf_op | source)
XLA Modules:
  0.0 122.6 jit_solution(8684124290138377893)
XLA Ops:
  0.6 0.6 pad_add_fusion.place
  1.3 3.2 %pack.2 = (bf16[192,1664]{1,0:T(8,128)(2,1)}, bf16[192,1664]{1,0:T(8,128)(2,1)}) custom-call(s32[2]{0:T(128)} %pad_add_fusion.place, bf16[192,4608]{1,0:T(8,128)(2,1)} %refs_8_.1, bf16[192,512]{1,0:T(8,128)(2,1)} %refs_10_.1), custom_call_target="tpu_custom_call" | custom-call | flops 884736 | bytes 3538944 | tf_op jit(solution)/shard_map/pack/pallas_call | solution.py:56
  4.5 1.4 %scaled_copies.1 = bf16[12,12,256]{2,1,0:T(8,128)(2,1)} custom-call(bf16[12,256]{1,0:T(8,128)(2,1)} %values, bf16[1,12]{1,0:T(2,128)(2,1)} %bitcast.3), custom_call_target="tpu_custom_call" | custom-call | tf_op jit(solution)/shard_map/scaled_copies/pallas_call | solution.py:265
  5.9 15.2 %all-to-all-start = ((bf16[12,12,256]{2,1,0:T(8,128)(2,1)}), bf16[12,12,256]{2,1,0:T(8,128)(2,1)S(1)}, u32[]{:S(2)}, u32[]{:S(2)}) async-start(bf16[12,12,256]{2,1,0:T(8,128)(2,1)} %scaled_copies.1), calls=%async_computation | async-start | bytes 196608 | tf_op jit(solution)/shard_map/all_to_all | solution.py:294
  21.1 0.0 copy-start.2
  21.1 0.0 copy-start.7
  21.1 3.5 %collective-permute-start = (bf16[192,1664]{1,0:T(8,128)(2,1)}, bf16[192,1664]{1,0:T(8,128)(2,1)S(1)}, u32[]{:S(2)}, u32[]{:S(2)}) collective-permute-start(bf16[192,1664]{1,0:T(8,128)(2,1)} %get-tuple-element.15), channel_id=1, source_target_pairs={{0,32},{16,48},{32,0},{48,16},{1,33},{17,49},{33,1},{49,17},{2,34}... | collective-permute-start | bytes 1916936 | tf_op jit(solution)/shard_map/ppermute | solution.py:279
  24.6 3.2 %pack.3 = (bf16[192,1664]{1,0:T(8,128)(2,1)}, bf16[192,1664]{1,0:T(8,128)(2,1)}) custom-call(s32[2]{0:T(128)} %pad_add_fusion.place, bf16[192,4608]{1,0:T(8,128)(2,1)} %refs_8_.1, bf16[192,512]{1,0:T(8,128)(2,1)} %refs_10_.1), custom_call_target="tpu_custom_call" | custom-call | flops 884736 | bytes 3538944 | tf_op jit(solution)/shard_map/pack/pallas_call | solution.py:56
  27.8 5.2 %all-to-all-done = bf16[12,12,256]{2,1,0:T(8,128)(2,1)S(1)} async-done(((bf16[12,12,256]{2,1,0:T(8,128)(2,1)}), bf16[12,12,256]{2,1,0:T(8,128)(2,1)S(1)}, u32[]{:S(2)}, u32[]{:S(2)}) %all-to-all-start) | async-done | bytes 73760 | tf_op jit(solution)/shard_map/all_to_all | solution.py:294
  33.1 2.4 %collective-permute-start.1 = (bf16[192,1664]{1,0:T(8,128)(2,1)}, bf16[192,1664]{1,0:T(8,128)(2,1)S(1)}, u32[]{:S(2)}, u32[]{:S(2)}) collective-permute-start(bf16[192,1664]{1,0:T(8,128)(2,1)} %get-tuple-element.22), channel_id=1, source_target_pairs={{0,16},{16,32},{32,48},{48,0},{1,17},{17,33},{33,49},{49,1},{2,18}... | collective-permute-start | bytes 1916936 | tf_op jit(solution)/shard_map/ppermute | solution.py:279
  35.5 3.4 %collective-permute-start.2 = (bf16[192,1664]{1,0:T(8,128)(2,1)}, bf16[192,1664]{1,0:T(8,128)(2,1)S(1)}, u32[]{:S(2)}, u32[]{:S(2)}) collective-permute-start(bf16[192,1664]{1,0:T(8,128)(2,1)} %get-tuple-element.23), channel_id=1, source_target_pairs={{0,48},{16,0},{32,16},{48,32},{1,49},{17,1},{33,17},{49,33},{2,50}... | collective-permute-start | bytes 1916936 | tf_op jit(solution)/shard_map/ppermute | solution.py:279
  38.9 0.9 broadcast_in_dim.8
  39.8 7.1 %all-to-all-start.1 = ((bf16[8,144,256]{2,1,0:T(8,128)(2,1)}), bf16[8,144,256]{2,1,0:T(8,128)(2,1)S(1)}, u32[]{:S(2)}, u32[]{:S(2)}) async-start(bf16[8,144,256]{2,1,0:T(8,128)(2,1)} %broadcast_in_dim.8), calls=%async_computation.1 | async-start | bytes 1179648 | tf_op jit(solution)/shard_map/all_to_all | solution.py:275
  46.9 0.0 collective-permute-done.refs_1_
  46.9 5.3 %collective-permute-done.1.refs_2_ = bf16[192,1664]{1,0:T(8,128)(2,1)S(1)} collective-permute-done((bf16[192,1664]{1,0:T(8,128)(2,1)}, bf16[192,1664]{1,0:T(8,128)(2,1)S(1)}, u32[]{:S(2)}, u32[]{:S(2)}) %collective-permute-start.1) | collective-permute-done | bytes 639008 | tf_op jit(solution)/shard_map/ppermute | solution.py:279
  52.3 2.1 %collective-permute-done.2.refs_3_ = bf16[192,1664]{1,0:T(8,128)(2,1)S(1)} collective-permute-done((bf16[192,1664]{1,0:T(8,128)(2,1)}, bf16[192,1664]{1,0:T(8,128)(2,1)S(1)}, u32[]{:S(2)}, u32[]{:S(2)}) %collective-permute-start.2) | collective-permute-done | bytes 639008 | tf_op jit(solution)/shard_map/ppermute | solution.py:279
  54.4 0.0 copy-done.2
  54.4 0.0 copy-done.7
  54.4 2.2 %other_half.1 = bf16[256,1152]{1,0:T(8,128)(2,1)} custom-call(s32[2]{0:T(128)S(1)} %copy-done.7, bf16[192,1664]{1,0:T(8,128)(2,1)S(1)} %copy-done.2, bf16[192,1664]{1,0:T(8,128)(2,1)S(1)} %collective-permute-done.refs_1_, bf16[192,1664]{1,0:T(8,128)(2,1)S(1)} %collective-permute-done.1.refs_2_, bf16[192,1664]{1,0:T(8,128)(2,1)S(1)} %collective-permute-done.2.refs_3_), custom_call_target="tpu_custom_call" | custom-call | flops 45298483200 | bytes 2555904 | tf_op jit(solution)/shard_map/other_half/pallas_call | solution.py:109
  56.6 0.0 copy-done.3
  56.6 1.9 %collective-permute-start.10 = (bf16[256,1152]{1,0:T(8,128)(2,1)}, bf16[256,1152]{1,0:T(8,128)(2,1)}, u32[]{:S(2)}, u32[]{:S(2)}) collective-permute-start(bf16[256,1152]{1,0:T(8,128)(2,1)} %other_half.1), channel_id=1, source_target_pairs={{0,1},{1,0},{2,3},{3,2},{4,5},{5,4},{6,7},{7,6},{8,9},{9,8},{10,11... | collective-permute-start | bytes 1769480 | tf_op jit(solution)/shard_map/ppermute | solution.py:283
  58.5 4.5 %all-to-all-done.1.parts = bf16[8,144,256]{2,1,0:T(8,128)(2,1)S(1)} async-done(((bf16[8,144,256]{2,1,0:T(8,128)(2,1)}), bf16[8,144,256]{2,1,0:T(8,128)(2,1)S(1)}, u32[]{:S(2)}, u32[]{:S(2)}) %all-to-all-start.1) | async-done | bytes 589856 | tf_op jit(solution)/shard_map/all_to_all | solution.py:275
  63.0 1.0 copy-done.6
  64.0 0.9 regroup.1.refs_0_
  64.9 3.3 %collective-permute-start.3 = (bf16[12,96,256]{2,1,0:T(8,128)(2,1)S(1)}, bf16[12,96,256]{2,1,0:T(8,128)(2,1)}, u32[]{:S(2)}, u32[]{:S(2)}) collective-permute-start(bf16[12,96,256]{2,1,0:T(8,128)(2,1)S(1)} %regroup.1.refs_0_), channel_id=1, source_target_pairs={{0,32},{16,48},{32,0},{48,16},{1,33},{17,49},{33,1},{49,17},{2,34}... | collective-permute-start | bytes 1769480 | tf_op jit(solution)/shard_map/ppermute | solution.py:279
  68.2 4.0 %collective-permute-start.4 = (bf16[12,96,256]{2,1,0:T(8,128)(2,1)S(1)}, bf16[12,96,256]{2,1,0:T(8,128)(2,1)}, u32[]{:S(2)}, u32[]{:S(2)}) collective-permute-start(bf16[12,96,256]{2,1,0:T(8,128)(2,1)S(1)} %regroup.1.refs_0_), channel_id=1, source_target_pairs={{0,16},{16,32},{32,48},{48,0},{1,17},{17,33},{33,49},{49,1},{2,18}... | collective-permute-start | bytes 1769480 | tf_op jit(solution)/shard_map/ppermute | solution.py:279
  72.2 1.9 %collective-permute-start.5 = (bf16[12,96,256]{2,1,0:T(8,128)(2,1)S(1)}, bf16[12,96,256]{2,1,0:T(8,128)(2,1)}, u32[]{:S(2)}, u32[]{:S(2)}) collective-permute-start(bf16[12,96,256]{2,1,0:T(8,128)(2,1)S(1)} %regroup.1.refs_0_), channel_id=1, source_target_pairs={{0,48},{16,0},{32,16},{48,32},{1,49},{17,1},{33,17},{49,33},{2,50}... | collective-permute-start | bytes 1769480 | tf_op jit(solution)/shard_map/ppermute | solution.py:279
  74.2 0.0 collective-permute-done.10.refs_4_
  74.2 0.0 copy-done.5
  74.2 3.9 %own_half.1 = bf16[8,144,256]{2,1,0:T(8,128)(2,1)} custom-call(s32[2]{0:T(128)S(1)} %copy-done.7, bf16[192,1664]{1,0:T(8,128)(2,1)S(1)} %copy-done.2, bf16[192,1664]{1,0:T(8,128)(2,1)S(1)} %collective-permute-done.refs_1_, bf16[192,1664]{1,0:T(8,128)(2,1)S(1)} %collective-permute-done.1.refs_2_, bf16[192,1664]{1,0:T(8,128)(2,1)S(1)} %copy-done.4, ...), custom_call_target="tpu_custom_call" | custom-call | flops 452984832 | bytes 2555904 | tf_op jit(solution)/shard_map/own_half/pallas_call | solution.py:109
  78.1 3.7 %all-to-all-start.2 = ((bf16[8,144,256]{2,1,0:T(8,128)(2,1)}), bf16[8,144,256]{2,1,0:T(8,128)(2,1)S(1)}, u32[]{:S(2)}, u32[]{:S(2)}) async-start(bf16[8,144,256]{2,1,0:T(8,128)(2,1)} %own_half.1), calls=%async_computation.2 | async-start | bytes 1179648 | tf_op jit(solution)/shard_map/all_to_all | solution.py:308
  81.7 1.9 %collective-permute-start.6 = (bf16[12,96,256]{2,1,0:T(8,128)(2,1)S(1)}, bf16[12,96,256]{2,1,0:T(8,128)(2,1)}, u32[]{:S(2)}, u32[]{:S(2)}) collective-permute-start(bf16[12,96,256]{2,1,0:T(8,128)(2,1)S(1)} %regroup.1.refs_0_), channel_id=1, source_target_pairs={{0,1},{1,0},{2,3},{3,2},{4,5},{5,4},{6,7},{7,6},{8,9},{9,8},{10,11... | collective-permute-start | bytes 1769480 | tf_op jit(solution)/shard_map/ppermute | solution.py:283
  83.7 1.0 collective-permute-done.3.refs_1_
  84.7 1.9 %collective-permute-start.7 = (bf16[12,96,256]{2,1,0:T(8,128)(2,1)}, bf16[12,96,256]{2,1,0:T(8,128)(2,1)}, u32[]{:S(2)}, u32[]{:S(2)}) collective-permute-start(bf16[12,96,256]{2,1,0:T(8,128)(2,1)} %collective-permute-done.3.refs_1_), channel_id=1, source_target_pairs={{0,1},{1,0},{2,3},{3,2},{4,5},{5,4},{6,7},{7,6},{8,9},{9,8},{10,11... | collective-permute-start | bytes 1769480 | tf_op jit(solution)/shard_map/ppermute | solution.py:283
  86.6 5.6 %collective-permute-done.4.refs_2_ = bf16[12,96,256]{2,1,0:T(8,128)(2,1)} collective-permute-done((bf16[12,96,256]{2,1,0:T(8,128)(2,1)S(1)}, bf16[12,96,256]{2,1,0:T(8,128)(2,1)}, u32[]{:S(2)}, u32[]{:S(2)}) %collective-permute-start.4) | collective-permute-done | bytes 589856 | tf_op jit(solution)/shard_map/ppermute | solution.py:279
  92.2 1.9 %collective-permute-start.8 = (bf16[12,96,256]{2,1,0:T(8,128)(2,1)}, bf16[12,96,256]{2,1,0:T(8,128)(2,1)}, u32[]{:S(2)}, u32[]{:S(2)}) collective-permute-start(bf16[12,96,256]{2,1,0:T(8,128)(2,1)} %collective-permute-done.4.refs_2_), channel_id=1, source_target_pairs={{0,1},{1,0},{2,3},{3,2},{4,5},{5,4},{6,7},{7,6},{8,9},{9,8},{10,11... | collective-permute-start | bytes 1769480 | tf_op jit(solution)/shard_map/ppermute | solution.py:283
  94.1 0.0 collective-permute-done.5.refs_3_
  94.2 2.4 %collective-permute-start.9 = (bf16[12,96,256]{2,1,0:T(8,128)(2,1)}, bf16[12,96,256]{2,1,0:T(8,128)(2,1)}, u32[]{:S(2)}, u32[]{:S(2)}) collective-permute-start(bf16[12,96,256]{2,1,0:T(8,128)(2,1)} %collective-permute-done.5.refs_3_), channel_id=1, source_target_pairs={{0,1},{1,0},{2,3},{3,2},{4,5},{5,4},{6,7},{7,6},{8,9},{9,8},{10,11... | collective-permute-start | bytes 1769480 | tf_op jit(solution)/shard_map/ppermute | solution.py:283
  96.6 3.2 %all-to-all-done.2.parts = bf16[8,144,256]{2,1,0:T(8,128)(2,1)S(1)} async-done(((bf16[8,144,256]{2,1,0:T(8,128)(2,1)}), bf16[8,144,256]{2,1,0:T(8,128)(2,1)S(1)}, u32[]{:S(2)}, u32[]{:S(2)}) %all-to-all-start.2) | async-done | bytes 589856 | tf_op jit(solution)/shard_map/all_to_all | solution.py:308
  99.8 0.7 sum_over_y.1
  100.5 9.3 %all-to-all-start.3 = ((bf16[12,12,256]{2,1,0:T(8,128)(2,1)}), bf16[12,12,256]{2,1,0:T(8,128)(2,1)S(1)}, u32[]{:S(2)}, u32[]{:S(2)}) async-start(bf16[12,12,256]{2,1,0:T(8,128)(2,1)} %sum_over_y.1), calls=%async_computation.3 | async-start | bytes 196608 | tf_op jit(solution)/shard_map/all_to_all | solution.py:310
  109.9 0.0 collective-permute-done.6.refs_4_
  109.9 0.0 collective-permute-done.7.refs_5_
  109.9 0.0 collective-permute-done.8.refs_6_
  109.9 0.0 collective-permute-done.9.refs_7_
  109.9 7.1 %project.1 = (bf16[192,512]{1,0:T(8,128)(2,1)}, bf16[192,4608]{1,0:T(8,128)(2,1)}) custom-call(s32[2]{0:T(128)S(1)} %copy-done.7, bf16[12,96,256]{2,1,0:T(8,128)(2,1)S(1)} %regroup.1.refs_0_, bf16[12,96,256]{2,1,0:T(8,128)(2,1)} %collective-permute-done.3.refs_1_, bf16[12,96,256]{2,1,0:T(8,128)(2,1)} %collective-permute-done.4.refs_2_, ...), custom_call_target="tpu_custom_call" | custom-call | flops 1811939328 | bytes 8257536 | tf_op jit(solution)/shard_map/project/pallas_call | solution.py:219
  117.0 4.9 %all-to-all-done.3 = bf16[12,12,256]{2,1,0:T(8,128)(2,1)S(1)} async-done(((bf16[12,12,256]{2,1,0:T(8,128)(2,1)}), bf16[12,12,256]{2,1,0:T(8,128)(2,1)S(1)}, u32[]{:S(2)}, u32[]{:S(2)}) %all-to-all-start.3) | async-done | bytes 73760 | tf_op jit(solution)/shard_map/all_to_all | solution.py:310
  122.0 0.6 broadcast_multiply_fusion
  (11 shorter events, 0.1 us)
Async XLA Ops:
  5.9 27.1 %all-to-all-start = ((bf16[12,12,256]{2,1,0:T(8,128)(2,1)}), bf16[12,12,256]{2,1,0:T(8,128)(2,1)S(1)}, u32[]{:S(2)}, u32[]{:S(2)}) async-start(bf16[12,12,256]{2,1,0:T(8,128)(2,1)} %scaled_copies.1), calls=%async_computation | async-start | bytes 196608 | tf_op jit(solution)/shard_map/all_to_all | solution.py:294
  21.1 33.3 %copy-start.2 = (bf16[192,1664]{1,0:T(8,128)(2,1)S(1)}, bf16[192,1664]{1,0:T(8,128)(2,1)}, u32[]{:S(2)}) copy-start(bf16[192,1664]{1,0:T(8,128)(2,1)} %get-tuple-element.21.refs_0_) | copy-start | bytes 1916932
  21.1 33.3 %copy-start.7 = (s32[2]{0:T(128)S(1)}, s32[2]{0:T(128)}, u32[]{:S(2)}) copy-start(s32[2]{0:T(128)} %pad_add_fusion.place) | copy-start | bytes 28
  21.1 25.8 %collective-permute-start = (bf16[192,1664]{1,0:T(8,128)(2,1)}, bf16[192,1664]{1,0:T(8,128)(2,1)S(1)}, u32[]{:S(2)}, u32[]{:S(2)}) collective-permute-start(bf16[192,1664]{1,0:T(8,128)(2,1)} %get-tuple-element.15), channel_id=1, source_target_pairs={{0,32},{16,48},{32,0},{48,16},{1,33},{17,49},{33,1},{49,17},{2,34}... | collective-permute-start | bytes 1916936 | tf_op jit(solution)/shard_map/ppermute | solution.py:279
  33.1 19.2 %collective-permute-start.1 = (bf16[192,1664]{1,0:T(8,128)(2,1)}, bf16[192,1664]{1,0:T(8,128)(2,1)S(1)}, u32[]{:S(2)}, u32[]{:S(2)}) collective-permute-start(bf16[192,1664]{1,0:T(8,128)(2,1)} %get-tuple-element.22), channel_id=1, source_target_pairs={{0,16},{16,32},{32,48},{48,0},{1,17},{17,33},{33,49},{49,1},{2,18}... | collective-permute-start | bytes 1916936 | tf_op jit(solution)/shard_map/ppermute | solution.py:279
  35.5 18.9 %collective-permute-start.2 = (bf16[192,1664]{1,0:T(8,128)(2,1)}, bf16[192,1664]{1,0:T(8,128)(2,1)S(1)}, u32[]{:S(2)}, u32[]{:S(2)}) collective-permute-start(bf16[192,1664]{1,0:T(8,128)(2,1)} %get-tuple-element.23), channel_id=1, source_target_pairs={{0,48},{16,0},{32,16},{48,32},{1,49},{17,1},{33,17},{49,33},{2,50}... | collective-permute-start | bytes 1916936 | tf_op jit(solution)/shard_map/ppermute | solution.py:279
  39.8 23.2 %all-to-all-start.1 = ((bf16[8,144,256]{2,1,0:T(8,128)(2,1)}), bf16[8,144,256]{2,1,0:T(8,128)(2,1)S(1)}, u32[]{:S(2)}, u32[]{:S(2)}) async-start(bf16[8,144,256]{2,1,0:T(8,128)(2,1)} %broadcast_in_dim.8), calls=%async_computation.1 | async-start | bytes 1179648 | tf_op jit(solution)/shard_map/all_to_all | solution.py:275
  54.4 2.2 %copy-start.3 = (bf16[192,1664]{1,0:T(8,128)(2,1)}, bf16[192,1664]{1,0:T(8,128)(2,1)S(1)}, u32[]{:S(2)}) copy-start(bf16[192,1664]{1,0:T(8,128)(2,1)S(1)} %collective-permute-done.2.refs_3_) | copy-start | bytes 1916932
  54.4 19.8 %copy-start.5 = (bf16[384,384]{1,0:T(8,128)(2,1)S(1)}, bf16[384,384]{1,0:T(8,128)(2,1)}, u32[]{:S(2)}) copy-start(bf16[384,384]{1,0:T(8,128)(2,1)} %constant.18.clone.refs_5_) | copy-start | bytes 884740
  56.6 17.5 %collective-permute-start.10 = (bf16[256,1152]{1,0:T(8,128)(2,1)}, bf16[256,1152]{1,0:T(8,128)(2,1)}, u32[]{:S(2)}, u32[]{:S(2)}) collective-permute-start(bf16[256,1152]{1,0:T(8,128)(2,1)} %other_half.1), channel_id=1, source_target_pairs={{0,1},{1,0},{2,3},{3,2},{4,5},{5,4},{6,7},{7,6},{8,9},{9,8},{10,11... | collective-permute-start | bytes 1769480 | tf_op jit(solution)/shard_map/ppermute | solution.py:283
  63.0 1.0 copy-start.6
  64.0 10.2 %copy-start.4 = (bf16[192,1664]{1,0:T(8,128)(2,1)S(1)}, bf16[192,1664]{1,0:T(8,128)(2,1)}, u32[]{:S(2)}) copy-start(bf16[192,1664]{1,0:T(8,128)(2,1)} %copy-done.3) | copy-start | bytes 1916932
  64.9 19.8 %collective-permute-start.3 = (bf16[12,96,256]{2,1,0:T(8,128)(2,1)S(1)}, bf16[12,96,256]{2,1,0:T(8,128)(2,1)}, u32[]{:S(2)}, u32[]{:S(2)}) collective-permute-start(bf16[12,96,256]{2,1,0:T(8,128)(2,1)S(1)} %regroup.1.refs_0_), channel_id=1, source_target_pairs={{0,32},{16,48},{32,0},{48,16},{1,33},{17,49},{33,1},{49,17},{2,34}... | collective-permute-start | bytes 1769480 | tf_op jit(solution)/shard_map/ppermute | solution.py:279
  68.2 24.0 %collective-permute-start.4 = (bf16[12,96,256]{2,1,0:T(8,128)(2,1)S(1)}, bf16[12,96,256]{2,1,0:T(8,128)(2,1)}, u32[]{:S(2)}, u32[]{:S(2)}) collective-permute-start(bf16[12,96,256]{2,1,0:T(8,128)(2,1)S(1)} %regroup.1.refs_0_), channel_id=1, source_target_pairs={{0,16},{16,32},{32,48},{48,0},{1,17},{17,33},{33,49},{49,1},{2,18}... | collective-permute-start | bytes 1769480 | tf_op jit(solution)/shard_map/ppermute | solution.py:279
  72.2 21.9 %collective-permute-start.5 = (bf16[12,96,256]{2,1,0:T(8,128)(2,1)S(1)}, bf16[12,96,256]{2,1,0:T(8,128)(2,1)}, u32[]{:S(2)}, u32[]{:S(2)}) collective-permute-start(bf16[12,96,256]{2,1,0:T(8,128)(2,1)S(1)} %regroup.1.refs_0_), channel_id=1, source_target_pairs={{0,48},{16,0},{32,16},{48,32},{1,49},{17,1},{33,17},{49,33},{2,50}... | collective-permute-start | bytes 1769480 | tf_op jit(solution)/shard_map/ppermute | solution.py:279
  78.1 31.8 %copy-start = (bf16[192,4608]{1,0:T(8,128)(2,1)S(1)}, bf16[192,4608]{1,0:T(8,128)(2,1)}, u32[]{:S(2)}) copy-start(bf16[192,4608]{1,0:T(8,128)(2,1)} %refs_8_.1) | copy-start | bytes 5308420
  78.1 31.8 %copy-start.1 = (bf16[192,512]{1,0:T(8,128)(2,1)S(1)}, bf16[192,512]{1,0:T(8,128)(2,1)}, u32[]{:S(2)}) copy-start(bf16[192,512]{1,0:T(8,128)(2,1)} %refs_10_.1) | copy-start | bytes 589828
  78.1 21.7 %all-to-all-start.2 = ((bf16[8,144,256]{2,1,0:T(8,128)(2,1)}), bf16[8,144,256]{2,1,0:T(8,128)(2,1)S(1)}, u32[]{:S(2)}, u32[]{:S(2)}) async-start(bf16[8,144,256]{2,1,0:T(8,128)(2,1)} %own_half.1), calls=%async_computation.2 | async-start | bytes 1179648 | tf_op jit(solution)/shard_map/all_to_all | solution.py:308
  81.7 28.1 %collective-permute-start.6 = (bf16[12,96,256]{2,1,0:T(8,128)(2,1)S(1)}, bf16[12,96,256]{2,1,0:T(8,128)(2,1)}, u32[]{:S(2)}, u32[]{:S(2)}) collective-permute-start(bf16[12,96,256]{2,1,0:T(8,128)(2,1)S(1)} %regroup.1.refs_0_), channel_id=1, source_target_pairs={{0,1},{1,0},{2,3},{3,2},{4,5},{5,4},{6,7},{7,6},{8,9},{9,8},{10,11... | collective-permute-start | bytes 1769480 | tf_op jit(solution)/shard_map/ppermute | solution.py:283
  84.7 25.2 %collective-permute-start.7 = (bf16[12,96,256]{2,1,0:T(8,128)(2,1)}, bf16[12,96,256]{2,1,0:T(8,128)(2,1)}, u32[]{:S(2)}, u32[]{:S(2)}) collective-permute-start(bf16[12,96,256]{2,1,0:T(8,128)(2,1)} %collective-permute-done.3.refs_1_), channel_id=1, source_target_pairs={{0,1},{1,0},{2,3},{3,2},{4,5},{5,4},{6,7},{7,6},{8,9},{9,8},{10,11... | collective-permute-start | bytes 1769480 | tf_op jit(solution)/shard_map/ppermute | solution.py:283
  92.2 17.7 %collective-permute-start.8 = (bf16[12,96,256]{2,1,0:T(8,128)(2,1)}, bf16[12,96,256]{2,1,0:T(8,128)(2,1)}, u32[]{:S(2)}, u32[]{:S(2)}) collective-permute-start(bf16[12,96,256]{2,1,0:T(8,128)(2,1)} %collective-permute-done.4.refs_2_), channel_id=1, source_target_pairs={{0,1},{1,0},{2,3},{3,2},{4,5},{5,4},{6,7},{7,6},{8,9},{9,8},{10,11... | collective-permute-start | bytes 1769480 | tf_op jit(solution)/shard_map/ppermute | solution.py:283
  94.2 15.7 %collective-permute-start.9 = (bf16[12,96,256]{2,1,0:T(8,128)(2,1)}, bf16[12,96,256]{2,1,0:T(8,128)(2,1)}, u32[]{:S(2)}, u32[]{:S(2)}) collective-permute-start(bf16[12,96,256]{2,1,0:T(8,128)(2,1)} %collective-permute-done.5.refs_3_), channel_id=1, source_target_pairs={{0,1},{1,0},{2,3},{3,2},{4,5},{5,4},{6,7},{7,6},{8,9},{9,8},{10,11... | collective-permute-start | bytes 1769480 | tf_op jit(solution)/shard_map/ppermute | solution.py:283
  100.5 21.4 %all-to-all-start.3 = ((bf16[12,12,256]{2,1,0:T(8,128)(2,1)}), bf16[12,12,256]{2,1,0:T(8,128)(2,1)S(1)}, u32[]{:S(2)}, u32[]{:S(2)}) async-start(bf16[12,12,256]{2,1,0:T(8,128)(2,1)} %sum_over_y.1), calls=%async_computation.3 | async-start | bytes 196608 | tf_op jit(solution)/shard_map/all_to_all | solution.py:310

commit v11 on v9

--- a/solution.py
+++ b/solution.py
@@ -287,18 +287,14 @@
     place = jnp.stack([lax.axis_index("c"), lax.axis_index("x")]).astype(jnp.int32)
     factor = 1.0 / math.sqrt(hidden.shape[0] * NZ * NX * NY * NC)
 
-    kept, far = pack(place, hidden, cotangent, (0, 2))
-
-    values, _ = lax.optimization_barrier((quant_weight, far))
+    packed = pack(place, hidden, cotangent, range(NX))
+    held = [packed[0]] + [shift(packed[r], r) for r in (2, 1, 3)]
+    ahead = other_half(place, held)
+    term = own_half(place, held, swap(ahead))
+
+    values, _ = lax.optimization_barrier((quant_weight, packed[0]))
     copies = scaled_copies(values, scales)
     w_z = lax.all_to_all(copies, "z", split_axis=0, concat_axis=0, tiled=True)
-    late, _ = lax.optimization_barrier((hidden, copies))
-    near = pack(place, late, cotangent, (1, 3))
-    w_z, near = lax.optimization_barrier((w_z, near))
-    held = [kept, shift(far, 2), shift(near[0], 1), shift(near[1], 3)]
-    ahead = other_half(place, held)
-    term = own_half(place, held, swap(ahead))
-
     w_y = to_all(w_z.reshape(NZ * ROWS, HALF), Y, NY)
 
     own = regroup(lax.optimization_barrier((w_y, term))[0])

time: 123 us -> 121 us (0.984)
  blocking collectives: 0 us -> 19.9 us
  starting transfers between devices: 66.9 us -> 50.1 us
  waiting for transfers between devices: 30.6 us -> 24.7 us
    all_to_all x0 -> x1, blocking collectives: none -> 19.9 us  [on_device(): w_z = lax.all_to_all(copies, 'z', split_axis=0, concat_axis=0, tiled=True)]
    all_to_all x1 -> x0, starting transfers between devices: 15.2 us -> none  [on_device(): w_z = lax.all_to_all(copies, 'z', split_axis=0, concat_axis=0, tiled=True)]
    ppermute x6, starting transfers between devices: 18.5 us -> 25.8 us  [shift(): return lax.ppermute(piece, 'x', [(k, (k + r) % NX) for k in range(NX)])]
    all_to_all x1, starting transfers between devices: 9.31 us -> 3.51 us  [on_device(): t_z = lax.all_to_all(sum_y, 'z', split_axis=0, concat_axis=0, tiled=True)]
    all_to_all x1, waiting for transfers between devices: 0.38 us -> 6.09 us  [to_all(): return lax.all_to_all(copies, axis, split_axis=0, concat_axis=0, tiled=True)]
    all_to_all x1 -> x0, waiting for transfers between devices: 5.24 us -> none  [on_device(): w_z = lax.all_to_all(copies, 'z', split_axis=0, concat_axis=0, tiled=True)]
    ppermute x6, waiting for transfers between devices: 16.8 us -> 11.7 us  [shift(): return lax.ppermute(piece, 'x', [(k, (k + r) % NX) for k in range(NX)])]
    all_to_all x1, starting transfers between devices: 6.77 us -> 3.55 us  [on_device(): t_y = lax.all_to_all(term, Y, split_axis=0, concat_axis=0, tiled=True)]
  transfers between devices with their start and end apart: 15 -> 14, of which waited for: 10 -> 5; matrix products, arithmetic and copies ran while one was open for 1% -> 1% of each run, Pallas kernels for 13% -> 13%
where the time goes in v11:
time: 121 us; the launch traced here: 118 us
  starting transfers between devices  50.1 us (41%)
  waiting for transfers between devices  24.7 us (20%)
  Pallas kernels  20.4 us (17%)
  blocking collectives  19.9 us (16%)
  other arithmetic  1.23 us (1%)
    ppermute x6, starting transfers between devices, shift(): return lax.ppermute(piece, 'x', [(k, (k + r) % NX) for k in range(NX)])  25.8 us
    all_to_all x1, blocking collectives, on_device(): w_z = lax.all_to_all(copies, 'z', split_axis=0, concat_axis=0, tiled=True)  19.9 us
    ppermute x6, waiting for transfers between devices, shift(): return lax.ppermute(piece, 'x', [(k, (k + r) % NX) for k in range(NX)])  11.7 us
    ppermute x5, starting transfers between devices, swap(): return lax.ppermute(piece, 'c', [(0, 1), (1, 0)])  10.2 us
    pallas_call x1, Pallas kernels, project(): pl.pallas_call(project_kernel, grid_spec=pltpu.PrefetchScalarGridSpec(num...  7.11 us
    all_to_all x1, starting transfers between devices, to_all(): return lax.all_to_all(copies, axis, split_axis=0, concat_axis=0, tiled=True)  7.1 us
    pallas_call x2, Pallas kernels, term_call(): pl.pallas_call(kernel, grid_spec=pltpu.PrefetchScalarGridSpec(num_scalar_...  6.35 us
    all_to_all x1, waiting for transfers between devices, to_all(): return lax.all_to_all(copies, axis, split_axis=0, concat_axis=0, tiled=True)  6.09 us
  transfers between devices with their start and end apart: 14, of which 5 were waited for; matrix products, arithmetic and copies ran while one was open for 1% of the time, Pallas kernels for 13%

profile of v11, /device:TPU:6, one launch (start us, length us, event | category | flops | bytes accessed | tf_op | source)
XLA Modules:
  0.0 118.2 jit_solution(11982622061501086088)
XLA Ops:
  0.6 0.6 pad_add_fusion.place
  1.2 0.0 copy-start.5
  1.2 3.9 %pack.1 = (bf16[192,1664]{1,0:T(8,128)(2,1)}, bf16[192,1664]{1,0:T(8,128)(2,1)}, bf16[192,1664]{1,0:T(8,128)(2,1)}, bf16[192,1664]{1,0:T(8,128)(2,1)}) custom-call(s32[2]{0:T(128)} %pad_add_fusion.place, bf16[192,4608]{1,0:T(8,128)(2,1)} %refs_8_.1, bf16[192,512]{1,0:T(8,128)(2,1)} %refs_10_.1), custom_call_target="tpu_custom_call" | custom-call | flops 884736 | bytes 3538944 | tf_op jit(solution)/shard_map/pack/pallas_call | solution.py:56
  5.2 0.0 copy-start.2
  5.2 3.4 %collective-permute-start = (bf16[192,1664]{1,0:T(8,128)(2,1)}, bf16[192,1664]{1,0:T(8,128)(2,1)S(1)}, u32[]{:S(2)}, u32[]{:S(2)}) collective-permute-start(bf16[192,1664]{1,0:T(8,128)(2,1)} %get-tuple-element.13), channel_id=1, source_target_pairs={{0,32},{16,48},{32,0},{48,16},{1,33},{17,49},{33,1},{49,17},{2,34}... | collective-permute-start | bytes 1916936 | tf_op jit(solution)/shard_map/ppermute | solution.py:279
  8.6 10.0 %collective-permute-start.1 = (bf16[192,1664]{1,0:T(8,128)(2,1)}, bf16[192,1664]{1,0:T(8,128)(2,1)S(1)}, u32[]{:S(2)}, u32[]{:S(2)}) collective-permute-start(bf16[192,1664]{1,0:T(8,128)(2,1)} %get-tuple-element.14), channel_id=1, source_target_pairs={{0,16},{16,32},{32,48},{48,0},{1,17},{17,33},{33,49},{49,1},{2,18}... | collective-permute-start | bytes 1916936 | tf_op jit(solution)/shard_map/ppermute | solution.py:279
  18.7 2.8 %collective-permute-start.2 = (bf16[192,1664]{1,0:T(8,128)(2,1)}, bf16[192,1664]{1,0:T(8,128)(2,1)}, u32[]{:S(2)}, u32[]{:S(2)}) collective-permute-start(bf16[192,1664]{1,0:T(8,128)(2,1)} %get-tuple-element.15), channel_id=1, source_target_pairs={{0,48},{16,0},{32,16},{48,32},{1,49},{17,1},{33,17},{49,33},{2,50}... | collective-permute-start | bytes 1916936 | tf_op jit(solution)/shard_map/ppermute | solution.py:279
  21.4 1.4 %scaled_copies.1 = bf16[12,12,256]{2,1,0:T(8,128)(2,1)} custom-call(bf16[12,256]{1,0:T(8,128)(2,1)} %values, bf16[1,12]{1,0:T(2,128)(2,1)} %bitcast.3), custom_call_target="tpu_custom_call" | custom-call | tf_op jit(solution)/shard_map/scaled_copies/pallas_call | solution.py:265
  22.9 19.9 %all_to_all.20 = bf16[12,12,256]{2,1,0:T(8,128)(2,1)S(1)} all-to-all(bf16[12,12,256]{2,1,0:T(8,128)(2,1)} %scaled_copies.1), channel_id=1, replica_groups=mesh['z'=12,'x'=4,'yh'=2,'yl'=4,'c'=2] {'z'}, dimensions={0} | all-to-all | bytes 147456 | tf_op jit(solution)/shard_map/all_to_all | solution.py:297
  42.8 0.9 broadcast_in_dim.8
  43.7 7.1 %all-to-all-start.1 = ((bf16[8,144,256]{2,1,0:T(8,128)(2,1)}), bf16[8,144,256]{2,1,0:T(8,128)(2,1)S(1)}, u32[]{:S(2)}, u32[]{:S(2)}) async-start(bf16[8,144,256]{2,1,0:T(8,128)(2,1)} %broadcast_in_dim.8), calls=%async_computation.1 | async-start | bytes 1179648 | tf_op jit(solution)/shard_map/all_to_all | solution.py:275
  50.8 0.0 collective-permute-done.refs_1_
  50.8 0.0 collective-permute-done.1.refs_2_
  50.8 0.0 collective-permute-done.2.refs_3_
  50.8 0.0 copy-done.5
  50.8 0.0 copy-done.2
  50.8 2.5 %other_half.1 = bf16[256,1152]{1,0:T(8,128)(2,1)S(1)} custom-call(s32[2]{0:T(128)S(1)} %copy-done.5, bf16[192,1664]{1,0:T(8,128)(2,1)S(1)} %copy-done.2, bf16[192,1664]{1,0:T(8,128)(2,1)S(1)} %collective-permute-done.refs_1_, bf16[192,1664]{1,0:T(8,128)(2,1)S(1)} %collective-permute-done.1.refs_2_, bf16[192,1664]{1,0:T(8,128)(2,1)} %collective-permute-done.2.refs_3_), custom_call_target="tpu_custom_call" | custom-call | flops 45298483200 | bytes 2555904 | tf_op jit(solution)/shard_map/other_half/pallas_call | solution.py:109
  53.3 0.0 copy-start.4
  53.3 2.1 %collective-permute-start.3 = (bf16[256,1152]{1,0:T(8,128)(2,1)S(1)}, bf16[256,1152]{1,0:T(8,128)(2,1)S(1)}, u32[]{:S(2)}, u32[]{:S(2)}) collective-permute-start(bf16[256,1152]{1,0:T(8,128)(2,1)S(1)} %other_half.1), channel_id=1, source_target_pairs={{0,1},{1,0},{2,3},{3,2},{4,5},{5,4},{6,7},{7,6},{8,9},{9,8},{10,11... | collective-permute-start | bytes 1769480 | tf_op jit(solution)/shard_map/ppermute | solution.py:283
  55.4 2.0 %collective-permute-done.3.refs_4_ = bf16[256,1152]{1,0:T(8,128)(2,1)S(1)} collective-permute-done((bf16[256,1152]{1,0:T(8,128)(2,1)S(1)}, bf16[256,1152]{1,0:T(8,128)(2,1)S(1)}, u32[]{:S(2)}, u32[]{:S(2)}) %collective-permute-start.3) | collective-permute-done | bytes 589856 | tf_op jit(solution)/shard_map/ppermute | solution.py:283
  57.3 0.0 copy-done.3
  57.3 3.9 %own_half.1 = bf16[8,144,256]{2,1,0:T(8,128)(2,1)} custom-call(s32[2]{0:T(128)S(1)} %copy-done.5, bf16[192,1664]{1,0:T(8,128)(2,1)S(1)} %copy-done.2, bf16[192,1664]{1,0:T(8,128)(2,1)S(1)} %collective-permute-done.refs_1_, bf16[192,1664]{1,0:T(8,128)(2,1)S(1)} %collective-permute-done.1.refs_2_, bf16[192,1664]{1,0:T(8,128)(2,1)} %collective-permute-done.2.refs_3_, ...), custom_call_target="tpu_custom_call" | custom-call | flops 452984832 | bytes 2555904 | tf_op jit(solution)/shard_map/own_half/pallas_call | solution.py:109
  61.2 6.1 %all-to-all-done.1.parts = bf16[8,144,256]{2,1,0:T(8,128)(2,1)S(1)} async-done(((bf16[8,144,256]{2,1,0:T(8,128)(2,1)}), bf16[8,144,256]{2,1,0:T(8,128)(2,1)S(1)}, u32[]{:S(2)}, u32[]{:S(2)}) %all-to-all-start.1) | async-done | bytes 589856 | tf_op jit(solution)/shard_map/all_to_all | solution.py:275
  67.3 0.0 copy-done.4
  67.3 0.9 regroup.1.refs_0_
  68.2 3.7 %collective-permute-start.6 = (bf16[12,96,256]{2,1,0:T(8,128)(2,1)S(1)}, bf16[12,96,256]{2,1,0:T(8,128)(2,1)}, u32[]{:S(2)}, u32[]{:S(2)}) collective-permute-start(bf16[12,96,256]{2,1,0:T(8,128)(2,1)S(1)} %regroup.1.refs_0_), channel_id=1, source_target_pairs={{0,32},{16,48},{32,0},{48,16},{1,33},{17,49},{33,1},{49,17},{2,34}... | collective-permute-start | bytes 1769480 | tf_op jit(solution)/shard_map/ppermute | solution.py:279
  71.9 3.1 %collective-permute-start.5 = (bf16[12,96,256]{2,1,0:T(8,128)(2,1)S(1)}, bf16[12,96,256]{2,1,0:T(8,128)(2,1)}, u32[]{:S(2)}, u32[]{:S(2)}) collective-permute-start(bf16[12,96,256]{2,1,0:T(8,128)(2,1)S(1)} %regroup.1.refs_0_), channel_id=1, source_target_pairs={{0,16},{16,32},{32,48},{48,0},{1,17},{17,33},{33,49},{49,1},{2,18}... | collective-permute-start | bytes 1769480 | tf_op jit(solution)/shard_map/ppermute | solution.py:279
  75.0 2.8 %collective-permute-start.4 = (bf16[12,96,256]{2,1,0:T(8,128)(2,1)S(1)}, bf16[12,96,256]{2,1,0:T(8,128)(2,1)}, u32[]{:S(2)}, u32[]{:S(2)}) collective-permute-start(bf16[12,96,256]{2,1,0:T(8,128)(2,1)S(1)} %regroup.1.refs_0_), channel_id=1, source_target_pairs={{0,48},{16,0},{32,16},{48,32},{1,49},{17,1},{33,17},{49,33},{2,50}... | collective-permute-start | bytes 1769480 | tf_op jit(solution)/shard_map/ppermute | solution.py:279
  77.8 3.6 %all-to-all-start.2 = ((bf16[8,144,256]{2,1,0:T(8,128)(2,1)}), bf16[8,144,256]{2,1,0:T(8,128)(2,1)S(1)}, u32[]{:S(2)}, u32[]{:S(2)}) async-start(bf16[8,144,256]{2,1,0:T(8,128)(2,1)} %own_half.1), calls=%async_computation.2 | async-start | bytes 1179648 | tf_op jit(solution)/shard_map/all_to_all | solution.py:304
  81.3 1.9 %collective-permute-start.7 = (bf16[12,96,256]{2,1,0:T(8,128)(2,1)S(1)}, bf16[12,96,256]{2,1,0:T(8,128)(2,1)}, u32[]{:S(2)}, u32[]{:S(2)}) collective-permute-start(bf16[12,96,256]{2,1,0:T(8,128)(2,1)S(1)} %regroup.1.refs_0_), channel_id=1, source_target_pairs={{0,1},{1,0},{2,3},{3,2},{4,5},{5,4},{6,7},{7,6},{8,9},{9,8},{10,11... | collective-permute-start | bytes 1769480 | tf_op jit(solution)/shard_map/ppermute | solution.py:283
  83.3 4.8 %collective-permute-done.6.refs_3_ = bf16[12,96,256]{2,1,0:T(8,128)(2,1)} collective-permute-done((bf16[12,96,256]{2,1,0:T(8,128)(2,1)S(1)}, bf16[12,96,256]{2,1,0:T(8,128)(2,1)}, u32[]{:S(2)}, u32[]{:S(2)}) %collective-permute-start.6) | collective-permute-done | bytes 589856 | tf_op jit(solution)/shard_map/ppermute | solution.py:279
  88.0 1.9 %collective-permute-start.10 = (bf16[12,96,256]{2,1,0:T(8,128)(2,1)}, bf16[12,96,256]{2,1,0:T(8,128)(2,1)}, u32[]{:S(2)}, u32[]{:S(2)}) collective-permute-start(bf16[12,96,256]{2,1,0:T(8,128)(2,1)} %collective-permute-done.6.refs_3_), channel_id=1, source_target_pairs={{0,1},{1,0},{2,3},{3,2},{4,5},{5,4},{6,7},{7,6},{8,9},{9,8},{10,11... | collective-permute-start | bytes 1769480 | tf_op jit(solution)/shard_map/ppermute | solution.py:283
  89.9 6.9 %collective-permute-done.5.refs_2_ = bf16[12,96,256]{2,1,0:T(8,128)(2,1)} collective-permute-done((bf16[12,96,256]{2,1,0:T(8,128)(2,1)S(1)}, bf16[12,96,256]{2,1,0:T(8,128)(2,1)}, u32[]{:S(2)}, u32[]{:S(2)}) %collective-permute-start.5) | collective-permute-done | bytes 589856 | tf_op jit(solution)/shard_map/ppermute | solution.py:279
  96.8 1.9 %collective-permute-start.9 = (bf16[12,96,256]{2,1,0:T(8,128)(2,1)}, bf16[12,96,256]{2,1,0:T(8,128)(2,1)}, u32[]{:S(2)}, u32[]{:S(2)}) collective-permute-start(bf16[12,96,256]{2,1,0:T(8,128)(2,1)} %collective-permute-done.5.refs_2_), channel_id=1, source_target_pairs={{0,1},{1,0},{2,3},{3,2},{4,5},{5,4},{6,7},{7,6},{8,9},{9,8},{10,11... | collective-permute-start | bytes 1769480 | tf_op jit(solution)/shard_map/ppermute | solution.py:283
  98.7 0.0 collective-permute-done.4.refs_1_
  98.8 2.4 %collective-permute-start.8 = (bf16[12,96,256]{2,1,0:T(8,128)(2,1)}, bf16[12,96,256]{2,1,0:T(8,128)(2,1)}, u32[]{:S(2)}, u32[]{:S(2)}) collective-permute-start(bf16[12,96,256]{2,1,0:T(8,128)(2,1)} %collective-permute-done.4.refs_1_), channel_id=1, source_target_pairs={{0,1},{1,0},{2,3},{3,2},{4,5},{5,4},{6,7},{7,6},{8,9},{9,8},{10,11... | collective-permute-start | bytes 1769480 | tf_op jit(solution)/shard_map/ppermute | solution.py:283
  101.2 0.0 all-to-all-done.2.parts
  101.2 0.7 sum_over_y.1
  101.9 3.5 %all-to-all-start.3 = ((bf16[12,12,256]{2,1,0:T(8,128)(2,1)}), bf16[12,12,256]{2,1,0:T(8,128)(2,1)S(1)}, u32[]{:S(2)}, u32[]{:S(2)}) async-start(bf16[12,12,256]{2,1,0:T(8,128)(2,1)} %sum_over_y.1), calls=%async_computation.3 | async-start | bytes 196608 | tf_op jit(solution)/shard_map/all_to_all | solution.py:306
  105.4 0.0 collective-permute-done.7.refs_4_
  105.4 0.0 collective-permute-done.10.refs_7_
  105.4 0.0 collective-permute-done.9.refs_6_
  105.4 0.0 collective-permute-done.8.refs_5_
  105.5 0.0 copy-done
  105.5 0.0 copy-done.1
  105.5 7.1 %project.1 = (bf16[192,512]{1,0:T(8,128)(2,1)}, bf16[192,4608]{1,0:T(8,128)(2,1)}) custom-call(s32[2]{0:T(128)S(1)} %copy-done.5, bf16[12,96,256]{2,1,0:T(8,128)(2,1)S(1)} %regroup.1.refs_0_, bf16[12,96,256]{2,1,0:T(8,128)(2,1)} %collective-permute-done.4.refs_1_, bf16[12,96,256]{2,1,0:T(8,128)(2,1)} %collective-permute-done.5.refs_2_, ...), custom_call_target="tpu_custom_call" | custom-call | flops 1811939328 | bytes 8257536 | tf_op jit(solution)/shard_map/project/pallas_call | solution.py:219
  112.6 5.0 %all-to-all-done.3 = bf16[12,12,256]{2,1,0:T(8,128)(2,1)S(1)} async-done(((bf16[12,12,256]{2,1,0:T(8,128)(2,1)}), bf16[12,12,256]{2,1,0:T(8,128)(2,1)S(1)}, u32[]{:S(2)}, u32[]{:S(2)}) %all-to-all-start.3) | async-done | bytes 73760 | tf_op jit(solution)/shard_map/all_to_all | solution.py:306
  117.6 0.6 broadcast_multiply_fusion
  (5 shorter events, 0.0 us)
Async XLA Ops:
  1.2 49.6 %copy-start.5 = (s32[2]{0:T(128)S(1)}, s32[2]{0:T(128)}, u32[]{:S(2)}) copy-start(s32[2]{0:T(128)} %pad_add_fusion.place) | copy-start | bytes 28
  5.2 45.6 %copy-start.2 = (bf16[192,1664]{1,0:T(8,128)(2,1)S(1)}, bf16[192,1664]{1,0:T(8,128)(2,1)}, u32[]{:S(2)}) copy-start(bf16[192,1664]{1,0:T(8,128)(2,1)} %get-tuple-element.11.refs_0_) | copy-start | bytes 1916932
  5.2 45.6 %collective-permute-start = (bf16[192,1664]{1,0:T(8,128)(2,1)}, bf16[192,1664]{1,0:T(8,128)(2,1)S(1)}, u32[]{:S(2)}, u32[]{:S(2)}) collective-permute-start(bf16[192,1664]{1,0:T(8,128)(2,1)} %get-tuple-element.13), channel_id=1, source_target_pairs={{0,32},{16,48},{32,0},{48,16},{1,33},{17,49},{33,1},{49,17},{2,34}... | collective-permute-start | bytes 1916936 | tf_op jit(solution)/shard_map/ppermute | solution.py:279
  8.6 42.2 %collective-permute-start.1 = (bf16[192,1664]{1,0:T(8,128)(2,1)}, bf16[192,1664]{1,0:T(8,128)(2,1)S(1)}, u32[]{:S(2)}, u32[]{:S(2)}) collective-permute-start(bf16[192,1664]{1,0:T(8,128)(2,1)} %get-tuple-element.14), channel_id=1, source_target_pairs={{0,16},{16,32},{32,48},{48,0},{1,17},{17,33},{33,49},{49,1},{2,18}... | collective-permute-start | bytes 1916936 | tf_op jit(solution)/shard_map/ppermute | solution.py:279
  18.7 32.1 %collective-permute-start.2 = (bf16[192,1664]{1,0:T(8,128)(2,1)}, bf16[192,1664]{1,0:T(8,128)(2,1)}, u32[]{:S(2)}, u32[]{:S(2)}) collective-permute-start(bf16[192,1664]{1,0:T(8,128)(2,1)} %get-tuple-element.15), channel_id=1, source_target_pairs={{0,48},{16,0},{32,16},{48,32},{1,49},{17,1},{33,17},{49,33},{2,50}... | collective-permute-start | bytes 1916936 | tf_op jit(solution)/shard_map/ppermute | solution.py:279
  43.7 23.6 %all-to-all-start.1 = ((bf16[8,144,256]{2,1,0:T(8,128)(2,1)}), bf16[8,144,256]{2,1,0:T(8,128)(2,1)S(1)}, u32[]{:S(2)}, u32[]{:S(2)}) async-start(bf16[8,144,256]{2,1,0:T(8,128)(2,1)} %broadcast_in_dim.8), calls=%async_computation.1 | async-start | bytes 1179648 | tf_op jit(solution)/shard_map/all_to_all | solution.py:275
  50.8 6.6 %copy-start.3 = (bf16[384,384]{1,0:T(8,128)(2,1)S(1)}, bf16[384,384]{1,0:T(8,128)(2,1)}, u32[]{:S(2)}) copy-start(bf16[384,384]{1,0:T(8,128)(2,1)} %constant.18.clone.refs_5_) | copy-start | bytes 884740
  53.3 14.0 %copy-start.4 = (bf16[384,384]{1,0:T(8,128)(2,1)S(1)}, bf16[384,384]{1,0:T(8,128)(2,1)}, u32[]{:S(2)}) copy-start(bf16[384,384]{1,0:T(8,128)(2,1)} %constant.19.clone.perm) | copy-start | bytes 884740
  53.3 4.0 %collective-permute-start.3 = (bf16[256,1152]{1,0:T(8,128)(2,1)S(1)}, bf16[256,1152]{1,0:T(8,128)(2,1)S(1)}, u32[]{:S(2)}, u32[]{:S(2)}) collective-permute-start(bf16[256,1152]{1,0:T(8,128)(2,1)S(1)} %other_half.1), channel_id=1, source_target_pairs={{0,1},{1,0},{2,3},{3,2},{4,5},{5,4},{6,7},{7,6},{8,9},{9,8},{10,11... | collective-permute-start | bytes 1769480 | tf_op jit(solution)/shard_map/ppermute | solution.py:283
  61.2 44.2 %copy-start = (bf16[192,4608]{1,0:T(8,128)(2,1)S(1)}, bf16[192,4608]{1,0:T(8,128)(2,1)}, u32[]{:S(2)}) copy-start(bf16[192,4608]{1,0:T(8,128)(2,1)} %refs_8_.1) | copy-start | bytes 5308420
  61.2 44.2 %copy-start.1 = (bf16[192,512]{1,0:T(8,128)(2,1)S(1)}, bf16[192,512]{1,0:T(8,128)(2,1)}, u32[]{:S(2)}) copy-start(bf16[192,512]{1,0:T(8,128)(2,1)} %refs_10_.1) | copy-start | bytes 589828
  68.2 19.8 %collective-permute-start.6 = (bf16[12,96,256]{2,1,0:T(8,128)(2,1)S(1)}, bf16[12,96,256]{2,1,0:T(8,128)(2,1)}, u32[]{:S(2)}, u32[]{:S(2)}) collective-permute-start(bf16[12,96,256]{2,1,0:T(8,128)(2,1)S(1)} %regroup.1.refs_0_), channel_id=1, source_target_pairs={{0,32},{16,48},{32,0},{48,16},{1,33},{17,49},{33,1},{49,17},{2,34}... | collective-permute-start | bytes 1769480 | tf_op jit(solution)/shard_map/ppermute | solution.py:279
  71.9 24.9 %collective-permute-start.5 = (bf16[12,96,256]{2,1,0:T(8,128)(2,1)S(1)}, bf16[12,96,256]{2,1,0:T(8,128)(2,1)}, u32[]{:S(2)}, u32[]{:S(2)}) collective-permute-start(bf16[12,96,256]{2,1,0:T(8,128)(2,1)S(1)} %regroup.1.refs_0_), channel_id=1, source_target_pairs={{0,16},{16,32},{32,48},{48,0},{1,17},{17,33},{33,49},{49,1},{2,18}... | collective-permute-start | bytes 1769480 | tf_op jit(solution)/shard_map/ppermute | solution.py:279
  75.0 23.7 %collective-permute-start.4 = (bf16[12,96,256]{2,1,0:T(8,128)(2,1)S(1)}, bf16[12,96,256]{2,1,0:T(8,128)(2,1)}, u32[]{:S(2)}, u32[]{:S(2)}) collective-permute-start(bf16[12,96,256]{2,1,0:T(8,128)(2,1)S(1)} %regroup.1.refs_0_), channel_id=1, source_target_pairs={{0,48},{16,0},{32,16},{48,32},{1,49},{17,1},{33,17},{49,33},{2,50}... | collective-permute-start | bytes 1769480 | tf_op jit(solution)/shard_map/ppermute | solution.py:279
  77.8 23.4 %all-to-all-start.2 = ((bf16[8,144,256]{2,1,0:T(8,128)(2,1)}), bf16[8,144,256]{2,1,0:T(8,128)(2,1)S(1)}, u32[]{:S(2)}, u32[]{:S(2)}) async-start(bf16[8,144,256]{2,1,0:T(8,128)(2,1)} %own_half.1), calls=%async_computation.2 | async-start | bytes 1179648 | tf_op jit(solution)/shard_map/all_to_all | solution.py:304
  81.3 24.1 %collective-permute-start.7 = (bf16[12,96,256]{2,1,0:T(8,128)(2,1)S(1)}, bf16[12,96,256]{2,1,0:T(8,128)(2,1)}, u32[]{:S(2)}, u32[]{:S(2)}) collective-permute-start(bf16[12,96,256]{2,1,0:T(8,128)(2,1)S(1)} %regroup.1.refs_0_), channel_id=1, source_target_pairs={{0,1},{1,0},{2,3},{3,2},{4,5},{5,4},{6,7},{7,6},{8,9},{9,8},{10,11... | collective-permute-start | bytes 1769480 | tf_op jit(solution)/shard_map/ppermute | solution.py:283
  88.0 17.4 %collective-permute-start.10 = (bf16[12,96,256]{2,1,0:T(8,128)(2,1)}, bf16[12,96,256]{2,1,0:T(8,128)(2,1)}, u32[]{:S(2)}, u32[]{:S(2)}) collective-permute-start(bf16[12,96,256]{2,1,0:T(8,128)(2,1)} %collective-permute-done.6.refs_3_), channel_id=1, source_target_pairs={{0,1},{1,0},{2,3},{3,2},{4,5},{5,4},{6,7},{7,6},{8,9},{9,8},{10,11... | collective-permute-start | bytes 1769480 | tf_op jit(solution)/shard_map/ppermute | solution.py:283
  96.8 8.6 %collective-permute-start.9 = (bf16[12,96,256]{2,1,0:T(8,128)(2,1)}, bf16[12,96,256]{2,1,0:T(8,128)(2,1)}, u32[]{:S(2)}, u32[]{:S(2)}) collective-permute-start(bf16[12,96,256]{2,1,0:T(8,128)(2,1)} %collective-permute-done.5.refs_2_), channel_id=1, source_target_pairs={{0,1},{1,0},{2,3},{3,2},{4,5},{5,4},{6,7},{7,6},{8,9},{9,8},{10,11... | collective-permute-start | bytes 1769480 | tf_op jit(solution)/shard_map/ppermute | solution.py:283
  98.8 6.7 %collective-permute-start.8 = (bf16[12,96,256]{2,1,0:T(8,128)(2,1)}, bf16[12,96,256]{2,1,0:T(8,128)(2,1)}, u32[]{:S(2)}, u32[]{:S(2)}) collective-permute-start(bf16[12,96,256]{2,1,0:T(8,128)(2,1)} %collective-permute-done.4.refs_1_), channel_id=1, source_target_pairs={{0,1},{1,0},{2,3},{3,2},{4,5},{5,4},{6,7},{7,6},{8,9},{9,8},{10,11... | collective-permute-start | bytes 1769480 | tf_op jit(solution)/shard_map/ppermute | solution.py:283
  101.9 15.7 %all-to-all-start.3 = ((bf16[12,12,256]{2,1,0:T(8,128)(2,1)}), bf16[12,12,256]{2,1,0:T(8,128)(2,1)S(1)}, u32[]{:S(2)}, u32[]{:S(2)}) async-start(bf16[12,12,256]{2,1,0:T(8,128)(2,1)} %sum_over_y.1), calls=%async_computation.3 | async-start | bytes 196608 | tf_op jit(solution)/shard_map/all_to_all | solution.py:306
